TPU v7x, 256 devices: a whole 4x4x8 slice. The times are simulated.
256 devices in a mesh: seq: 32 (over y_lo, z, core), head: 8 (over y_hi, x).
Axes of the slice: x: 4, y: 4 (y_hi: 2, y_lo: 2; y = y_hi * 2 + y_lo), z: 8, core: 2. Of those that a mesh axis runs over, the one named last changes fastest.
Arguments:
- cotangent: bfloat16 [4096, 6144], P('seq', 'head'), may hold values from -0.1875 to 0.1875
- queries: bfloat16 [4096, 8192], P('seq', 'head'), may hold values from -0.5 to 0.5
- key_proj: bfloat16 [4096, 8192], P('seq', 'head'), may hold values from -0.5 to 0.5
- value_proj: bfloat16 [4096, 8192], P('seq', 'head'), may hold values from -1.5 to 1.5
- log_decay: float32 [4096, 64], P('seq', 'head'), may hold values from -0.8 to 0
- out_weight: bfloat16 [6144, 8192], P('seq', 'head'), may hold values from -0.0625 to 0.0625
Outputs:
- grad_queries: bfloat16 [4096, 8192], P('seq', 'head')
- grad_keys: bfloat16 [4096, 8192], P('seq', 'head')
- grad_values: bfloat16 [4096, 8192], P('seq', 'head')
- grad_weight: bfloat16 [6144, 8192], P('seq', 'head')
All inputs are finite; a program needn't handle non-finite values.
Results may differ from a plain program's by a relative error of at most 0.03.
Values may be sent and summed in bfloat16 or wider, within the bound.
No kernel may reach another device: no remote copies, remote signals or barrier semaphores. Data moves between devices by JAX's collectives and lax.ppermute only.
A program may use at most 128 MiB of HBM per device.

v0:
```python
import jax
import jax.numpy as jnp
from jax import lax
from jax.sharding import PartitionSpec as P

HEAD_DIM = 128
BLOCK = 128


def entering(array, axis, combine, identity, reverse):
    devices, position = (lax.axis_size(axis), lax.axis_index(axis))
    everything = jax.tree.map(lambda part: lax.all_gather(part, axis), array)
    start = jax.tree.map(
        lambda part, zero: jnp.broadcast_to(jnp.asarray(zero, part.dtype), part.shape),
        array,
        identity,
    )

    def turn(k, before):
        at = devices - 1 - k if reverse else k
        reached = at > position if reverse else at < position
        new = combine(before, jax.tree.map(lambda part: part[at], everything))
        return jax.tree.map(lambda a, b: jnp.where(reached, a, b), new, before)

    return lax.fori_loop(0, devices, turn, start)


def advance(running, element):
    factor, addend = element
    return (jnp.exp(factor)[:, None, None] * running + addend, running)


def chain_link(earlier, subsequent):
    return (earlier[0] * subsequent[0], subsequent[0][:, None, None] * earlier[1] + subsequent[1])


def body(cotangent, queries, key_proj, value_proj, log_decay, out_weight):
    row_count = queries.shape[0]
    col_count = queries.shape[1]
    head_count = col_count // HEAD_DIM
    block_count = row_count // BLOCK
    gathered = lax.all_gather(cotangent, "head", axis=1, tiled=True)
    columns = gathered
    grad_attn = jnp.dot(
        columns,
        lax.all_gather(out_weight, "seq", axis=0, tiled=True),
        preferred_element_type=jnp.float32,
    ).astype(jnp.bfloat16)
    block_shape = (block_count, BLOCK, head_count, HEAD_DIM)
    query_blk = queries.reshape(block_shape)
    key_blk = key_proj.reshape(block_shape)
    value_blk = value_proj.reshape(block_shape)
    grad_blk = grad_attn.reshape(block_shape)
    decays = log_decay.reshape(block_count, BLOCK, head_count)
    within = jnp.cumsum(decays, axis=1)
    block_decay = within[:, -1, :]
    key_weight = jnp.exp(block_decay[:, None, :] - within)
    query_weight = jnp.exp(within)
    zero_state = jnp.zeros((head_count, HEAD_DIM, HEAD_DIM), jnp.float32)
    device_decay = jnp.exp(jnp.sum(block_decay, axis=0))
    identity = (jnp.ones_like(device_decay), zero_state)
    key_scaled = (key_weight[..., None] * key_blk).astype(jnp.bfloat16)
    key_terms = jnp.einsum(
        "nbhe,nbhf->nhef", key_scaled, value_blk, preferred_element_type=jnp.float32
    )
    local_end, local_before = lax.scan(advance, zero_state, (block_decay, key_terms))
    _, incoming = entering((device_decay, local_end), "seq", chain_link, identity, False)
    leading = jnp.exp(jnp.cumsum(block_decay, axis=0) - block_decay)
    states_before = leading[:, :, None, None] * incoming[None] + local_before
    query_scaled = (query_weight[..., None] * query_blk).astype(jnp.bfloat16)
    query_terms = jnp.einsum(
        "nbhe,nbhf->nhef", query_scaled, grad_blk, preferred_element_type=jnp.float32
    )
    local_start, local_after = lax.scan(
        advance, zero_state, (block_decay, query_terms), reverse=True
    )
    _, returning = entering((device_decay, local_start), "seq", chain_link, identity, True)
    trailing = jnp.exp(jnp.flip(jnp.cumsum(jnp.flip(block_decay, 0), axis=0), 0) - block_decay)
    states_after = trailing[:, :, None, None] * returning[None] + local_after
    states_low = states_before.astype(jnp.bfloat16)
    after_low = states_after.astype(jnp.bfloat16)
    within_heads = jnp.transpose(within, (0, 2, 1))
    gaps = within_heads[:, :, :, None] - within_heads[:, :, None, :]
    causal = jnp.arange(BLOCK)[:, None] >= jnp.arange(BLOCK)[None, :]
    mask = jnp.exp(jnp.where(causal[None, None], gaps, -jnp.inf))
    scores = (
        jnp.einsum("nthe,nshe->nhts", query_blk, key_blk, preferred_element_type=jnp.float32) * mask
    ).astype(jnp.bfloat16)
    attended = query_weight[..., None] * jnp.einsum(
        "nthe,nhef->nthf", query_blk, states_low, preferred_element_type=jnp.float32
    )
    attended = attended + jnp.einsum(
        "nhts,nshf->nthf", scores, value_blk, preferred_element_type=jnp.float32
    )
    attended = attended.astype(jnp.bfloat16).reshape(row_count, col_count)
    grad_scores = (
        jnp.einsum("nthf,nshf->nhts", grad_blk, value_blk, preferred_element_type=jnp.float32)
        * mask
    ).astype(jnp.bfloat16)
    grad_queries = query_weight[..., None] * jnp.einsum(
        "nthf,nhef->nthe", grad_blk, states_low, preferred_element_type=jnp.float32
    )
    grad_queries = grad_queries + jnp.einsum(
        "nhts,nshe->nthe", grad_scores, key_blk, preferred_element_type=jnp.float32
    )
    grad_keys = key_weight[..., None] * jnp.einsum(
        "nshf,nhef->nshe", value_blk, after_low, preferred_element_type=jnp.float32
    )
    grad_keys = grad_keys + jnp.einsum(
        "nhts,nthe->nshe", grad_scores, query_blk, preferred_element_type=jnp.float32
    )
    grad_values = key_weight[..., None] * jnp.einsum(
        "nshe,nhef->nshf", key_blk, after_low, preferred_element_type=jnp.float32
    )
    grad_values = grad_values + jnp.einsum(
        "nhts,nthf->nshf", scores, grad_blk, preferred_element_type=jnp.float32
    )
    columns = gathered
    grad_weight = lax.psum_scatter(
        lax.dot_general(
            columns, attended, (((0,), (0,)), ((), ())), preferred_element_type=jnp.float32
        ).astype(jnp.bfloat16),
        "seq",
        scatter_dimension=0,
        tiled=True,
    )
    return (
        grad_queries.reshape(row_count, col_count).astype(jnp.bfloat16),
        grad_keys.reshape(row_count, col_count).astype(jnp.bfloat16),
        grad_values.reshape(row_count, col_count).astype(jnp.bfloat16),
        grad_weight,
    )


def solution(mesh):
    placed = (
        P("seq", "head"),
        P("seq", "head"),
        P("seq", "head"),
        P("seq", "head"),
        P("seq", "head"),
        P("seq", "head"),
    )
    return jax.shard_map(
        body,
        mesh=mesh,
        in_specs=placed,
        out_specs=(P("seq", "head"), P("seq", "head"), P("seq", "head"), P("seq", "head")),
        check_vma=False,
    )
```

profile of v0, /device:TPU:8, one launch (start us, length us, event | category | flops | bytes accessed | tf_op | source)
XLA Modules:
  0.0 499.6 jit_solution(15544030766121163034)
XLA Ops:
  14.4 54.2 %all-gather.8.cloned.1.call-done = bf16[128,6144]{1,0:T(8,128)(2,1)} async-done(((bf16[128,768]{1,0:T(8,128)(2,1)}), bf16[128,6144]{1,0:T(8,128)(2,1)}) %all-gather.8.cloned.1.call-update) | async-done | bytes 1572880 | tf_op jit(solution)/shard_map/all_gather | solution.py:42
  68.6 81.4 %all-gather.10.cloned.1.call-done = bf16[6144,1024]{1,0:T(8,128)(2,1)} async-done(((bf16[192,1024]{1,0:T(8,128)(2,1)}), bf16[6144,1024]{1,0:T(8,128)(2,1)}) %all-gather.10.cloned.1.call-update) | async-done | bytes 12582928 | tf_op jit(solution)/shard_map/all_gather | solution.py:46
  150.0 6.9 %convolution_convert_fusion = bf16[128,1024]{1,0:T(8,128)(2,1)S(1)} fusion(bf16[128,6144]{1,0:T(8,128)(2,1)} %all-gather.8.cloned.1.call-done, bf16[6144,1024]{1,0:T(8,128)(2,1)} %all-gather.10.cloned.1.call-done), kind=kOutput, calls=%fused_computation.27 | convolution fusion | flops 1610743808 | bytes 14417920 | tf_op jit(solution)/shard_map/dot_general | solution.py:44
  158.3 32.5 %all-gather = f32[32,1,8]{2,1,0:T(1,128)S(1)} all-gather(f32[1,1,8]{2,1,0:T(1,128)S(1)} %get-tuple-element.333), channel_id=2, replica_groups=mesh['seq'=32,'head'=8] {'seq'}, dimensions={0}, use_global_device_ids=true | all-gather | bytes 1056 | tf_op jit(solution)/shard_map/all_gather | solution.py:12
  192.3 59.6 %all-gather.12.cloned.1.call-done = f32[256,128,128]{2,1,0:T(8,128)} async-done(((f32[8,128,128]{2,1,0:T(8,128)}), f32[256,128,128]{2,1,0:T(8,128)}) %all-gather.12.cloned.1.call-update) | async-done | bytes 16777232 | tf_op jit(solution)/shard_map/all_gather | solution.py:12
  251.9 39.2 %while.40 = (s32[]{:T(128)}, f32[8,128,128]{2,1,0:T(8,128)S(1)}, s32[]{:T(128)}, f32[32,8]{1,0:T(8,128)S(1)}, f32[32,8,128,128]{3,2,1,0:T(8,128)}, /*index=5*/s32[]{:T(128)}, s32[]{:T(128)}) while((s32[]{:T(128)}, f32[8,128,128]{2,1,0:T(8,128)S(1)}, s32[]{:T(128)}, f32[32,8]{1,0:T(8,128)S(1)}, f32[32,8,128,128]{3,2,1,0:T(8,128)}, ...), condition=%wide.region_2.3_spmd.clone, body=%wide.region_1.2_spmd.clone.sunk | while | flops 524292 | bytes 1573065 | solution.py:25
  265.2 1.3 fusion.43
  269.0 1.2 fusion.43
  272.7 1.2 fusion.43
  273.9 1.2 fusion.43
  277.6 1.2 fusion.43
  282.5 1.2 fusion.43
  283.7 1.2 fusion.43
  287.4 1.2 fusion.43
  291.0 1.4 fusion.10
  292.4 6.5 %convert_bitcast_fusion = bf16[6144,1024]{0,1:T(8,128)(2,1)} fusion(bf16[128,1024]{0,1:T(8,128)(2,1)S(1)} %bitcast.149, bf16[128,6144]{1,0:T(8,128)(2,1)S(1)} %copy-done), kind=kOutput, calls=%fused_computation.6 | convolution fusion | flops 1616904192 | bytes 14417920 | tf_op jit(solution)/shard_map/dot_general | solution.py:120
  298.9 16.7 %copy.96 = bf16[6144,1024]{1,0:T(8,128)(2,1)} copy(bf16[6144,1024]{0,1:T(8,128)(2,1)} %convert_bitcast_fusion) | data formatting | bytes 25165824
  317.9 35.8 %all-gather.14.cloned.1.call-done = f32[256,128,128]{2,1,0:T(8,128)} async-done(((f32[8,128,128]{2,1,0:T(8,128)}), f32[256,128,128]{2,1,0:T(8,128)}) %all-gather.14.cloned.1.call-update) | async-done | bytes 16777232 | tf_op jit(solution)/shard_map/all_gather | solution.py:12
  353.7 39.4 %while.41 = (s32[]{:T(128)}, f32[8,128,128]{2,1,0:T(8,128)S(1)}, s32[]{:T(128)}, f32[32,8]{1,0:T(8,128)S(1)}, f32[32,8,128,128]{3,2,1,0:T(8,128)}, /*index=5*/s32[]{:T(128)}, s32[]{:T(128)}, s32[]{:T(128)}, s32[]{:T(128)}) while((s32[]{:T(128)}, f32[8,128,128]{2,1,0:T(8,128)S(1)}, s32[]{:T(128)}, f32[32,8]{1,0:T(8,128)S(1)}, ...), condition=%wide.region_4.5_spmd.clone, body=%wide.region_3.4_spmd.clone.sunk | while | flops 524296 | bytes 1573127 | solution.py:25
  368.5 1.2 fusion.44
  373.4 1.2 fusion.44
  374.6 1.2 fusion.44
  375.9 1.2 fusion.44
  377.1 1.2 fusion.44
  380.8 1.2 fusion.44
  382.0 1.2 fusion.44
  384.5 1.2 fusion.44
  385.8 1.2 fusion.44
  389.4 1.2 fusion.44
  390.7 1.2 fusion.44
  391.9 1.2 fusion.44
  395.5 97.6 %reduce-scatter.4.cloned.1.call-done = bf16[192,1024]{1,0:T(8,128)(2,1)} async-done(((bf16[6144,1024]{1,0:T(8,128)(2,1)}), bf16[192,1024]{1,0:T(8,128)(2,1)}) %reduce-scatter.4.cloned.1.call-update) | async-done | bytes 393232
  (148 shorter events, 66.8 us)
Async XLA Ops:
  7.2 61.4 %all-gather.8.cloned.1.call-start = ((), (), s32[]{:S(2)}) async-start(), calls=%async_computation.1 | async-start | bytes 1769472 | tf_op jit(solution)/shard_map/all_gather | solution.py:42
  7.9 142.1 %all-gather.10.cloned.1.call-start = ((), (), s32[]{:S(2)}) async-start(), calls=%async_computation.2 | async-start | bytes 12976128 | tf_op jit(solution)/shard_map/all_gather | solution.py:46
  8.6 243.2 %all-gather.12.cloned.1.call-start = ((), (), s32[]{:S(2)}) async-start(), calls=%async_computation.3 | async-start | bytes 17301504 | tf_op jit(solution)/shard_map/all_gather | solution.py:12
  13.2 340.6 %all-gather.14.cloned.1.call-start = ((), (), s32[]{:S(2)}) async-start(), calls=%async_computation.4 | async-start | bytes 17301504 | tf_op jit(solution)/shard_map/all_gather | solution.py:12
  68.6 223.8 %copy-start = (bf16[128,6144]{1,0:T(8,128)(2,1)S(1)}, bf16[128,6144]{1,0:T(8,128)(2,1)}, u32[]{:S(2)}) copy-start(bf16[128,6144]{1,0:T(8,128)(2,1)} %all-gather.8.cloned.1.call-done) | copy-start | bytes 4718596
  158.2 334.8 %reduce-scatter.4.cloned.1.call-start = ((), (), s32[]{:S(2)}) async-start(), calls=%async_computation.5 | async-start | bytes 12976128
Sparse Core Ops, SparseCore 0:
  10.6 57.9 all-gather.7
  70.4 79.5 all-gather.9
  151.9 99.9 all-gather.11
  253.6 100.1 all-gather.13
  356.7 136.2 reduce-scatter.3
where the time goes:
time: 504 us; the launch traced here: 500 us
  waiting for transfers between devices  330 us (65%)
  other arithmetic  75.9 us (15%)
  blocking collectives  32.5 us (6%)
  local copies, waits for them, and re-layouts  24.3 us (5%)
  matrix products  20.3 us (4%)
  between operations  13.9 us (3%)
    unnamed x6, waiting for transfers between devices  99 us
    all_gather x2, waiting for transfers between devices, entering(): everything = jax.tree.map(lambda part: lax.all_gather(part, axis), array)  95.4 us
    all_gather x1, waiting for transfers between devices, body(): lax.all_gather(out_weight, 'seq', axis=0, tiled=True)  81.4 us
    select_n x64, other arithmetic, turn(): return jax.tree.map(lambda a, b: jnp.where(reached, a, b), new, before)  75.6 us
    all_gather x1, waiting for transfers between devices, body(): gathered = lax.all_gather(cotangent, 'head', axis=1, tiled=True)  54.2 us
    all_gather x1, blocking collectives, entering(): everything = jax.tree.map(lambda part: lax.all_gather(part, axis), array)  32.5 us
    unnamed x6, local copies, waits for them, and re-layouts  19.3 us
  transfers between devices with their start and end apart: 5, of which 5 were waited for; matrix products, arithmetic and copies ran while one was open for 24% of the time, Pallas kernels for 0%

commit v1 on v0

v1 whole, which is shorter than its diff:
```python
import functools

import jax
import jax.numpy as jnp
from jax import lax
from jax.experimental import pallas as pl
from jax.experimental.pallas import tpu as pltpu
from jax.sharding import PartitionSpec as P

HEAD_DIM = 128
BLOCK = 128
HEADS_LOCAL = 8
N_SEQ = 32
ROWS = 32
NZ = 8
BF = jnp.bfloat16
F32 = jnp.float32
AXES = ("seq", "head")
PARAMS = pltpu.CompilerParams(vmem_limit_bytes=48 * 1024 * 1024)


def pairs(move):
    out = []
    for yl in range(2):
        for z in range(8):
            for c in range(2):
                for yh in range(2):
                    for x in range(4):
                        a, b, d, e, f = move(yl, z, c, yh, x)
                        out.append(
                            (
                                (yl * 16 + z * 2 + c) * 8 + yh * 4 + x,
                                (a * 16 + (b % 8) * 2 + d) * 8 + e * 4 + f % 4,
                            )
                        )
    return out


Z_UP = pairs(lambda yl, z, c, yh, x: (yl, z + 1, c, yh, x))
Z_DOWN = pairs(lambda yl, z, c, yh, x: (yl, z + 7, c, yh, x))
X_UP = pairs(lambda yl, z, c, yh, x: (yl, z, c, yh, x + 1))
X_DOWN = pairs(lambda yl, z, c, yh, x: (yl, z, c, yh, x + 3))
CORE = pairs(lambda yl, z, c, yh, x: (yl, z, 1 - c, yh, x))
Y_LO = pairs(lambda yl, z, c, yh, x: (1 - yl, z, c, yh, x))


def send(array, table):
    return lax.ppermute(array, AXES, table)


def mm(a, b, ca, cb):
    return lax.dot_general(a, b, (((ca,), (cb,)), ((), ())), preferred_element_type=F32)


def within_columns(decay):
    at = lax.broadcasted_iota(jnp.int32, (BLOCK, BLOCK), 0)
    of = lax.broadcasted_iota(jnp.int32, (BLOCK, BLOCK), 1)
    lower = (of <= at).astype(F32)
    return lax.dot_general(
        lower, decay, (((1,), (0,)), ((), ())),
        precision=lax.Precision.HIGHEST, preferred_element_type=F32,
    )


def causal_mask(within_col):
    gaps = within_col - jnp.transpose(within_col)
    at = lax.broadcasted_iota(jnp.int32, (BLOCK, BLOCK), 0)
    of = lax.broadcasted_iota(jnp.int32, (BLOCK, BLOCK), 1)
    return jnp.exp(jnp.where(at >= of, gaps, -jnp.inf))


def head_cols(h):
    return pl.ds(h * HEAD_DIM, HEAD_DIM)


def key_terms_kernel(decay_ref, key_ref, value_ref, out_ref):
    within = within_columns(decay_ref[...])
    row = lax.broadcasted_iota(jnp.int32, (16, HEAD_DIM), 0)
    for h in range(HEADS_LOCAL):
        col = within[:, h : h + 1]
        last = within[BLOCK - 1 : BLOCK, h : h + 1]
        scaled = (jnp.exp(last - col) * key_ref[:, head_cols(h)].astype(F32)).astype(BF)
        terms = mm(scaled, value_ref[:, head_cols(h)], 0, 0).astype(BF)
        high = last.astype(BF).astype(F32)
        middle = (last - high).astype(BF).astype(F32)
        low = last - high - middle
        parts = jnp.where(row == 0, high, jnp.where(row == 1, middle, jnp.where(row == 2, low, 0.0)))
        parts = parts.astype(BF)
        for i in range(4):
            out_ref[4 * h + i, 0:ROWS, :] = terms[i * ROWS : (i + 1) * ROWS]
            out_ref[4 * h + i, ROWS : ROWS + 16, :] = parts


def recurrence_kernel(reverse, decay_ref, terms_ref, out_ref):
    state = jnp.zeros((ROWS, HEAD_DIM), F32)
    for k in reversed(range(N_SEQ)) if reverse else range(N_SEQ):
        out_ref[k] = state.astype(BF)
        parts = decay_ref[k, ROWS : ROWS + 16, :].astype(F32)
        factor = jnp.exp(parts[0:1] + (parts[1:2] + parts[2:3]))
        state = factor * state + terms_ref[k, 0:ROWS, :].astype(F32)


def attended_kernel(decay_ref, query_ref, key_ref, value_ref, state_ref, att_ref, score_ref):
    within = within_columns(decay_ref[...])
    for h in range(HEADS_LOCAL):
        cols = head_cols(h)
        col = within[:, h : h + 1]
        query = query_ref[:, cols]
        scores = (mm(query, key_ref[:, cols], 1, 1) * causal_mask(col)).astype(BF)
        score_ref[:, cols] = scores
        att = jnp.exp(col) * mm(query, state_ref[pl.ds(h * HEAD_DIM, HEAD_DIM), :], 1, 0)
        att_ref[:, cols] = (att + mm(scores, value_ref[:, cols], 1, 0)).astype(BF)


def query_terms_kernel(decay_ref, query_ref, own_ref, other_ref, grad_ref, out_ref):
    within = within_columns(decay_ref[...])
    for h in range(HEADS_LOCAL):
        cols = head_cols(h)
        grad = (own_ref[:, cols] + other_ref[:, cols].astype(F32)).astype(BF)
        grad_ref[:, cols] = grad
        scaled = (jnp.exp(within[:, h : h + 1]) * query_ref[:, cols].astype(F32)).astype(BF)
        terms = mm(scaled, grad, 0, 0).astype(BF)
        for i in range(4):
            out_ref[4 * h + i] = terms[i * ROWS : (i + 1) * ROWS]


def grads_kernel(
    decay_ref, query_ref, key_ref, value_ref, grad_ref, score_ref, state_ref, after_ref,
    gq_ref, gk_ref, gv_ref,
):
    within = within_columns(decay_ref[...])
    for h in range(HEADS_LOCAL):
        cols = head_cols(h)
        rows = pl.ds(h * HEAD_DIM, HEAD_DIM)
        col = within[:, h : h + 1]
        last = within[BLOCK - 1 : BLOCK, h : h + 1]
        key_weight = jnp.exp(last - col)
        grad, key, value = grad_ref[:, cols], key_ref[:, cols], value_ref[:, cols]
        after = after_ref[rows, :]
        grad_scores = (mm(grad, value, 1, 1) * causal_mask(col)).astype(BF)
        gq = jnp.exp(col) * mm(grad, state_ref[rows, :], 1, 1) + mm(grad_scores, key, 1, 0)
        gq_ref[:, cols] = gq.astype(BF)
        gk = key_weight * mm(value, after, 1, 1) + mm(grad_scores, query_ref[:, cols], 0, 0)
        gk_ref[:, cols] = gk.astype(BF)
        gv = key_weight * mm(key, after, 1, 0) + mm(score_ref[:, cols], grad, 0, 0)
        gv_ref[:, cols] = gv.astype(BF)


def kernel_call(body, outs, name, flops, moved):
    return pl.pallas_call(
        body,
        out_shape=outs,
        compiler_params=PARAMS,
        name=name,
        cost_estimate=pl.CostEstimate(flops=flops, bytes_accessed=moved, transcendentals=0),
    )


def shape(dims, dtype=BF):
    return jax.ShapeDtypeStruct(dims, dtype)


def exchange(array):
    return lax.all_to_all(array, "seq", 0, 0, tiled=True)


def body(cotangent, queries, key_proj, value_proj, log_decay, out_weight):
    tokens, cols = queries.shape
    seq, head = lax.axis_index("seq"), lax.axis_index("head")
    core, z = seq % 2, (seq // 2) % 8
    y_lo, y_hi, x = seq // 16, head // 4, head % 4
    flip = y_lo ^ y_hi
    share = out_weight.shape[0]

    up, down = send(out_weight, Z_UP), send(out_weight, Z_DOWN)
    below, above = [up], [down]
    for _ in range(2):
        below.append(send(below[-1], Z_UP))
        above.append(send(above[-1], Z_DOWN))
    half = share // 2
    far_low = send(below[-1][:half], Z_UP)
    far_high = send(above[-1][half:], Z_DOWN)
    weights = jnp.concatenate(
        [out_weight] + above + [far_low, far_high] + below[::-1], axis=0
    )

    cot = jnp.transpose(cotangent).reshape(2, 2, share, tokens)
    pieces = []
    for a in range(2):
        part = lax.dynamic_index_in_dim(cot, core ^ a, 1, keepdims=False).reshape(2 * share, tokens)
        for b in range(2):
            table = pairs(lambda yl, z, c, yh, x, a=a, b=b: (yh, z, c ^ a, yl ^ b, x))
            pieces.append(send(part, table))
    own = jnp.concatenate(pieces, axis=1)
    left, right = send(own, X_UP), send(own, X_DOWN)
    opposite = jnp.concatenate([send(left[:share], X_UP), send(right[share:], X_DOWN)], axis=0)
    around = [own, right, opposite, left]
    block = jnp.concatenate(around + around, axis=0)
    start = ((z - 2 * x) % NZ) * share
    block = lax.dynamic_slice_in_dim(block, start, NZ * share, axis=0)

    terms = kernel_call(
        key_terms_kernel, shape((N_SEQ, ROWS + 16, HEAD_DIM)), "key_terms", 40_000_000, 1_000_000
    )(log_decay, key_proj, value_proj)
    gathered = exchange(terms)
    befores = kernel_call(
        functools.partial(recurrence_kernel, False),
        shape((N_SEQ, ROWS, HEAD_DIM)), "states_before", 1_000_000, 1_000_000,
    )(gathered, gathered)
    states = exchange(befores).reshape(cols, HEAD_DIM)
    attended, scores = kernel_call(
        attended_kernel, (shape((tokens, cols)), shape((tokens, cols))), "attended",
        110_000_000, 2_000_000,
    )(log_decay, queries, key_proj, value_proj, states)

    def project(part):
        return lax.dot_general(part, weights, (((0,), (0,)), ((), ())), preferred_element_type=F32)

    crossing = send(project(block[:, 2 * tokens :]).astype(BF), CORE)
    summed = project(block[:, : 2 * tokens]) + crossing.astype(F32)
    mine = lax.dynamic_slice_in_dim(summed, flip * tokens, tokens, axis=0)
    theirs = lax.dynamic_slice_in_dim(summed, (1 - flip) * tokens, tokens, axis=0)
    arrived = send(theirs.astype(BF), Y_LO)
    grad_attn, query_terms = kernel_call(
        query_terms_kernel, (shape((tokens, cols)), shape((N_SEQ, ROWS, HEAD_DIM))), "query_terms",
        40_000_000, 1_000_000,
    )(log_decay, queries, mine, arrived)

    neighbour = send(attended, Y_LO)
    pair = jnp.where(
        flip == 0,
        jnp.concatenate([attended, neighbour], axis=0),
        jnp.concatenate([neighbour, attended], axis=0),
    )
    all_attended = jnp.concatenate([pair, send(pair, CORE)], axis=0)
    partial = lax.dot_general(
        block, all_attended, (((1,), (0,)), ((), ())), preferred_element_type=F32
    ).astype(BF)
    part = partial.reshape(NZ, share, cols)
    going_up = send(part[4, :half], Z_UP)
    going_down = send(part[4, half:], Z_DOWN)
    going_up = jnp.concatenate(
        [(part[3, :half].astype(F32) + going_up.astype(F32)).astype(BF), part[3, half:]], axis=0
    )
    going_down = jnp.concatenate(
        [part[5, :half], (part[5, half:].astype(F32) + going_down.astype(F32)).astype(BF)], axis=0
    )
    for k in (2, 1):
        going_up = (part[k].astype(F32) + send(going_up, Z_UP).astype(F32)).astype(BF)
        going_down = (part[8 - k].astype(F32) + send(going_down, Z_DOWN).astype(F32)).astype(BF)
    grad_weight = (
        part[0].astype(F32)
        + send(going_up, Z_UP).astype(F32)
        + send(going_down, Z_DOWN).astype(F32)
    ).astype(BF)

    afters = kernel_call(
        functools.partial(recurrence_kernel, True),
        shape((N_SEQ, ROWS, HEAD_DIM)), "states_after", 1_000_000, 1_000_000,
    )(gathered, exchange(query_terms))
    after = exchange(afters).reshape(cols, HEAD_DIM)
    grad_queries, grad_keys, grad_values = kernel_call(
        grads_kernel, (shape((tokens, cols)),) * 3, "grads", 270_000_000, 3_000_000
    )(log_decay, queries, key_proj, value_proj, grad_attn, scores, states, after)
    return grad_queries, grad_keys, grad_values, grad_weight


def solution(mesh):
    placed = P("seq", "head")
    return jax.shard_map(
        body,
        mesh=mesh,
        in_specs=(placed,) * 6,
        out_specs=(placed,) * 4,
        check_vma=False,
    )
```

time: 504 us -> 169 us (0.34)
  waiting for transfers between devices: 330 us -> 48.4 us
  other arithmetic: 75.9 us -> 8.53 us
  starting transfers between devices: 0.2 us -> 65.3 us
  blocking collectives: 32.5 us -> 0 us
  between operations: 13.9 us -> 1.05 us
  matrix products: 20.3 us -> 9.63 us
  Pallas kernels: 0 us -> 8.8 us
    all_gather x4 -> x0, waiting for transfers between devices: 231 us -> none  [the longest x2 95.4 us: entering(): everything = jax.tree.map(lambda part: lax.all_gather(part, axis), array)]
    unnamed x6 -> x0, waiting for transfers between devices: 99 us -> none
    select_n x64 -> x1, other arithmetic: 75.6 us -> 0.13 us  [body(): jnp.where(flip == 0, jnp.concatenate([attended, neighbour], axis=0), jnp....]
    ppermute x0 -> x28, starting transfers between devices: none -> 40.9 us  [send(): return lax.ppermute(array, AXES, table)]
    all_gather x1 -> x0, blocking collectives: 32.5 us -> none  [entering(): everything = jax.tree.map(lambda part: lax.all_gather(part, axis), array)]
    ppermute x0 -> x28, waiting for transfers between devices: none -> 27.4 us  [send(): return lax.ppermute(array, AXES, table)]
    all_to_all x0 -> x4, starting transfers between devices: none -> 24.4 us  [exchange(): return lax.all_to_all(array, 'seq', 0, 0, tiled=True)]
    all_to_all x0 -> x4, waiting for transfers between devices: none -> 21.1 us  [exchange(): return lax.all_to_all(array, 'seq', 0, 0, tiled=True)]
  transfers between devices with their start and end apart: 5 -> 32, of which waited for: 5 -> 16; matrix products, arithmetic and copies ran while one was open for 24% -> 21% of each run, Pallas kernels for 0% -> 5%
where the time goes in v1:
time: 169 us; the launch traced here: 167 us
  starting transfers between devices  65.3 us (39%)
  waiting for transfers between devices  48.4 us (29%)
  local copies, waits for them, and re-layouts  25.4 us (15%)
  matrix products  9.63 us (6%)
  Pallas kernels  8.8 us (5%)
  other arithmetic  8.53 us (5%)
    ppermute x28, starting transfers between devices, send(): return lax.ppermute(array, AXES, table)  40.9 us
    ppermute x28, waiting for transfers between devices, send(): return lax.ppermute(array, AXES, table)  27.4 us
    all_to_all x4, starting transfers between devices, exchange(): return lax.all_to_all(array, 'seq', 0, 0, tiled=True)  24.4 us
    unnamed x42, local copies, waits for them, and re-layouts  22.9 us
    all_to_all x4, waiting for transfers between devices, exchange(): return lax.all_to_all(array, 'seq', 0, 0, tiled=True)  21.1 us
    dot_general x2, matrix products, project(): lax.dot_general(part, weights, (((0,), (0,)), ((), ())), preferred_elemen...  6.38 us
    convert_element_type x2, other arithmetic, body(): (part[k].astype(F32) + send(going_up, Z_UP).astype(F32)).astype(BF)  3.53 us
  transfers between devices with their start and end apart: 32, of which 16 were waited for; matrix products, arithmetic and copies ran while one was open for 21% of the time, Pallas kernels for 5%

profile of v1, /device:TPU:8, one launch (start us, length us, event | category | flops | bytes accessed | tf_op | source)
XLA Modules:
  0.0 167.1 jit_solution(15333547052384473244)
XLA Ops:
  1.8 3.5 %collective-permute-start = (bf16[384,128]{1,0:T(8,128)(2,1)S(1)}, bf16[384,128]{1,0:T(8,128)(2,1)S(1)}, u32[]{:S(2)}, u32[]{:S(2)}) collective-permute-start(bf16[384,128]{1,0:T(8,128)(2,1)S(1)} %bitcast.36), channel_id=1, source_target_pairs={{0,0},{1,1},{2,2},{3,3},{4,128},{5,129},{6,130},{7,131},{8,8},{9,9... | collective-permute-start | bytes 294920 | tf_op jit(solution)/shard_map/ppermute | solution.py:48
  5.3 5.9 %collective-permute-start.8 = (bf16[192,1024]{1,0:T(8,128)(2,1)}, bf16[192,1024]{1,0:T(8,128)(2,1)}, u32[]{:S(2)}, u32[]{:S(2)}) collective-permute-start(bf16[192,1024]{1,0:T(8,128)(2,1)} %param.11), channel_id=1, source_target_pairs={{0,112},{1,113},{2,114},{3,115},{4,116},{5,117},{6,118},{7,119},{8... | collective-permute-start | bytes 1179656 | tf_op jit(solution)/shard_map/ppermute | solution.py:48
  11.3 2.6 %collective-permute-start.3 = (bf16[384,128]{1,0:T(8,128)(2,1)S(1)}, bf16[384,128]{1,0:T(8,128)(2,1)S(1)}, u32[]{:S(2)}, u32[]{:S(2)}) collective-permute-start(bf16[384,128]{1,0:T(8,128)(2,1)S(1)} %bitcast.35), channel_id=1, source_target_pairs={{0,12},{1,13},{2,14},{3,15},{4,140},{5,141},{6,142},{7,143},{8,4},... | collective-permute-start | bytes 294920 | tf_op jit(solution)/shard_map/ppermute | solution.py:48
  14.6 3.7 %collective-permute-done.1 = bf16[384,128]{1,0:T(8,128)(2,1)S(1)} collective-permute-done((bf16[384,128]{1,0:T(8,128)(2,1)S(1)}, bf16[384,128]{1,0:T(8,128)(2,1)S(1)}, u32[]{:S(2)}, u32[]{:S(2)}) %collective-permute-start.1) | collective-permute-done | bytes 98336 | tf_op jit(solution)/shard_map/ppermute | solution.py:48
  28.9 6.0 %all-to-all-start = ((bf16[32,48,128]{2,1,0:T(8,128)(2,1)}), bf16[32,48,128]{2,1,0:T(8,128)(2,1)S(1)}, u32[]{:S(2)}, u32[]{:S(2)}) async-start(bf16[32,48,128]{2,1,0:T(8,128)(2,1)} %key_terms.1), calls=%async_computation | async-start | bytes 786432 | tf_op jit(solution)/shard_map/all_to_all | solution.py:164
  35.7 2.8 %collective-permute-start.9 = (bf16[192,1024]{1,0:T(8,128)(2,1)}, bf16[192,1024]{1,0:T(8,128)(2,1)}, u32[]{:S(2)}, u32[]{:S(2)}) collective-permute-start(bf16[192,1024]{1,0:T(8,128)(2,1)} %collective-permute-done.8), channel_id=1, source_target_pairs={{0,112},{1,113},{2,114},{3,115},{4,116},{5,117},{6,118},{7,119},{8... | collective-permute-start | bytes 1179656 | tf_op jit(solution)/shard_map/ppermute | solution.py:48
  38.9 1.8 %constant_dynamic-update-slice_fusion.24 = bf16[1536,1024]{1,0:T(8,128)(2,1)} fusion(bf16[1536,1024]{1,0:T(8,128)(2,1)} %constant_dynamic-update-slice_fusion.25, bf16[192,1024]{1,0:T(8,128)(2,1)} %collective-permute-done.8), kind=kLoop, calls=%fused_computation.52 | loop fusion | bytes 786432
  40.7 3.0 %collective-permute-start.7 = (bf16[192,512]{1,0:T(8,128)(2,1)S(1)}, bf16[192,512]{1,0:T(8,128)(2,1)S(1)}, u32[]{:S(2)}, u32[]{:S(2)}) collective-permute-start(bf16[192,512]{1,0:T(8,128)(2,1)S(1)} %slice.74), channel_id=1, source_target_pairs={{0,3},{1,0},{2,1},{3,2},{4,7},{5,4},{6,5},{7,6},{8,11},{9,8},{10,9... | collective-permute-start | bytes 589832 | tf_op jit(solution)/shard_map/ppermute | solution.py:48
  44.5 2.0 %collective-permute-done.6 = bf16[192,512]{1,0:T(8,128)(2,1)S(1)} collective-permute-done((bf16[192,512]{1,0:T(8,128)(2,1)S(1)}, bf16[192,512]{1,0:T(8,128)(2,1)S(1)}, u32[]{:S(2)}, u32[]{:S(2)}) %collective-permute-start.6) | collective-permute-done | bytes 196640 | tf_op jit(solution)/shard_map/ppermute | solution.py:48
  50.2 7.0 %all-to-all-start.1 = ((bf16[32,32,128]{2,1,0:T(8,128)(2,1)}), bf16[32,32,128]{2,1,0:T(8,128)(2,1)S(1)}, u32[]{:S(2)}, u32[]{:S(2)}) async-start(bf16[32,32,128]{2,1,0:T(8,128)(2,1)} %states_before.1), calls=%async_computation.1 | async-start | bytes 524288 | tf_op jit(solution)/shard_map/all_to_all | solution.py:164
  62.2 7.0 %all-to-all-done.1 = bf16[32,32,128]{2,1,0:T(8,128)(2,1)S(1)} async-done(((bf16[32,32,128]{2,1,0:T(8,128)(2,1)}), bf16[32,32,128]{2,1,0:T(8,128)(2,1)S(1)}, u32[]{:S(2)}, u32[]{:S(2)}) %all-to-all-start.1) | async-done | bytes 262176 | tf_op jit(solution)/shard_map/all_to_all | solution.py:164
  77.8 1.8 %constant_dynamic-update-slice_fusion.23 = bf16[1536,1024]{1,0:T(8,128)(2,1)} fusion(bf16[1536,1024]{1,0:T(8,128)(2,1)} %constant_dynamic-update-slice_fusion.24, bf16[192,1024]{1,0:T(8,128)(2,1)} %collective-permute-done.9), kind=kLoop, calls=%fused_computation.51 | loop fusion | bytes 786432
  79.6 3.0 %collective-permute-done.10 = bf16[192,1024]{1,0:T(8,128)(2,1)S(1)} collective-permute-done((bf16[192,1024]{1,0:T(8,128)(2,1)}, bf16[192,1024]{1,0:T(8,128)(2,1)S(1)}, u32[]{:S(2)}, u32[]{:S(2)}) %collective-permute-start.10) | collective-permute-done | bytes 393248 | tf_op jit(solution)/shard_map/ppermute | solution.py:48
  85.7 2.7 %collective-permute-done.15 = bf16[96,1024]{1,0:T(8,128)(2,1)S(1)} collective-permute-done((bf16[96,1024]{1,0:T(8,128)(2,1)S(1)}, bf16[96,1024]{1,0:T(8,128)(2,1)S(1)}, u32[]{:S(2)}, u32[]{:S(2)}) %collective-permute-start.15) | collective-permute-done | bytes 196640 | tf_op jit(solution)/shard_map/ppermute | solution.py:48
  89.9 3.3 %convolution_convert_fusion = bf16[1536,1024]{1,0:T(8,128)(2,1)S(1)} fusion(bf16[3072,512]{1,0:T(8,128)(2,1)} %constant_dynamic-update-slice_fusion.4, s32[]{:T(128)S(6)} %select_n.60, bf16[256,1024]{1,0:T(8,128)(2,1)S(1)} %collective-permute-done.19, bf16[256,1024]{1,0:T(8,128)(2,1)S(1)} %maximum_select_fusion), kind=kOutput, calls=%fused_computation | convolution fusion | flops 1614282752 | bytes 5767172 | tf_op jit(solution)/shard_map/dot_general | solution.py:236
  94.1 2.4 %collective-permute-start.24 = (bf16[96,1024]{1,0:T(8,128)(2,1)S(1)}, bf16[96,1024]{1,0:T(8,128)(2,1)S(1)}, u32[]{:S(2)}, u32[]{:S(2)}) collective-permute-start(bf16[96,1024]{1,0:T(8,128)(2,1)S(1)} %get-tuple-element.23), channel_id=1, source_target_pairs={{0,112},{1,113},{2,114},{3,115},{4,116},{5,117},{6,118},{7,119},{8... | collective-permute-start | bytes 589832 | tf_op jit(solution)/shard_map/ppermute | solution.py:48
  96.5 1.8 %constant_dynamic-update-slice_fusion.18 = bf16[1536,1024]{1,0:T(8,128)(2,1)} fusion(bf16[1536,1024]{1,0:T(8,128)(2,1)} %constant_dynamic-update-slice_fusion.19, bf16[192,1024]{1,0:T(8,128)(2,1)} %collective-permute-done.12), kind=kLoop, calls=%fused_computation.46 | loop fusion | bytes 786432
  102.1 3.1 %convolution_convert_fusion.1 = bf16[256,1024]{1,0:T(8,128)(2,1)S(1)} fusion(bf16[1536,1024]{1,0:T(8,128)(2,1)} %constant_dynamic-update-slice_fusion.17, bf16[3072,512]{1,0:T(8,128)(2,1)} %constant_dynamic-update-slice_fusion.4, s32[]{:T(128)S(6)} %select_n.60, s32[]{:T(128)S(6)} %add.77), kind=kOutput, calls=%fused_computation.3 | convolution fusion | flops 805568512 | bytes 4456456 | tf_op jit(solution)/shard_map/dot_general | solution.py:217
  106.1 1.9 %collective-permute-start.25 = (bf16[192,1024]{1,0:T(8,128)(2,1)}, bf16[192,1024]{1,0:T(8,128)(2,1)}, u32[]{:S(2)}, u32[]{:S(2)}) collective-permute-start(bf16[192,1024]{1,0:T(8,128)(2,1)} %pad_maximum_fusion.1), channel_id=1, source_target_pairs={{0,112},{1,113},{2,114},{3,115},{4,116},{5,117},{6,118},{7,119},{8... | collective-permute-start | bytes 1179656 | tf_op jit(solution)/shard_map/ppermute | solution.py:48
  109.7 1.9 %add_convert_fusion.4 = bf16[192,1024]{1,0:T(8,128)(2,1)} fusion(bf16[192,1024]{1,0:T(8,128)(2,1)S(1)} %collective-permute-done.21, bf16[1536,1024]{1,0:T(8,128)(2,1)} %copy-done.5), kind=kLoop, calls=%fused_computation.13 | loop fusion | flops 786432 | bytes 1179648 | tf_op jit(solution)/shard_map/convert_element_type | solution.py:249
  111.7 3.2 %convolution_add_fusion = f32[256,1024]{1,0:T(8,128)S(1)} fusion(bf16[1536,1024]{1,0:T(8,128)(2,1)} %constant_dynamic-update-slice_fusion.17, bf16[256,1024]{1,0:T(8,128)(2,1)} %collective-permute-done.16, bf16[3072,512]{1,0:T(8,128)(2,1)} %constant_dynamic-update-slice_fusion.4, s32[]{:T(128)S(6)} %select_n.60), kind=kOutput, calls=%fused_computation.2 | convolution fusion | flops 805830656 | bytes 5505028 | tf_op jit(solution)/shard_map/dot_general | solution.py:217
  115.7 6.1 %collective-permute-done.17.other_ref = bf16[128,1024]{1,0:T(8,128)(2,1)S(1)} collective-permute-done((bf16[128,1024]{1,0:T(8,128)(2,1)S(1)}, bf16[128,1024]{1,0:T(8,128)(2,1)S(1)}, u32[]{:S(2)}, u32[]{:S(2)}) %collective-permute-start.17) | collective-permute-done | bytes 262176 | tf_op jit(solution)/shard_map/ppermute | solution.py:48
  123.3 6.1 %all-to-all-start.2 = ((bf16[32,32,128]{2,1,0:T(8,128)(2,1)}), bf16[32,32,128]{2,1,0:T(8,128)(2,1)S(1)}, u32[]{:S(2)}, u32[]{:S(2)}) async-start(bf16[32,32,128]{2,1,0:T(8,128)(2,1)} %get-tuple-element.13), calls=%async_computation.2 | async-start | bytes 524288 | tf_op jit(solution)/shard_map/all_to_all | solution.py:164
  131.1 2.8 %collective-permute-start.26 = (bf16[192,1024]{1,0:T(8,128)(2,1)S(1)}, bf16[192,1024]{1,0:T(8,128)(2,1)}, u32[]{:S(2)}, u32[]{:S(2)}) collective-permute-start(bf16[192,1024]{1,0:T(8,128)(2,1)S(1)} %get-tuple-element.19), channel_id=1, source_target_pairs={{0,112},{1,113},{2,114},{3,115},{4,116},{5,117},{6,118},{7,119},{8... | collective-permute-start | bytes 1179656 | tf_op jit(solution)/shard_map/ppermute | solution.py:48
  133.9 7.3 %all-to-all-done.2.terms_ref = bf16[32,32,128]{2,1,0:T(8,128)(2,1)S(1)} async-done(((bf16[32,32,128]{2,1,0:T(8,128)(2,1)}), bf16[32,32,128]{2,1,0:T(8,128)(2,1)S(1)}, u32[]{:S(2)}, u32[]{:S(2)}) %all-to-all-start.2) | async-done | bytes 262176 | tf_op jit(solution)/shard_map/all_to_all | solution.py:164
  142.0 5.2 %all-to-all-start.3 = ((bf16[32,32,128]{2,1,0:T(8,128)(2,1)}), bf16[32,32,128]{2,1,0:T(8,128)(2,1)S(1)}, u32[]{:S(2)}, u32[]{:S(2)}) async-start(bf16[32,32,128]{2,1,0:T(8,128)(2,1)} %states_after.1), calls=%async_computation.3 | async-start | bytes 524288 | tf_op jit(solution)/shard_map/all_to_all | solution.py:164
  148.8 2.0 %add_convert_fusion.1 = bf16[192,1024]{1,0:T(8,128)(2,1)} fusion(bf16[192,1024]{1,0:T(8,128)(2,1)} %collective-permute-done.26, bf16[1536,1024]{1,0:T(8,128)(2,1)} %copy-done.5), kind=kLoop, calls=%fused_computation.10 | loop fusion | flops 786432 | bytes 1179648 | tf_op jit(solution)/shard_map/convert_element_type | solution.py:250
  150.8 1.8 %collective-permute-start.27 = (bf16[192,1024]{1,0:T(8,128)(2,1)}, bf16[192,1024]{1,0:T(8,128)(2,1)S(1)}, u32[]{:S(2)}, u32[]{:S(2)}) collective-permute-start(bf16[192,1024]{1,0:T(8,128)(2,1)} %add_convert_fusion.1), channel_id=1, source_target_pairs={{0,112},{1,113},{2,114},{3,115},{4,116},{5,117},{6,118},{7,119},{8... | collective-permute-start | bytes 1179656 | tf_op jit(solution)/shard_map/ppermute | solution.py:48
  152.6 6.5 %all-to-all-done.3 = bf16[32,32,128]{2,1,0:T(8,128)(2,1)S(1)} async-done(((bf16[32,32,128]{2,1,0:T(8,128)(2,1)}), bf16[32,32,128]{2,1,0:T(8,128)(2,1)S(1)}, u32[]{:S(2)}, u32[]{:S(2)}) %all-to-all-start.3) | async-done | bytes 262176 | tf_op jit(solution)/shard_map/all_to_all | solution.py:164
  159.1 3.1 %grads.1 = (bf16[128,1024]{1,0:T(8,128)(2,1)}, bf16[128,1024]{1,0:T(8,128)(2,1)}, bf16[128,1024]{1,0:T(8,128)(2,1)}) custom-call(f32[128,8]{1,0:T(8,128)S(1)} %copy.18.decay_ref, bf16[128,1024]{1,0:T(8,128)(2,1)S(1)} %copy-done, bf16[128,1024]{1,0:T(8,128)(2,1)S(1)} %copy-done.2, bf16[128,1024]{1,0:T(8,128)(2,1)S(1)} %copy-done.4, ...), custom_call_target="tpu_custom_call" | custom-call | flops 270000000 | bytes 3000000 | tf_op jit(solution)/shard_map/grads/pallas_call | solution.py:262
  162.2 3.0 %collective-permute-done.23 = bf16[192,1024]{1,0:T(8,128)(2,1)S(1)} collective-permute-done((bf16[192,1024]{1,0:T(8,128)(2,1)S(1)}, bf16[192,1024]{1,0:T(8,128)(2,1)S(1)}, u32[]{:S(2)}, u32[]{:S(2)}) %collective-permute-start.23) | collective-permute-done | bytes 393248 | tf_op jit(solution)/shard_map/ppermute | solution.py:48
  165.1 1.9 %add_convert_fusion = bf16[192,1024]{1,0:T(8,128)(2,1)} fusion(bf16[192,1024]{1,0:T(8,128)(2,1)S(1)} %collective-permute-done.27, bf16[192,1024]{1,0:T(8,128)(2,1)S(1)} %collective-permute-done.23, bf16[1536,1024]{1,0:T(8,128)(2,1)} %copy-done.5), kind=kLoop, calls=%fused_computation.9 | loop fusion | flops 1179648 | bytes 1572864 | tf_op jit(solution)/shard_map/convert_element_type | solution.py:255
  (102 shorter events, 49.8 us)
Async XLA Ops:
  1.8 9.4 %collective-permute-start = (bf16[384,128]{1,0:T(8,128)(2,1)S(1)}, bf16[384,128]{1,0:T(8,128)(2,1)S(1)}, u32[]{:S(2)}, u32[]{:S(2)}) collective-permute-start(bf16[384,128]{1,0:T(8,128)(2,1)S(1)} %bitcast.36), channel_id=1, source_target_pairs={{0,0},{1,1},{2,2},{3,3},{4,128},{5,129},{6,130},{7,131},{8,8},{9,9... | collective-permute-start | bytes 294920 | tf_op jit(solution)/shard_map/ppermute | solution.py:48
  5.3 30.4 %collective-permute-start.8 = (bf16[192,1024]{1,0:T(8,128)(2,1)}, bf16[192,1024]{1,0:T(8,128)(2,1)}, u32[]{:S(2)}, u32[]{:S(2)}) collective-permute-start(bf16[192,1024]{1,0:T(8,128)(2,1)} %param.11), channel_id=1, source_target_pairs={{0,112},{1,113},{2,114},{3,115},{4,116},{5,117},{6,118},{7,119},{8... | collective-permute-start | bytes 1179656 | tf_op jit(solution)/shard_map/ppermute | solution.py:48
  11.3 27.2 %collective-permute-start.11 = (bf16[192,1024]{1,0:T(8,128)(2,1)}, bf16[192,1024]{1,0:T(8,128)(2,1)S(1)}, u32[]{:S(2)}, u32[]{:S(2)}) collective-permute-start(bf16[192,1024]{1,0:T(8,128)(2,1)} %param.11), channel_id=1, source_target_pairs={{0,16},{1,17},{2,18},{3,19},{4,20},{5,21},{6,22},{7,23},{8,24},{9,... | collective-permute-start | bytes 1179656 | tf_op jit(solution)/shard_map/ppermute | solution.py:48
  11.3 7.1 %collective-permute-start.1 = (bf16[384,128]{1,0:T(8,128)(2,1)S(1)}, bf16[384,128]{1,0:T(8,128)(2,1)S(1)}, u32[]{:S(2)}, u32[]{:S(2)}) collective-permute-start(bf16[384,128]{1,0:T(8,128)(2,1)S(1)} %bitcast.37), channel_id=1, source_target_pairs={{0,4},{1,5},{2,6},{3,7},{4,132},{5,133},{6,134},{7,135},{8,12},{9,... | collective-permute-start | bytes 294920 | tf_op jit(solution)/shard_map/ppermute | solution.py:48
  11.3 8.8 %collective-permute-start.2 = (bf16[384,128]{1,0:T(8,128)(2,1)S(1)}, bf16[384,128]{1,0:T(8,128)(2,1)S(1)}, u32[]{:S(2)}, u32[]{:S(2)}) collective-permute-start(bf16[384,128]{1,0:T(8,128)(2,1)S(1)} %bitcast.34), channel_id=1, source_target_pairs={{0,8},{1,9},{2,10},{3,11},{4,136},{5,137},{6,138},{7,139},{8,0},{9... | collective-permute-start | bytes 294920 | tf_op jit(solution)/shard_map/ppermute | solution.py:48
  11.3 9.5 %collective-permute-start.3 = (bf16[384,128]{1,0:T(8,128)(2,1)S(1)}, bf16[384,128]{1,0:T(8,128)(2,1)S(1)}, u32[]{:S(2)}, u32[]{:S(2)}) collective-permute-start(bf16[384,128]{1,0:T(8,128)(2,1)S(1)} %bitcast.35), channel_id=1, source_target_pairs={{0,12},{1,13},{2,14},{3,15},{4,140},{5,141},{6,142},{7,143},{8,4},... | collective-permute-start | bytes 294920 | tf_op jit(solution)/shard_map/ppermute | solution.py:48
  21.5 17.0 %collective-permute-start.5 = (bf16[384,512]{1,0:T(8,128)(2,1)}, bf16[384,512]{1,0:T(8,128)(2,1)S(1)}, u32[]{:S(2)}, u32[]{:S(2)}) collective-permute-start(bf16[384,512]{1,0:T(8,128)(2,1)} %get-tuple-element.28), channel_id=1, source_target_pairs={{0,1},{1,2},{2,3},{3,0},{4,5},{5,6},{6,7},{7,4},{8,9},{9,10},{10,1... | collective-permute-start | bytes 1179656 | tf_op jit(solution)/shard_map/ppermute | solution.py:48
  23.0 17.7 %collective-permute-start.4 = (bf16[384,512]{1,0:T(8,128)(2,1)}, bf16[384,512]{1,0:T(8,128)(2,1)S(1)}, u32[]{:S(2)}, u32[]{:S(2)}) collective-permute-start(bf16[384,512]{1,0:T(8,128)(2,1)} %get-tuple-element.28), channel_id=1, source_target_pairs={{0,3},{1,0},{2,1},{3,2},{4,7},{5,4},{6,5},{7,6},{8,11},{9,8},{10,9... | collective-permute-start | bytes 1179656 | tf_op jit(solution)/shard_map/ppermute | solution.py:48
  28.9 20.5 %all-to-all-start = ((bf16[32,48,128]{2,1,0:T(8,128)(2,1)}), bf16[32,48,128]{2,1,0:T(8,128)(2,1)S(1)}, u32[]{:S(2)}, u32[]{:S(2)}) async-start(bf16[32,48,128]{2,1,0:T(8,128)(2,1)} %key_terms.1), calls=%async_computation | async-start | bytes 786432 | tf_op jit(solution)/shard_map/all_to_all | solution.py:164
  35.7 37.0 %collective-permute-start.9 = (bf16[192,1024]{1,0:T(8,128)(2,1)}, bf16[192,1024]{1,0:T(8,128)(2,1)}, u32[]{:S(2)}, u32[]{:S(2)}) collective-permute-start(bf16[192,1024]{1,0:T(8,128)(2,1)} %collective-permute-done.8), channel_id=1, source_target_pairs={{0,112},{1,113},{2,114},{3,115},{4,116},{5,117},{6,118},{7,119},{8... | collective-permute-start | bytes 1179656 | tf_op jit(solution)/shard_map/ppermute | solution.py:48
  38.5 21.4 %collective-permute-start.12 = (bf16[192,1024]{1,0:T(8,128)(2,1)S(1)}, bf16[192,1024]{1,0:T(8,128)(2,1)}, u32[]{:S(2)}, u32[]{:S(2)}) collective-permute-start(bf16[192,1024]{1,0:T(8,128)(2,1)S(1)} %collective-permute-done.11), channel_id=1, source_target_pairs={{0,16},{1,17},{2,18},{3,19},{4,20},{5,21},{6,22},{7,23},{8,24},{9,... | collective-permute-start | bytes 1179656 | tf_op jit(solution)/shard_map/ppermute | solution.py:48
  38.5 8.0 %collective-permute-start.6 = (bf16[192,512]{1,0:T(8,128)(2,1)S(1)}, bf16[192,512]{1,0:T(8,128)(2,1)S(1)}, u32[]{:S(2)}, u32[]{:S(2)}) collective-permute-start(bf16[192,512]{1,0:T(8,128)(2,1)S(1)} %slice.73), channel_id=1, source_target_pairs={{0,1},{1,2},{2,3},{3,0},{4,5},{5,6},{6,7},{7,4},{8,9},{9,10},{10,1... | collective-permute-start | bytes 589832 | tf_op jit(solution)/shard_map/ppermute | solution.py:48
  40.7 6.9 %collective-permute-start.7 = (bf16[192,512]{1,0:T(8,128)(2,1)S(1)}, bf16[192,512]{1,0:T(8,128)(2,1)S(1)}, u32[]{:S(2)}, u32[]{:S(2)}) collective-permute-start(bf16[192,512]{1,0:T(8,128)(2,1)S(1)} %slice.74), channel_id=1, source_target_pairs={{0,3},{1,0},{2,1},{3,2},{4,7},{5,4},{6,5},{7,6},{8,11},{9,8},{10,9... | collective-permute-start | bytes 589832 | tf_op jit(solution)/shard_map/ppermute | solution.py:48
  50.2 19.0 %all-to-all-start.1 = ((bf16[32,32,128]{2,1,0:T(8,128)(2,1)}), bf16[32,32,128]{2,1,0:T(8,128)(2,1)S(1)}, u32[]{:S(2)}, u32[]{:S(2)}) async-start(bf16[32,32,128]{2,1,0:T(8,128)(2,1)} %states_before.1), calls=%async_computation.1 | async-start | bytes 524288 | tf_op jit(solution)/shard_map/all_to_all | solution.py:164
  59.9 15.2 %collective-permute-start.13 = (bf16[192,1024]{1,0:T(8,128)(2,1)}, bf16[192,1024]{1,0:T(8,128)(2,1)S(1)}, u32[]{:S(2)}, u32[]{:S(2)}) collective-permute-start(bf16[192,1024]{1,0:T(8,128)(2,1)} %collective-permute-done.12), channel_id=1, source_target_pairs={{0,16},{1,17},{2,18},{3,19},{4,20},{5,21},{6,22},{7,23},{8,24},{9,... | collective-permute-start | bytes 1179656 | tf_op jit(solution)/shard_map/ppermute | solution.py:48
  70.4 7.1 %collective-permute-start.18 = (bf16[128,1024]{1,0:T(8,128)(2,1)S(1)}, bf16[128,1024]{1,0:T(8,128)(2,1)S(1)}, u32[]{:S(2)}, u32[]{:S(2)}) collective-permute-start(bf16[128,1024]{1,0:T(8,128)(2,1)S(1)} %get-tuple-element.17), channel_id=1, source_target_pairs={{0,128},{1,129},{2,130},{3,131},{4,132},{5,133},{6,134},{7,135},{8... | collective-permute-start | bytes 786440 | tf_op jit(solution)/shard_map/ppermute | solution.py:48
  72.7 9.9 %collective-permute-start.10 = (bf16[192,1024]{1,0:T(8,128)(2,1)}, bf16[192,1024]{1,0:T(8,128)(2,1)S(1)}, u32[]{:S(2)}, u32[]{:S(2)}) collective-permute-start(bf16[192,1024]{1,0:T(8,128)(2,1)} %collective-permute-done.9), channel_id=1, source_target_pairs={{0,112},{1,113},{2,114},{3,115},{4,116},{5,117},{6,118},{7,119},{8... | collective-permute-start | bytes 1179656 | tf_op jit(solution)/shard_map/ppermute | solution.py:48
  75.2 9.8 %collective-permute-start.14 = (bf16[96,1024]{1,0:T(8,128)(2,1)S(1)}, bf16[96,1024]{1,0:T(8,128)(2,1)S(1)}, u32[]{:S(2)}, u32[]{:S(2)}) collective-permute-start(bf16[96,1024]{1,0:T(8,128)(2,1)S(1)} %slice.75), channel_id=1, source_target_pairs={{0,16},{1,17},{2,18},{3,19},{4,20},{5,21},{6,22},{7,23},{8,24},{9,... | collective-permute-start | bytes 589832 | tf_op jit(solution)/shard_map/ppermute | solution.py:48
  77.7 12.2 %collective-permute-start.19 = (bf16[256,1024]{1,0:T(8,128)(2,1)S(1)}, bf16[256,1024]{1,0:T(8,128)(2,1)S(1)}, u32[]{:S(2)}, u32[]{:S(2)}) collective-permute-start(bf16[256,1024]{1,0:T(8,128)(2,1)S(1)} %maximum_select_fusion), channel_id=1, source_target_pairs={{0,8},{1,9},{2,10},{3,11},{4,12},{5,13},{6,14},{7,15},{8,0},{9,1},... | collective-permute-start | bytes 1572872 | tf_op jit(solution)/shard_map/ppermute | solution.py:48
  82.6 5.7 %collective-permute-start.15 = (bf16[96,1024]{1,0:T(8,128)(2,1)S(1)}, bf16[96,1024]{1,0:T(8,128)(2,1)S(1)}, u32[]{:S(2)}, u32[]{:S(2)}) collective-permute-start(bf16[96,1024]{1,0:T(8,128)(2,1)S(1)} %slice.76), channel_id=1, source_target_pairs={{0,112},{1,113},{2,114},{3,115},{4,116},{5,117},{6,118},{7,119},{8... | collective-permute-start | bytes 589832 | tf_op jit(solution)/shard_map/ppermute | solution.py:48
  93.2 7.3 %collective-permute-start.20 = (bf16[96,1024]{1,0:T(8,128)(2,1)S(1)}, bf16[96,1024]{1,0:T(8,128)(2,1)S(1)}, u32[]{:S(2)}, u32[]{:S(2)}) collective-permute-start(bf16[96,1024]{1,0:T(8,128)(2,1)S(1)} %get-tuple-element.22), channel_id=1, source_target_pairs={{0,16},{1,17},{2,18},{3,19},{4,20},{5,21},{6,22},{7,23},{8,24},{9,... | collective-permute-start | bytes 589832 | tf_op jit(solution)/shard_map/ppermute | solution.py:48
  94.1 6.3 %collective-permute-start.24 = (bf16[96,1024]{1,0:T(8,128)(2,1)S(1)}, bf16[96,1024]{1,0:T(8,128)(2,1)S(1)}, u32[]{:S(2)}, u32[]{:S(2)}) collective-permute-start(bf16[96,1024]{1,0:T(8,128)(2,1)S(1)} %get-tuple-element.23), channel_id=1, source_target_pairs={{0,112},{1,113},{2,114},{3,115},{4,116},{5,117},{6,118},{7,119},{8... | collective-permute-start | bytes 589832 | tf_op jit(solution)/shard_map/ppermute | solution.py:48
  100.6 9.1 %collective-permute-start.21 = (bf16[192,1024]{1,0:T(8,128)(2,1)S(1)}, bf16[192,1024]{1,0:T(8,128)(2,1)S(1)}, u32[]{:S(2)}, u32[]{:S(2)}) collective-permute-start(bf16[192,1024]{1,0:T(8,128)(2,1)S(1)} %pad_maximum_fusion), channel_id=1, source_target_pairs={{0,16},{1,17},{2,18},{3,19},{4,20},{5,21},{6,22},{7,23},{8,24},{9,... | collective-permute-start | bytes 1179656 | tf_op jit(solution)/shard_map/ppermute | solution.py:48
  105.2 6.5 %collective-permute-start.16 = (bf16[256,1024]{1,0:T(8,128)(2,1)S(1)}, bf16[256,1024]{1,0:T(8,128)(2,1)}, u32[]{:S(2)}, u32[]{:S(2)}) collective-permute-start(bf16[256,1024]{1,0:T(8,128)(2,1)S(1)} %convolution_convert_fusion.1), channel_id=1, source_target_pairs={{0,8},{1,9},{2,10},{3,11},{4,12},{5,13},{6,14},{7,15},{8,0},{9,1},... | collective-permute-start | bytes 1572872 | tf_op jit(solution)/shard_map/ppermute | solution.py:48
  106.1 23.3 %collective-permute-start.25 = (bf16[192,1024]{1,0:T(8,128)(2,1)}, bf16[192,1024]{1,0:T(8,128)(2,1)}, u32[]{:S(2)}, u32[]{:S(2)}) collective-permute-start(bf16[192,1024]{1,0:T(8,128)(2,1)} %pad_maximum_fusion.1), channel_id=1, source_target_pairs={{0,112},{1,113},{2,114},{3,115},{4,116},{5,117},{6,118},{7,119},{8... | collective-permute-start | bytes 1179656 | tf_op jit(solution)/shard_map/ppermute | solution.py:48
  111.6 17.8 %collective-permute-start.22 = (bf16[192,1024]{1,0:T(8,128)(2,1)}, bf16[192,1024]{1,0:T(8,128)(2,1)}, u32[]{:S(2)}, u32[]{:S(2)}) collective-permute-start(bf16[192,1024]{1,0:T(8,128)(2,1)} %add_convert_fusion.4), channel_id=1, source_target_pairs={{0,16},{1,17},{2,18},{3,19},{4,20},{5,21},{6,22},{7,23},{8,24},{9,... | collective-permute-start | bytes 1179656 | tf_op jit(solution)/shard_map/ppermute | solution.py:48
  115.0 6.8 %collective-permute-start.17 = (bf16[128,1024]{1,0:T(8,128)(2,1)S(1)}, bf16[128,1024]{1,0:T(8,128)(2,1)S(1)}, u32[]{:S(2)}, u32[]{:S(2)}) collective-permute-start(bf16[128,1024]{1,0:T(8,128)(2,1)S(1)} %dynamic-slice_convert_fusion), channel_id=1, source_target_pairs={{0,128},{1,129},{2,130},{3,131},{4,132},{5,133},{6,134},{7,135},{8... | collective-permute-start | bytes 786440 | tf_op jit(solution)/shard_map/ppermute | solution.py:48
  123.3 18.0 %all-to-all-start.2 = ((bf16[32,32,128]{2,1,0:T(8,128)(2,1)}), bf16[32,32,128]{2,1,0:T(8,128)(2,1)S(1)}, u32[]{:S(2)}, u32[]{:S(2)}) async-start(bf16[32,32,128]{2,1,0:T(8,128)(2,1)} %get-tuple-element.13), calls=%async_computation.2 | async-start | bytes 524288 | tf_op jit(solution)/shard_map/all_to_all | solution.py:164
  131.1 17.7 %collective-permute-start.26 = (bf16[192,1024]{1,0:T(8,128)(2,1)S(1)}, bf16[192,1024]{1,0:T(8,128)(2,1)}, u32[]{:S(2)}, u32[]{:S(2)}) collective-permute-start(bf16[192,1024]{1,0:T(8,128)(2,1)S(1)} %get-tuple-element.19), channel_id=1, source_target_pairs={{0,112},{1,113},{2,114},{3,115},{4,116},{5,117},{6,118},{7,119},{8... | collective-permute-start | bytes 1179656 | tf_op jit(solution)/shard_map/ppermute | solution.py:48
  142.0 17.0 %all-to-all-start.3 = ((bf16[32,32,128]{2,1,0:T(8,128)(2,1)}), bf16[32,32,128]{2,1,0:T(8,128)(2,1)S(1)}, u32[]{:S(2)}, u32[]{:S(2)}) async-start(bf16[32,32,128]{2,1,0:T(8,128)(2,1)} %states_after.1), calls=%async_computation.3 | async-start | bytes 524288 | tf_op jit(solution)/shard_map/all_to_all | solution.py:164
  147.2 17.9 %collective-permute-start.23 = (bf16[192,1024]{1,0:T(8,128)(2,1)S(1)}, bf16[192,1024]{1,0:T(8,128)(2,1)S(1)}, u32[]{:S(2)}, u32[]{:S(2)}) collective-permute-start(bf16[192,1024]{1,0:T(8,128)(2,1)S(1)} %get-tuple-element.18), channel_id=1, source_target_pairs={{0,16},{1,17},{2,18},{3,19},{4,20},{5,21},{6,22},{7,23},{8,24},{9,... | collective-permute-start | bytes 1179656 | tf_op jit(solution)/shard_map/ppermute | solution.py:48
  150.8 14.4 %collective-permute-start.27 = (bf16[192,1024]{1,0:T(8,128)(2,1)}, bf16[192,1024]{1,0:T(8,128)(2,1)S(1)}, u32[]{:S(2)}, u32[]{:S(2)}) collective-permute-start(bf16[192,1024]{1,0:T(8,128)(2,1)} %add_convert_fusion.1), channel_id=1, source_target_pairs={{0,112},{1,113},{2,114},{3,115},{4,116},{5,117},{6,118},{7,119},{8... | collective-permute-start | bytes 1179656 | tf_op jit(solution)/shard_map/ppermute | solution.py:48
  (9 other events, 163.8 us)

commit v2 on v1

--- a/solution.py
+++ b/solution.py
@@ -36,8 +36,7 @@
     return out
 
 
-Z_UP = pairs(lambda yl, z, c, yh, x: (yl, z + 1, c, yh, x))
-Z_DOWN = pairs(lambda yl, z, c, yh, x: (yl, z + 7, c, yh, x))
+Z_GROUPS = [[yl * 16 + z * 2 + c for z in range(NZ)] for yl in range(2) for c in range(2)]
 X_UP = pairs(lambda yl, z, c, yh, x: (yl, z, c, yh, x + 1))
 X_DOWN = pairs(lambda yl, z, c, yh, x: (yl, z, c, yh, x + 3))
 CORE = pairs(lambda yl, z, c, yh, x: (yl, z, 1 - c, yh, x))
@@ -146,6 +145,40 @@
         gv_ref[:, cols] = gv.astype(BF)
 
 
+def flip_bit():
+    return (lax.axis_index("seq") // 16) ^ (lax.axis_index("head") // 4)
+
+
+def assemble_kernel(share, own_ref, left_ref, right_ref, low_ref, high_ref, out_ref, out_t_ref):
+    x = lax.axis_index("head") % 4
+    features = NZ * share
+    for off, ref, start, count in (
+        (0, own_ref, 0, 2 * share),
+        (1, right_ref, 0, 2 * share),
+        (2, low_ref, 0, share),
+        (2, high_ref, share, share),
+        (3, left_ref, 0, 2 * share),
+    ):
+        at = pl.multiple_of(((x + off) % 4) * (2 * share) + start, 64)
+        out_ref[pl.ds(at, count), :] = ref[...]
+    for i in range(features // 256):
+        rows = pl.ds(i * 256, 256)
+        out_t_ref[:, rows] = jnp.transpose(out_ref[rows, :])
+
+
+def project_kernel(block_ref, weight_ref, kept_ref, crossing_ref):
+    half = kept_ref.shape[0]
+    crossing_ref[...] = mm(block_ref[half:, :], weight_ref[...], 1, 0).astype(BF)
+    kept_ref[...] = mm(block_ref[:half, :], weight_ref[...], 1, 0)
+
+
+def weight_kernel(block_ref, own_ref, neighbour_ref, across_ref, diagonal_ref, out_ref, tokens_ref):
+    flip = flip_bit()
+    for i, ref in ((flip, own_ref), (1 - flip, neighbour_ref), (2 + flip, across_ref), (3 - flip, diagonal_ref)):
+        tokens_ref[pl.ds(pl.multiple_of(i * BLOCK, BLOCK), BLOCK), :] = ref[...]
+    out_ref[...] = mm(block_ref[...], tokens_ref[...], 1, 0).astype(BF)
+
+
 def kernel_call(body, outs, name, flops, moved):
     return pl.pallas_call(
         body,
@@ -166,22 +199,12 @@
 
 def body(cotangent, queries, key_proj, value_proj, log_decay, out_weight):
     tokens, cols = queries.shape
-    seq, head = lax.axis_index("seq"), lax.axis_index("head")
-    core, z = seq % 2, (seq // 2) % 8
-    y_lo, y_hi, x = seq // 16, head // 4, head % 4
-    flip = y_lo ^ y_hi
+    core = lax.axis_index("seq") % 2
+    flip = flip_bit()
     share = out_weight.shape[0]
 
-    up, down = send(out_weight, Z_UP), send(out_weight, Z_DOWN)
-    below, above = [up], [down]
-    for _ in range(2):
-        below.append(send(below[-1], Z_UP))
-        above.append(send(above[-1], Z_DOWN))
-    half = share // 2
-    far_low = send(below[-1][:half], Z_UP)
-    far_high = send(above[-1][half:], Z_DOWN)
-    weights = jnp.concatenate(
-        [out_weight] + above + [far_low, far_high] + below[::-1], axis=0
+    weights = lax.all_gather(
+        out_weight, "seq", axis=0, tiled=True, axis_index_groups=Z_GROUPS
     )
 
     cot = jnp.transpose(cotangent).reshape(2, 2, share, tokens)
@@ -193,11 +216,14 @@
             pieces.append(send(part, table))
     own = jnp.concatenate(pieces, axis=1)
     left, right = send(own, X_UP), send(own, X_DOWN)
-    opposite = jnp.concatenate([send(left[:share], X_UP), send(right[share:], X_DOWN)], axis=0)
-    around = [own, right, opposite, left]
-    block = jnp.concatenate(around + around, axis=0)
-    start = ((z - 2 * x) % NZ) * share
-    block = lax.dynamic_slice_in_dim(block, start, NZ * share, axis=0)
+    opposite_low = send(left[:share], X_UP)
+    opposite_high = send(right[share:], X_DOWN)
+    features = NZ * share
+    block, block_t = kernel_call(
+        functools.partial(assemble_kernel, share),
+        (shape((features, 4 * tokens)), shape((4 * tokens, features))), "assemble",
+        1_000_000, 5_000_000,
+    )(own, left, right, opposite_low, opposite_high)
 
     terms = kernel_call(
         key_terms_kernel, shape((N_SEQ, ROWS + 16, HEAD_DIM)), "key_terms", 40_000_000, 1_000_000
@@ -213,11 +239,22 @@
         110_000_000, 2_000_000,
     )(log_decay, queries, key_proj, value_proj, states)
 
-    def project(part):
-        return lax.dot_general(part, weights, (((0,), (0,)), ((), ())), preferred_element_type=F32)
-
-    crossing = send(project(block[:, 2 * tokens :]).astype(BF), CORE)
-    summed = project(block[:, : 2 * tokens]) + crossing.astype(F32)
+    kept, crossing = pl.pallas_call(
+        project_kernel,
+        grid=(4,),
+        in_specs=[
+            pl.BlockSpec((4 * tokens, features), lambda i: (0, 0)),
+            pl.BlockSpec((features, cols // 4), lambda i: (0, i)),
+        ],
+        out_specs=(pl.BlockSpec((2 * tokens, cols // 4), lambda i: (0, i)),) * 2,
+        out_shape=(shape((2 * tokens, cols), F32), shape((2 * tokens, cols))),
+        compiler_params=PARAMS,
+        name="project",
+        cost_estimate=pl.CostEstimate(
+            flops=1_600_000_000, bytes_accessed=6_000_000, transcendentals=0
+        ),
+    )(block_t, weights)
+    summed = kept + send(crossing, CORE).astype(F32)
     mine = lax.dynamic_slice_in_dim(summed, flip * tokens, tokens, axis=0)
     theirs = lax.dynamic_slice_in_dim(summed, (1 - flip) * tokens, tokens, axis=0)
     arrived = send(theirs.astype(BF), Y_LO)
@@ -226,33 +263,26 @@
         40_000_000, 1_000_000,
     )(log_decay, queries, mine, arrived)
 
+    across = send(attended, CORE)
     neighbour = send(attended, Y_LO)
-    pair = jnp.where(
-        flip == 0,
-        jnp.concatenate([attended, neighbour], axis=0),
-        jnp.concatenate([neighbour, attended], axis=0),
-    )
-    all_attended = jnp.concatenate([pair, send(pair, CORE)], axis=0)
-    partial = lax.dot_general(
-        block, all_attended, (((1,), (0,)), ((), ())), preferred_element_type=F32
-    ).astype(BF)
-    part = partial.reshape(NZ, share, cols)
-    going_up = send(part[4, :half], Z_UP)
-    going_down = send(part[4, half:], Z_DOWN)
-    going_up = jnp.concatenate(
-        [(part[3, :half].astype(F32) + going_up.astype(F32)).astype(BF), part[3, half:]], axis=0
-    )
-    going_down = jnp.concatenate(
-        [part[5, :half], (part[5, half:].astype(F32) + going_down.astype(F32)).astype(BF)], axis=0
-    )
-    for k in (2, 1):
-        going_up = (part[k].astype(F32) + send(going_up, Z_UP).astype(F32)).astype(BF)
-        going_down = (part[8 - k].astype(F32) + send(going_down, Z_DOWN).astype(F32)).astype(BF)
-    grad_weight = (
-        part[0].astype(F32)
-        + send(going_up, Z_UP).astype(F32)
-        + send(going_down, Z_DOWN).astype(F32)
-    ).astype(BF)
+    diagonal = send(neighbour, CORE)
+    column_spec = pl.BlockSpec((tokens, cols // 4), lambda i: (0, i))
+    partial = pl.pallas_call(
+        weight_kernel,
+        grid=(4,),
+        in_specs=[pl.BlockSpec((features, 4 * tokens), lambda i: (0, 0))] + [column_spec] * 4,
+        out_specs=pl.BlockSpec((features, cols // 4), lambda i: (0, i)),
+        out_shape=shape((features, cols)),
+        scratch_shapes=[pltpu.VMEM((4 * tokens, cols // 4), BF)],
+        compiler_params=PARAMS,
+        name="weight_partial",
+        cost_estimate=pl.CostEstimate(
+            flops=1_600_000_000, bytes_accessed=6_000_000, transcendentals=0
+        ),
+    )(block, attended, neighbour, across, diagonal)
+    grad_weight = lax.psum_scatter(
+        partial, "seq", scatter_dimension=0, tiled=True, axis_index_groups=Z_GROUPS
+    )
 
     afters = kernel_call(
         functools.partial(recurrence_kernel, True),

time: 169 us -> 151 us (0.89)
  blocking collectives: 0 us -> 35.5 us
  starting transfers between devices: 65.3 us -> 31.7 us
  local copies, waits for them, and re-layouts: 25.4 us -> 8.56 us
  between operations: 1.05 us -> 14.4 us
  matrix products: 9.63 us -> 0 us
  other arithmetic: 8.53 us -> 1.24 us
  Pallas kernels: 8.8 us -> 16 us
  waiting for transfers between devices: 48.4 us -> 41.5 us
    all_to_all x0 -> x2, blocking collectives: none -> 35.5 us  [exchange(): return lax.all_to_all(array, 'seq', 0, 0, tiled=True)]
    ppermute x28 -> x13, starting transfers between devices: 40.9 us -> 16.5 us  [send(): return lax.ppermute(array, AXES, table)]
    unnamed x42 -> x21, local copies, waits for them, and re-layouts: 22.9 us -> 7.37 us
    dot_general x3 -> x0, matrix products: 9.63 us -> none  [the longest x2 6.38 us: project(): lax.dot_general(part, weights, (((0,), (0,)), ((), ())), preferred_elemen...]
    all_to_all x4 -> x2, starting transfers between devices: 24.4 us -> 15.2 us  [exchange(): return lax.all_to_all(array, 'seq', 0, 0, tiled=True)]
    pallas_call x0 -> x3, Pallas kernels: none -> 8.64 us  [the longest x1 4.13 us: body(): pl.pallas_call(project_kernel, grid=(4,), in_specs=[pl.BlockSpec((4 * tok...]
    ppermute x28 -> x13, waiting for transfers between devices: 27.4 us -> 19.5 us  [send(): return lax.ppermute(array, AXES, table)]
    convert_element_type x5 -> x0, other arithmetic: 7.6 us -> none  [the longest x2 3.53 us: body(): (part[k].astype(F32) + send(going_up, Z_UP).astype(F32)).astype(BF)]
  transfers between devices with their start and end apart: 32 -> 17, of which waited for: 16 -> 7; matrix products, arithmetic and copies ran while one was open for 21% -> 3% of each run, Pallas kernels for 5% -> 11%
where the time goes in v2:
time: 151 us; the launch traced here: 149 us
  waiting for transfers between devices  41.5 us (27%)
  blocking collectives  35.5 us (24%)
  starting transfers between devices  31.7 us (21%)
  Pallas kernels  16 us (11%)
  between operations  14.4 us (10%)
  local copies, waits for them, and re-layouts  8.56 us (6%)
    all_to_all x2, blocking collectives, exchange(): return lax.all_to_all(array, 'seq', 0, 0, tiled=True)  35.5 us
    all_to_all x2, waiting for transfers between devices, exchange(): return lax.all_to_all(array, 'seq', 0, 0, tiled=True)  21.3 us
    ppermute x13, waiting for transfers between devices, send(): return lax.ppermute(array, AXES, table)  19.5 us
    ppermute x13, starting transfers between devices, send(): return lax.ppermute(array, AXES, table)  16.5 us
    all_to_all x2, starting transfers between devices, exchange(): return lax.all_to_all(array, 'seq', 0, 0, tiled=True)  15.2 us
    unnamed x21, local copies, waits for them, and re-layouts  7.37 us
    pallas_call x1, Pallas kernels, body(): pl.pallas_call(project_kernel, grid=(4,), in_specs=[pl.BlockSpec((4 * tok...  4.13 us
    pallas_call x1, Pallas kernels, body(): pl.pallas_call(weight_kernel, grid=(4,), in_specs=[pl.BlockSpec((features...  3.94 us
  transfers between devices with their start and end apart: 17, of which 7 were waited for; matrix products, arithmetic and copies ran while one was open for 3% of the time, Pallas kernels for 11%

profile of v2, /device:TPU:8, one launch (start us, length us, event | category | flops | bytes accessed | tf_op | source)
XLA Modules:
  0.0 148.9 jit_solution(2729898804148519838)
XLA Ops:
  8.7 0.9 copy-done.1
  9.7 0.9 copy-done.3
  10.6 1.4 key_terms.1
  12.1 10.1 %all-to-all-start = ((bf16[32,48,128]{2,1,0:T(8,128)(2,1)}), bf16[32,48,128]{2,1,0:T(8,128)(2,1)S(1)}, u32[]{:S(2)}, u32[]{:S(2)}) async-start(bf16[32,48,128]{2,1,0:T(8,128)(2,1)} %key_terms.1), calls=%async_computation | async-start | bytes 786432 | tf_op jit(solution)/shard_map/all_to_all | solution.py:197
  22.2 1.1 copy.16
  23.3 3.0 %collective-permute-start = (bf16[384,128]{1,0:T(8,128)(2,1)S(1)}, bf16[384,128]{1,0:T(8,128)(2,1)S(1)}, u32[]{:S(2)}, u32[]{:S(2)}) collective-permute-start(bf16[384,128]{1,0:T(8,128)(2,1)S(1)} %bitcast.13), channel_id=1, source_target_pairs={{0,0},{1,1},{2,2},{3,3},{4,128},{5,129},{6,130},{7,131},{8,8},{9,9... | collective-permute-start | bytes 294920 | tf_op jit(solution)/shard_map/ppermute | solution.py:47
  26.9 2.6 %collective-permute-start.3 = (bf16[384,128]{1,0:T(8,128)(2,1)S(1)}, bf16[384,128]{1,0:T(8,128)(2,1)S(1)}, u32[]{:S(2)}, u32[]{:S(2)}) collective-permute-start(bf16[384,128]{1,0:T(8,128)(2,1)S(1)} %bitcast.12), channel_id=1, source_target_pairs={{0,12},{1,13},{2,14},{3,15},{4,140},{5,141},{6,142},{7,143},{8,4},... | collective-permute-start | bytes 294920 | tf_op jit(solution)/shard_map/ppermute | solution.py:47
  29.5 10.6 %all-to-all-done.decay_ref.terms_ref = bf16[32,48,128]{2,1,0:T(8,128)(2,1)S(1)} async-done(((bf16[32,48,128]{2,1,0:T(8,128)(2,1)}), bf16[32,48,128]{2,1,0:T(8,128)(2,1)S(1)}, u32[]{:S(2)}, u32[]{:S(2)}) %all-to-all-start) | async-done | bytes 393248 | tf_op jit(solution)/shard_map/all_to_all | solution.py:197
  40.1 0.8 states_before.1
  40.9 5.1 %all-to-all-start.1 = ((bf16[32,32,128]{2,1,0:T(8,128)(2,1)}), bf16[32,32,128]{2,1,0:T(8,128)(2,1)S(1)}, u32[]{:S(2)}, u32[]{:S(2)}) async-start(bf16[32,32,128]{2,1,0:T(8,128)(2,1)} %states_before.1), calls=%async_computation.1 | async-start | bytes 524288 | tf_op jit(solution)/shard_map/all_to_all | solution.py:197
  46.2 1.6 %collective-permute-start.4 = (bf16[384,512]{1,0:T(8,128)(2,1)S(1)}, bf16[384,512]{1,0:T(8,128)(2,1)S(1)}, u32[]{:S(2)}, u32[]{:S(2)}) collective-permute-start(bf16[384,512]{1,0:T(8,128)(2,1)S(1)} %constant_dynamic-update-slice_fusion.own_ref), channel_id=1, source_target_pairs={{0,1},{1,2},{2,3},{3,0},{4,5},{5,6},{6,7},{7,4},{8,9},{9,10},{10,1... | collective-permute-start | bytes 1179656 | tf_op jit(solution)/shard_map/ppermute | solution.py:47
  47.8 1.7 %collective-permute-start.5 = (bf16[384,512]{1,0:T(8,128)(2,1)S(1)}, bf16[384,512]{1,0:T(8,128)(2,1)S(1)}, u32[]{:S(2)}, u32[]{:S(2)}) collective-permute-start(bf16[384,512]{1,0:T(8,128)(2,1)S(1)} %constant_dynamic-update-slice_fusion.own_ref), channel_id=1, source_target_pairs={{0,3},{1,0},{2,1},{3,2},{4,7},{5,4},{6,5},{7,6},{8,11},{9,8},{10,9... | collective-permute-start | bytes 1179656 | tf_op jit(solution)/shard_map/ppermute | solution.py:47
  49.5 10.8 %all-to-all-done.1 = bf16[32,32,128]{2,1,0:T(8,128)(2,1)S(1)} async-done(((bf16[32,32,128]{2,1,0:T(8,128)(2,1)}), bf16[32,32,128]{2,1,0:T(8,128)(2,1)S(1)}, u32[]{:S(2)}, u32[]{:S(2)}) %all-to-all-start.1) | async-done | bytes 262176 | tf_op jit(solution)/shard_map/all_to_all | solution.py:197
  60.3 1.2 attended.1
  61.5 1.6 %collective-permute-start.10 = (bf16[128,1024]{1,0:T(8,128)(2,1)S(1)}, bf16[128,1024]{1,0:T(8,128)(2,1)S(1)}, u32[]{:S(2)}, u32[]{:S(2)}) collective-permute-start(bf16[128,1024]{1,0:T(8,128)(2,1)S(1)} %get-tuple-element.25.own_ref), channel_id=1, source_target_pairs={{0,128},{1,129},{2,130},{3,131},{4,132},{5,133},{6,134},{7,135},{8... | collective-permute-start | bytes 786440 | tf_op jit(solution)/shard_map/ppermute | solution.py:47
  63.1 6.4 %collective-permute-done.10.neighbour_ref = bf16[128,1024]{1,0:T(8,128)(2,1)S(1)} collective-permute-done((bf16[128,1024]{1,0:T(8,128)(2,1)S(1)}, bf16[128,1024]{1,0:T(8,128)(2,1)S(1)}, u32[]{:S(2)}, u32[]{:S(2)}) %collective-permute-start.10) | collective-permute-done | bytes 262176 | tf_op jit(solution)/shard_map/ppermute | solution.py:47
  69.6 1.6 %collective-permute-start.6 = (bf16[192,512]{1,0:T(8,128)(2,1)S(1)}, bf16[192,512]{1,0:T(8,128)(2,1)S(1)}, u32[]{:S(2)}, u32[]{:S(2)}) collective-permute-start(bf16[192,512]{1,0:T(8,128)(2,1)S(1)} %slice.8), channel_id=1, source_target_pairs={{0,1},{1,2},{2,3},{3,0},{4,5},{5,6},{6,7},{7,4},{8,9},{9,10},{10,1... | collective-permute-start | bytes 589832 | tf_op jit(solution)/shard_map/ppermute | solution.py:47
  71.3 1.8 %collective-permute-start.7 = (bf16[192,512]{1,0:T(8,128)(2,1)S(1)}, bf16[192,512]{1,0:T(8,128)(2,1)S(1)}, u32[]{:S(2)}, u32[]{:S(2)}) collective-permute-start(bf16[192,512]{1,0:T(8,128)(2,1)S(1)} %slice.9), channel_id=1, source_target_pairs={{0,3},{1,0},{2,1},{3,2},{4,7},{5,4},{6,5},{7,6},{8,11},{9,8},{10,9... | collective-permute-start | bytes 589832 | tf_op jit(solution)/shard_map/ppermute | solution.py:47
  73.0 5.2 %collective-permute-done.6.low_ref = bf16[192,512]{1,0:T(8,128)(2,1)S(1)} collective-permute-done((bf16[192,512]{1,0:T(8,128)(2,1)S(1)}, bf16[192,512]{1,0:T(8,128)(2,1)S(1)}, u32[]{:S(2)}, u32[]{:S(2)}) %collective-permute-start.6) | collective-permute-done | bytes 196640 | tf_op jit(solution)/shard_map/ppermute | solution.py:47
  79.0 1.1 copy-done.5
  80.1 3.9 %weight_partial.1 = bf16[1536,1024]{1,0:T(8,128)(2,1)} custom-call(bf16[1536,512]{1,0:T(8,128)(2,1)S(1)} %get-tuple-element.24.block_ref, bf16[128,1024]{1,0:T(8,128)(2,1)S(1)} %get-tuple-element.25.own_ref, bf16[128,1024]{1,0:T(8,128)(2,1)S(1)} %collective-permute-done.10.neighbour_ref, bf16[128,1024]{1,0:T(8,128)(2,1)S(1)} %collective-permute-done.11.across_ref, ...), custom_call_target="tpu_custom_call" | custom-call | flops 1600000000 | bytes 6000000 | tf_op jit(solution)/shard_map/weight_partial/pallas_call | solution.py:270
  84.1 1.4 copy-done.6
  85.5 4.1 %project.1 = (f32[256,1024]{1,0:T(8,128)S(1)}, bf16[256,1024]{1,0:T(8,128)(2,1)S(1)}) custom-call(bf16[512,1536]{1,0:T(8,128)(2,1)S(1)} %copy-done.6, bf16[1536,1024]{1,0:T(8,128)(2,1)} %all-gather.2.cloned.1.call-done.weight_ref), custom_call_target="tpu_custom_call" | custom-call | flops 1600000000 | bytes 6000000 | tf_op jit(solution)/shard_map/project/pallas_call | solution.py:242
  90.0 2.0 %collective-permute-done.8 = bf16[256,1024]{1,0:T(8,128)(2,1)} collective-permute-done((bf16[256,1024]{1,0:T(8,128)(2,1)S(1)}, bf16[256,1024]{1,0:T(8,128)(2,1)}, u32[]{:S(2)}, u32[]{:S(2)}) %collective-permute-start.8) | collective-permute-done | bytes 524320 | tf_op jit(solution)/shard_map/ppermute | solution.py:47
  91.9 1.2 convert_add_fusion
  93.2 1.0 copy-done.7
  94.2 1.7 %collective-permute-start.9 = (bf16[128,1024]{1,0:T(8,128)(2,1)S(1)}, bf16[128,1024]{1,0:T(8,128)(2,1)S(1)}, u32[]{:S(2)}, u32[]{:S(2)}) collective-permute-start(bf16[128,1024]{1,0:T(8,128)(2,1)S(1)} %dynamic-slice_convert_fusion), channel_id=1, source_target_pairs={{0,128},{1,129},{2,130},{3,131},{4,132},{5,133},{6,134},{7,135},{8... | collective-permute-start | bytes 786440 | tf_op jit(solution)/shard_map/ppermute | solution.py:47
  95.9 1.1 constant_dynamic-slice_fusion.own_ref
  97.0 5.7 %collective-permute-done.9.other_ref = bf16[128,1024]{1,0:T(8,128)(2,1)S(1)} collective-permute-done((bf16[128,1024]{1,0:T(8,128)(2,1)S(1)}, bf16[128,1024]{1,0:T(8,128)(2,1)S(1)}, u32[]{:S(2)}, u32[]{:S(2)}) %collective-permute-start.9) | collective-permute-done | bytes 262176 | tf_op jit(solution)/shard_map/ppermute | solution.py:47
  103.4 18.9 %all_to_all.20.terms_ref = bf16[32,32,128]{2,1,0:T(8,128)(2,1)S(1)} all-to-all(bf16[32,32,128]{2,1,0:T(8,128)(2,1)S(1)} %get-tuple-element.20), channel_id=1, replica_groups=mesh['seq'=32,'head'=8] {'seq'}, dimensions={0} | all-to-all | bytes 524288 | tf_op jit(solution)/shard_map/all_to_all | solution.py:197
  122.4 16.6 %all_to_all.21 = bf16[32,32,128]{2,1,0:T(8,128)(2,1)S(1)} all-to-all(bf16[32,32,128]{2,1,0:T(8,128)(2,1)S(1)} %states_after.1), channel_id=1, replica_groups=mesh['seq'=32,'head'=8] {'seq'}, dimensions={0} | all-to-all | bytes 524288 | tf_op jit(solution)/shard_map/all_to_all | solution.py:197
  139.0 3.1 %grads.1 = (bf16[128,1024]{1,0:T(8,128)(2,1)}, bf16[128,1024]{1,0:T(8,128)(2,1)}, bf16[128,1024]{1,0:T(8,128)(2,1)}) custom-call(f32[128,8]{1,0:T(8,128)S(1)} %copy.20.decay_ref, bf16[128,1024]{1,0:T(8,128)(2,1)S(1)} %copy-done, bf16[128,1024]{1,0:T(8,128)(2,1)S(1)} %copy-done.2, bf16[128,1024]{1,0:T(8,128)(2,1)S(1)} %copy-done.4, ...), custom_call_target="tpu_custom_call" | custom-call | flops 270000000 | bytes 3000000 | tf_op jit(solution)/shard_map/grads/pallas_call | solution.py:292
  (43 shorter events, 4.2 us)
Async XLA Ops:
  7.2 53.1 %copy-start = (bf16[128,1024]{1,0:T(8,128)(2,1)S(1)}, bf16[128,1024]{1,0:T(8,128)(2,1)}, u32[]{:S(2)}) copy-start(bf16[128,1024]{1,0:T(8,128)(2,1)} %query_ref.5) | copy-start | bytes 786436
  7.2 76.9 %all-gather.2.cloned.1.call-start = ((), (), s32[]{:S(2)}) async-start(), calls=%async_computation.5 | async-start | bytes 3538944 | tf_op jit(solution)/shard_map/all_gather | solution.py:206
  8.7 0.9 copy-start.1
  9.6 0.9 copy-start.3
  10.6 49.7 %copy-start.2 = (bf16[128,1024]{1,0:T(8,128)(2,1)S(1)}, bf16[128,1024]{1,0:T(8,128)(2,1)}, u32[]{:S(2)}) copy-start(bf16[128,1024]{1,0:T(8,128)(2,1)} %key_ref.5) | copy-start | bytes 786436
  10.6 49.7 %copy-start.4 = (bf16[128,1024]{1,0:T(8,128)(2,1)S(1)}, bf16[128,1024]{1,0:T(8,128)(2,1)}, u32[]{:S(2)}) copy-start(bf16[128,1024]{1,0:T(8,128)(2,1)} %value_ref.5) | copy-start | bytes 786436
  12.1 28.0 %all-to-all-start = ((bf16[32,48,128]{2,1,0:T(8,128)(2,1)}), bf16[32,48,128]{2,1,0:T(8,128)(2,1)S(1)}, u32[]{:S(2)}, u32[]{:S(2)}) async-start(bf16[32,48,128]{2,1,0:T(8,128)(2,1)} %key_terms.1), calls=%async_computation | async-start | bytes 786432 | tf_op jit(solution)/shard_map/all_to_all | solution.py:197
  23.3 22.7 %collective-permute-start = (bf16[384,128]{1,0:T(8,128)(2,1)S(1)}, bf16[384,128]{1,0:T(8,128)(2,1)S(1)}, u32[]{:S(2)}, u32[]{:S(2)}) collective-permute-start(bf16[384,128]{1,0:T(8,128)(2,1)S(1)} %bitcast.13), channel_id=1, source_target_pairs={{0,0},{1,1},{2,2},{3,3},{4,128},{5,129},{6,130},{7,131},{8,8},{9,9... | collective-permute-start | bytes 294920 | tf_op jit(solution)/shard_map/ppermute | solution.py:47
  26.3 19.8 %collective-permute-start.1 = (bf16[384,128]{1,0:T(8,128)(2,1)S(1)}, bf16[384,128]{1,0:T(8,128)(2,1)S(1)}, u32[]{:S(2)}, u32[]{:S(2)}) collective-permute-start(bf16[384,128]{1,0:T(8,128)(2,1)S(1)} %bitcast.14), channel_id=1, source_target_pairs={{0,4},{1,5},{2,6},{3,7},{4,132},{5,133},{6,134},{7,135},{8,12},{9,... | collective-permute-start | bytes 294920 | tf_op jit(solution)/shard_map/ppermute | solution.py:47
  26.4 19.7 %collective-permute-start.2 = (bf16[384,128]{1,0:T(8,128)(2,1)S(1)}, bf16[384,128]{1,0:T(8,128)(2,1)S(1)}, u32[]{:S(2)}, u32[]{:S(2)}) collective-permute-start(bf16[384,128]{1,0:T(8,128)(2,1)S(1)} %bitcast.11), channel_id=1, source_target_pairs={{0,8},{1,9},{2,10},{3,11},{4,136},{5,137},{6,138},{7,139},{8,0},{9... | collective-permute-start | bytes 294920 | tf_op jit(solution)/shard_map/ppermute | solution.py:47
  26.9 19.2 %collective-permute-start.3 = (bf16[384,128]{1,0:T(8,128)(2,1)S(1)}, bf16[384,128]{1,0:T(8,128)(2,1)S(1)}, u32[]{:S(2)}, u32[]{:S(2)}) collective-permute-start(bf16[384,128]{1,0:T(8,128)(2,1)S(1)} %bitcast.12), channel_id=1, source_target_pairs={{0,12},{1,13},{2,14},{3,15},{4,140},{5,141},{6,142},{7,143},{8,4},... | collective-permute-start | bytes 294920 | tf_op jit(solution)/shard_map/ppermute | solution.py:47
  40.9 19.4 %all-to-all-start.1 = ((bf16[32,32,128]{2,1,0:T(8,128)(2,1)}), bf16[32,32,128]{2,1,0:T(8,128)(2,1)S(1)}, u32[]{:S(2)}, u32[]{:S(2)}) async-start(bf16[32,32,128]{2,1,0:T(8,128)(2,1)} %states_before.1), calls=%async_computation.1 | async-start | bytes 524288 | tf_op jit(solution)/shard_map/all_to_all | solution.py:197
  46.0 96.2 %reduce-scatter.2.cloned.1.call-start = ((), (), s32[]{:S(2)}) async-start(), calls=%async_computation.6 | async-start | bytes 3538944 | tf_op jit(solution)/shard_map/reduce_scatter | solution.py:283
  46.2 23.4 %collective-permute-start.4 = (bf16[384,512]{1,0:T(8,128)(2,1)S(1)}, bf16[384,512]{1,0:T(8,128)(2,1)S(1)}, u32[]{:S(2)}, u32[]{:S(2)}) collective-permute-start(bf16[384,512]{1,0:T(8,128)(2,1)S(1)} %constant_dynamic-update-slice_fusion.own_ref), channel_id=1, source_target_pairs={{0,1},{1,2},{2,3},{3,0},{4,5},{5,6},{6,7},{7,4},{8,9},{9,10},{10,1... | collective-permute-start | bytes 1179656 | tf_op jit(solution)/shard_map/ppermute | solution.py:47
  47.8 23.4 %collective-permute-start.5 = (bf16[384,512]{1,0:T(8,128)(2,1)S(1)}, bf16[384,512]{1,0:T(8,128)(2,1)S(1)}, u32[]{:S(2)}, u32[]{:S(2)}) collective-permute-start(bf16[384,512]{1,0:T(8,128)(2,1)S(1)} %constant_dynamic-update-slice_fusion.own_ref), channel_id=1, source_target_pairs={{0,3},{1,0},{2,1},{3,2},{4,7},{5,4},{6,5},{7,6},{8,11},{9,8},{10,9... | collective-permute-start | bytes 1179656 | tf_op jit(solution)/shard_map/ppermute | solution.py:47
  61.5 8.1 %collective-permute-start.10 = (bf16[128,1024]{1,0:T(8,128)(2,1)S(1)}, bf16[128,1024]{1,0:T(8,128)(2,1)S(1)}, u32[]{:S(2)}, u32[]{:S(2)}) collective-permute-start(bf16[128,1024]{1,0:T(8,128)(2,1)S(1)} %get-tuple-element.25.own_ref), channel_id=1, source_target_pairs={{0,128},{1,129},{2,130},{3,131},{4,132},{5,133},{6,134},{7,135},{8... | collective-permute-start | bytes 786440 | tf_op jit(solution)/shard_map/ppermute | solution.py:47
  63.1 17.0 %collective-permute-start.11 = (bf16[128,1024]{1,0:T(8,128)(2,1)S(1)}, bf16[128,1024]{1,0:T(8,128)(2,1)S(1)}, u32[]{:S(2)}, u32[]{:S(2)}) collective-permute-start(bf16[128,1024]{1,0:T(8,128)(2,1)S(1)} %get-tuple-element.25.own_ref), channel_id=1, source_target_pairs={{0,8},{1,9},{2,10},{3,11},{4,12},{5,13},{6,14},{7,15},{8,0},{9,1},... | collective-permute-start | bytes 786440 | tf_op jit(solution)/shard_map/ppermute | solution.py:47
  69.6 10.5 %collective-permute-start.12 = (bf16[128,1024]{1,0:T(8,128)(2,1)S(1)}, bf16[128,1024]{1,0:T(8,128)(2,1)S(1)}, u32[]{:S(2)}, u32[]{:S(2)}) collective-permute-start(bf16[128,1024]{1,0:T(8,128)(2,1)S(1)} %collective-permute-done.10.neighbour_ref), channel_id=1, source_target_pairs={{0,8},{1,9},{2,10},{3,11},{4,12},{5,13},{6,14},{7,15},{8,0},{9,1},... | collective-permute-start | bytes 786440 | tf_op jit(solution)/shard_map/ppermute | solution.py:47
  69.6 8.6 %collective-permute-start.6 = (bf16[192,512]{1,0:T(8,128)(2,1)S(1)}, bf16[192,512]{1,0:T(8,128)(2,1)S(1)}, u32[]{:S(2)}, u32[]{:S(2)}) collective-permute-start(bf16[192,512]{1,0:T(8,128)(2,1)S(1)} %slice.8), channel_id=1, source_target_pairs={{0,1},{1,2},{2,3},{3,0},{4,5},{5,6},{6,7},{7,4},{8,9},{9,10},{10,1... | collective-permute-start | bytes 589832 | tf_op jit(solution)/shard_map/ppermute | solution.py:47
  71.3 7.1 %collective-permute-start.7 = (bf16[192,512]{1,0:T(8,128)(2,1)S(1)}, bf16[192,512]{1,0:T(8,128)(2,1)S(1)}, u32[]{:S(2)}, u32[]{:S(2)}) collective-permute-start(bf16[192,512]{1,0:T(8,128)(2,1)S(1)} %slice.9), channel_id=1, source_target_pairs={{0,3},{1,0},{2,1},{3,2},{4,7},{5,4},{6,5},{7,6},{8,11},{9,8},{10,9... | collective-permute-start | bytes 589832 | tf_op jit(solution)/shard_map/ppermute | solution.py:47
  78.9 1.1 copy-start.5
  84.1 1.4 copy-start.6
  89.6 2.3 %collective-permute-start.8 = (bf16[256,1024]{1,0:T(8,128)(2,1)S(1)}, bf16[256,1024]{1,0:T(8,128)(2,1)}, u32[]{:S(2)}, u32[]{:S(2)}) collective-permute-start(bf16[256,1024]{1,0:T(8,128)(2,1)S(1)} %get-tuple-element.17), channel_id=1, source_target_pairs={{0,8},{1,9},{2,10},{3,11},{4,12},{5,13},{6,14},{7,15},{8,0},{9,1},... | collective-permute-start | bytes 1572872 | tf_op jit(solution)/shard_map/ppermute | solution.py:47
  93.2 1.0 copy-start.7
  94.2 8.4 %collective-permute-start.9 = (bf16[128,1024]{1,0:T(8,128)(2,1)S(1)}, bf16[128,1024]{1,0:T(8,128)(2,1)S(1)}, u32[]{:S(2)}, u32[]{:S(2)}) collective-permute-start(bf16[128,1024]{1,0:T(8,128)(2,1)S(1)} %dynamic-slice_convert_fusion), channel_id=1, source_target_pairs={{0,128},{1,129},{2,130},{3,131},{4,132},{5,133},{6,134},{7,135},{8... | collective-permute-start | bytes 786440 | tf_op jit(solution)/shard_map/ppermute | solution.py:47
Sparse Core Ops, SparseCore 0:
  9.8 60.3 all-gather.1
  84.2 53.5 reduce-scatter.1

commit v3 on v1

v3 whole, which is shorter than its diff:
```python
import functools

import jax
import jax.numpy as jnp
from jax import lax
from jax.experimental import pallas as pl
from jax.experimental.pallas import tpu as pltpu
from jax.sharding import PartitionSpec as P

HEAD_DIM = 128
BLOCK = 128
HEADS_LOCAL = 8
N_SEQ = 32
ROWS = 32
NZ = 8
TILES = 4
BF = jnp.bfloat16
F32 = jnp.float32
AXES = ("seq", "head")
PARAMS = pltpu.CompilerParams(vmem_limit_bytes=48 * 1024 * 1024)


def pairs(move):
    out = []
    for yl in range(2):
        for z in range(8):
            for c in range(2):
                for yh in range(2):
                    for x in range(4):
                        a, b, d, e, f = move(yl, z, c, yh, x)
                        out.append(
                            (
                                (yl * 16 + z * 2 + c) * 8 + yh * 4 + x,
                                (a * 16 + (b % 8) * 2 + d) * 8 + e * 4 + f % 4,
                            )
                        )
    return out


Z_UP = pairs(lambda yl, z, c, yh, x: (yl, z + 1, c, yh, x))
Z_DOWN = pairs(lambda yl, z, c, yh, x: (yl, z + 7, c, yh, x))
X_UP = pairs(lambda yl, z, c, yh, x: (yl, z, c, yh, x + 1))
X_DOWN = pairs(lambda yl, z, c, yh, x: (yl, z, c, yh, x + 3))
CORE = pairs(lambda yl, z, c, yh, x: (yl, z, 1 - c, yh, x))
Y_LO = pairs(lambda yl, z, c, yh, x: (1 - yl, z, c, yh, x))


def send(array, table):
    return lax.ppermute(array, AXES, table)


def mm(a, b, ca, cb):
    return lax.dot_general(a, b, (((ca,), (cb,)), ((), ())), preferred_element_type=F32)


def coordinates():
    seq, head = lax.axis_index("seq"), lax.axis_index("head")
    y_lo = seq // 16
    rest = seq - 16 * y_lo
    z = rest // 2
    core = rest - 2 * z
    y_hi = head // 4
    return y_lo, z, core, y_hi, head - 4 * y_hi


def flip_bit():
    y_lo, _, _, y_hi, _ = coordinates()
    return y_lo + y_hi - 2 * y_lo * y_hi


def within_columns(decay):
    at = lax.broadcasted_iota(jnp.int32, (BLOCK, BLOCK), 0)
    of = lax.broadcasted_iota(jnp.int32, (BLOCK, BLOCK), 1)
    lower = (of <= at).astype(F32)
    return lax.dot_general(
        lower, decay, (((1,), (0,)), ((), ())),
        precision=lax.Precision.HIGHEST, preferred_element_type=F32,
    )


def causal_mask(within_col):
    gaps = within_col - jnp.transpose(within_col)
    at = lax.broadcasted_iota(jnp.int32, (BLOCK, BLOCK), 0)
    of = lax.broadcasted_iota(jnp.int32, (BLOCK, BLOCK), 1)
    return jnp.exp(jnp.where(at >= of, gaps, -jnp.inf))


def head_cols(h):
    return pl.ds(h * HEAD_DIM, HEAD_DIM)


def cotangent_kernel(cot_ref, same_ref, swap_ref):
    _, _, core, _, _ = coordinates()
    turned = jnp.transpose(cot_ref[...])
    share = turned.shape[0] // 4
    for i in range(2):
        first = turned[(2 * i) * share : (2 * i + 1) * share]
        second = turned[(2 * i + 1) * share : (2 * i + 2) * share]
        rows = pl.ds(i * share, share)

        @pl.when(core == 0)
        def _():
            same_ref[rows, :] = first
            swap_ref[rows, :] = second

        @pl.when(core == 1)
        def _():
            same_ref[rows, :] = second
            swap_ref[rows, :] = first


def key_terms_kernel(decay_ref, key_ref, value_ref, out_ref):
    within = within_columns(decay_ref[...])
    row = lax.broadcasted_iota(jnp.int32, (16, HEAD_DIM), 0)
    for h in range(HEADS_LOCAL):
        col = within[:, h : h + 1]
        last = within[BLOCK - 1 : BLOCK, h : h + 1]
        scaled = (jnp.exp(last - col) * key_ref[:, head_cols(h)].astype(F32)).astype(BF)
        terms = mm(scaled, value_ref[:, head_cols(h)], 0, 0).astype(BF)
        high = last.astype(BF).astype(F32)
        middle = (last - high).astype(BF).astype(F32)
        low = last - high - middle
        parts = jnp.where(row == 0, high, jnp.where(row == 1, middle, jnp.where(row == 2, low, 0.0)))
        parts = parts.astype(BF)
        for i in range(4):
            out_ref[4 * h + i, 0:ROWS, :] = terms[i * ROWS : (i + 1) * ROWS]
            out_ref[4 * h + i, ROWS : ROWS + 16, :] = parts


def recurrence_kernel(reverse, decay_ref, terms_ref, *rest):
    out_ref = rest[-1]
    state = jnp.zeros((ROWS, HEAD_DIM), F32)
    for k in reversed(range(N_SEQ)) if reverse else range(N_SEQ):
        out_ref[k] = state.astype(BF)
        parts = decay_ref[k, ROWS : ROWS + 16, :].astype(F32)
        factor = jnp.exp(parts[0:1] + (parts[1:2] + parts[2:3]))
        state = factor * state + terms_ref[k, 0:ROWS, :].astype(F32)


def attended_kernel(decay_ref, query_ref, key_ref, value_ref, state_ref, *rest):
    att_ref, score_ref = rest[-2:]
    within = within_columns(decay_ref[...])
    for h in range(HEADS_LOCAL):
        cols = head_cols(h)
        col = within[:, h : h + 1]
        query = query_ref[:, cols]
        scores = (mm(query, key_ref[:, cols], 1, 1) * causal_mask(col)).astype(BF)
        score_ref[:, cols] = scores
        att = jnp.exp(col) * mm(query, state_ref[pl.ds(h * HEAD_DIM, HEAD_DIM), :], 1, 0)
        att_ref[:, cols] = (att + mm(scores, value_ref[:, cols], 1, 0)).astype(BF)


def query_terms_kernel(decay_ref, query_ref, own_ref, core_ref, other_ref, *rest):
    grad_ref, out_ref = rest[-2:]
    within = within_columns(decay_ref[...])
    for h in range(HEADS_LOCAL):
        cols = head_cols(h)
        grad = own_ref[:, cols] + core_ref[:, cols].astype(F32) + other_ref[:, cols].astype(F32)
        grad = grad.astype(BF)
        grad_ref[:, cols] = grad
        scaled = (jnp.exp(within[:, h : h + 1]) * query_ref[:, cols].astype(F32)).astype(BF)
        terms = mm(scaled, grad, 0, 0).astype(BF)
        for i in range(4):
            out_ref[4 * h + i] = terms[i * ROWS : (i + 1) * ROWS]


def inner_grads_kernel(
    decay_ref, query_ref, key_ref, value_ref, grad_ref, score_ref, state_ref,
    gq_ref, gk_ref, gv_ref,
):
    within = within_columns(decay_ref[...])
    for h in range(HEADS_LOCAL):
        cols = head_cols(h)
        col = within[:, h : h + 1]
        grad, key = grad_ref[:, cols], key_ref[:, cols]
        grad_scores = (mm(grad, value_ref[:, cols], 1, 1) * causal_mask(col)).astype(BF)
        state = state_ref[pl.ds(h * HEAD_DIM, HEAD_DIM), :]
        gq = jnp.exp(col) * mm(grad, state, 1, 1) + mm(grad_scores, key, 1, 0)
        gq_ref[:, cols] = gq.astype(BF)
        gk_ref[:, cols] = mm(grad_scores, query_ref[:, cols], 0, 0)
        gv_ref[:, cols] = mm(score_ref[:, cols], grad, 0, 0)


def outer_grads_kernel(
    decay_ref, key_ref, value_ref, inner_k_ref, inner_v_ref, after_ref, gk_ref, gv_ref
):
    within = within_columns(decay_ref[...])
    for h in range(HEADS_LOCAL):
        cols = head_cols(h)
        key_weight = jnp.exp(within[BLOCK - 1 : BLOCK, h : h + 1] - within[:, h : h + 1])
        after = after_ref[pl.ds(h * HEAD_DIM, HEAD_DIM), :]
        gk = key_weight * mm(value_ref[:, cols], after, 1, 1) + inner_k_ref[:, cols]
        gk_ref[:, cols] = gk.astype(BF)
        gv = key_weight * mm(key_ref[:, cols], after, 1, 0) + inner_v_ref[:, cols]
        gv_ref[:, cols] = gv.astype(BF)


def collect_kernel(a_ref, b_ref, c_ref, d_ref, out_ref):
    flip = flip_bit()
    for i, ref in ((flip, a_ref), (1 - flip, b_ref), (2 + flip, c_ref), (3 - flip, d_ref)):
        out_ref[:, pl.ds(pl.multiple_of(i * BLOCK, BLOCK), BLOCK)] = ref[...]


def assemble_kernel(share, own_ref, left_ref, right_ref, low_ref, high_ref, out_ref, out_t_ref):
    _, z, _, _, x = coordinates()
    for off, ref, start, part in (
        (0, own_ref, 0, 0), (0, own_ref, share, 1),
        (1, right_ref, 0, 0), (1, right_ref, share, 1),
        (2, low_ref, 0, 0), (2, high_ref, 0, 1),
        (3, left_ref, 0, 0), (3, left_ref, share, 1),
    ):
        k = (2 * ((x + off) % 4) + part - z + NZ) % NZ
        at = pl.multiple_of(k * share, 64)
        out_ref[pl.ds(at, share), :] = ref[start : start + share, :]
    for i in range(NZ * share // 256):
        rows = pl.ds(i * 256, 256)
        out_t_ref[:, rows] = jnp.transpose(out_ref[rows, :])


def project_kernel(block_ref, *refs):
    pieces, (kept_ref, theirs_ref, cross_ref, cross_theirs_ref), weight_ref = refs[:9], refs[-5:-1], refs[-1]
    at = 0
    for ref in pieces:
        weight_ref[at : at + ref.shape[0], :] = ref[...]
        at += ref.shape[0]
    out = mm(block_ref[...], weight_ref[...], 1, 0)
    kept_ref[...] = out[0:BLOCK]
    theirs_ref[...] = out[BLOCK : 2 * BLOCK]
    cross_ref[...] = out[2 * BLOCK : 3 * BLOCK].astype(BF)
    cross_theirs_ref[...] = out[3 * BLOCK : 4 * BLOCK].astype(BF)


def weight_kernel(block_ref, own_ref, neighbour_ref, across_ref, diagonal_ref, *rest):
    outs, tokens_ref = rest[-10:-1], rest[-1]
    for i, ref in enumerate((own_ref, neighbour_ref, across_ref, diagonal_ref)):
        tokens_ref[i * BLOCK : (i + 1) * BLOCK, :] = ref[...]
    out = mm(block_ref[...], tokens_ref[...], 1, 0).astype(BF)
    at = 0
    for ref in outs:
        ref[...] = out[at : at + ref.shape[0]]
        at += ref.shape[0]


def add_kernel(a_ref, b_ref, out_ref):
    out_ref[...] = (a_ref[...].astype(F32) + b_ref[...].astype(F32)).astype(BF)


def first_adds_kernel(up_part_ref, up_ref, down_part_ref, down_ref, up_out_ref, down_out_ref):
    half = up_ref.shape[0]
    up_out_ref[:half] = (up_part_ref[:half].astype(F32) + up_ref[...].astype(F32)).astype(BF)
    up_out_ref[half:] = up_part_ref[half:]
    down_out_ref[:half] = down_part_ref[:half]
    down_out_ref[half:] = (down_part_ref[half:].astype(F32) + down_ref[...].astype(F32)).astype(BF)


def adds_kernel(up_part_ref, up_ref, down_part_ref, down_ref, up_out_ref, down_out_ref):
    up_out_ref[...] = (up_part_ref[...].astype(F32) + up_ref[...].astype(F32)).astype(BF)
    down_out_ref[...] = (down_part_ref[...].astype(F32) + down_ref[...].astype(F32)).astype(BF)


def last_add_kernel(part_ref, up_ref, down_ref, out_ref):
    out_ref[...] = (
        part_ref[...].astype(F32) + (up_ref[...].astype(F32) + down_ref[...].astype(F32))
    ).astype(BF)


def shape(dims, dtype=BF):
    return jax.ShapeDtypeStruct(dims, dtype)


def call(body, outs, name, flops, moved, args, after=()):
    return pl.pallas_call(
        body,
        in_specs=[pl.BlockSpec(a.shape, lambda n=a.ndim: (0,) * n) for a in args]
        + [pl.BlockSpec(memory_space=pl.ANY)] * len(after),
        out_shape=outs,
        compiler_params=PARAMS,
        name=name,
        cost_estimate=pl.CostEstimate(flops=flops, bytes_accessed=moved, transcendentals=0),
    )(*args, *after)


def exchange(array):
    return lax.all_to_all(array, "seq", 0, 0, tiled=True)


def body(cotangent, queries, key_proj, value_proj, log_decay, out_weight):
    tokens, cols = queries.shape
    share = out_weight.shape[0]
    half = share // 2
    features = NZ * share
    row = shape((tokens, cols))
    row32 = shape((tokens, cols), F32)
    piece = shape((share, cols))
    state = shape((N_SEQ, ROWS, HEAD_DIM))

    below, above = [send(out_weight, Z_UP)], [send(out_weight, Z_DOWN)]

    terms = call(
        key_terms_kernel, shape((N_SEQ, ROWS + 16, HEAD_DIM)), "key_terms", 40_000_000, 1_000_000,
        (log_decay, key_proj, value_proj),
    )
    parts = call(
        cotangent_kernel, (shape((2 * share, tokens)),) * 2, "cotangent_parts", 0, 400_000, (cotangent,)
    )
    pieces = []
    for a in range(2):
        for b in range(2):
            table = pairs(lambda yl, z, c, yh, x, a=a, b=b: (yh, z, c ^ a, yl ^ b, x))
            pieces.append(send(parts[a], table))
    gathered = exchange(terms)
    own = call(collect_kernel, shape((2 * share, 4 * tokens)), "collect", 0, 800_000, pieces)
    left, right = send(own, X_UP), send(own, X_DOWN)

    befores = call(
        functools.partial(recurrence_kernel, False), state, "states_before", 1_000_000, 1_000_000,
        (gathered, gathered), (below[0], above[0], own),
    )
    below.append(send(below[-1], Z_UP))
    above.append(send(above[-1], Z_DOWN))
    states = exchange(befores).reshape(cols, HEAD_DIM)
    attended, scores = call(
        attended_kernel, (row, row), "attended", 110_000_000, 2_000_000,
        (log_decay, queries, key_proj, value_proj, states), (below[1], above[1], left, right),
    )
    below.append(send(below[-1], Z_UP))
    above.append(send(above[-1], Z_DOWN))
    across = send(attended, CORE)
    neighbour = send(attended, Y_LO)
    opposite_low = send(left[:share], X_UP)
    opposite_high = send(right[share:], X_DOWN)
    block, block_t = call(
        functools.partial(assemble_kernel, share),
        (shape((features, 4 * tokens)), shape((4 * tokens, features))), "assemble",
        1_000_000, 5_000_000, (own, left, right, opposite_low, opposite_high),
    )
    diagonal = send(neighbour, CORE)
    far_low = send(below[2][:half], Z_UP)
    far_high = send(above[2][half:], Z_DOWN)

    width = cols // TILES
    column_spec = pl.BlockSpec((tokens, width), lambda i: (0, i))
    piece_spec = pl.BlockSpec((share, width), lambda i: (0, i))
    half_spec = pl.BlockSpec((half, width), lambda i: (0, i))
    ring_specs = [piece_spec] * 4 + [half_spec] * 2 + [piece_spec] * 3
    cost = pl.CostEstimate(flops=1_600_000_000, bytes_accessed=6_000_000, transcendentals=0)
    part = pl.pallas_call(
        weight_kernel,
        grid=(TILES,),
        in_specs=[pl.BlockSpec((features, 4 * tokens), lambda i: (0, 0))]
        + [column_spec] * 4
        + [pl.BlockSpec(memory_space=pl.ANY)] * 2,
        out_specs=ring_specs,
        out_shape=[piece] * 4 + [shape((half, cols))] * 2 + [piece] * 3,
        scratch_shapes=[pltpu.VMEM((4 * tokens, width), BF)],
        compiler_params=PARAMS,
        name="weight_partial",
        cost_estimate=cost,
    )(block, attended, neighbour, across, diagonal, below[2], above[2])
    up, down = send(part[4], Z_UP), send(part[5], Z_DOWN)

    weights = [out_weight] + above + [far_low, far_high] + below[::-1]
    kept, theirs, cross, cross_theirs = pl.pallas_call(
        project_kernel,
        grid=(TILES,),
        in_specs=[pl.BlockSpec((4 * tokens, features), lambda i: (0, 0))] + ring_specs,
        out_specs=[column_spec] * 4,
        out_shape=[row32, row32, row, row],
        scratch_shapes=[pltpu.VMEM((features, width), BF)],
        compiler_params=PARAMS,
        name="project",
        cost_estimate=cost,
    )(block_t, *weights)
    from_core_theirs = send(cross_theirs, CORE)
    from_core = send(cross, CORE)
    passed = call(add_kernel, row, "sum_theirs", 100_000, 1_000_000, (theirs, from_core_theirs))
    arrived = send(passed, Y_LO)
    up, down = call(
        first_adds_kernel, (piece, piece), "ring_sum_3", 400_000, 2_000_000,
        (part[3], up, part[6], down),
    )
    up, down = send(up, Z_UP), send(down, Z_DOWN)
    grad_attn, query_terms = call(
        query_terms_kernel, (row, state), "query_terms", 40_000_000, 1_000_000,
        (log_decay, queries, kept, from_core, arrived),
    )
    returned = exchange(query_terms)
    up, down = call(
        adds_kernel, (piece, piece), "ring_sum_2", 400_000, 2_000_000, (part[2], up, part[7], down)
    )
    afters = call(
        functools.partial(recurrence_kernel, True), state, "states_after", 1_000_000, 1_000_000,
        (gathered, returned), (up, down),
    )
    up, down = send(up, Z_UP), send(down, Z_DOWN)
    after = exchange(afters).reshape(cols, HEAD_DIM)
    grad_queries, inner_k, inner_v = call(
        inner_grads_kernel, (row, row32, row32), "inner_grads", 200_000_000, 3_000_000,
        (log_decay, queries, key_proj, value_proj, grad_attn, scores, states),
    )
    up, down = call(
        adds_kernel, (piece, piece), "ring_sum_1", 400_000, 2_000_000, (part[1], up, part[8], down)
    )
    up, down = send(up, Z_UP), send(down, Z_DOWN)
    grad_keys, grad_values = call(
        outer_grads_kernel, (row, row), "outer_grads", 70_000_000, 3_000_000,
        (log_decay, key_proj, value_proj, inner_k, inner_v, after),
    )
    grad_weight = call(last_add_kernel, piece, "ring_sum_0", 400_000, 2_000_000, (part[0], up, down))
    return grad_queries, grad_keys, grad_values, grad_weight


def solution(mesh):
    placed = P("seq", "head")
    return jax.shard_map(
        body,
        mesh=mesh,
        in_specs=(placed,) * 6,
        out_specs=(placed,) * 4,
        check_vma=False,
    )
```

time: 169 us -> 154 us (0.911)
  Pallas kernels: 8.8 us -> 26.3 us
  local copies, waits for them, and re-layouts: 25.4 us -> 9.66 us
  matrix products: 9.63 us -> 0 us
  other arithmetic: 8.53 us -> 0 us
  starting transfers between devices: 65.3 us -> 72.1 us
  waiting for transfers between devices: 48.4 us -> 43.5 us
    pallas_call x6 -> x17, Pallas kernels: 8.8 us -> 26.3 us  [the longest x15 17.3 us: call(): pl.pallas_call(body, in_specs=[pl.BlockSpec(a.shape, lambda n=a.ndim: (0,...]
    unnamed x42 -> x41, local copies, waits for them, and re-layouts: 22.9 us -> 7.75 us
    all_to_all x4, waiting for transfers between devices: 21.1 us -> 8.07 us  [exchange(): return lax.all_to_all(array, 'seq', 0, 0, tiled=True)]
    dot_general x3 -> x0, matrix products: 9.63 us -> none  [the longest x2 6.38 us: project(): lax.dot_general(part, weights, (((0,), (0,)), ((), ())), preferred_elemen...]
    ppermute x28 -> x30, waiting for transfers between devices: 27.4 us -> 35.4 us  [send(): return lax.ppermute(array, AXES, table)]
    convert_element_type x5 -> x0, other arithmetic: 7.6 us -> none  [the longest x2 3.53 us: body(): (part[k].astype(F32) + send(going_up, Z_UP).astype(F32)).astype(BF)]
    all_to_all x4, starting transfers between devices: 24.4 us -> 29.3 us  [exchange(): return lax.all_to_all(array, 'seq', 0, 0, tiled=True)]
    concatenate x3 -> x0, local copies, waits for them, and re-layouts: 2.29 us -> none  [the longest x1 0.78 us: body(): jnp.concatenate([out_weight] + above + [far_low, far_high] + below[::-1],...]
  transfers between devices with their start and end apart: 32 -> 34, of which waited for: 16 -> 10; matrix products, arithmetic and copies ran while one was open for 21% -> 1% of each run, Pallas kernels for 5% -> 15%
where the time goes in v3:
time: 154 us; the launch traced here: 153 us
  starting transfers between devices  72.1 us (47%)
  waiting for transfers between devices  43.5 us (28%)
  Pallas kernels  26.3 us (17%)
  local copies, waits for them, and re-layouts  9.66 us (6%)
    ppermute x30, starting transfers between devices, send(): return lax.ppermute(array, AXES, table)  42.8 us
    ppermute x30, waiting for transfers between devices, send(): return lax.ppermute(array, AXES, table)  35.4 us
    all_to_all x4, starting transfers between devices, exchange(): return lax.all_to_all(array, 'seq', 0, 0, tiled=True)  29.3 us
    pallas_call x15, Pallas kernels, call(): pl.pallas_call(body, in_specs=[pl.BlockSpec(a.shape, lambda n=a.ndim: (0,...  17.3 us
    all_to_all x4, waiting for transfers between devices, exchange(): return lax.all_to_all(array, 'seq', 0, 0, tiled=True)  8.07 us
    unnamed x41, local copies, waits for them, and re-layouts  7.75 us
    pallas_call x1, Pallas kernels, body(): pl.pallas_call(project_kernel, grid=(TILES,), in_specs=[pl.BlockSpec((4 *...  4.74 us
    pallas_call x1, Pallas kernels, body(): pl.pallas_call(weight_kernel, grid=(TILES,), in_specs=[pl.BlockSpec((feat...  4.3 us
  transfers between devices with their start and end apart: 34, of which 10 were waited for; matrix products, arithmetic and copies ran while one was open for 1% of the time, Pallas kernels for 15%

profile of v3, /device:TPU:8, one launch (start us, length us, event | category | flops | bytes accessed | tf_op | source)
XLA Modules:
  0.0 152.5 jit_solution(9518260547584621387)
XLA Ops:
  4.8 10.1 %all-to-all-start = ((bf16[32,48,128]{2,1,0:T(8,128)(2,1)}), bf16[32,48,128]{2,1,0:T(8,128)(2,1)S(1)}, u32[]{:S(2)}, u32[]{:S(2)}) async-start(bf16[32,48,128]{2,1,0:T(8,128)(2,1)} %key_terms.1), calls=%async_computation | async-start | bytes 786432 | tf_op jit(solution)/shard_map/all_to_all | solution.py:284
  16.4 1.8 %collective-permute-start.8 = (bf16[192,1024]{1,0:T(8,128)(2,1)S(1)}, bf16[192,1024]{1,0:T(8,128)(2,1)S(1)}, u32[]{:S(2)}, u32[]{:S(2)}) collective-permute-start(bf16[192,1024]{1,0:T(8,128)(2,1)S(1)} %copy-done.18), channel_id=1, source_target_pairs={{0,112},{1,113},{2,114},{3,115},{4,116},{5,117},{6,118},{7,119},{8... | collective-permute-start | bytes 1179656 | tf_op jit(solution)/shard_map/ppermute | solution.py:49
  18.3 3.0 %collective-permute-start = (bf16[384,128]{1,0:T(8,128)(2,1)S(1)}, bf16[384,128]{1,0:T(8,128)(2,1)S(1)}, u32[]{:S(2)}, u32[]{:S(2)}) collective-permute-start(bf16[384,128]{1,0:T(8,128)(2,1)S(1)} %get-tuple-element.36), channel_id=1, source_target_pairs={{0,0},{1,1},{2,2},{3,3},{4,128},{5,129},{6,130},{7,131},{8,8},{9,9... | collective-permute-start | bytes 294920 | tf_op jit(solution)/shard_map/ppermute | solution.py:49
  21.3 14.3 %collective-permute-done.11.refs_8_.rest_0_ = bf16[192,1024]{1,0:T(8,128)(2,1)S(1)} collective-permute-done((bf16[192,1024]{1,0:T(8,128)(2,1)S(1)}, bf16[192,1024]{1,0:T(8,128)(2,1)S(1)}, u32[]{:S(2)}, u32[]{:S(2)}) %collective-permute-start.11) | collective-permute-done | bytes 393248 | tf_op jit(solution)/shard_map/ppermute | solution.py:49
  35.6 3.2 %collective-permute-start.9 = (bf16[192,1024]{1,0:T(8,128)(2,1)S(1)}, bf16[192,1024]{1,0:T(8,128)(2,1)}, u32[]{:S(2)}, u32[]{:S(2)}) collective-permute-start(bf16[192,1024]{1,0:T(8,128)(2,1)S(1)} %collective-permute-done.8.refs_1_.rest_1_), channel_id=1, source_target_pairs={{0,112},{1,113},{2,114},{3,115},{4,116},{5,117},{6,118},{7,119},{8... | collective-permute-start | bytes 1179656 | tf_op jit(solution)/shard_map/ppermute | solution.py:49
  40.1 2.2 %collective-permute-start.3 = (bf16[384,128]{1,0:T(8,128)(2,1)S(1)}, bf16[384,128]{1,0:T(8,128)(2,1)S(1)}, u32[]{:S(2)}, u32[]{:S(2)}) collective-permute-start(bf16[384,128]{1,0:T(8,128)(2,1)S(1)} %get-tuple-element.37), channel_id=1, source_target_pairs={{0,12},{1,13},{2,14},{3,15},{4,140},{5,141},{6,142},{7,143},{8,4},... | collective-permute-start | bytes 294920 | tf_op jit(solution)/shard_map/ppermute | solution.py:49
  42.3 3.1 %collective-permute-done.1.b_ref = bf16[384,128]{1,0:T(8,128)(2,1)S(1)} collective-permute-done((bf16[384,128]{1,0:T(8,128)(2,1)S(1)}, bf16[384,128]{1,0:T(8,128)(2,1)S(1)}, u32[]{:S(2)}, u32[]{:S(2)}) %collective-permute-start.1) | collective-permute-done | bytes 98336 | tf_op jit(solution)/shard_map/ppermute | solution.py:49
  45.4 2.7 %collective-permute-done.2.c_ref = bf16[384,128]{1,0:T(8,128)(2,1)S(1)} collective-permute-done((bf16[384,128]{1,0:T(8,128)(2,1)S(1)}, bf16[384,128]{1,0:T(8,128)(2,1)S(1)}, u32[]{:S(2)}, u32[]{:S(2)}) %collective-permute-start.2) | collective-permute-done | bytes 98336 | tf_op jit(solution)/shard_map/ppermute | solution.py:49
  49.1 6.3 %all-to-all-start.1 = ((bf16[32,32,128]{2,1,0:T(8,128)(2,1)}), bf16[32,32,128]{2,1,0:T(8,128)(2,1)S(1)}, u32[]{:S(2)}, u32[]{:S(2)}) async-start(bf16[32,32,128]{2,1,0:T(8,128)(2,1)} %states_before.1), calls=%async_computation.1 | async-start | bytes 524288 | tf_op jit(solution)/shard_map/all_to_all | solution.py:284
  57.0 1.7 %collective-permute-start.5 = (bf16[384,512]{1,0:T(8,128)(2,1)S(1)}, bf16[384,512]{1,0:T(8,128)(2,1)S(1)}, u32[]{:S(2)}, u32[]{:S(2)}) collective-permute-start(bf16[384,512]{1,0:T(8,128)(2,1)S(1)} %collect.1.own_ref.rest_2_), channel_id=1, source_target_pairs={{0,3},{1,0},{2,1},{3,2},{4,7},{5,4},{6,5},{7,6},{8,11},{9,8},{10,9... | collective-permute-start | bytes 1179656 | tf_op jit(solution)/shard_map/ppermute | solution.py:49
  60.2 1.8 %collective-permute-start.10 = (bf16[192,1024]{1,0:T(8,128)(2,1)}, bf16[192,1024]{1,0:T(8,128)(2,1)}, u32[]{:S(2)}, u32[]{:S(2)}) collective-permute-start(bf16[192,1024]{1,0:T(8,128)(2,1)} %collective-permute-done.9.refs_2_.rest_1_), channel_id=1, source_target_pairs={{0,112},{1,113},{2,114},{3,115},{4,116},{5,117},{6,118},{7,119},{8... | collective-permute-start | bytes 1179656 | tf_op jit(solution)/shard_map/ppermute | solution.py:49
  61.9 5.9 %collective-permute-done.4.left_ref.rest_2_ = bf16[384,512]{1,0:T(8,128)(2,1)S(1)} collective-permute-done((bf16[384,512]{1,0:T(8,128)(2,1)S(1)}, bf16[384,512]{1,0:T(8,128)(2,1)S(1)}, u32[]{:S(2)}, u32[]{:S(2)}) %collective-permute-start.4) | collective-permute-done | bytes 393248 | tf_op jit(solution)/shard_map/ppermute | solution.py:49
  70.2 1.7 %collective-permute-start.6 = (bf16[192,512]{1,0:T(8,128)(2,1)S(1)}, bf16[192,512]{1,0:T(8,128)(2,1)S(1)}, u32[]{:S(2)}, u32[]{:S(2)}) collective-permute-start(bf16[192,512]{1,0:T(8,128)(2,1)S(1)} %slice.16), channel_id=1, source_target_pairs={{0,1},{1,2},{2,3},{3,0},{4,5},{5,6},{6,7},{7,4},{8,9},{9,10},{10,1... | collective-permute-start | bytes 589832 | tf_op jit(solution)/shard_map/ppermute | solution.py:49
  71.9 1.9 %collective-permute-start.7 = (bf16[192,512]{1,0:T(8,128)(2,1)S(1)}, bf16[192,512]{1,0:T(8,128)(2,1)S(1)}, u32[]{:S(2)}, u32[]{:S(2)}) collective-permute-start(bf16[192,512]{1,0:T(8,128)(2,1)S(1)} %slice.17), channel_id=1, source_target_pairs={{0,3},{1,0},{2,1},{3,2},{4,7},{5,4},{6,5},{7,6},{8,11},{9,8},{10,9... | collective-permute-start | bytes 589832 | tf_op jit(solution)/shard_map/ppermute | solution.py:49
  76.8 2.3 %collective-permute-start.15 = (bf16[96,1024]{1,0:T(8,128)(2,1)S(1)}, bf16[96,1024]{1,0:T(8,128)(2,1)S(1)}, u32[]{:S(2)}, u32[]{:S(2)}) collective-permute-start(bf16[96,1024]{1,0:T(8,128)(2,1)S(1)} %slice.19), channel_id=1, source_target_pairs={{0,112},{1,113},{2,114},{3,115},{4,116},{5,117},{6,118},{7,119},{8... | collective-permute-start | bytes 589832 | tf_op jit(solution)/shard_map/ppermute | solution.py:49
  82.5 4.7 %project.1 = (f32[128,1024]{1,0:T(8,128)S(1)}, f32[128,1024]{1,0:T(8,128)S(1)}, bf16[128,1024]{1,0:T(8,128)(2,1)S(1)}, bf16[128,1024]{1,0:T(8,128)(2,1)S(1)}) custom-call(bf16[512,1536]{1,0:T(8,128)(2,1)} %copy-done.17, bf16[192,1024]{1,0:T(8,128)(2,1)S(1)} %copy-done.19, bf16[192,1024]{1,0:T(8,128)(2,1)S(1)} %collective-permute-done.8.refs_1_.rest_1_, ...), custom_call_target="tpu_custom_call" | custom-call | flops 1600000000 | bytes 6000000 | tf_op jit(solution)/shard_map/project/pallas_call | solution.py:363
  87.5 4.3 %weight_partial.1 = (bf16[192,1024]{1,0:T(8,128)(2,1)S(1)}, bf16[192,1024]{1,0:T(8,128)(2,1)S(1)}, bf16[192,1024]{1,0:T(8,128)(2,1)S(1)}, bf16[192,1024]{1,0:T(8...) custom-call(bf16[1536,512]{1,0:T(8,128)(2,1)} %copy-done.16, ...), custom_call_target="tpu_custom_call" | custom-call | flops 1600000000 | bytes 6000000 | tf_op jit(solution)/shard_map/weight_partial/pallas_call | solution.py:347
  93.3 2.1 %collective-permute-start.23 = (bf16[96,1024]{1,0:T(8,128)(2,1)S(1)}, bf16[96,1024]{1,0:T(8,128)(2,1)S(1)}, u32[]{:S(2)}, u32[]{:S(2)}) collective-permute-start(bf16[96,1024]{1,0:T(8,128)(2,1)S(1)} %get-tuple-element.55), channel_id=1, source_target_pairs={{0,112},{1,113},{2,114},{3,115},{4,116},{5,117},{6,118},{7,119},{8... | collective-permute-start | bytes 589832 | tf_op jit(solution)/shard_map/ppermute | solution.py:49
  96.7 4.2 %collective-permute-done.22.up_ref = bf16[96,1024]{1,0:T(8,128)(2,1)S(1)} collective-permute-done((bf16[96,1024]{1,0:T(8,128)(2,1)S(1)}, bf16[96,1024]{1,0:T(8,128)(2,1)S(1)}, u32[]{:S(2)}, u32[]{:S(2)}) %collective-permute-start.22) | collective-permute-done | bytes 196640 | tf_op jit(solution)/shard_map/ppermute | solution.py:49
  101.7 3.0 %collective-permute-start.24 = (bf16[192,1024]{1,0:T(8,128)(2,1)}, bf16[192,1024]{1,0:T(8,128)(2,1)S(1)}, u32[]{:S(2)}, u32[]{:S(2)}) collective-permute-start(bf16[192,1024]{1,0:T(8,128)(2,1)} %get-tuple-element.56), channel_id=1, source_target_pairs={{0,16},{1,17},{2,18},{3,19},{4,20},{5,21},{6,22},{7,23},{8,24},{9,... | collective-permute-start | bytes 1179656 | tf_op jit(solution)/shard_map/ppermute | solution.py:49
  107.1 7.8 %all-to-all-start.2 = ((bf16[32,32,128]{2,1,0:T(8,128)(2,1)}), bf16[32,32,128]{2,1,0:T(8,128)(2,1)S(1)}, u32[]{:S(2)}, u32[]{:S(2)}) async-start(bf16[32,32,128]{2,1,0:T(8,128)(2,1)} %get-tuple-element.48), calls=%async_computation.2 | async-start | bytes 524288 | tf_op jit(solution)/shard_map/all_to_all | solution.py:284
  117.2 2.0 %ring_sum_2.1 = (bf16[192,1024]{1,0:T(8,128)(2,1)}, bf16[192,1024]{1,0:T(8,128)(2,1)}) custom-call(bf16[192,1024]{1,0:T(8,128)(2,1)S(1)} %copy-done.8, bf16[192,1024]{1,0:T(8,128)(2,1)S(1)} %collective-permute-done.24.up_ref, bf16[192,1024]{1,0:T(8,128)(2,1)S(1)} %copy-done.10, bf16[192,1024]{1,0:T(8,128)(2,1)} %collective-permute-done.25.down_ref), custom_call_target="tpu_custom_call" | custom-call | flops 400000 | bytes 2000000 | tf_op jit(solution)/shard_map/ring_sum_2/pallas_call | solution.py:272
  119.2 1.6 %collective-permute-start.26 = (bf16[192,1024]{1,0:T(8,128)(2,1)}, bf16[192,1024]{1,0:T(8,128)(2,1)S(1)}, u32[]{:S(2)}, u32[]{:S(2)}) collective-permute-start(bf16[192,1024]{1,0:T(8,128)(2,1)} %get-tuple-element.59.rest_0_), channel_id=1, source_target_pairs={{0,16},{1,17},{2,18},{3,19},{4,20},{5,21},{6,22},{7,23},{8,24},{9,... | collective-permute-start | bytes 1179656 | tf_op jit(solution)/shard_map/ppermute | solution.py:49
  120.8 1.7 %collective-permute-start.27 = (bf16[192,1024]{1,0:T(8,128)(2,1)}, bf16[192,1024]{1,0:T(8,128)(2,1)}, u32[]{:S(2)}, u32[]{:S(2)}) collective-permute-start(bf16[192,1024]{1,0:T(8,128)(2,1)} %get-tuple-element.60.rest_1_), channel_id=1, source_target_pairs={{0,112},{1,113},{2,114},{3,115},{4,116},{5,117},{6,118},{7,119},{8... | collective-permute-start | bytes 1179656 | tf_op jit(solution)/shard_map/ppermute | solution.py:49
  122.5 4.3 %all-to-all-done.2.terms_ref = bf16[32,32,128]{2,1,0:T(8,128)(2,1)S(1)} async-done(((bf16[32,32,128]{2,1,0:T(8,128)(2,1)}), bf16[32,32,128]{2,1,0:T(8,128)(2,1)S(1)}, u32[]{:S(2)}, u32[]{:S(2)}) %all-to-all-start.2) | async-done | bytes 262176 | tf_op jit(solution)/shard_map/all_to_all | solution.py:284
  127.6 5.1 %all-to-all-start.3 = ((bf16[32,32,128]{2,1,0:T(8,128)(2,1)}), bf16[32,32,128]{2,1,0:T(8,128)(2,1)S(1)}, u32[]{:S(2)}, u32[]{:S(2)}) async-start(bf16[32,32,128]{2,1,0:T(8,128)(2,1)} %states_after.1), calls=%async_computation.3 | async-start | bytes 524288 | tf_op jit(solution)/shard_map/all_to_all | solution.py:284
  132.8 2.0 %ring_sum_1.1 = (bf16[192,1024]{1,0:T(8,128)(2,1)}, bf16[192,1024]{1,0:T(8,128)(2,1)}) custom-call(bf16[192,1024]{1,0:T(8,128)(2,1)S(1)} %get-tuple-element.64.up_part_ref, bf16[192,1024]{1,0:T(8,128)(2,1)S(1)} %collective-permute-done.26.up_ref, bf16[192,1024]{1,0:T(8,128)(2,1)S(1)} %copy-done.6, bf16[192,1024]{1,0:T(8,128)(2,1)} %collective-permute-done.27.down_ref), custom_call_target="tpu_custom_call" | custom-call | flops 400000 | bytes 2000000 | tf_op jit(solution)/shard_map/ring_sum_1/pallas_call | solution.py:272
  136.3 1.8 %collective-permute-start.29 = (bf16[192,1024]{1,0:T(8,128)(2,1)}, bf16[192,1024]{1,0:T(8,128)(2,1)}, u32[]{:S(2)}, u32[]{:S(2)}) collective-permute-start(bf16[192,1024]{1,0:T(8,128)(2,1)} %get-tuple-element.67), channel_id=1, source_target_pairs={{0,112},{1,113},{2,114},{3,115},{4,116},{5,117},{6,118},{7,119},{8... | collective-permute-start | bytes 1179656 | tf_op jit(solution)/shard_map/ppermute | solution.py:49
  138.1 2.8 %inner_grads.1 = (bf16[128,1024]{1,0:T(8,128)(2,1)}, f32[128,1024]{1,0:T(8,128)S(1)}, f32[128,1024]{1,0:T(8,128)S(1)}) custom-call(f32[128,8]{1,0:T(8,128)S(1)} %copy.13.decay_ref, bf16[128,1024]{1,0:T(8,128)(2,1)S(1)} %copy-done.4, bf16[128,1024]{1,0:T(8,128)(2,1)S(1)} %copy-done.1, bf16[128,1024]{1,0:T(8,128)(2,1)S(1)} %copy-done.3, ...), custom_call_target="tpu_custom_call" | custom-call | flops 200000000 | bytes 3000000 | tf_op jit(solution)/shard_map/inner_grads/pallas_call | solution.py:272
  140.8 3.7 %all-to-all-done.3 = bf16[32,32,128]{2,1,0:T(8,128)(2,1)S(1)} async-done(((bf16[32,32,128]{2,1,0:T(8,128)(2,1)}), bf16[32,32,128]{2,1,0:T(8,128)(2,1)S(1)}, u32[]{:S(2)}, u32[]{:S(2)}) %all-to-all-start.3) | async-done | bytes 262176 | tf_op jit(solution)/shard_map/all_to_all | solution.py:284
  145.8 4.8 %collective-permute-done.28.up_ref = bf16[192,1024]{1,0:T(8,128)(2,1)S(1)} collective-permute-done((bf16[192,1024]{1,0:T(8,128)(2,1)}, bf16[192,1024]{1,0:T(8,128)(2,1)S(1)}, u32[]{:S(2)}, u32[]{:S(2)}) %collective-permute-start.28) | collective-permute-done | bytes 393248 | tf_op jit(solution)/shard_map/ppermute | solution.py:49
  150.7 1.9 %ring_sum_0.1 = bf16[192,1024]{1,0:T(8,128)(2,1)} custom-call(bf16[192,1024]{1,0:T(8,128)(2,1)S(1)} %get-tuple-element.63.part_ref, bf16[192,1024]{1,0:T(8,128)(2,1)S(1)} %collective-permute-done.28.up_ref, bf16[192,1024]{1,0:T(8,128)(2,1)} %collective-permute-done.29.down_ref), custom_call_target="tpu_custom_call" | custom-call | flops 400000 | bytes 2000000 | tf_op jit(solution)/shard_map/ring_sum_0/pallas_call | solution.py:272
  (98 shorter events, 31.8 us)
Async XLA Ops:
  4.8 43.5 %all-to-all-start = ((bf16[32,48,128]{2,1,0:T(8,128)(2,1)}), bf16[32,48,128]{2,1,0:T(8,128)(2,1)S(1)}, u32[]{:S(2)}, u32[]{:S(2)}) async-start(bf16[32,48,128]{2,1,0:T(8,128)(2,1)} %key_terms.1), calls=%async_computation | async-start | bytes 786432 | tf_op jit(solution)/shard_map/all_to_all | solution.py:284
  14.9 20.7 %collective-permute-start.11 = (bf16[192,1024]{1,0:T(8,128)(2,1)S(1)}, bf16[192,1024]{1,0:T(8,128)(2,1)S(1)}, u32[]{:S(2)}, u32[]{:S(2)}) collective-permute-start(bf16[192,1024]{1,0:T(8,128)(2,1)S(1)} %copy-done.18), channel_id=1, source_target_pairs={{0,16},{1,17},{2,18},{3,19},{4,20},{5,21},{6,22},{7,23},{8,24},{9,... | collective-permute-start | bytes 1179656 | tf_op jit(solution)/shard_map/ppermute | solution.py:49
  16.4 19.2 %collective-permute-start.8 = (bf16[192,1024]{1,0:T(8,128)(2,1)S(1)}, bf16[192,1024]{1,0:T(8,128)(2,1)S(1)}, u32[]{:S(2)}, u32[]{:S(2)}) collective-permute-start(bf16[192,1024]{1,0:T(8,128)(2,1)S(1)} %copy-done.18), channel_id=1, source_target_pairs={{0,112},{1,113},{2,114},{3,115},{4,116},{5,117},{6,118},{7,119},{8... | collective-permute-start | bytes 1179656 | tf_op jit(solution)/shard_map/ppermute | solution.py:49
  18.3 21.8 %collective-permute-start = (bf16[384,128]{1,0:T(8,128)(2,1)S(1)}, bf16[384,128]{1,0:T(8,128)(2,1)S(1)}, u32[]{:S(2)}, u32[]{:S(2)}) collective-permute-start(bf16[384,128]{1,0:T(8,128)(2,1)S(1)} %get-tuple-element.36), channel_id=1, source_target_pairs={{0,0},{1,1},{2,2},{3,3},{4,128},{5,129},{6,130},{7,131},{8,8},{9,9... | collective-permute-start | bytes 294920 | tf_op jit(solution)/shard_map/ppermute | solution.py:49
  35.6 23.1 %collective-permute-start.12 = (bf16[192,1024]{1,0:T(8,128)(2,1)S(1)}, bf16[192,1024]{1,0:T(8,128)(2,1)}, u32[]{:S(2)}, u32[]{:S(2)}) collective-permute-start(bf16[192,1024]{1,0:T(8,128)(2,1)S(1)} %collective-permute-done.11.refs_8_.rest_0_), channel_id=1, source_target_pairs={{0,16},{1,17},{2,18},{3,19},{4,20},{5,21},{6,22},{7,23},{8,24},{9,... | collective-permute-start | bytes 1179656 | tf_op jit(solution)/shard_map/ppermute | solution.py:49
  35.6 24.6 %collective-permute-start.9 = (bf16[192,1024]{1,0:T(8,128)(2,1)S(1)}, bf16[192,1024]{1,0:T(8,128)(2,1)}, u32[]{:S(2)}, u32[]{:S(2)}) collective-permute-start(bf16[192,1024]{1,0:T(8,128)(2,1)S(1)} %collective-permute-done.8.refs_1_.rest_1_), channel_id=1, source_target_pairs={{0,112},{1,113},{2,114},{3,115},{4,116},{5,117},{6,118},{7,119},{8... | collective-permute-start | bytes 1179656 | tf_op jit(solution)/shard_map/ppermute | solution.py:49
  39.3 8.8 %collective-permute-start.2 = (bf16[384,128]{1,0:T(8,128)(2,1)S(1)}, bf16[384,128]{1,0:T(8,128)(2,1)S(1)}, u32[]{:S(2)}, u32[]{:S(2)}) collective-permute-start(bf16[384,128]{1,0:T(8,128)(2,1)S(1)} %get-tuple-element.37), channel_id=1, source_target_pairs={{0,8},{1,9},{2,10},{3,11},{4,136},{5,137},{6,138},{7,139},{8,0},{9... | collective-permute-start | bytes 294920 | tf_op jit(solution)/shard_map/ppermute | solution.py:49
  40.1 8.1 %collective-permute-start.3 = (bf16[384,128]{1,0:T(8,128)(2,1)S(1)}, bf16[384,128]{1,0:T(8,128)(2,1)S(1)}, u32[]{:S(2)}, u32[]{:S(2)}) collective-permute-start(bf16[384,128]{1,0:T(8,128)(2,1)S(1)} %get-tuple-element.37), channel_id=1, source_target_pairs={{0,12},{1,13},{2,14},{3,15},{4,140},{5,141},{6,142},{7,143},{8,4},... | collective-permute-start | bytes 294920 | tf_op jit(solution)/shard_map/ppermute | solution.py:49
  49.1 18.8 %all-to-all-start.1 = ((bf16[32,32,128]{2,1,0:T(8,128)(2,1)}), bf16[32,32,128]{2,1,0:T(8,128)(2,1)S(1)}, u32[]{:S(2)}, u32[]{:S(2)}) async-start(bf16[32,32,128]{2,1,0:T(8,128)(2,1)} %states_before.1), calls=%async_computation.1 | async-start | bytes 524288 | tf_op jit(solution)/shard_map/all_to_all | solution.py:284
  55.4 12.5 %collective-permute-start.4 = (bf16[384,512]{1,0:T(8,128)(2,1)S(1)}, bf16[384,512]{1,0:T(8,128)(2,1)S(1)}, u32[]{:S(2)}, u32[]{:S(2)}) collective-permute-start(bf16[384,512]{1,0:T(8,128)(2,1)S(1)} %collect.1.own_ref.rest_2_), channel_id=1, source_target_pairs={{0,1},{1,2},{2,3},{3,0},{4,5},{5,6},{6,7},{7,4},{8,9},{9,10},{10,1... | collective-permute-start | bytes 1179656 | tf_op jit(solution)/shard_map/ppermute | solution.py:49
  57.0 10.9 %collective-permute-start.5 = (bf16[384,512]{1,0:T(8,128)(2,1)S(1)}, bf16[384,512]{1,0:T(8,128)(2,1)S(1)}, u32[]{:S(2)}, u32[]{:S(2)}) collective-permute-start(bf16[384,512]{1,0:T(8,128)(2,1)S(1)} %collect.1.own_ref.rest_2_), channel_id=1, source_target_pairs={{0,3},{1,0},{2,1},{3,2},{4,7},{5,4},{6,5},{7,6},{8,11},{9,8},{10,9... | collective-permute-start | bytes 1179656 | tf_op jit(solution)/shard_map/ppermute | solution.py:49
  58.7 15.1 %collective-permute-start.13 = (bf16[192,1024]{1,0:T(8,128)(2,1)}, bf16[192,1024]{1,0:T(8,128)(2,1)}, u32[]{:S(2)}, u32[]{:S(2)}) collective-permute-start(bf16[192,1024]{1,0:T(8,128)(2,1)} %collective-permute-done.12.refs_7_.rest_0_), channel_id=1, source_target_pairs={{0,16},{1,17},{2,18},{3,19},{4,20},{5,21},{6,22},{7,23},{8,24},{9,... | collective-permute-start | bytes 1179656 | tf_op jit(solution)/shard_map/ppermute | solution.py:49
  60.2 15.7 %collective-permute-start.10 = (bf16[192,1024]{1,0:T(8,128)(2,1)}, bf16[192,1024]{1,0:T(8,128)(2,1)}, u32[]{:S(2)}, u32[]{:S(2)}) collective-permute-start(bf16[192,1024]{1,0:T(8,128)(2,1)} %collective-permute-done.9.refs_2_.rest_1_), channel_id=1, source_target_pairs={{0,112},{1,113},{2,114},{3,115},{4,116},{5,117},{6,118},{7,119},{8... | collective-permute-start | bytes 1179656 | tf_op jit(solution)/shard_map/ppermute | solution.py:49
  69.1 9.9 %collective-permute-start.19 = (bf16[128,1024]{1,0:T(8,128)(2,1)S(1)}, bf16[128,1024]{1,0:T(8,128)(2,1)S(1)}, u32[]{:S(2)}, u32[]{:S(2)}) collective-permute-start(bf16[128,1024]{1,0:T(8,128)(2,1)S(1)} %get-tuple-element.50.own_ref), channel_id=1, source_target_pairs={{0,128},{1,129},{2,130},{3,131},{4,132},{5,133},{6,134},{7,135},{8... | collective-permute-start | bytes 786440 | tf_op jit(solution)/shard_map/ppermute | solution.py:49
  70.2 8.9 %collective-permute-start.6 = (bf16[192,512]{1,0:T(8,128)(2,1)S(1)}, bf16[192,512]{1,0:T(8,128)(2,1)S(1)}, u32[]{:S(2)}, u32[]{:S(2)}) collective-permute-start(bf16[192,512]{1,0:T(8,128)(2,1)S(1)} %slice.16), channel_id=1, source_target_pairs={{0,1},{1,2},{2,3},{3,0},{4,5},{5,6},{6,7},{7,4},{8,9},{9,10},{10,1... | collective-permute-start | bytes 589832 | tf_op jit(solution)/shard_map/ppermute | solution.py:49
  71.9 7.7 %collective-permute-start.7 = (bf16[192,512]{1,0:T(8,128)(2,1)S(1)}, bf16[192,512]{1,0:T(8,128)(2,1)S(1)}, u32[]{:S(2)}, u32[]{:S(2)}) collective-permute-start(bf16[192,512]{1,0:T(8,128)(2,1)S(1)} %slice.17), channel_id=1, source_target_pairs={{0,3},{1,0},{2,1},{3,2},{4,7},{5,4},{6,5},{7,6},{8,11},{9,8},{10,9... | collective-permute-start | bytes 589832 | tf_op jit(solution)/shard_map/ppermute | solution.py:49
  74.7 7.8 %collective-permute-start.14 = (bf16[96,1024]{1,0:T(8,128)(2,1)S(1)}, bf16[96,1024]{1,0:T(8,128)(2,1)S(1)}, u32[]{:S(2)}, u32[]{:S(2)}) collective-permute-start(bf16[96,1024]{1,0:T(8,128)(2,1)S(1)} %slice.18), channel_id=1, source_target_pairs={{0,16},{1,17},{2,18},{3,19},{4,20},{5,21},{6,22},{7,23},{8,24},{9,... | collective-permute-start | bytes 589832 | tf_op jit(solution)/shard_map/ppermute | solution.py:49
  79.0 8.4 %collective-permute-start.20 = (bf16[128,1024]{1,0:T(8,128)(2,1)S(1)}, bf16[128,1024]{1,0:T(8,128)(2,1)S(1)}, u32[]{:S(2)}, u32[]{:S(2)}) collective-permute-start(bf16[128,1024]{1,0:T(8,128)(2,1)S(1)} %get-tuple-element.50.own_ref), channel_id=1, source_target_pairs={{0,8},{1,9},{2,10},{3,11},{4,12},{5,13},{6,14},{7,15},{8,0},{9,1},... | collective-permute-start | bytes 786440 | tf_op jit(solution)/shard_map/ppermute | solution.py:49
  79.1 8.4 %collective-permute-start.21 = (bf16[128,1024]{1,0:T(8,128)(2,1)S(1)}, bf16[128,1024]{1,0:T(8,128)(2,1)S(1)}, u32[]{:S(2)}, u32[]{:S(2)}) collective-permute-start(bf16[128,1024]{1,0:T(8,128)(2,1)S(1)} %collective-permute-done.19.neighbour_ref), channel_id=1, source_target_pairs={{0,8},{1,9},{2,10},{3,11},{4,12},{5,13},{6,14},{7,15},{8,0},{9,1},... | collective-permute-start | bytes 786440 | tf_op jit(solution)/shard_map/ppermute | solution.py:49
  87.3 8.3 %collective-permute-start.17 = (bf16[128,1024]{1,0:T(8,128)(2,1)S(1)}, bf16[128,1024]{1,0:T(8,128)(2,1)S(1)}, u32[]{:S(2)}, u32[]{:S(2)}) collective-permute-start(bf16[128,1024]{1,0:T(8,128)(2,1)S(1)} %get-tuple-element.42), channel_id=1, source_target_pairs={{0,8},{1,9},{2,10},{3,11},{4,12},{5,13},{6,14},{7,15},{8,0},{9,1},... | collective-permute-start | bytes 786440 | tf_op jit(solution)/shard_map/ppermute | solution.py:49
  91.8 9.1 %collective-permute-start.22 = (bf16[96,1024]{1,0:T(8,128)(2,1)S(1)}, bf16[96,1024]{1,0:T(8,128)(2,1)S(1)}, u32[]{:S(2)}, u32[]{:S(2)}) collective-permute-start(bf16[96,1024]{1,0:T(8,128)(2,1)S(1)} %get-tuple-element.53), channel_id=1, source_target_pairs={{0,16},{1,17},{2,18},{3,19},{4,20},{5,21},{6,22},{7,23},{8,24},{9,... | collective-permute-start | bytes 589832 | tf_op jit(solution)/shard_map/ppermute | solution.py:49
  93.3 7.6 %collective-permute-start.23 = (bf16[96,1024]{1,0:T(8,128)(2,1)S(1)}, bf16[96,1024]{1,0:T(8,128)(2,1)S(1)}, u32[]{:S(2)}, u32[]{:S(2)}) collective-permute-start(bf16[96,1024]{1,0:T(8,128)(2,1)S(1)} %get-tuple-element.55), channel_id=1, source_target_pairs={{0,112},{1,113},{2,114},{3,115},{4,116},{5,117},{6,118},{7,119},{8... | collective-permute-start | bytes 589832 | tf_op jit(solution)/shard_map/ppermute | solution.py:49
  95.4 9.5 %collective-permute-start.16 = (bf16[128,1024]{1,0:T(8,128)(2,1)S(1)}, bf16[128,1024]{1,0:T(8,128)(2,1)S(1)}, u32[]{:S(2)}, u32[]{:S(2)}) collective-permute-start(bf16[128,1024]{1,0:T(8,128)(2,1)S(1)} %get-tuple-element.40), channel_id=1, source_target_pairs={{0,8},{1,9},{2,10},{3,11},{4,12},{5,13},{6,14},{7,15},{8,0},{9,1},... | collective-permute-start | bytes 786440 | tf_op jit(solution)/shard_map/ppermute | solution.py:49
  95.7 9.2 %collective-permute-start.18 = (bf16[128,1024]{1,0:T(8,128)(2,1)S(1)}, bf16[128,1024]{1,0:T(8,128)(2,1)S(1)}, u32[]{:S(2)}, u32[]{:S(2)}) collective-permute-start(bf16[128,1024]{1,0:T(8,128)(2,1)S(1)} %sum_theirs.1), channel_id=1, source_target_pairs={{0,128},{1,129},{2,130},{3,131},{4,132},{5,133},{6,134},{7,135},{8... | collective-permute-start | bytes 786440 | tf_op jit(solution)/shard_map/ppermute | solution.py:49
  101.7 13.2 %collective-permute-start.24 = (bf16[192,1024]{1,0:T(8,128)(2,1)}, bf16[192,1024]{1,0:T(8,128)(2,1)S(1)}, u32[]{:S(2)}, u32[]{:S(2)}) collective-permute-start(bf16[192,1024]{1,0:T(8,128)(2,1)} %get-tuple-element.56), channel_id=1, source_target_pairs={{0,16},{1,17},{2,18},{3,19},{4,20},{5,21},{6,22},{7,23},{8,24},{9,... | collective-permute-start | bytes 1179656 | tf_op jit(solution)/shard_map/ppermute | solution.py:49
  104.7 10.5 %collective-permute-start.25 = (bf16[192,1024]{1,0:T(8,128)(2,1)S(1)}, bf16[192,1024]{1,0:T(8,128)(2,1)}, u32[]{:S(2)}, u32[]{:S(2)}) collective-permute-start(bf16[192,1024]{1,0:T(8,128)(2,1)S(1)} %get-tuple-element.58), channel_id=1, source_target_pairs={{0,112},{1,113},{2,114},{3,115},{4,116},{5,117},{6,118},{7,119},{8... | collective-permute-start | bytes 1179656 | tf_op jit(solution)/shard_map/ppermute | solution.py:49
  107.1 19.7 %all-to-all-start.2 = ((bf16[32,32,128]{2,1,0:T(8,128)(2,1)}), bf16[32,32,128]{2,1,0:T(8,128)(2,1)S(1)}, u32[]{:S(2)}, u32[]{:S(2)}) async-start(bf16[32,32,128]{2,1,0:T(8,128)(2,1)} %get-tuple-element.48), calls=%async_computation.2 | async-start | bytes 524288 | tf_op jit(solution)/shard_map/all_to_all | solution.py:284
  119.2 13.5 %collective-permute-start.26 = (bf16[192,1024]{1,0:T(8,128)(2,1)}, bf16[192,1024]{1,0:T(8,128)(2,1)S(1)}, u32[]{:S(2)}, u32[]{:S(2)}) collective-permute-start(bf16[192,1024]{1,0:T(8,128)(2,1)} %get-tuple-element.59.rest_0_), channel_id=1, source_target_pairs={{0,16},{1,17},{2,18},{3,19},{4,20},{5,21},{6,22},{7,23},{8,24},{9,... | collective-permute-start | bytes 1179656 | tf_op jit(solution)/shard_map/ppermute | solution.py:49
  120.8 12.0 %collective-permute-start.27 = (bf16[192,1024]{1,0:T(8,128)(2,1)}, bf16[192,1024]{1,0:T(8,128)(2,1)}, u32[]{:S(2)}, u32[]{:S(2)}) collective-permute-start(bf16[192,1024]{1,0:T(8,128)(2,1)} %get-tuple-element.60.rest_1_), channel_id=1, source_target_pairs={{0,112},{1,113},{2,114},{3,115},{4,116},{5,117},{6,118},{7,119},{8... | collective-permute-start | bytes 1179656 | tf_op jit(solution)/shard_map/ppermute | solution.py:49
  127.6 17.0 %all-to-all-start.3 = ((bf16[32,32,128]{2,1,0:T(8,128)(2,1)}), bf16[32,32,128]{2,1,0:T(8,128)(2,1)S(1)}, u32[]{:S(2)}, u32[]{:S(2)}) async-start(bf16[32,32,128]{2,1,0:T(8,128)(2,1)} %states_after.1), calls=%async_computation.3 | async-start | bytes 524288 | tf_op jit(solution)/shard_map/all_to_all | solution.py:284
  134.8 15.8 %collective-permute-start.28 = (bf16[192,1024]{1,0:T(8,128)(2,1)}, bf16[192,1024]{1,0:T(8,128)(2,1)S(1)}, u32[]{:S(2)}, u32[]{:S(2)}) collective-permute-start(bf16[192,1024]{1,0:T(8,128)(2,1)} %get-tuple-element.66), channel_id=1, source_target_pairs={{0,16},{1,17},{2,18},{3,19},{4,20},{5,21},{6,22},{7,23},{8,24},{9,... | collective-permute-start | bytes 1179656 | tf_op jit(solution)/shard_map/ppermute | solution.py:49
  136.3 14.3 %collective-permute-start.29 = (bf16[192,1024]{1,0:T(8,128)(2,1)}, bf16[192,1024]{1,0:T(8,128)(2,1)}, u32[]{:S(2)}, u32[]{:S(2)}) collective-permute-start(bf16[192,1024]{1,0:T(8,128)(2,1)} %get-tuple-element.67), channel_id=1, source_target_pairs={{0,112},{1,113},{2,114},{3,115},{4,116},{5,117},{6,118},{7,119},{8... | collective-permute-start | bytes 1179656 | tf_op jit(solution)/shard_map/ppermute | solution.py:49
  (22 other events, 188.4 us)

commit v4 on v3

--- a/solution.py
+++ b/solution.py
@@ -17,7 +17,7 @@
 BF = jnp.bfloat16
 F32 = jnp.float32
 AXES = ("seq", "head")
-PARAMS = pltpu.CompilerParams(vmem_limit_bytes=48 * 1024 * 1024)
+PARAMS = pltpu.CompilerParams(vmem_limit_bytes=16 * 1024 * 1024)
 
 
 def pairs(move):
@@ -73,7 +73,7 @@
     of = lax.broadcasted_iota(jnp.int32, (BLOCK, BLOCK), 1)
     lower = (of <= at).astype(F32)
     return lax.dot_general(
-        lower, decay, (((1,), (0,)), ((), ())),
+        lower, decay, (((1,), (1,)), ((), ())),
         precision=lax.Precision.HIGHEST, preferred_element_type=F32,
     )
 
@@ -109,12 +109,20 @@
             swap_ref[rows, :] = first
 
 
-def key_terms_kernel(decay_ref, key_ref, value_ref, out_ref):
+def key_terms_kernel(decay_ref, key_hbm, value_hbm, out_ref, key_ref, value_ref, sems):
+    copies = (
+        pltpu.make_async_copy(key_hbm, key_ref, sems.at[0]),
+        pltpu.make_async_copy(value_hbm, value_ref, sems.at[1]),
+    )
+    for copy in copies:
+        copy.start()
     within = within_columns(decay_ref[...])
     row = lax.broadcasted_iota(jnp.int32, (16, HEAD_DIM), 0)
+    for copy in copies:
+        copy.wait()
     for h in range(HEADS_LOCAL):
         col = within[:, h : h + 1]
-        last = within[BLOCK - 1 : BLOCK, h : h + 1]
+        last = col[BLOCK - 1 : BLOCK]
         scaled = (jnp.exp(last - col) * key_ref[:, head_cols(h)].astype(F32)).astype(BF)
         terms = mm(scaled, value_ref[:, head_cols(h)], 0, 0).astype(BF)
         high = last.astype(BF).astype(F32)
@@ -219,26 +227,38 @@
 
 def project_kernel(block_ref, *refs):
     pieces, (kept_ref, theirs_ref, cross_ref, cross_theirs_ref), weight_ref = refs[:9], refs[-5:-1], refs[-1]
-    at = 0
-    for ref in pieces:
-        weight_ref[at : at + ref.shape[0], :] = ref[...]
-        at += ref.shape[0]
-    out = mm(block_ref[...], weight_ref[...], 1, 0)
-    kept_ref[...] = out[0:BLOCK]
-    theirs_ref[...] = out[BLOCK : 2 * BLOCK]
-    cross_ref[...] = out[2 * BLOCK : 3 * BLOCK].astype(BF)
-    cross_theirs_ref[...] = out[3 * BLOCK : 4 * BLOCK].astype(BF)
+    width = weight_ref.shape[1]
+    for tile in range(kept_ref.shape[1] // width):
+        cols = slice(tile * width, (tile + 1) * width)
+        at = 0
+        for ref in pieces:
+            weight_ref[at : at + ref.shape[0], :] = ref[:, cols]
+            at += ref.shape[0]
+        out = mm(block_ref[...], weight_ref[...], 1, 0)
+        kept_ref[:, cols] = out[0:BLOCK]
+        theirs_ref[:, cols] = out[BLOCK : 2 * BLOCK]
+        cross_ref[:, cols] = out[2 * BLOCK : 3 * BLOCK].astype(BF)
+        cross_theirs_ref[:, cols] = out[3 * BLOCK : 4 * BLOCK].astype(BF)
 
 
 def weight_kernel(block_ref, own_ref, neighbour_ref, across_ref, diagonal_ref, *rest):
     outs, tokens_ref = rest[-10:-1], rest[-1]
-    for i, ref in enumerate((own_ref, neighbour_ref, across_ref, diagonal_ref)):
-        tokens_ref[i * BLOCK : (i + 1) * BLOCK, :] = ref[...]
-    out = mm(block_ref[...], tokens_ref[...], 1, 0).astype(BF)
-    at = 0
-    for ref in outs:
-        ref[...] = out[at : at + ref.shape[0]]
-        at += ref.shape[0]
+    width = tokens_ref.shape[1]
+    for tile in range(own_ref.shape[1] // width):
+        cols = slice(tile * width, (tile + 1) * width)
+        for i, ref in enumerate((own_ref, neighbour_ref, across_ref, diagonal_ref)):
+            tokens_ref[i * BLOCK : (i + 1) * BLOCK, :] = ref[:, cols]
+        at = 0
+        for ref in outs:
+            rows = slice(at, at + ref.shape[0])
+            ref[:, cols] = mm(block_ref[rows, :], tokens_ref[...], 1, 0).astype(BF)
+            at += ref.shape[0]
+
+
+def pass_kernel(a_ref, b_ref, after_ref, a_out_ref, b_out_ref):
+    del after_ref
+    a_out_ref[...] = a_ref[...]
+    b_out_ref[...] = b_ref[...]
 
 
 def add_kernel(a_ref, b_ref, out_ref):
@@ -272,7 +292,7 @@
     return pl.pallas_call(
         body,
         in_specs=[pl.BlockSpec(a.shape, lambda n=a.ndim: (0,) * n) for a in args]
-        + [pl.BlockSpec(memory_space=pl.ANY)] * len(after),
+        + [pl.BlockSpec(memory_space=pltpu.VMEM)] * len(after),
         out_shape=outs,
         compiler_params=PARAMS,
         name=name,
@@ -296,10 +316,16 @@
 
     below, above = [send(out_weight, Z_UP)], [send(out_weight, Z_DOWN)]
 
-    terms = call(
-        key_terms_kernel, shape((N_SEQ, ROWS + 16, HEAD_DIM)), "key_terms", 40_000_000, 1_000_000,
-        (log_decay, key_proj, value_proj),
-    )
+    log_decay = jnp.transpose(log_decay)
+    terms = pl.pallas_call(
+        key_terms_kernel,
+        in_specs=[pl.BlockSpec(memory_space=pltpu.VMEM)] + [pl.BlockSpec(memory_space=pltpu.HBM)] * 2,
+        out_shape=shape((N_SEQ, ROWS + 16, HEAD_DIM)),
+        scratch_shapes=[pltpu.VMEM((tokens, cols), BF)] * 2 + [pltpu.SemaphoreType.DMA((2,))],
+        compiler_params=PARAMS,
+        name="key_terms",
+        cost_estimate=pl.CostEstimate(flops=40_000_000, bytes_accessed=1_000_000, transcendentals=0),
+    )(log_decay, key_proj, value_proj)
     parts = call(
         cotangent_kernel, (shape((2 * share, tokens)),) * 2, "cotangent_parts", 0, 400_000, (cotangent,)
     )
@@ -314,7 +340,10 @@
 
     befores = call(
         functools.partial(recurrence_kernel, False), state, "states_before", 1_000_000, 1_000_000,
-        (gathered, gathered), (below[0], above[0], own),
+        (gathered, gathered),
+    )
+    below[0], above[0] = call(
+        pass_kernel, (piece, piece), "pass_on", 0, 1_600_000, (below[0], above[0]), (own,)
     )
     below.append(send(below[-1], Z_UP))
     above.append(send(above[-1], Z_DOWN))
@@ -338,38 +367,29 @@
     far_low = send(below[2][:half], Z_UP)
     far_high = send(above[2][half:], Z_DOWN)
 
-    width = cols // TILES
-    column_spec = pl.BlockSpec((tokens, width), lambda i: (0, i))
-    piece_spec = pl.BlockSpec((share, width), lambda i: (0, i))
-    half_spec = pl.BlockSpec((half, width), lambda i: (0, i))
-    ring_specs = [piece_spec] * 4 + [half_spec] * 2 + [piece_spec] * 3
-    cost = pl.CostEstimate(flops=1_600_000_000, bytes_accessed=6_000_000, transcendentals=0)
     part = pl.pallas_call(
         weight_kernel,
-        grid=(TILES,),
-        in_specs=[pl.BlockSpec((features, 4 * tokens), lambda i: (0, 0))]
-        + [column_spec] * 4
-        + [pl.BlockSpec(memory_space=pl.ANY)] * 2,
-        out_specs=ring_specs,
+        in_specs=[pl.BlockSpec(memory_space=pltpu.VMEM)] * 7,
         out_shape=[piece] * 4 + [shape((half, cols))] * 2 + [piece] * 3,
-        scratch_shapes=[pltpu.VMEM((4 * tokens, width), BF)],
+        scratch_shapes=[pltpu.VMEM((4 * tokens, cols // TILES), BF)],
         compiler_params=PARAMS,
         name="weight_partial",
-        cost_estimate=cost,
+        cost_estimate=pl.CostEstimate(
+            flops=1_600_000_000, bytes_accessed=6_000_000, transcendentals=0
+        ),
     )(block, attended, neighbour, across, diagonal, below[2], above[2])
     up, down = send(part[4], Z_UP), send(part[5], Z_DOWN)
 
     weights = [out_weight] + above + [far_low, far_high] + below[::-1]
     kept, theirs, cross, cross_theirs = pl.pallas_call(
         project_kernel,
-        grid=(TILES,),
-        in_specs=[pl.BlockSpec((4 * tokens, features), lambda i: (0, 0))] + ring_specs,
-        out_specs=[column_spec] * 4,
         out_shape=[row32, row32, row, row],
-        scratch_shapes=[pltpu.VMEM((features, width), BF)],
+        scratch_shapes=[pltpu.VMEM((features, cols // TILES), BF)],
         compiler_params=PARAMS,
         name="project",
-        cost_estimate=cost,
+        cost_estimate=pl.CostEstimate(
+            flops=1_600_000_000, bytes_accessed=6_000_000, transcendentals=0
+        ),
     )(block_t, *weights)
     from_core_theirs = send(cross_theirs, CORE)
     from_core = send(cross, CORE)

time: 154 us -> 143 us (0.929)
  waiting for transfers between devices: 43.5 us -> 39.8 us
  starting transfers between devices: 72.1 us -> 68.6 us
  local copies, waits for them, and re-layouts: 9.66 us -> 7.25 us
    ppermute x30, waiting for transfers between devices: 35.4 us -> 31.7 us  [send(): return lax.ppermute(array, AXES, table)]
    ppermute x30, starting transfers between devices: 42.8 us -> 39.5 us  [send(): return lax.ppermute(array, AXES, table)]
    unnamed x41 -> x40, local copies, waits for them, and re-layouts: 7.75 us -> 5.34 us
    pallas_call x2 -> x3, Pallas kernels: 9.05 us -> 7.71 us  [the longest x1 3.14 us: body(): pl.pallas_call(project_kernel, out_shape=[row32, row32, row, row], scratc...]
  transfers between devices with their start and end apart: 34 -> 34, of which waited for: 10 -> 13; matrix products, arithmetic and copies ran while one was open for 1% -> 1% of each run, Pallas kernels for 15% -> 16%
where the time goes in v4:
time: 143 us; the launch traced here: 142 us
  starting transfers between devices  68.6 us (48%)
  waiting for transfers between devices  39.8 us (28%)
  Pallas kernels  25.5 us (18%)
  local copies, waits for them, and re-layouts  7.25 us (5%)
    ppermute x30, starting transfers between devices, send(): return lax.ppermute(array, AXES, table)  39.5 us
    ppermute x30, waiting for transfers between devices, send(): return lax.ppermute(array, AXES, table)  31.7 us
    all_to_all x4, starting transfers between devices, exchange(): return lax.all_to_all(array, 'seq', 0, 0, tiled=True)  29.1 us
    pallas_call x15, Pallas kernels, call(): pl.pallas_call(body, in_specs=[pl.BlockSpec(a.shape, lambda n=a.ndim: (0,...  17.8 us
    all_to_all x4, waiting for transfers between devices, exchange(): return lax.all_to_all(array, 'seq', 0, 0, tiled=True)  8.08 us
    unnamed x40, local copies, waits for them, and re-layouts  5.34 us
    pallas_call x1, Pallas kernels, body(): pl.pallas_call(project_kernel, out_shape=[row32, row32, row, row], scratc...  3.14 us
    pallas_call x1, Pallas kernels, body(): pl.pallas_call(weight_kernel, in_specs=[pl.BlockSpec(memory_space=pltpu.V...  3.02 us
  transfers between devices with their start and end apart: 34, of which 13 were waited for; matrix products, arithmetic and copies ran while one was open for 1% of the time, Pallas kernels for 16%

profile of v4, /device:TPU:8, one launch (start us, length us, event | category | flops | bytes accessed | tf_op | source)
XLA Modules:
  0.0 142.1 jit_solution(14603594552683881801)
XLA Ops:
  4.8 10.1 %all-to-all-start = ((bf16[32,48,128]{2,1,0:T(8,128)(2,1)}), bf16[32,48,128]{2,1,0:T(8,128)(2,1)S(1)}, u32[]{:S(2)}, u32[]{:S(2)}) async-start(bf16[32,48,128]{2,1,0:T(8,128)(2,1)} %key_terms.1), calls=%async_computation | async-start | bytes 786432 | tf_op jit(solution)/shard_map/all_to_all | solution.py:304
  16.4 1.8 %collective-permute-start.9 = (bf16[192,1024]{1,0:T(8,128)(2,1)S(1)}, bf16[192,1024]{1,0:T(8,128)(2,1)S(1)}, u32[]{:S(2)}, u32[]{:S(2)}) collective-permute-start(bf16[192,1024]{1,0:T(8,128)(2,1)S(1)} %copy-done.18), channel_id=1, source_target_pairs={{0,112},{1,113},{2,114},{3,115},{4,116},{5,117},{6,118},{7,119},{8... | collective-permute-start | bytes 1179656 | tf_op jit(solution)/shard_map/ppermute | solution.py:49
  18.3 3.0 %collective-permute-start = (bf16[384,128]{1,0:T(8,128)(2,1)S(1)}, bf16[384,128]{1,0:T(8,128)(2,1)S(1)}, u32[]{:S(2)}, u32[]{:S(2)}) collective-permute-start(bf16[384,128]{1,0:T(8,128)(2,1)S(1)} %get-tuple-element.38), channel_id=1, source_target_pairs={{0,0},{1,1},{2,2},{3,3},{4,128},{5,129},{6,130},{7,131},{8,8},{9,9... | collective-permute-start | bytes 294920 | tf_op jit(solution)/shard_map/ppermute | solution.py:49
  21.5 3.8 %collective-permute-done.a_ref = bf16[384,128]{1,0:T(8,128)(2,1)S(1)} collective-permute-done((bf16[384,128]{1,0:T(8,128)(2,1)S(1)}, bf16[384,128]{1,0:T(8,128)(2,1)S(1)}, u32[]{:S(2)}, u32[]{:S(2)}) %collective-permute-start) | collective-permute-done | bytes 98336 | tf_op jit(solution)/shard_map/ppermute | solution.py:49
  25.3 3.2 %collective-permute-done.1.b_ref = bf16[384,128]{1,0:T(8,128)(2,1)S(1)} collective-permute-done((bf16[384,128]{1,0:T(8,128)(2,1)S(1)}, bf16[384,128]{1,0:T(8,128)(2,1)S(1)}, u32[]{:S(2)}, u32[]{:S(2)}) %collective-permute-start.1) | collective-permute-done | bytes 98336 | tf_op jit(solution)/shard_map/ppermute | solution.py:49
  29.2 1.8 %collective-permute-done.3.d_ref = bf16[384,128]{1,0:T(8,128)(2,1)S(1)} collective-permute-done((bf16[384,128]{1,0:T(8,128)(2,1)S(1)}, bf16[384,128]{1,0:T(8,128)(2,1)S(1)}, u32[]{:S(2)}, u32[]{:S(2)}) %collective-permute-start.3) | collective-permute-done | bytes 98336 | tf_op jit(solution)/shard_map/ppermute | solution.py:49
  31.1 4.5 %collective-permute-done.8.a_ref = bf16[192,1024]{1,0:T(8,128)(2,1)S(1)} collective-permute-done((bf16[192,1024]{1,0:T(8,128)(2,1)S(1)}, bf16[192,1024]{1,0:T(8,128)(2,1)S(1)}, u32[]{:S(2)}, u32[]{:S(2)}) %collective-permute-start.8) | collective-permute-done | bytes 393248 | tf_op jit(solution)/shard_map/ppermute | solution.py:49
  36.7 3.1 %collective-permute-start.10 = (bf16[192,1024]{1,0:T(8,128)(2,1)}, bf16[192,1024]{1,0:T(8,128)(2,1)S(1)}, u32[]{:S(2)}, u32[]{:S(2)}) collective-permute-start(bf16[192,1024]{1,0:T(8,128)(2,1)} %get-tuple-element.41.refs_1_), channel_id=1, source_target_pairs={{0,112},{1,113},{2,114},{3,115},{4,116},{5,117},{6,118},{7,119},{8... | collective-permute-start | bytes 1179656 | tf_op jit(solution)/shard_map/ppermute | solution.py:49
  40.6 6.1 %all-to-all-start.1 = ((bf16[32,32,128]{2,1,0:T(8,128)(2,1)}), bf16[32,32,128]{2,1,0:T(8,128)(2,1)S(1)}, u32[]{:S(2)}, u32[]{:S(2)}) async-start(bf16[32,32,128]{2,1,0:T(8,128)(2,1)} %states_before.1), calls=%async_computation.1 | async-start | bytes 524288 | tf_op jit(solution)/shard_map/all_to_all | solution.py:304
  48.3 1.7 %collective-permute-start.5 = (bf16[384,512]{1,0:T(8,128)(2,1)S(1)}, bf16[384,512]{1,0:T(8,128)(2,1)S(1)}, u32[]{:S(2)}, u32[]{:S(2)}) collective-permute-start(bf16[384,512]{1,0:T(8,128)(2,1)S(1)} %collect.1.own_ref.after_ref), channel_id=1, source_target_pairs={{0,3},{1,0},{2,1},{3,2},{4,7},{5,4},{6,5},{7,6},{8,11},{9,8},{10,9... | collective-permute-start | bytes 1179656 | tf_op jit(solution)/shard_map/ppermute | solution.py:49
  51.5 1.8 %collective-permute-start.11 = (bf16[192,1024]{1,0:T(8,128)(2,1)S(1)}, bf16[192,1024]{1,0:T(8,128)(2,1)}, u32[]{:S(2)}, u32[]{:S(2)}) collective-permute-start(bf16[192,1024]{1,0:T(8,128)(2,1)S(1)} %collective-permute-done.10.refs_2_.rest_1_), channel_id=1, source_target_pairs={{0,112},{1,113},{2,114},{3,115},{4,116},{5,117},{6,118},{7,119},{8... | collective-permute-start | bytes 1179656 | tf_op jit(solution)/shard_map/ppermute | solution.py:49
  53.3 5.9 %collective-permute-done.4.left_ref.rest_2_ = bf16[384,512]{1,0:T(8,128)(2,1)S(1)} collective-permute-done((bf16[384,512]{1,0:T(8,128)(2,1)S(1)}, bf16[384,512]{1,0:T(8,128)(2,1)S(1)}, u32[]{:S(2)}, u32[]{:S(2)}) %collective-permute-start.4) | collective-permute-done | bytes 393248 | tf_op jit(solution)/shard_map/ppermute | solution.py:49
  61.4 1.7 %collective-permute-start.6 = (bf16[192,512]{1,0:T(8,128)(2,1)S(1)}, bf16[192,512]{1,0:T(8,128)(2,1)S(1)}, u32[]{:S(2)}, u32[]{:S(2)}) collective-permute-start(bf16[192,512]{1,0:T(8,128)(2,1)S(1)} %slice.16), channel_id=1, source_target_pairs={{0,1},{1,2},{2,3},{3,0},{4,5},{5,6},{6,7},{7,4},{8,9},{9,10},{10,1... | collective-permute-start | bytes 589832 | tf_op jit(solution)/shard_map/ppermute | solution.py:49
  63.1 1.9 %collective-permute-start.7 = (bf16[192,512]{1,0:T(8,128)(2,1)S(1)}, bf16[192,512]{1,0:T(8,128)(2,1)S(1)}, u32[]{:S(2)}, u32[]{:S(2)}) collective-permute-start(bf16[192,512]{1,0:T(8,128)(2,1)S(1)} %slice.17), channel_id=1, source_target_pairs={{0,3},{1,0},{2,1},{3,2},{4,7},{5,4},{6,5},{7,6},{8,11},{9,8},{10,9... | collective-permute-start | bytes 589832 | tf_op jit(solution)/shard_map/ppermute | solution.py:49
  68.1 2.2 %collective-permute-start.15 = (bf16[96,1024]{1,0:T(8,128)(2,1)S(1)}, bf16[96,1024]{1,0:T(8,128)(2,1)S(1)}, u32[]{:S(2)}, u32[]{:S(2)}) collective-permute-start(bf16[96,1024]{1,0:T(8,128)(2,1)S(1)} %slice.19), channel_id=1, source_target_pairs={{0,112},{1,113},{2,114},{3,115},{4,116},{5,117},{6,118},{7,119},{8... | collective-permute-start | bytes 589832 | tf_op jit(solution)/shard_map/ppermute | solution.py:49
  71.4 2.0 %collective-permute-done.14.refs_4_ = bf16[96,1024]{1,0:T(8,128)(2,1)S(1)} collective-permute-done((bf16[96,1024]{1,0:T(8,128)(2,1)S(1)}, bf16[96,1024]{1,0:T(8,128)(2,1)S(1)}, u32[]{:S(2)}, u32[]{:S(2)}) %collective-permute-start.14) | collective-permute-done | bytes 196640 | tf_op jit(solution)/shard_map/ppermute | solution.py:49
  73.8 3.1 %project.1 = (f32[128,1024]{1,0:T(8,128)S(1)}, f32[128,1024]{1,0:T(8,128)S(1)}, bf16[128,1024]{1,0:T(8,128)(2,1)S(1)}, bf16[128,1024]{1,0:T(8,128)(2,1)S(1)}) custom-call(bf16[512,1536]{1,0:T(8,128)(2,1)S(1)} %get-tuple-element.40.block_ref, bf16[192,1024]{1,0:T(8,128)(2,1)S(1)} %copy-done.19, bf16[192,1024]{1,0:T(8,128)(2,1)} %get-tuple-element.41.refs_1_, ...), custom_call_target="tpu_custom_call" | custom-call | flops 1600000000 | bytes 6000000 | tf_op jit(solution)/shard_map/project/pallas_call | solution.py:384
  77.1 3.0 %weight_partial.1 = (bf16[192,1024]{1,0:T(8,128)(2,1)S(1)}, bf16[192,1024]{1,0:T(8,128)(2,1)S(1)}, bf16[192,1024]{1,0:T(8,128)(2,1)S(1)}, bf16[192,1024]{1,0:T(8...) custom-call(bf16[1536,512]{1,0:T(8,128)(2,1)S(1)} %get-tuple-element, ...), custom_call_target="tpu_custom_call" | custom-call | flops 1600000000 | bytes 6000000 | tf_op jit(solution)/shard_map/weight_partial/pallas_call | solution.py:370
  81.7 2.2 %collective-permute-start.23 = (bf16[96,1024]{1,0:T(8,128)(2,1)S(1)}, bf16[96,1024]{1,0:T(8,128)(2,1)S(1)}, u32[]{:S(2)}, u32[]{:S(2)}) collective-permute-start(bf16[96,1024]{1,0:T(8,128)(2,1)S(1)} %get-tuple-element.59), channel_id=1, source_target_pairs={{0,112},{1,113},{2,114},{3,115},{4,116},{5,117},{6,118},{7,119},{8... | collective-permute-start | bytes 589832 | tf_op jit(solution)/shard_map/ppermute | solution.py:49
  85.1 4.2 %collective-permute-done.22.up_ref = bf16[96,1024]{1,0:T(8,128)(2,1)S(1)} collective-permute-done((bf16[96,1024]{1,0:T(8,128)(2,1)S(1)}, bf16[96,1024]{1,0:T(8,128)(2,1)S(1)}, u32[]{:S(2)}, u32[]{:S(2)}) %collective-permute-start.22) | collective-permute-done | bytes 196640 | tf_op jit(solution)/shard_map/ppermute | solution.py:49
  90.1 3.0 %collective-permute-start.24 = (bf16[192,1024]{1,0:T(8,128)(2,1)}, bf16[192,1024]{1,0:T(8,128)(2,1)S(1)}, u32[]{:S(2)}, u32[]{:S(2)}) collective-permute-start(bf16[192,1024]{1,0:T(8,128)(2,1)} %get-tuple-element.60), channel_id=1, source_target_pairs={{0,16},{1,17},{2,18},{3,19},{4,20},{5,21},{6,22},{7,23},{8,24},{9,... | collective-permute-start | bytes 1179656 | tf_op jit(solution)/shard_map/ppermute | solution.py:49
  95.5 7.7 %all-to-all-start.2 = ((bf16[32,32,128]{2,1,0:T(8,128)(2,1)}), bf16[32,32,128]{2,1,0:T(8,128)(2,1)S(1)}, u32[]{:S(2)}, u32[]{:S(2)}) async-start(bf16[32,32,128]{2,1,0:T(8,128)(2,1)} %get-tuple-element.52), calls=%async_computation.2 | async-start | bytes 524288 | tf_op jit(solution)/shard_map/all_to_all | solution.py:304
  105.7 2.0 %ring_sum_2.1 = (bf16[192,1024]{1,0:T(8,128)(2,1)}, bf16[192,1024]{1,0:T(8,128)(2,1)}) custom-call(bf16[192,1024]{1,0:T(8,128)(2,1)S(1)} %copy-done.8, bf16[192,1024]{1,0:T(8,128)(2,1)S(1)} %collective-permute-done.24.up_ref, bf16[192,1024]{1,0:T(8,128)(2,1)S(1)} %copy-done.10, bf16[192,1024]{1,0:T(8,128)(2,1)} %collective-permute-done.25.down_ref), custom_call_target="tpu_custom_call" | custom-call | flops 400000 | bytes 2000000 | tf_op jit(solution)/shard_map/ring_sum_2/pallas_call | solution.py:292
  110.9 4.3 %all-to-all-done.2.terms_ref = bf16[32,32,128]{2,1,0:T(8,128)(2,1)S(1)} async-done(((bf16[32,32,128]{2,1,0:T(8,128)(2,1)}), bf16[32,32,128]{2,1,0:T(8,128)(2,1)S(1)}, u32[]{:S(2)}, u32[]{:S(2)}) %all-to-all-start.2) | async-done | bytes 262176 | tf_op jit(solution)/shard_map/all_to_all | solution.py:304
  115.2 1.9 %states_after.1 = bf16[32,32,128]{2,1,0:T(8,128)(2,1)} custom-call(bf16[32,48,128]{2,1,0:T(8,128)(2,1)S(1)} %all-to-all-done.decay_ref.terms_ref, bf16[32,32,128]{2,1,0:T(8,128)(2,1)S(1)} %all-to-all-done.2.terms_ref, bf16[192,1024]{1,0:T(8,128)(2,1)} %get-tuple-element.63.rest_0_, bf16[192,1024]{1,0:T(8,128)(2,1)} %get-tuple-element.64.rest_1_), custom_call_target="tpu_custom_call" | custom-call | flops 1000000 | bytes 1000000 | tf_op jit(solution)/shard_map/states_after/pallas_call | solution.py:292
  117.1 5.1 %all-to-all-start.3 = ((bf16[32,32,128]{2,1,0:T(8,128)(2,1)}), bf16[32,32,128]{2,1,0:T(8,128)(2,1)S(1)}, u32[]{:S(2)}, u32[]{:S(2)}) async-start(bf16[32,32,128]{2,1,0:T(8,128)(2,1)} %states_after.1), calls=%async_computation.3 | async-start | bytes 524288 | tf_op jit(solution)/shard_map/all_to_all | solution.py:304
  122.3 2.0 %ring_sum_1.1 = (bf16[192,1024]{1,0:T(8,128)(2,1)}, bf16[192,1024]{1,0:T(8,128)(2,1)}) custom-call(bf16[192,1024]{1,0:T(8,128)(2,1)S(1)} %get-tuple-element.68.up_part_ref, bf16[192,1024]{1,0:T(8,128)(2,1)S(1)} %collective-permute-done.26.up_ref, bf16[192,1024]{1,0:T(8,128)(2,1)S(1)} %copy-done.6, bf16[192,1024]{1,0:T(8,128)(2,1)} %collective-permute-done.27.down_ref), custom_call_target="tpu_custom_call" | custom-call | flops 400000 | bytes 2000000 | tf_op jit(solution)/shard_map/ring_sum_1/pallas_call | solution.py:292
  125.8 1.8 %collective-permute-start.29 = (bf16[192,1024]{1,0:T(8,128)(2,1)}, bf16[192,1024]{1,0:T(8,128)(2,1)}, u32[]{:S(2)}, u32[]{:S(2)}) collective-permute-start(bf16[192,1024]{1,0:T(8,128)(2,1)} %get-tuple-element.71), channel_id=1, source_target_pairs={{0,112},{1,113},{2,114},{3,115},{4,116},{5,117},{6,118},{7,119},{8... | collective-permute-start | bytes 1179656 | tf_op jit(solution)/shard_map/ppermute | solution.py:49
  127.6 2.7 %inner_grads.1 = (bf16[128,1024]{1,0:T(8,128)(2,1)}, f32[128,1024]{1,0:T(8,128)S(1)}, f32[128,1024]{1,0:T(8,128)S(1)}) custom-call(f32[8,128]{1,0:T(8,128)S(1)} %bitcast.9, bf16[128,1024]{1,0:T(8,128)(2,1)S(1)} %copy-done.4, bf16[128,1024]{1,0:T(8,128)(2,1)S(1)} %copy-done.1, bf16[128,1024]{1,0:T(8,128)(2,1)S(1)} %copy-done.3, ...), custom_call_target="tpu_custom_call" | custom-call | flops 200000000 | bytes 3000000 | tf_op jit(solution)/shard_map/inner_grads/pallas_call | solution.py:292
  130.3 3.8 %all-to-all-done.3 = bf16[32,32,128]{2,1,0:T(8,128)(2,1)S(1)} async-done(((bf16[32,32,128]{2,1,0:T(8,128)(2,1)}), bf16[32,32,128]{2,1,0:T(8,128)(2,1)S(1)}, u32[]{:S(2)}, u32[]{:S(2)}) %all-to-all-start.3) | async-done | bytes 262176 | tf_op jit(solution)/shard_map/all_to_all | solution.py:304
  135.4 4.8 %collective-permute-done.28.up_ref = bf16[192,1024]{1,0:T(8,128)(2,1)S(1)} collective-permute-done((bf16[192,1024]{1,0:T(8,128)(2,1)}, bf16[192,1024]{1,0:T(8,128)(2,1)S(1)}, u32[]{:S(2)}, u32[]{:S(2)}) %collective-permute-start.28) | collective-permute-done | bytes 393248 | tf_op jit(solution)/shard_map/ppermute | solution.py:49
  140.2 1.9 %ring_sum_0.1 = bf16[192,1024]{1,0:T(8,128)(2,1)} custom-call(bf16[192,1024]{1,0:T(8,128)(2,1)S(1)} %get-tuple-element.67.part_ref, bf16[192,1024]{1,0:T(8,128)(2,1)S(1)} %collective-permute-done.28.up_ref, bf16[192,1024]{1,0:T(8,128)(2,1)} %collective-permute-done.29.down_ref), custom_call_target="tpu_custom_call" | custom-call | flops 400000 | bytes 2000000 | tf_op jit(solution)/shard_map/ring_sum_0/pallas_call | solution.py:292
  (98 shorter events, 32.9 us)
Async XLA Ops:
  4.8 35.0 %all-to-all-start = ((bf16[32,48,128]{2,1,0:T(8,128)(2,1)}), bf16[32,48,128]{2,1,0:T(8,128)(2,1)S(1)}, u32[]{:S(2)}, u32[]{:S(2)}) async-start(bf16[32,48,128]{2,1,0:T(8,128)(2,1)} %key_terms.1), calls=%async_computation | async-start | bytes 786432 | tf_op jit(solution)/shard_map/all_to_all | solution.py:304
  14.9 20.7 %collective-permute-start.8 = (bf16[192,1024]{1,0:T(8,128)(2,1)S(1)}, bf16[192,1024]{1,0:T(8,128)(2,1)S(1)}, u32[]{:S(2)}, u32[]{:S(2)}) collective-permute-start(bf16[192,1024]{1,0:T(8,128)(2,1)S(1)} %copy-done.18), channel_id=1, source_target_pairs={{0,16},{1,17},{2,18},{3,19},{4,20},{5,21},{6,22},{7,23},{8,24},{9,... | collective-permute-start | bytes 1179656 | tf_op jit(solution)/shard_map/ppermute | solution.py:49
  16.4 19.2 %collective-permute-start.9 = (bf16[192,1024]{1,0:T(8,128)(2,1)S(1)}, bf16[192,1024]{1,0:T(8,128)(2,1)S(1)}, u32[]{:S(2)}, u32[]{:S(2)}) collective-permute-start(bf16[192,1024]{1,0:T(8,128)(2,1)S(1)} %copy-done.18), channel_id=1, source_target_pairs={{0,112},{1,113},{2,114},{3,115},{4,116},{5,117},{6,118},{7,119},{8... | collective-permute-start | bytes 1179656 | tf_op jit(solution)/shard_map/ppermute | solution.py:49
  18.3 6.9 %collective-permute-start = (bf16[384,128]{1,0:T(8,128)(2,1)S(1)}, bf16[384,128]{1,0:T(8,128)(2,1)S(1)}, u32[]{:S(2)}, u32[]{:S(2)}) collective-permute-start(bf16[384,128]{1,0:T(8,128)(2,1)S(1)} %get-tuple-element.38), channel_id=1, source_target_pairs={{0,0},{1,1},{2,2},{3,3},{4,128},{5,129},{6,130},{7,131},{8,8},{9,9... | collective-permute-start | bytes 294920 | tf_op jit(solution)/shard_map/ppermute | solution.py:49
  21.3 7.2 %collective-permute-start.1 = (bf16[384,128]{1,0:T(8,128)(2,1)S(1)}, bf16[384,128]{1,0:T(8,128)(2,1)S(1)}, u32[]{:S(2)}, u32[]{:S(2)}) collective-permute-start(bf16[384,128]{1,0:T(8,128)(2,1)S(1)} %get-tuple-element.38), channel_id=1, source_target_pairs={{0,4},{1,5},{2,6},{3,7},{4,132},{5,133},{6,134},{7,135},{8,12},{9,... | collective-permute-start | bytes 294920 | tf_op jit(solution)/shard_map/ppermute | solution.py:49
  21.4 7.7 %collective-permute-start.2 = (bf16[384,128]{1,0:T(8,128)(2,1)S(1)}, bf16[384,128]{1,0:T(8,128)(2,1)S(1)}, u32[]{:S(2)}, u32[]{:S(2)}) collective-permute-start(bf16[384,128]{1,0:T(8,128)(2,1)S(1)} %get-tuple-element.39), channel_id=1, source_target_pairs={{0,8},{1,9},{2,10},{3,11},{4,136},{5,137},{6,138},{7,139},{8,0},{9... | collective-permute-start | bytes 294920 | tf_op jit(solution)/shard_map/ppermute | solution.py:49
  36.5 13.5 %collective-permute-start.12 = (bf16[192,1024]{1,0:T(8,128)(2,1)}, bf16[192,1024]{1,0:T(8,128)(2,1)S(1)}, u32[]{:S(2)}, u32[]{:S(2)}) collective-permute-start(bf16[192,1024]{1,0:T(8,128)(2,1)} %get-tuple-element.42.refs_8_), channel_id=1, source_target_pairs={{0,16},{1,17},{2,18},{3,19},{4,20},{5,21},{6,22},{7,23},{8,24},{9,... | collective-permute-start | bytes 1179656 | tf_op jit(solution)/shard_map/ppermute | solution.py:49
  36.7 14.8 %collective-permute-start.10 = (bf16[192,1024]{1,0:T(8,128)(2,1)}, bf16[192,1024]{1,0:T(8,128)(2,1)S(1)}, u32[]{:S(2)}, u32[]{:S(2)}) collective-permute-start(bf16[192,1024]{1,0:T(8,128)(2,1)} %get-tuple-element.41.refs_1_), channel_id=1, source_target_pairs={{0,112},{1,113},{2,114},{3,115},{4,116},{5,117},{6,118},{7,119},{8... | collective-permute-start | bytes 1179656 | tf_op jit(solution)/shard_map/ppermute | solution.py:49
  40.6 18.6 %all-to-all-start.1 = ((bf16[32,32,128]{2,1,0:T(8,128)(2,1)}), bf16[32,32,128]{2,1,0:T(8,128)(2,1)S(1)}, u32[]{:S(2)}, u32[]{:S(2)}) async-start(bf16[32,32,128]{2,1,0:T(8,128)(2,1)} %states_before.1), calls=%async_computation.1 | async-start | bytes 524288 | tf_op jit(solution)/shard_map/all_to_all | solution.py:304
  46.7 12.5 %collective-permute-start.4 = (bf16[384,512]{1,0:T(8,128)(2,1)S(1)}, bf16[384,512]{1,0:T(8,128)(2,1)S(1)}, u32[]{:S(2)}, u32[]{:S(2)}) collective-permute-start(bf16[384,512]{1,0:T(8,128)(2,1)S(1)} %collect.1.own_ref.after_ref), channel_id=1, source_target_pairs={{0,1},{1,2},{2,3},{3,0},{4,5},{5,6},{6,7},{7,4},{8,9},{9,10},{10,1... | collective-permute-start | bytes 1179656 | tf_op jit(solution)/shard_map/ppermute | solution.py:49
  48.3 10.9 %collective-permute-start.5 = (bf16[384,512]{1,0:T(8,128)(2,1)S(1)}, bf16[384,512]{1,0:T(8,128)(2,1)S(1)}, u32[]{:S(2)}, u32[]{:S(2)}) collective-permute-start(bf16[384,512]{1,0:T(8,128)(2,1)S(1)} %collect.1.own_ref.after_ref), channel_id=1, source_target_pairs={{0,3},{1,0},{2,1},{3,2},{4,7},{5,4},{6,5},{7,6},{8,11},{9,8},{10,9... | collective-permute-start | bytes 1179656 | tf_op jit(solution)/shard_map/ppermute | solution.py:49
  50.0 15.0 %collective-permute-start.13 = (bf16[192,1024]{1,0:T(8,128)(2,1)S(1)}, bf16[192,1024]{1,0:T(8,128)(2,1)}, u32[]{:S(2)}, u32[]{:S(2)}) collective-permute-start(bf16[192,1024]{1,0:T(8,128)(2,1)S(1)} %collective-permute-done.12.refs_7_.rest_0_), channel_id=1, source_target_pairs={{0,16},{1,17},{2,18},{3,19},{4,20},{5,21},{6,22},{7,23},{8,24},{9,... | collective-permute-start | bytes 1179656 | tf_op jit(solution)/shard_map/ppermute | solution.py:49
  51.5 15.6 %collective-permute-start.11 = (bf16[192,1024]{1,0:T(8,128)(2,1)S(1)}, bf16[192,1024]{1,0:T(8,128)(2,1)}, u32[]{:S(2)}, u32[]{:S(2)}) collective-permute-start(bf16[192,1024]{1,0:T(8,128)(2,1)S(1)} %collective-permute-done.10.refs_2_.rest_1_), channel_id=1, source_target_pairs={{0,112},{1,113},{2,114},{3,115},{4,116},{5,117},{6,118},{7,119},{8... | collective-permute-start | bytes 1179656 | tf_op jit(solution)/shard_map/ppermute | solution.py:49
  60.4 9.9 %collective-permute-start.19 = (bf16[128,1024]{1,0:T(8,128)(2,1)S(1)}, bf16[128,1024]{1,0:T(8,128)(2,1)S(1)}, u32[]{:S(2)}, u32[]{:S(2)}) collective-permute-start(bf16[128,1024]{1,0:T(8,128)(2,1)S(1)} %get-tuple-element.54.own_ref), channel_id=1, source_target_pairs={{0,128},{1,129},{2,130},{3,131},{4,132},{5,133},{6,134},{7,135},{8... | collective-permute-start | bytes 786440 | tf_op jit(solution)/shard_map/ppermute | solution.py:49
  61.4 8.9 %collective-permute-start.6 = (bf16[192,512]{1,0:T(8,128)(2,1)S(1)}, bf16[192,512]{1,0:T(8,128)(2,1)S(1)}, u32[]{:S(2)}, u32[]{:S(2)}) collective-permute-start(bf16[192,512]{1,0:T(8,128)(2,1)S(1)} %slice.16), channel_id=1, source_target_pairs={{0,1},{1,2},{2,3},{3,0},{4,5},{5,6},{6,7},{7,4},{8,9},{9,10},{10,1... | collective-permute-start | bytes 589832 | tf_op jit(solution)/shard_map/ppermute | solution.py:49
  63.1 7.7 %collective-permute-start.7 = (bf16[192,512]{1,0:T(8,128)(2,1)S(1)}, bf16[192,512]{1,0:T(8,128)(2,1)S(1)}, u32[]{:S(2)}, u32[]{:S(2)}) collective-permute-start(bf16[192,512]{1,0:T(8,128)(2,1)S(1)} %slice.17), channel_id=1, source_target_pairs={{0,3},{1,0},{2,1},{3,2},{4,7},{5,4},{6,5},{7,6},{8,11},{9,8},{10,9... | collective-permute-start | bytes 589832 | tf_op jit(solution)/shard_map/ppermute | solution.py:49
  66.0 7.4 %collective-permute-start.14 = (bf16[96,1024]{1,0:T(8,128)(2,1)S(1)}, bf16[96,1024]{1,0:T(8,128)(2,1)S(1)}, u32[]{:S(2)}, u32[]{:S(2)}) collective-permute-start(bf16[96,1024]{1,0:T(8,128)(2,1)S(1)} %slice.18), channel_id=1, source_target_pairs={{0,16},{1,17},{2,18},{3,19},{4,20},{5,21},{6,22},{7,23},{8,24},{9,... | collective-permute-start | bytes 589832 | tf_op jit(solution)/shard_map/ppermute | solution.py:49
  70.3 6.8 %collective-permute-start.20 = (bf16[128,1024]{1,0:T(8,128)(2,1)S(1)}, bf16[128,1024]{1,0:T(8,128)(2,1)S(1)}, u32[]{:S(2)}, u32[]{:S(2)}) collective-permute-start(bf16[128,1024]{1,0:T(8,128)(2,1)S(1)} %get-tuple-element.54.own_ref), channel_id=1, source_target_pairs={{0,8},{1,9},{2,10},{3,11},{4,12},{5,13},{6,14},{7,15},{8,0},{9,1},... | collective-permute-start | bytes 786440 | tf_op jit(solution)/shard_map/ppermute | solution.py:49
  70.3 6.8 %collective-permute-start.21 = (bf16[128,1024]{1,0:T(8,128)(2,1)S(1)}, bf16[128,1024]{1,0:T(8,128)(2,1)S(1)}, u32[]{:S(2)}, u32[]{:S(2)}) collective-permute-start(bf16[128,1024]{1,0:T(8,128)(2,1)S(1)} %collective-permute-done.19.neighbour_ref), channel_id=1, source_target_pairs={{0,8},{1,9},{2,10},{3,11},{4,12},{5,13},{6,14},{7,15},{8,0},{9,1},... | collective-permute-start | bytes 786440 | tf_op jit(solution)/shard_map/ppermute | solution.py:49
  77.0 7.1 %collective-permute-start.17 = (bf16[128,1024]{1,0:T(8,128)(2,1)S(1)}, bf16[128,1024]{1,0:T(8,128)(2,1)S(1)}, u32[]{:S(2)}, u32[]{:S(2)}) collective-permute-start(bf16[128,1024]{1,0:T(8,128)(2,1)S(1)} %get-tuple-element.46), channel_id=1, source_target_pairs={{0,8},{1,9},{2,10},{3,11},{4,12},{5,13},{6,14},{7,15},{8,0},{9,1},... | collective-permute-start | bytes 786440 | tf_op jit(solution)/shard_map/ppermute | solution.py:49
  80.2 9.2 %collective-permute-start.22 = (bf16[96,1024]{1,0:T(8,128)(2,1)S(1)}, bf16[96,1024]{1,0:T(8,128)(2,1)S(1)}, u32[]{:S(2)}, u32[]{:S(2)}) collective-permute-start(bf16[96,1024]{1,0:T(8,128)(2,1)S(1)} %get-tuple-element.57), channel_id=1, source_target_pairs={{0,16},{1,17},{2,18},{3,19},{4,20},{5,21},{6,22},{7,23},{8,24},{9,... | collective-permute-start | bytes 589832 | tf_op jit(solution)/shard_map/ppermute | solution.py:49
  81.7 7.6 %collective-permute-start.23 = (bf16[96,1024]{1,0:T(8,128)(2,1)S(1)}, bf16[96,1024]{1,0:T(8,128)(2,1)S(1)}, u32[]{:S(2)}, u32[]{:S(2)}) collective-permute-start(bf16[96,1024]{1,0:T(8,128)(2,1)S(1)} %get-tuple-element.59), channel_id=1, source_target_pairs={{0,112},{1,113},{2,114},{3,115},{4,116},{5,117},{6,118},{7,119},{8... | collective-permute-start | bytes 589832 | tf_op jit(solution)/shard_map/ppermute | solution.py:49
  83.9 9.5 %collective-permute-start.16 = (bf16[128,1024]{1,0:T(8,128)(2,1)S(1)}, bf16[128,1024]{1,0:T(8,128)(2,1)S(1)}, u32[]{:S(2)}, u32[]{:S(2)}) collective-permute-start(bf16[128,1024]{1,0:T(8,128)(2,1)S(1)} %get-tuple-element.44), channel_id=1, source_target_pairs={{0,8},{1,9},{2,10},{3,11},{4,12},{5,13},{6,14},{7,15},{8,0},{9,1},... | collective-permute-start | bytes 786440 | tf_op jit(solution)/shard_map/ppermute | solution.py:49
  84.1 9.3 %collective-permute-start.18 = (bf16[128,1024]{1,0:T(8,128)(2,1)S(1)}, bf16[128,1024]{1,0:T(8,128)(2,1)S(1)}, u32[]{:S(2)}, u32[]{:S(2)}) collective-permute-start(bf16[128,1024]{1,0:T(8,128)(2,1)S(1)} %sum_theirs.1), channel_id=1, source_target_pairs={{0,128},{1,129},{2,130},{3,131},{4,132},{5,133},{6,134},{7,135},{8... | collective-permute-start | bytes 786440 | tf_op jit(solution)/shard_map/ppermute | solution.py:49
  90.1 13.1 %collective-permute-start.24 = (bf16[192,1024]{1,0:T(8,128)(2,1)}, bf16[192,1024]{1,0:T(8,128)(2,1)S(1)}, u32[]{:S(2)}, u32[]{:S(2)}) collective-permute-start(bf16[192,1024]{1,0:T(8,128)(2,1)} %get-tuple-element.60), channel_id=1, source_target_pairs={{0,16},{1,17},{2,18},{3,19},{4,20},{5,21},{6,22},{7,23},{8,24},{9,... | collective-permute-start | bytes 1179656 | tf_op jit(solution)/shard_map/ppermute | solution.py:49
  93.1 10.5 %collective-permute-start.25 = (bf16[192,1024]{1,0:T(8,128)(2,1)S(1)}, bf16[192,1024]{1,0:T(8,128)(2,1)}, u32[]{:S(2)}, u32[]{:S(2)}) collective-permute-start(bf16[192,1024]{1,0:T(8,128)(2,1)S(1)} %get-tuple-element.62), channel_id=1, source_target_pairs={{0,112},{1,113},{2,114},{3,115},{4,116},{5,117},{6,118},{7,119},{8... | collective-permute-start | bytes 1179656 | tf_op jit(solution)/shard_map/ppermute | solution.py:49
  95.5 19.7 %all-to-all-start.2 = ((bf16[32,32,128]{2,1,0:T(8,128)(2,1)}), bf16[32,32,128]{2,1,0:T(8,128)(2,1)S(1)}, u32[]{:S(2)}, u32[]{:S(2)}) async-start(bf16[32,32,128]{2,1,0:T(8,128)(2,1)} %get-tuple-element.52), calls=%async_computation.2 | async-start | bytes 524288 | tf_op jit(solution)/shard_map/all_to_all | solution.py:304
  107.7 14.6 %collective-permute-start.26 = (bf16[192,1024]{1,0:T(8,128)(2,1)}, bf16[192,1024]{1,0:T(8,128)(2,1)S(1)}, u32[]{:S(2)}, u32[]{:S(2)}) collective-permute-start(bf16[192,1024]{1,0:T(8,128)(2,1)} %get-tuple-element.63.rest_0_), channel_id=1, source_target_pairs={{0,16},{1,17},{2,18},{3,19},{4,20},{5,21},{6,22},{7,23},{8,24},{9,... | collective-permute-start | bytes 1179656 | tf_op jit(solution)/shard_map/ppermute | solution.py:49
  109.3 13.0 %collective-permute-start.27 = (bf16[192,1024]{1,0:T(8,128)(2,1)}, bf16[192,1024]{1,0:T(8,128)(2,1)}, u32[]{:S(2)}, u32[]{:S(2)}) collective-permute-start(bf16[192,1024]{1,0:T(8,128)(2,1)} %get-tuple-element.64.rest_1_), channel_id=1, source_target_pairs={{0,112},{1,113},{2,114},{3,115},{4,116},{5,117},{6,118},{7,119},{8... | collective-permute-start | bytes 1179656 | tf_op jit(solution)/shard_map/ppermute | solution.py:49
  117.1 17.0 %all-to-all-start.3 = ((bf16[32,32,128]{2,1,0:T(8,128)(2,1)}), bf16[32,32,128]{2,1,0:T(8,128)(2,1)S(1)}, u32[]{:S(2)}, u32[]{:S(2)}) async-start(bf16[32,32,128]{2,1,0:T(8,128)(2,1)} %states_after.1), calls=%async_computation.3 | async-start | bytes 524288 | tf_op jit(solution)/shard_map/all_to_all | solution.py:304
  124.3 15.8 %collective-permute-start.28 = (bf16[192,1024]{1,0:T(8,128)(2,1)}, bf16[192,1024]{1,0:T(8,128)(2,1)S(1)}, u32[]{:S(2)}, u32[]{:S(2)}) collective-permute-start(bf16[192,1024]{1,0:T(8,128)(2,1)} %get-tuple-element.70), channel_id=1, source_target_pairs={{0,16},{1,17},{2,18},{3,19},{4,20},{5,21},{6,22},{7,23},{8,24},{9,... | collective-permute-start | bytes 1179656 | tf_op jit(solution)/shard_map/ppermute | solution.py:49
  125.8 14.4 %collective-permute-start.29 = (bf16[192,1024]{1,0:T(8,128)(2,1)}, bf16[192,1024]{1,0:T(8,128)(2,1)}, u32[]{:S(2)}, u32[]{:S(2)}) collective-permute-start(bf16[192,1024]{1,0:T(8,128)(2,1)} %get-tuple-element.71), channel_id=1, source_target_pairs={{0,112},{1,113},{2,114},{3,115},{4,116},{5,117},{6,118},{7,119},{8... | collective-permute-start | bytes 1179656 | tf_op jit(solution)/shard_map/ppermute | solution.py:49
  (22 other events, 260.4 us)

commit v5 on v4

--- a/solution.py
+++ b/solution.py
@@ -89,7 +89,8 @@
     return pl.ds(h * HEAD_DIM, HEAD_DIM)
 
 
-def cotangent_kernel(cot_ref, same_ref, swap_ref):
+def cotangent_kernel(cot_ref, *rest):
+    same_ref, swap_ref = rest[-2:]
     _, _, core, _, _ = coordinates()
     turned = jnp.transpose(cot_ref[...])
     share = turned.shape[0] // 4
@@ -255,17 +256,12 @@
             at += ref.shape[0]
 
 
-def pass_kernel(a_ref, b_ref, after_ref, a_out_ref, b_out_ref):
-    del after_ref
-    a_out_ref[...] = a_ref[...]
-    b_out_ref[...] = b_ref[...]
-
-
 def add_kernel(a_ref, b_ref, out_ref):
     out_ref[...] = (a_ref[...].astype(F32) + b_ref[...].astype(F32)).astype(BF)
 
 
-def first_adds_kernel(up_part_ref, up_ref, down_part_ref, down_ref, up_out_ref, down_out_ref):
+def first_adds_kernel(up_part_ref, up_ref, down_part_ref, down_ref, *rest):
+    up_out_ref, down_out_ref = rest[-2:]
     half = up_ref.shape[0]
     up_out_ref[:half] = (up_part_ref[:half].astype(F32) + up_ref[...].astype(F32)).astype(BF)
     up_out_ref[half:] = up_part_ref[half:]
@@ -327,8 +323,11 @@
         cost_estimate=pl.CostEstimate(flops=40_000_000, bytes_accessed=1_000_000, transcendentals=0),
     )(log_decay, key_proj, value_proj)
     parts = call(
-        cotangent_kernel, (shape((2 * share, tokens)),) * 2, "cotangent_parts", 0, 400_000, (cotangent,)
-    )
+        cotangent_kernel, (shape((2 * share, tokens)),) * 2, "cotangent_parts", 40_000_000_000, 400_000,
+        (cotangent,), (below[0], above[0]),
+    )
+    below.append(send(below[0], Z_UP))
+    above.append(send(above[0], Z_DOWN))
     pieces = []
     for a in range(2):
         for b in range(2):
@@ -342,15 +341,10 @@
         functools.partial(recurrence_kernel, False), state, "states_before", 1_000_000, 1_000_000,
         (gathered, gathered),
     )
-    below[0], above[0] = call(
-        pass_kernel, (piece, piece), "pass_on", 0, 1_600_000, (below[0], above[0]), (own,)
-    )
-    below.append(send(below[-1], Z_UP))
-    above.append(send(above[-1], Z_DOWN))
     states = exchange(befores).reshape(cols, HEAD_DIM)
     attended, scores = call(
         attended_kernel, (row, row), "attended", 110_000_000, 2_000_000,
-        (log_decay, queries, key_proj, value_proj, states), (below[1], above[1], left, right),
+        (log_decay, queries, key_proj, value_proj, states), (below[1], above[1]),
     )
     below.append(send(below[-1], Z_UP))
     above.append(send(above[-1], Z_DOWN))
@@ -366,19 +360,6 @@
     diagonal = send(neighbour, CORE)
     far_low = send(below[2][:half], Z_UP)
     far_high = send(above[2][half:], Z_DOWN)
-
-    part = pl.pallas_call(
-        weight_kernel,
-        in_specs=[pl.BlockSpec(memory_space=pltpu.VMEM)] * 7,
-        out_shape=[piece] * 4 + [shape((half, cols))] * 2 + [piece] * 3,
-        scratch_shapes=[pltpu.VMEM((4 * tokens, cols // TILES), BF)],
-        compiler_params=PARAMS,
-        name="weight_partial",
-        cost_estimate=pl.CostEstimate(
-            flops=1_600_000_000, bytes_accessed=6_000_000, transcendentals=0
-        ),
-    )(block, attended, neighbour, across, diagonal, below[2], above[2])
-    up, down = send(part[4], Z_UP), send(part[5], Z_DOWN)
 
     weights = [out_weight] + above + [far_low, far_high] + below[::-1]
     kept, theirs, cross, cross_theirs = pl.pallas_call(
@@ -395,9 +376,23 @@
     from_core = send(cross, CORE)
     passed = call(add_kernel, row, "sum_theirs", 100_000, 1_000_000, (theirs, from_core_theirs))
     arrived = send(passed, Y_LO)
+
+    part = pl.pallas_call(
+        weight_kernel,
+        in_specs=[pl.BlockSpec(memory_space=pltpu.VMEM)] * 6,
+        out_shape=[piece] * 4 + [shape((half, cols))] * 2 + [piece] * 3,
+        scratch_shapes=[pltpu.VMEM((4 * tokens, cols // TILES), BF)],
+        compiler_params=PARAMS,
+        name="weight_partial",
+        cost_estimate=pl.CostEstimate(
+            flops=1_600_000_000, bytes_accessed=6_000_000, transcendentals=0
+        ),
+    )(block, attended, neighbour, across, diagonal, passed)
+    up, down = send(part[4], Z_UP), send(part[5], Z_DOWN)
+
     up, down = call(
         first_adds_kernel, (piece, piece), "ring_sum_3", 400_000, 2_000_000,
-        (part[3], up, part[6], down),
+        (part[3], up, part[6], down), (arrived,),
     )
     up, down = send(up, Z_UP), send(down, Z_DOWN)
     grad_attn, query_terms = call(

time: 143 us -> 140 us (0.979)
  waiting for transfers between devices: 39.8 us -> 34.5 us
    ppermute x30, waiting for transfers between devices: 31.7 us -> 23.1 us  [send(): return lax.ppermute(array, AXES, table)]
    all_to_all x4, waiting for transfers between devices: 8.08 us -> 11.4 us  [exchange(): return lax.all_to_all(array, 'seq', 0, 0, tiled=True)]
    pallas_call x15 -> x14, Pallas kernels: 17.8 us -> 19.2 us  [call(): pl.pallas_call(body, in_specs=[pl.BlockSpec(a.shape, lambda n=a.ndim: (0,...]
    unnamed x40 -> x38, local copies, waits for them, and re-layouts: 5.34 us -> 4.41 us
  transfers between devices with their start and end apart: 34 -> 34, of which waited for: 13 -> 15; matrix products, arithmetic and copies ran while one was open for 1% -> 2% of each run, Pallas kernels for 16% -> 17%
where the time goes in v5:
time: 140 us; the launch traced here: 138 us
  starting transfers between devices  70 us (50%)
  waiting for transfers between devices  34.5 us (25%)
  Pallas kernels  25.7 us (18%)
  local copies, waits for them, and re-layouts  7.26 us (5%)
    ppermute x30, starting transfers between devices, send(): return lax.ppermute(array, AXES, table)  40.8 us
    all_to_all x4, starting transfers between devices, exchange(): return lax.all_to_all(array, 'seq', 0, 0, tiled=True)  29.2 us
    ppermute x30, waiting for transfers between devices, send(): return lax.ppermute(array, AXES, table)  23.1 us
    pallas_call x14, Pallas kernels, call(): pl.pallas_call(body, in_specs=[pl.BlockSpec(a.shape, lambda n=a.ndim: (0,...  19.2 us
    all_to_all x4, waiting for transfers between devices, exchange(): return lax.all_to_all(array, 'seq', 0, 0, tiled=True)  11.4 us
    unnamed x38, local copies, waits for them, and re-layouts  4.41 us
    pallas_call x1, Pallas kernels, body(): pl.pallas_call(project_kernel, out_shape=[row32, row32, row, row], scratc...  3.07 us
  transfers between devices with their start and end apart: 34, of which 15 were waited for; matrix products, arithmetic and copies ran while one was open for 2% of the time, Pallas kernels for 17%

profile of v5, /device:TPU:8, one launch (start us, length us, event | category | flops | bytes accessed | tf_op | source)
XLA Modules:
  0.0 138.4 jit_solution(12386319315671826432)
XLA Ops:
  0.6 2.0 %collective-permute-start = (bf16[192,1024]{1,0:T(8,128)(2,1)}, bf16[192,1024]{1,0:T(8,128)(2,1)}, u32[]{:S(2)}, u32[]{:S(2)}) collective-permute-start(bf16[192,1024]{1,0:T(8,128)(2,1)} %refs_0_.1), channel_id=1, source_target_pairs={{0,16},{1,17},{2,18},{3,19},{4,20},{5,21},{6,22},{7,23},{8,24},{9,... | collective-permute-start | bytes 1179656 | tf_op jit(solution)/shard_map/ppermute | solution.py:49
  2.6 4.0 %collective-permute-start.1 = (bf16[192,1024]{1,0:T(8,128)(2,1)}, bf16[192,1024]{1,0:T(8,128)(2,1)}, u32[]{:S(2)}, u32[]{:S(2)}) collective-permute-start(bf16[192,1024]{1,0:T(8,128)(2,1)} %refs_0_.1), channel_id=1, source_target_pairs={{0,112},{1,113},{2,114},{3,115},{4,116},{5,117},{6,118},{7,119},{8... | collective-permute-start | bytes 1179656 | tf_op jit(solution)/shard_map/ppermute | solution.py:49
  10.8 7.4 %all-to-all-start = ((bf16[32,48,128]{2,1,0:T(8,128)(2,1)}), bf16[32,48,128]{2,1,0:T(8,128)(2,1)S(1)}, u32[]{:S(2)}, u32[]{:S(2)}) async-start(bf16[32,48,128]{2,1,0:T(8,128)(2,1)} %key_terms.1), calls=%async_computation | async-start | bytes 786432 | tf_op jit(solution)/shard_map/all_to_all | solution.py:300
  19.8 1.8 %collective-permute-start.10 = (bf16[192,1024]{1,0:T(8,128)(2,1)}, bf16[192,1024]{1,0:T(8,128)(2,1)S(1)}, u32[]{:S(2)}, u32[]{:S(2)}) collective-permute-start(bf16[192,1024]{1,0:T(8,128)(2,1)} %collective-permute-done.1.rest_1_.refs_1_), channel_id=1, source_target_pairs={{0,112},{1,113},{2,114},{3,115},{4,116},{5,117},{6,118},{7,119},{8... | collective-permute-start | bytes 1179656 | tf_op jit(solution)/shard_map/ppermute | solution.py:49
  22.8 3.0 %collective-permute-start.2 = (bf16[384,128]{1,0:T(8,128)(2,1)S(1)}, bf16[384,128]{1,0:T(8,128)(2,1)S(1)}, u32[]{:S(2)}, u32[]{:S(2)}) collective-permute-start(bf16[384,128]{1,0:T(8,128)(2,1)S(1)} %get-tuple-element.36), channel_id=1, source_target_pairs={{0,0},{1,1},{2,2},{3,3},{4,128},{5,129},{6,130},{7,131},{8,8},{9,9... | collective-permute-start | bytes 294920 | tf_op jit(solution)/shard_map/ppermute | solution.py:49
  26.0 4.6 %collective-permute-done.2.a_ref = bf16[384,128]{1,0:T(8,128)(2,1)S(1)} collective-permute-done((bf16[384,128]{1,0:T(8,128)(2,1)S(1)}, bf16[384,128]{1,0:T(8,128)(2,1)S(1)}, u32[]{:S(2)}, u32[]{:S(2)}) %collective-permute-start.2) | collective-permute-done | bytes 98336 | tf_op jit(solution)/shard_map/ppermute | solution.py:49
  30.5 2.3 %all-to-all-done.decay_ref.terms_ref = bf16[32,48,128]{2,1,0:T(8,128)(2,1)S(1)} async-done(((bf16[32,48,128]{2,1,0:T(8,128)(2,1)}), bf16[32,48,128]{2,1,0:T(8,128)(2,1)S(1)}, u32[]{:S(2)}, u32[]{:S(2)}) %all-to-all-start) | async-done | bytes 393248 | tf_op jit(solution)/shard_map/all_to_all | solution.py:300
  33.6 9.5 %all-to-all-start.1 = ((bf16[32,32,128]{2,1,0:T(8,128)(2,1)}), bf16[32,32,128]{2,1,0:T(8,128)(2,1)S(1)}, u32[]{:S(2)}, u32[]{:S(2)}) async-start(bf16[32,32,128]{2,1,0:T(8,128)(2,1)} %states_before.1), calls=%async_computation.1 | async-start | bytes 524288 | tf_op jit(solution)/shard_map/all_to_all | solution.py:300
  44.8 1.7 %collective-permute-start.7 = (bf16[384,512]{1,0:T(8,128)(2,1)S(1)}, bf16[384,512]{1,0:T(8,128)(2,1)S(1)}, u32[]{:S(2)}, u32[]{:S(2)}) collective-permute-start(bf16[384,512]{1,0:T(8,128)(2,1)S(1)} %collect.1.own_ref), channel_id=1, source_target_pairs={{0,3},{1,0},{2,1},{3,2},{4,7},{5,4},{6,5},{7,6},{8,11},{9,8},{10,9... | collective-permute-start | bytes 1179656 | tf_op jit(solution)/shard_map/ppermute | solution.py:49
  48.0 1.8 %collective-permute-start.11 = (bf16[192,1024]{1,0:T(8,128)(2,1)S(1)}, bf16[192,1024]{1,0:T(8,128)(2,1)S(1)}, u32[]{:S(2)}, u32[]{:S(2)}) collective-permute-start(bf16[192,1024]{1,0:T(8,128)(2,1)S(1)} %collective-permute-done.10.refs_2_.rest_1_), channel_id=1, source_target_pairs={{0,112},{1,113},{2,114},{3,115},{4,116},{5,117},{6,118},{7,119},{8... | collective-permute-start | bytes 1179656 | tf_op jit(solution)/shard_map/ppermute | solution.py:49
  49.8 5.9 %collective-permute-done.6.left_ref = bf16[384,512]{1,0:T(8,128)(2,1)S(1)} collective-permute-done((bf16[384,512]{1,0:T(8,128)(2,1)S(1)}, bf16[384,512]{1,0:T(8,128)(2,1)S(1)}, u32[]{:S(2)}, u32[]{:S(2)}) %collective-permute-start.6) | collective-permute-done | bytes 393248 | tf_op jit(solution)/shard_map/ppermute | solution.py:49
  57.4 3.0 %collective-permute-start.9 = (bf16[192,512]{1,0:T(8,128)(2,1)}, bf16[192,512]{1,0:T(8,128)(2,1)}, u32[]{:S(2)}, u32[]{:S(2)}) collective-permute-start(bf16[192,512]{1,0:T(8,128)(2,1)} %slice.17), channel_id=1, source_target_pairs={{0,3},{1,0},{2,1},{3,2},{4,7},{5,4},{6,5},{7,6},{8,11},{9,8},{10,9... | collective-permute-start | bytes 589832 | tf_op jit(solution)/shard_map/ppermute | solution.py:49
  63.3 2.4 %collective-permute-start.15 = (bf16[96,1024]{1,0:T(8,128)(2,1)}, bf16[96,1024]{1,0:T(8,128)(2,1)}, u32[]{:S(2)}, u32[]{:S(2)}) collective-permute-start(bf16[96,1024]{1,0:T(8,128)(2,1)} %slice.19), channel_id=1, source_target_pairs={{0,112},{1,113},{2,114},{3,115},{4,116},{5,117},{6,118},{7,119},{8... | collective-permute-start | bytes 589832 | tf_op jit(solution)/shard_map/ppermute | solution.py:49
  67.6 1.6 %assemble.1 = (bf16[1536,512]{1,0:T(8,128)(2,1)S(1)}, bf16[512,1536]{1,0:T(8,128)(2,1)S(1)}) custom-call(bf16[384,512]{1,0:T(8,128)(2,1)S(1)} %collect.1.own_ref, bf16[384,512]{1,0:T(8,128)(2,1)S(1)} %collective-permute-done.6.left_ref, bf16[384,512]{1,0:T(8,128)(2,1)S(1)} %collective-permute-done.7.right_ref, ...), custom_call_target="tpu_custom_call" | custom-call | flops 1000000 | bytes 5000000 | tf_op jit(solution)/shard_map/assemble/pallas_call | solution.py:288
  69.8 3.1 %project.1 = (f32[128,1024]{1,0:T(8,128)S(1)}, f32[128,1024]{1,0:T(8,128)S(1)}, bf16[128,1024]{1,0:T(8,128)(2,1)S(1)}, bf16[128,1024]{1,0:T(8,128)(2,1)S(1)}) custom-call(bf16[512,1536]{1,0:T(8,128)(2,1)S(1)} %get-tuple-element.38.block_ref, bf16[192,1024]{1,0:T(8,128)(2,1)S(1)} %copy-done.17, bf16[192,1024]{1,0:T(8,128)(2,1)} %collective-permute-done.1.rest_1_.refs_1_, ...), custom_call_target="tpu_custom_call" | custom-call | flops 1600000000 | bytes 6000000 | tf_op jit(solution)/shard_map/project/pallas_call | solution.py:365
  75.9 1.9 %weight_partial.1 = (bf16[192,1024]{1,0:T(8,128)(2,1)S(1)}, bf16[192,1024]{1,0:T(8,128)(2,1)S(1)}, bf16[192,1024]{1,0:T(8,128)(2,1)S(1)}, bf16[192,1024]{1,0:T(8...) custom-call(bf16[1536,512]{1,0:T(8,128)(2,1)S(1)} %get-tuple-element, ...), custom_call_target="tpu_custom_call" | custom-call | flops 1600000000 | bytes 6000000 | tf_op jit(solution)/shard_map/weight_partial/pallas_call | solution.py:380
  78.3 2.9 %collective-permute-start.23 = (bf16[96,1024]{1,0:T(8,128)(2,1)S(1)}, bf16[96,1024]{1,0:T(8,128)(2,1)S(1)}, u32[]{:S(2)}, u32[]{:S(2)}) collective-permute-start(bf16[96,1024]{1,0:T(8,128)(2,1)S(1)} %get-tuple-element.55), channel_id=1, source_target_pairs={{0,112},{1,113},{2,114},{3,115},{4,116},{5,117},{6,118},{7,119},{8... | collective-permute-start | bytes 589832 | tf_op jit(solution)/shard_map/ppermute | solution.py:49
  81.2 2.1 %collective-permute-done.18.other_ref.rest_0_ = bf16[128,1024]{1,0:T(8,128)(2,1)S(1)} collective-permute-done((bf16[128,1024]{1,0:T(8,128)(2,1)S(1)}, bf16[128,1024]{1,0:T(8,128)(2,1)S(1)}, u32[]{:S(2)}, u32[]{:S(2)}) %collective-permute-start.18) | collective-permute-done | bytes 262176 | tf_op jit(solution)/shard_map/ppermute | solution.py:49
  83.3 2.9 %collective-permute-done.22.up_ref = bf16[96,1024]{1,0:T(8,128)(2,1)S(1)} collective-permute-done((bf16[96,1024]{1,0:T(8,128)(2,1)S(1)}, bf16[96,1024]{1,0:T(8,128)(2,1)S(1)}, u32[]{:S(2)}, u32[]{:S(2)}) %collective-permute-start.22) | collective-permute-done | bytes 196640 | tf_op jit(solution)/shard_map/ppermute | solution.py:49
  87.1 2.4 %collective-permute-start.24 = (bf16[192,1024]{1,0:T(8,128)(2,1)}, bf16[192,1024]{1,0:T(8,128)(2,1)}, u32[]{:S(2)}, u32[]{:S(2)}) collective-permute-start(bf16[192,1024]{1,0:T(8,128)(2,1)} %get-tuple-element.56), channel_id=1, source_target_pairs={{0,16},{1,17},{2,18},{3,19},{4,20},{5,21},{6,22},{7,23},{8,24},{9,... | collective-permute-start | bytes 1179656 | tf_op jit(solution)/shard_map/ppermute | solution.py:49
  92.5 7.1 %all-to-all-start.2 = ((bf16[32,32,128]{2,1,0:T(8,128)(2,1)}), bf16[32,32,128]{2,1,0:T(8,128)(2,1)S(1)}, u32[]{:S(2)}, u32[]{:S(2)}) async-start(bf16[32,32,128]{2,1,0:T(8,128)(2,1)} %get-tuple-element.48), calls=%async_computation.2 | async-start | bytes 524288 | tf_op jit(solution)/shard_map/all_to_all | solution.py:300
  100.9 2.1 %ring_sum_2.1 = (bf16[192,1024]{1,0:T(8,128)(2,1)}, bf16[192,1024]{1,0:T(8,128)(2,1)}) custom-call(bf16[192,1024]{1,0:T(8,128)(2,1)S(1)} %get-tuple-element.51.up_part_ref, bf16[192,1024]{1,0:T(8,128)(2,1)} %collective-permute-done.24.up_ref, bf16[192,1024]{1,0:T(8,128)(2,1)S(1)} %copy-done.6, bf16[192,1024]{1,0:T(8,128)(2,1)} %collective-permute-done.25.down_ref), custom_call_target="tpu_custom_call" | custom-call | flops 400000 | bytes 2000000 | tf_op jit(solution)/shard_map/ring_sum_2/pallas_call | solution.py:288
  104.4 1.8 %collective-permute-start.27 = (bf16[192,1024]{1,0:T(8,128)(2,1)}, bf16[192,1024]{1,0:T(8,128)(2,1)}, u32[]{:S(2)}, u32[]{:S(2)}) collective-permute-start(bf16[192,1024]{1,0:T(8,128)(2,1)} %get-tuple-element.60.rest_1_), channel_id=1, source_target_pairs={{0,112},{1,113},{2,114},{3,115},{4,116},{5,117},{6,118},{7,119},{8... | collective-permute-start | bytes 1179656 | tf_op jit(solution)/shard_map/ppermute | solution.py:49
  106.2 5.4 %all-to-all-done.2.terms_ref = bf16[32,32,128]{2,1,0:T(8,128)(2,1)S(1)} async-done(((bf16[32,32,128]{2,1,0:T(8,128)(2,1)}), bf16[32,32,128]{2,1,0:T(8,128)(2,1)S(1)}, u32[]{:S(2)}, u32[]{:S(2)}) %all-to-all-start.2) | async-done | bytes 262176 | tf_op jit(solution)/shard_map/all_to_all | solution.py:300
  111.6 1.9 %states_after.1 = bf16[32,32,128]{2,1,0:T(8,128)(2,1)} custom-call(bf16[32,48,128]{2,1,0:T(8,128)(2,1)S(1)} %all-to-all-done.decay_ref.terms_ref, bf16[32,32,128]{2,1,0:T(8,128)(2,1)S(1)} %all-to-all-done.2.terms_ref, bf16[192,1024]{1,0:T(8,128)(2,1)} %get-tuple-element.59.rest_0_, bf16[192,1024]{1,0:T(8,128)(2,1)} %get-tuple-element.60.rest_1_), custom_call_target="tpu_custom_call" | custom-call | flops 1000000 | bytes 1000000 | tf_op jit(solution)/shard_map/states_after/pallas_call | solution.py:288
  113.5 5.1 %all-to-all-start.3 = ((bf16[32,32,128]{2,1,0:T(8,128)(2,1)}), bf16[32,32,128]{2,1,0:T(8,128)(2,1)S(1)}, u32[]{:S(2)}, u32[]{:S(2)}) async-start(bf16[32,32,128]{2,1,0:T(8,128)(2,1)} %states_after.1), calls=%async_computation.3 | async-start | bytes 524288 | tf_op jit(solution)/shard_map/all_to_all | solution.py:300
  118.6 2.0 %ring_sum_1.1 = (bf16[192,1024]{1,0:T(8,128)(2,1)}, bf16[192,1024]{1,0:T(8,128)(2,1)}) custom-call(bf16[192,1024]{1,0:T(8,128)(2,1)S(1)} %get-tuple-element.64.up_part_ref, bf16[192,1024]{1,0:T(8,128)(2,1)S(1)} %collective-permute-done.26.up_ref, bf16[192,1024]{1,0:T(8,128)(2,1)S(1)} %get-tuple-element.65.down_part_ref, ...), custom_call_target="tpu_custom_call" | custom-call | flops 400000 | bytes 2000000 | tf_op jit(solution)/shard_map/ring_sum_1/pallas_call | solution.py:288
  122.1 1.8 %collective-permute-start.29 = (bf16[192,1024]{1,0:T(8,128)(2,1)}, bf16[192,1024]{1,0:T(8,128)(2,1)}, u32[]{:S(2)}, u32[]{:S(2)}) collective-permute-start(bf16[192,1024]{1,0:T(8,128)(2,1)} %get-tuple-element.67), channel_id=1, source_target_pairs={{0,112},{1,113},{2,114},{3,115},{4,116},{5,117},{6,118},{7,119},{8... | collective-permute-start | bytes 1179656 | tf_op jit(solution)/shard_map/ppermute | solution.py:49
  123.9 2.7 %inner_grads.1 = (bf16[128,1024]{1,0:T(8,128)(2,1)}, f32[128,1024]{1,0:T(8,128)S(1)}, f32[128,1024]{1,0:T(8,128)S(1)}) custom-call(f32[8,128]{1,0:T(8,128)S(1)} %bitcast.9, bf16[128,1024]{1,0:T(8,128)(2,1)S(1)} %copy-done.4, bf16[128,1024]{1,0:T(8,128)(2,1)S(1)} %copy-done.1, bf16[128,1024]{1,0:T(8,128)(2,1)S(1)} %copy-done.3, ...), custom_call_target="tpu_custom_call" | custom-call | flops 200000000 | bytes 3000000 | tf_op jit(solution)/shard_map/inner_grads/pallas_call | solution.py:288
  126.6 3.8 %all-to-all-done.3 = bf16[32,32,128]{2,1,0:T(8,128)(2,1)S(1)} async-done(((bf16[32,32,128]{2,1,0:T(8,128)(2,1)}), bf16[32,32,128]{2,1,0:T(8,128)(2,1)S(1)}, u32[]{:S(2)}, u32[]{:S(2)}) %all-to-all-start.3) | async-done | bytes 262176 | tf_op jit(solution)/shard_map/all_to_all | solution.py:300
  131.7 4.8 %collective-permute-done.28.up_ref = bf16[192,1024]{1,0:T(8,128)(2,1)S(1)} collective-permute-done((bf16[192,1024]{1,0:T(8,128)(2,1)}, bf16[192,1024]{1,0:T(8,128)(2,1)S(1)}, u32[]{:S(2)}, u32[]{:S(2)}) %collective-permute-start.28) | collective-permute-done | bytes 393248 | tf_op jit(solution)/shard_map/ppermute | solution.py:49
  136.5 1.9 %ring_sum_0.1 = bf16[192,1024]{1,0:T(8,128)(2,1)} custom-call(bf16[192,1024]{1,0:T(8,128)(2,1)S(1)} %get-tuple-element.63.part_ref, bf16[192,1024]{1,0:T(8,128)(2,1)S(1)} %collective-permute-done.28.up_ref, bf16[192,1024]{1,0:T(8,128)(2,1)} %collective-permute-done.29.down_ref), custom_call_target="tpu_custom_call" | custom-call | flops 400000 | bytes 2000000 | tf_op jit(solution)/shard_map/ring_sum_0/pallas_call | solution.py:288
  (95 shorter events, 30.9 us)
Async XLA Ops:
  0.6 17.6 %collective-permute-start = (bf16[192,1024]{1,0:T(8,128)(2,1)}, bf16[192,1024]{1,0:T(8,128)(2,1)}, u32[]{:S(2)}, u32[]{:S(2)}) collective-permute-start(bf16[192,1024]{1,0:T(8,128)(2,1)} %refs_0_.1), channel_id=1, source_target_pairs={{0,16},{1,17},{2,18},{3,19},{4,20},{5,21},{6,22},{7,23},{8,24},{9,... | collective-permute-start | bytes 1179656 | tf_op jit(solution)/shard_map/ppermute | solution.py:49
  2.6 17.1 %collective-permute-start.1 = (bf16[192,1024]{1,0:T(8,128)(2,1)}, bf16[192,1024]{1,0:T(8,128)(2,1)}, u32[]{:S(2)}, u32[]{:S(2)}) collective-permute-start(bf16[192,1024]{1,0:T(8,128)(2,1)} %refs_0_.1), channel_id=1, source_target_pairs={{0,112},{1,113},{2,114},{3,115},{4,116},{5,117},{6,118},{7,119},{8... | collective-permute-start | bytes 1179656 | tf_op jit(solution)/shard_map/ppermute | solution.py:49
  10.8 22.0 %all-to-all-start = ((bf16[32,48,128]{2,1,0:T(8,128)(2,1)}), bf16[32,48,128]{2,1,0:T(8,128)(2,1)S(1)}, u32[]{:S(2)}, u32[]{:S(2)}) async-start(bf16[32,48,128]{2,1,0:T(8,128)(2,1)} %key_terms.1), calls=%async_computation | async-start | bytes 786432 | tf_op jit(solution)/shard_map/all_to_all | solution.py:300
  18.2 28.3 %collective-permute-start.12 = (bf16[192,1024]{1,0:T(8,128)(2,1)}, bf16[192,1024]{1,0:T(8,128)(2,1)S(1)}, u32[]{:S(2)}, u32[]{:S(2)}) collective-permute-start(bf16[192,1024]{1,0:T(8,128)(2,1)} %collective-permute-done.rest_0_.refs_8_), channel_id=1, source_target_pairs={{0,16},{1,17},{2,18},{3,19},{4,20},{5,21},{6,22},{7,23},{8,24},{9,... | collective-permute-start | bytes 1179656 | tf_op jit(solution)/shard_map/ppermute | solution.py:49
  19.8 28.3 %collective-permute-start.10 = (bf16[192,1024]{1,0:T(8,128)(2,1)}, bf16[192,1024]{1,0:T(8,128)(2,1)S(1)}, u32[]{:S(2)}, u32[]{:S(2)}) collective-permute-start(bf16[192,1024]{1,0:T(8,128)(2,1)} %collective-permute-done.1.rest_1_.refs_1_), channel_id=1, source_target_pairs={{0,112},{1,113},{2,114},{3,115},{4,116},{5,117},{6,118},{7,119},{8... | collective-permute-start | bytes 1179656 | tf_op jit(solution)/shard_map/ppermute | solution.py:49
  22.8 7.7 %collective-permute-start.2 = (bf16[384,128]{1,0:T(8,128)(2,1)S(1)}, bf16[384,128]{1,0:T(8,128)(2,1)S(1)}, u32[]{:S(2)}, u32[]{:S(2)}) collective-permute-start(bf16[384,128]{1,0:T(8,128)(2,1)S(1)} %get-tuple-element.36), channel_id=1, source_target_pairs={{0,0},{1,1},{2,2},{3,3},{4,128},{5,129},{6,130},{7,131},{8,8},{9,9... | collective-permute-start | bytes 294920 | tf_op jit(solution)/shard_map/ppermute | solution.py:49
  25.8 17.4 %collective-permute-start.3 = (bf16[384,128]{1,0:T(8,128)(2,1)S(1)}, bf16[384,128]{1,0:T(8,128)(2,1)S(1)}, u32[]{:S(2)}, u32[]{:S(2)}) collective-permute-start(bf16[384,128]{1,0:T(8,128)(2,1)S(1)} %get-tuple-element.36), channel_id=1, source_target_pairs={{0,4},{1,5},{2,6},{3,7},{4,132},{5,133},{6,134},{7,135},{8,12},{9,... | collective-permute-start | bytes 294920 | tf_op jit(solution)/shard_map/ppermute | solution.py:49
  25.9 17.3 %collective-permute-start.4 = (bf16[384,128]{1,0:T(8,128)(2,1)S(1)}, bf16[384,128]{1,0:T(8,128)(2,1)S(1)}, u32[]{:S(2)}, u32[]{:S(2)}) collective-permute-start(bf16[384,128]{1,0:T(8,128)(2,1)S(1)} %get-tuple-element.37), channel_id=1, source_target_pairs={{0,8},{1,9},{2,10},{3,11},{4,136},{5,137},{6,138},{7,139},{8,0},{9... | collective-permute-start | bytes 294920 | tf_op jit(solution)/shard_map/ppermute | solution.py:49
  30.5 12.6 %collective-permute-start.5 = (bf16[384,128]{1,0:T(8,128)(2,1)S(1)}, bf16[384,128]{1,0:T(8,128)(2,1)S(1)}, u32[]{:S(2)}, u32[]{:S(2)}) collective-permute-start(bf16[384,128]{1,0:T(8,128)(2,1)S(1)} %get-tuple-element.37), channel_id=1, source_target_pairs={{0,12},{1,13},{2,14},{3,15},{4,140},{5,141},{6,142},{7,143},{8,4},... | collective-permute-start | bytes 294920 | tf_op jit(solution)/shard_map/ppermute | solution.py:49
  33.6 32.2 %all-to-all-start.1 = ((bf16[32,32,128]{2,1,0:T(8,128)(2,1)}), bf16[32,32,128]{2,1,0:T(8,128)(2,1)S(1)}, u32[]{:S(2)}, u32[]{:S(2)}) async-start(bf16[32,32,128]{2,1,0:T(8,128)(2,1)} %states_before.1), calls=%async_computation.1 | async-start | bytes 524288 | tf_op jit(solution)/shard_map/all_to_all | solution.py:300
  43.2 12.5 %collective-permute-start.6 = (bf16[384,512]{1,0:T(8,128)(2,1)S(1)}, bf16[384,512]{1,0:T(8,128)(2,1)S(1)}, u32[]{:S(2)}, u32[]{:S(2)}) collective-permute-start(bf16[384,512]{1,0:T(8,128)(2,1)S(1)} %collect.1.own_ref), channel_id=1, source_target_pairs={{0,1},{1,2},{2,3},{3,0},{4,5},{5,6},{6,7},{7,4},{8,9},{9,10},{10,1... | collective-permute-start | bytes 1179656 | tf_op jit(solution)/shard_map/ppermute | solution.py:49
  44.8 11.9 %collective-permute-start.7 = (bf16[384,512]{1,0:T(8,128)(2,1)S(1)}, bf16[384,512]{1,0:T(8,128)(2,1)S(1)}, u32[]{:S(2)}, u32[]{:S(2)}) collective-permute-start(bf16[384,512]{1,0:T(8,128)(2,1)S(1)} %collect.1.own_ref), channel_id=1, source_target_pairs={{0,3},{1,0},{2,1},{3,2},{4,7},{5,4},{6,5},{7,6},{8,11},{9,8},{10,9... | collective-permute-start | bytes 1179656 | tf_op jit(solution)/shard_map/ppermute | solution.py:49
  46.6 14.4 %collective-permute-start.13 = (bf16[192,1024]{1,0:T(8,128)(2,1)S(1)}, bf16[192,1024]{1,0:T(8,128)(2,1)S(1)}, u32[]{:S(2)}, u32[]{:S(2)}) collective-permute-start(bf16[192,1024]{1,0:T(8,128)(2,1)S(1)} %collective-permute-done.12.refs_7_.rest_0_), channel_id=1, source_target_pairs={{0,16},{1,17},{2,18},{3,19},{4,20},{5,21},{6,22},{7,23},{8,24},{9,... | collective-permute-start | bytes 1179656 | tf_op jit(solution)/shard_map/ppermute | solution.py:49
  48.0 14.5 %collective-permute-start.11 = (bf16[192,1024]{1,0:T(8,128)(2,1)S(1)}, bf16[192,1024]{1,0:T(8,128)(2,1)S(1)}, u32[]{:S(2)}, u32[]{:S(2)}) collective-permute-start(bf16[192,1024]{1,0:T(8,128)(2,1)S(1)} %collective-permute-done.10.refs_2_.rest_1_), channel_id=1, source_target_pairs={{0,112},{1,113},{2,114},{3,115},{4,116},{5,117},{6,118},{7,119},{8... | collective-permute-start | bytes 1179656 | tf_op jit(solution)/shard_map/ppermute | solution.py:49
  56.4 11.2 %collective-permute-start.8 = (bf16[192,512]{1,0:T(8,128)(2,1)}, bf16[192,512]{1,0:T(8,128)(2,1)}, u32[]{:S(2)}, u32[]{:S(2)}) collective-permute-start(bf16[192,512]{1,0:T(8,128)(2,1)} %slice.16), channel_id=1, source_target_pairs={{0,1},{1,2},{2,3},{3,0},{4,5},{5,6},{6,7},{7,4},{8,9},{9,10},{10,1... | collective-permute-start | bytes 589832 | tf_op jit(solution)/shard_map/ppermute | solution.py:49
  57.4 10.2 %collective-permute-start.9 = (bf16[192,512]{1,0:T(8,128)(2,1)}, bf16[192,512]{1,0:T(8,128)(2,1)}, u32[]{:S(2)}, u32[]{:S(2)}) collective-permute-start(bf16[192,512]{1,0:T(8,128)(2,1)} %slice.17), channel_id=1, source_target_pairs={{0,3},{1,0},{2,1},{3,2},{4,7},{5,4},{6,5},{7,6},{8,11},{9,8},{10,9... | collective-permute-start | bytes 589832 | tf_op jit(solution)/shard_map/ppermute | solution.py:49
  61.7 8.0 %collective-permute-start.14 = (bf16[96,1024]{1,0:T(8,128)(2,1)}, bf16[96,1024]{1,0:T(8,128)(2,1)}, u32[]{:S(2)}, u32[]{:S(2)}) collective-permute-start(bf16[96,1024]{1,0:T(8,128)(2,1)} %slice.18), channel_id=1, source_target_pairs={{0,16},{1,17},{2,18},{3,19},{4,20},{5,21},{6,22},{7,23},{8,24},{9,... | collective-permute-start | bytes 589832 | tf_op jit(solution)/shard_map/ppermute | solution.py:49
  63.3 6.4 %collective-permute-start.15 = (bf16[96,1024]{1,0:T(8,128)(2,1)}, bf16[96,1024]{1,0:T(8,128)(2,1)}, u32[]{:S(2)}, u32[]{:S(2)}) collective-permute-start(bf16[96,1024]{1,0:T(8,128)(2,1)} %slice.19), channel_id=1, source_target_pairs={{0,112},{1,113},{2,114},{3,115},{4,116},{5,117},{6,118},{7,119},{8... | collective-permute-start | bytes 589832 | tf_op jit(solution)/shard_map/ppermute | solution.py:49
  67.0 7.4 %collective-permute-start.19 = (bf16[128,1024]{1,0:T(8,128)(2,1)S(1)}, bf16[128,1024]{1,0:T(8,128)(2,1)S(1)}, u32[]{:S(2)}, u32[]{:S(2)}) collective-permute-start(bf16[128,1024]{1,0:T(8,128)(2,1)S(1)} %get-tuple-element.50.own_ref), channel_id=1, source_target_pairs={{0,128},{1,129},{2,130},{3,131},{4,132},{5,133},{6,134},{7,135},{8... | collective-permute-start | bytes 786440 | tf_op jit(solution)/shard_map/ppermute | solution.py:49
  73.0 2.7 %collective-permute-start.20 = (bf16[128,1024]{1,0:T(8,128)(2,1)S(1)}, bf16[128,1024]{1,0:T(8,128)(2,1)S(1)}, u32[]{:S(2)}, u32[]{:S(2)}) collective-permute-start(bf16[128,1024]{1,0:T(8,128)(2,1)S(1)} %get-tuple-element.50.own_ref), channel_id=1, source_target_pairs={{0,8},{1,9},{2,10},{3,11},{4,12},{5,13},{6,14},{7,15},{8,0},{9,1},... | collective-permute-start | bytes 786440 | tf_op jit(solution)/shard_map/ppermute | solution.py:49
  74.5 8.7 %collective-permute-start.18 = (bf16[128,1024]{1,0:T(8,128)(2,1)S(1)}, bf16[128,1024]{1,0:T(8,128)(2,1)S(1)}, u32[]{:S(2)}, u32[]{:S(2)}) collective-permute-start(bf16[128,1024]{1,0:T(8,128)(2,1)S(1)} %sum_theirs.1.rest_0_), channel_id=1, source_target_pairs={{0,128},{1,129},{2,130},{3,131},{4,132},{5,133},{6,134},{7,135},{8... | collective-permute-start | bytes 786440 | tf_op jit(solution)/shard_map/ppermute | solution.py:49
  77.8 8.3 %collective-permute-start.22 = (bf16[96,1024]{1,0:T(8,128)(2,1)S(1)}, bf16[96,1024]{1,0:T(8,128)(2,1)S(1)}, u32[]{:S(2)}, u32[]{:S(2)}) collective-permute-start(bf16[96,1024]{1,0:T(8,128)(2,1)S(1)} %get-tuple-element.53), channel_id=1, source_target_pairs={{0,16},{1,17},{2,18},{3,19},{4,20},{5,21},{6,22},{7,23},{8,24},{9,... | collective-permute-start | bytes 589832 | tf_op jit(solution)/shard_map/ppermute | solution.py:49
  78.3 7.9 %collective-permute-start.23 = (bf16[96,1024]{1,0:T(8,128)(2,1)S(1)}, bf16[96,1024]{1,0:T(8,128)(2,1)S(1)}, u32[]{:S(2)}, u32[]{:S(2)}) collective-permute-start(bf16[96,1024]{1,0:T(8,128)(2,1)S(1)} %get-tuple-element.55), channel_id=1, source_target_pairs={{0,112},{1,113},{2,114},{3,115},{4,116},{5,117},{6,118},{7,119},{8... | collective-permute-start | bytes 589832 | tf_op jit(solution)/shard_map/ppermute | solution.py:49
  81.2 9.2 %collective-permute-start.16 = (bf16[128,1024]{1,0:T(8,128)(2,1)S(1)}, bf16[128,1024]{1,0:T(8,128)(2,1)S(1)}, u32[]{:S(2)}, u32[]{:S(2)}) collective-permute-start(bf16[128,1024]{1,0:T(8,128)(2,1)S(1)} %get-tuple-element.40), channel_id=1, source_target_pairs={{0,8},{1,9},{2,10},{3,11},{4,12},{5,13},{6,14},{7,15},{8,0},{9,1},... | collective-permute-start | bytes 786440 | tf_op jit(solution)/shard_map/ppermute | solution.py:49
  87.1 12.5 %collective-permute-start.24 = (bf16[192,1024]{1,0:T(8,128)(2,1)}, bf16[192,1024]{1,0:T(8,128)(2,1)}, u32[]{:S(2)}, u32[]{:S(2)}) collective-permute-start(bf16[192,1024]{1,0:T(8,128)(2,1)} %get-tuple-element.56), channel_id=1, source_target_pairs={{0,16},{1,17},{2,18},{3,19},{4,20},{5,21},{6,22},{7,23},{8,24},{9,... | collective-permute-start | bytes 1179656 | tf_op jit(solution)/shard_map/ppermute | solution.py:49
  89.5 10.4 %collective-permute-start.25 = (bf16[192,1024]{1,0:T(8,128)(2,1)}, bf16[192,1024]{1,0:T(8,128)(2,1)}, u32[]{:S(2)}, u32[]{:S(2)}) collective-permute-start(bf16[192,1024]{1,0:T(8,128)(2,1)} %get-tuple-element.58), channel_id=1, source_target_pairs={{0,112},{1,113},{2,114},{3,115},{4,116},{5,117},{6,118},{7,119},{8... | collective-permute-start | bytes 1179656 | tf_op jit(solution)/shard_map/ppermute | solution.py:49
  92.5 19.1 %all-to-all-start.2 = ((bf16[32,32,128]{2,1,0:T(8,128)(2,1)}), bf16[32,32,128]{2,1,0:T(8,128)(2,1)S(1)}, u32[]{:S(2)}, u32[]{:S(2)}) async-start(bf16[32,32,128]{2,1,0:T(8,128)(2,1)} %get-tuple-element.48), calls=%async_computation.2 | async-start | bytes 524288 | tf_op jit(solution)/shard_map/all_to_all | solution.py:300
  102.9 15.7 %collective-permute-start.26 = (bf16[192,1024]{1,0:T(8,128)(2,1)}, bf16[192,1024]{1,0:T(8,128)(2,1)S(1)}, u32[]{:S(2)}, u32[]{:S(2)}) collective-permute-start(bf16[192,1024]{1,0:T(8,128)(2,1)} %get-tuple-element.59.rest_0_), channel_id=1, source_target_pairs={{0,16},{1,17},{2,18},{3,19},{4,20},{5,21},{6,22},{7,23},{8,24},{9,... | collective-permute-start | bytes 1179656 | tf_op jit(solution)/shard_map/ppermute | solution.py:49
  104.4 14.3 %collective-permute-start.27 = (bf16[192,1024]{1,0:T(8,128)(2,1)}, bf16[192,1024]{1,0:T(8,128)(2,1)}, u32[]{:S(2)}, u32[]{:S(2)}) collective-permute-start(bf16[192,1024]{1,0:T(8,128)(2,1)} %get-tuple-element.60.rest_1_), channel_id=1, source_target_pairs={{0,112},{1,113},{2,114},{3,115},{4,116},{5,117},{6,118},{7,119},{8... | collective-permute-start | bytes 1179656 | tf_op jit(solution)/shard_map/ppermute | solution.py:49
  113.5 17.0 %all-to-all-start.3 = ((bf16[32,32,128]{2,1,0:T(8,128)(2,1)}), bf16[32,32,128]{2,1,0:T(8,128)(2,1)S(1)}, u32[]{:S(2)}, u32[]{:S(2)}) async-start(bf16[32,32,128]{2,1,0:T(8,128)(2,1)} %states_after.1), calls=%async_computation.3 | async-start | bytes 524288 | tf_op jit(solution)/shard_map/all_to_all | solution.py:300
  120.6 15.9 %collective-permute-start.28 = (bf16[192,1024]{1,0:T(8,128)(2,1)}, bf16[192,1024]{1,0:T(8,128)(2,1)S(1)}, u32[]{:S(2)}, u32[]{:S(2)}) collective-permute-start(bf16[192,1024]{1,0:T(8,128)(2,1)} %get-tuple-element.66), channel_id=1, source_target_pairs={{0,16},{1,17},{2,18},{3,19},{4,20},{5,21},{6,22},{7,23},{8,24},{9,... | collective-permute-start | bytes 1179656 | tf_op jit(solution)/shard_map/ppermute | solution.py:49
  122.1 14.4 %collective-permute-start.29 = (bf16[192,1024]{1,0:T(8,128)(2,1)}, bf16[192,1024]{1,0:T(8,128)(2,1)}, u32[]{:S(2)}, u32[]{:S(2)}) collective-permute-start(bf16[192,1024]{1,0:T(8,128)(2,1)} %get-tuple-element.67), channel_id=1, source_target_pairs={{0,112},{1,113},{2,114},{3,115},{4,116},{5,117},{6,118},{7,119},{8... | collective-permute-start | bytes 1179656 | tf_op jit(solution)/shard_map/ppermute | solution.py:49
  (21 other events, 205.1 us)

commit v6 on v5

--- a/solution.py
+++ b/solution.py
@@ -42,6 +42,7 @@
 X_UP = pairs(lambda yl, z, c, yh, x: (yl, z, c, yh, x + 1))
 X_DOWN = pairs(lambda yl, z, c, yh, x: (yl, z, c, yh, x + 3))
 CORE = pairs(lambda yl, z, c, yh, x: (yl, z, 1 - c, yh, x))
+Y_HI = pairs(lambda yl, z, c, yh, x: (yl, z, c, 1 - yh, x))
 Y_LO = pairs(lambda yl, z, c, yh, x: (1 - yl, z, c, yh, x))
 
 
@@ -210,20 +211,63 @@
         out_ref[:, pl.ds(pl.multiple_of(i * BLOCK, BLOCK), BLOCK)] = ref[...]
 
 
-def assemble_kernel(share, own_ref, left_ref, right_ref, low_ref, high_ref, out_ref, out_t_ref):
+def assemble_kernel(share, own_ref, left_ref, right_ref, opposite_ref, out_ref, turned_ref):
     _, z, _, _, x = coordinates()
-    for off, ref, start, part in (
-        (0, own_ref, 0, 0), (0, own_ref, share, 1),
-        (1, right_ref, 0, 0), (1, right_ref, share, 1),
-        (2, low_ref, 0, 0), (2, high_ref, 0, 1),
-        (3, left_ref, 0, 0), (3, left_ref, share, 1),
-    ):
-        k = (2 * ((x + off) % 4) + part - z + NZ) % NZ
-        at = pl.multiple_of(k * share, 64)
-        out_ref[pl.ds(at, share), :] = ref[start : start + share, :]
+    for off, ref in ((0, own_ref), (1, right_ref), (2, opposite_ref), (3, left_ref)):
+        for part in range(2):
+            k = (2 * ((x + off) % 4) + part - z + NZ) % NZ
+            at = pl.multiple_of(k * share, 64)
+            turned_ref[pl.ds(at, share), :] = ref[part * share : (part + 1) * share, :]
     for i in range(NZ * share // 256):
-        rows = pl.ds(i * 256, 256)
-        out_t_ref[:, rows] = jnp.transpose(out_ref[rows, :])
+        rows = slice(i * 256, (i + 1) * 256)
+        out_ref[:, rows] = jnp.transpose(turned_ref[rows, :])
+
+
+def halves_kernel(cot_ref, *rest):
+    same_ref, swap_ref = rest[-2:]
+    _, z, _, _, _ = coordinates()
+    turned = jnp.transpose(cot_ref[...])
+    half = turned.shape[0] // 2
+
+    @pl.when(z % 2 == 0)
+    def _():
+        same_ref[...] = turned[:half]
+        swap_ref[...] = turned[half:]
+
+    @pl.when(z % 2 == 1)
+    def _():
+        same_ref[...] = turned[half:]
+        swap_ref[...] = turned[:half]
+
+
+def join_kernel(own_same_ref, own_swap_ref, other_ref, out_ref):
+    half = other_ref.shape[0]
+    out_ref[:half, :BLOCK] = own_same_ref[...]
+    out_ref[:half, BLOCK:] = own_swap_ref[...]
+    out_ref[half:, :] = other_ref[...]
+
+
+def pair_kernel(a_ref, b_ref, out_ref):
+    out_ref[:, :BLOCK] = a_ref[...]
+    out_ref[:, BLOCK:] = b_ref[...]
+
+
+def assemble_weight_kernel(share, own_ref, left_ref, right_ref, opposite_ref, out_ref):
+    y_lo, z, core, y_hi, x = coordinates()
+    parity = z % 2
+    for off, ref in ((0, own_ref), (1, right_ref), (2, opposite_ref), (3, left_ref)):
+        for r in range(2):
+            bit = parity + r - 2 * parity * r
+            k = (2 * ((x + off) % 4) + bit - z + NZ) % NZ
+            lanes = pl.ds(pl.multiple_of(k * BLOCK, BLOCK), BLOCK)
+            for group, (a, b) in enumerate(((0, 0), (0, 1), (1, 0), (1, 1))):
+                of_core = core + a - 2 * core * a
+                of_y = y_lo + b - 2 * y_lo * b
+                far = of_y + y_hi - 2 * of_y * y_hi
+                rows = pl.ds(pl.multiple_of((2 * far + of_core) * share, 64), share)
+                out_ref[group * share : (group + 1) * share, lanes] = ref[
+                    rows, r * BLOCK : (r + 1) * BLOCK
+                ]
 
 
 def project_kernel(block_ref, *refs):
@@ -242,41 +286,30 @@
         cross_theirs_ref[:, cols] = out[3 * BLOCK : 4 * BLOCK].astype(BF)
 
 
-def weight_kernel(block_ref, own_ref, neighbour_ref, across_ref, diagonal_ref, *rest):
-    outs, tokens_ref = rest[-10:-1], rest[-1]
+def weight_kernel(block_ref, *refs):
+    pieces, (kept_ref, theirs_ref, cross_ref, cross_theirs_ref), tokens_ref = refs[:9], refs[-5:-1], refs[-1]
+    share = kept_ref.shape[0]
     width = tokens_ref.shape[1]
-    for tile in range(own_ref.shape[1] // width):
+    for tile in range(kept_ref.shape[1] // width):
         cols = slice(tile * width, (tile + 1) * width)
-        for i, ref in enumerate((own_ref, neighbour_ref, across_ref, diagonal_ref)):
-            tokens_ref[i * BLOCK : (i + 1) * BLOCK, :] = ref[:, cols]
         at = 0
-        for ref in outs:
-            rows = slice(at, at + ref.shape[0])
-            ref[:, cols] = mm(block_ref[rows, :], tokens_ref[...], 1, 0).astype(BF)
+        for ref in pieces:
+            tokens_ref[at : at + ref.shape[0], :] = ref[:, cols]
             at += ref.shape[0]
+        out = mm(block_ref[...], tokens_ref[...], 1, 0)
+        kept_ref[:, cols] = out[0:share]
+        theirs_ref[:, cols] = out[share : 2 * share]
+        cross_ref[:, cols] = out[2 * share : 3 * share].astype(BF)
+        cross_theirs_ref[:, cols] = out[3 * share : 4 * share].astype(BF)
 
 
 def add_kernel(a_ref, b_ref, out_ref):
     out_ref[...] = (a_ref[...].astype(F32) + b_ref[...].astype(F32)).astype(BF)
 
 
-def first_adds_kernel(up_part_ref, up_ref, down_part_ref, down_ref, *rest):
-    up_out_ref, down_out_ref = rest[-2:]
-    half = up_ref.shape[0]
-    up_out_ref[:half] = (up_part_ref[:half].astype(F32) + up_ref[...].astype(F32)).astype(BF)
-    up_out_ref[half:] = up_part_ref[half:]
-    down_out_ref[:half] = down_part_ref[:half]
-    down_out_ref[half:] = (down_part_ref[half:].astype(F32) + down_ref[...].astype(F32)).astype(BF)
-
-
-def adds_kernel(up_part_ref, up_ref, down_part_ref, down_ref, up_out_ref, down_out_ref):
-    up_out_ref[...] = (up_part_ref[...].astype(F32) + up_ref[...].astype(F32)).astype(BF)
-    down_out_ref[...] = (down_part_ref[...].astype(F32) + down_ref[...].astype(F32)).astype(BF)
-
-
-def last_add_kernel(part_ref, up_ref, down_ref, out_ref):
+def last_add_kernel(kept_ref, core_ref, other_ref, out_ref):
     out_ref[...] = (
-        part_ref[...].astype(F32) + (up_ref[...].astype(F32) + down_ref[...].astype(F32))
+        kept_ref[...] + core_ref[...].astype(F32) + other_ref[...].astype(F32)
     ).astype(BF)
 
 
@@ -284,12 +317,13 @@
     return jax.ShapeDtypeStruct(dims, dtype)
 
 
-def call(body, outs, name, flops, moved, args, after=()):
+def call(body, outs, name, flops, moved, args, after=(), scratch=()):
     return pl.pallas_call(
         body,
         in_specs=[pl.BlockSpec(a.shape, lambda n=a.ndim: (0,) * n) for a in args]
         + [pl.BlockSpec(memory_space=pltpu.VMEM)] * len(after),
         out_shape=outs,
+        scratch_shapes=list(scratch),
         compiler_params=PARAMS,
         name=name,
         cost_estimate=pl.CostEstimate(flops=flops, bytes_accessed=moved, transcendentals=0),
@@ -346,82 +380,88 @@
         attended_kernel, (row, row), "attended", 110_000_000, 2_000_000,
         (log_decay, queries, key_proj, value_proj, states), (below[1], above[1]),
     )
-    below.append(send(below[-1], Z_UP))
-    above.append(send(above[-1], Z_DOWN))
-    across = send(attended, CORE)
-    neighbour = send(attended, Y_LO)
-    opposite_low = send(left[:share], X_UP)
-    opposite_high = send(right[share:], X_DOWN)
-    block, block_t = call(
-        functools.partial(assemble_kernel, share),
-        (shape((features, 4 * tokens)), shape((4 * tokens, features))), "assemble",
-        1_000_000, 5_000_000, (own, left, right, opposite_low, opposite_high),
-    )
-    diagonal = send(neighbour, CORE)
+    below.append(send(below[1], Z_UP))
+    above.append(send(above[1], Z_DOWN))
+    att_below, att_above = [send(attended, Z_UP)], [send(attended, Z_DOWN)]
+    opposite = send(left, X_UP)
+    block_t = call(
+        functools.partial(assemble_kernel, share), shape((4 * tokens, features)), "assemble",
+        1_000_000, 3_000_000, (own, left, right, opposite),
+        scratch=[pltpu.VMEM((features, 4 * tokens), BF)],
+    )
     far_low = send(below[2][:half], Z_UP)
     far_high = send(above[2][half:], Z_DOWN)
+    for _ in range(2):
+        att_below.append(send(att_below[-1], Z_UP))
+        att_above.append(send(att_above[-1], Z_DOWN))
+    att_low = send(att_below[2][: tokens // 2], Z_UP)
+    att_high = send(att_above[2][tokens // 2 :], Z_DOWN)
+
+    halves = call(
+        halves_kernel, (shape((2 * share, tokens)),) * 2, "cotangent_halves", 0, 400_000,
+        (cotangent,), (own,),
+    )
+    turned = []
+    for r in range(2):
+        table = pairs(
+            lambda yl, z, c, yh, x, r=r: (yl, 2 * x + ((z % 2) ^ r), c, yh, z // 2)
+        )
+        turned.append(send(halves[r], table))
+    pair = call(pair_kernel, shape((2 * share, 2 * tokens)), "pair", 0, 400_000, turned)
+    joined = call(
+        join_kernel, shape((4 * share, 2 * tokens)), "join", 0, 800_000, (*turned, send(pair, Y_HI))
+    )
+    joined_left, joined_right = send(joined, X_UP), send(joined, X_DOWN)
+    joined_opposite = send(joined_left, X_UP)
+    block = call(
+        functools.partial(assemble_weight_kernel, share), shape((4 * share, NZ * tokens)),
+        "assemble_weight", 1_000_000, 3_000_000,
+        (joined, joined_left, joined_right, joined_opposite),
+    )
 
     weights = [out_weight] + above + [far_low, far_high] + below[::-1]
-    kept, theirs, cross, cross_theirs = pl.pallas_call(
-        project_kernel,
-        out_shape=[row32, row32, row, row],
-        scratch_shapes=[pltpu.VMEM((features, cols // TILES), BF)],
-        compiler_params=PARAMS,
-        name="project",
-        cost_estimate=pl.CostEstimate(
-            flops=1_600_000_000, bytes_accessed=6_000_000, transcendentals=0
-        ),
-    )(block_t, *weights)
+    kept, theirs, cross, cross_theirs = call(
+        project_kernel, (row32, row32, row, row), "project", 1_600_000_000, 6_000_000,
+        (block_t, *weights), scratch=[pltpu.VMEM((features, cols // TILES), BF)],
+    )
     from_core_theirs = send(cross_theirs, CORE)
     from_core = send(cross, CORE)
     passed = call(add_kernel, row, "sum_theirs", 100_000, 1_000_000, (theirs, from_core_theirs))
     arrived = send(passed, Y_LO)
-
-    part = pl.pallas_call(
-        weight_kernel,
-        in_specs=[pl.BlockSpec(memory_space=pltpu.VMEM)] * 6,
-        out_shape=[piece] * 4 + [shape((half, cols))] * 2 + [piece] * 3,
-        scratch_shapes=[pltpu.VMEM((4 * tokens, cols // TILES), BF)],
-        compiler_params=PARAMS,
-        name="weight_partial",
-        cost_estimate=pl.CostEstimate(
-            flops=1_600_000_000, bytes_accessed=6_000_000, transcendentals=0
-        ),
-    )(block, attended, neighbour, across, diagonal, passed)
-    up, down = send(part[4], Z_UP), send(part[5], Z_DOWN)
-
-    up, down = call(
-        first_adds_kernel, (piece, piece), "ring_sum_3", 400_000, 2_000_000,
-        (part[3], up, part[6], down), (arrived,),
-    )
-    up, down = send(up, Z_UP), send(down, Z_DOWN)
     grad_attn, query_terms = call(
         query_terms_kernel, (row, state), "query_terms", 40_000_000, 1_000_000,
         (log_decay, queries, kept, from_core, arrived),
     )
     returned = exchange(query_terms)
-    up, down = call(
-        adds_kernel, (piece, piece), "ring_sum_2", 400_000, 2_000_000, (part[2], up, part[7], down)
-    )
     afters = call(
         functools.partial(recurrence_kernel, True), state, "states_after", 1_000_000, 1_000_000,
-        (gathered, returned), (up, down),
-    )
-    up, down = send(up, Z_UP), send(down, Z_DOWN)
+        (gathered, returned),
+    )
     after = exchange(afters).reshape(cols, HEAD_DIM)
     grad_queries, inner_k, inner_v = call(
         inner_grads_kernel, (row, row32, row32), "inner_grads", 200_000_000, 3_000_000,
         (log_decay, queries, key_proj, value_proj, grad_attn, scores, states),
     )
-    up, down = call(
-        adds_kernel, (piece, piece), "ring_sum_1", 400_000, 2_000_000, (part[1], up, part[8], down)
-    )
-    up, down = send(up, Z_UP), send(down, Z_DOWN)
+
+    attendeds = [attended] + att_above + [att_low, att_high] + att_below[::-1]
+    piece32 = shape((share, cols), F32)
+    w_kept, w_theirs, w_cross, w_cross_theirs = call(
+        weight_kernel, (piece32, piece32, piece, piece), "weight_terms", 1_600_000_000, 6_000_000,
+        (block, *attendeds), scratch=[pltpu.VMEM((NZ * tokens, cols // TILES), BF)],
+    )
+    w_from_core_theirs = send(w_cross_theirs, CORE)
+    w_from_core = send(w_cross, CORE)
+    w_passed = call(
+        add_kernel, piece, "sum_weight_theirs", 200_000, 1_500_000, (w_theirs, w_from_core_theirs)
+    )
+    w_arrived = send(w_passed, Y_LO)
+    grad_weight = call(
+        last_add_kernel, piece, "weight_sum", 400_000, 2_000_000, (w_kept, w_from_core, w_arrived)
+    )
     grad_keys, grad_values = call(
         outer_grads_kernel, (row, row), "outer_grads", 70_000_000, 3_000_000,
         (log_decay, key_proj, value_proj, inner_k, inner_v, after),
     )
-    grad_weight = call(last_add_kernel, piece, "ring_sum_0", 400_000, 2_000_000, (part[0], up, down))
     return grad_queries, grad_keys, grad_values, grad_weight
 
 

time: 140 us -> 163 us (1.16)
  starting transfers between devices: 70 us -> 97.2 us
  waiting for transfers between devices: 34.5 us -> 23.1 us
  local copies, waits for them, and re-layouts: 7.26 us -> 14.3 us
    ppermute x30 -> x35, starting transfers between devices: 40.8 us -> 70.2 us  [send(): return lax.ppermute(array, AXES, table)]
    ppermute x30 -> x35, waiting for transfers between devices: 23.1 us -> 7.41 us  [send(): return lax.ppermute(array, AXES, table)]
    unnamed x38 -> x70, local copies, waits for them, and re-layouts: 4.41 us -> 11 us
    pallas_call x2 -> x0, Pallas kernels: 4.98 us -> none  [the longest x1 3.07 us: body(): pl.pallas_call(project_kernel, out_shape=[row32, row32, row, row], scratc...]
    pallas_call x14 -> x18, Pallas kernels: 19.2 us -> 23.9 us  [call(): pl.pallas_call(body, in_specs=[pl.BlockSpec(a.shape, lambda n=a.ndim: (0,...]
    all_to_all x4, waiting for transfers between devices: 11.4 us -> 15.7 us  [exchange(): return lax.all_to_all(array, 'seq', 0, 0, tiled=True)]
    all_to_all x4, starting transfers between devices: 29.2 us -> 27.1 us  [exchange(): return lax.all_to_all(array, 'seq', 0, 0, tiled=True)]
  transfers between devices with their start and end apart: 34 -> 39, of which waited for: 15 -> 8; matrix products, arithmetic and copies ran while one was open for 2% -> 2% of each run, Pallas kernels for 17% -> 15%
where the time goes in v6:
time: 163 us; the launch traced here: 161 us
  starting transfers between devices  97.2 us (60%)
  Pallas kernels  25.5 us (16%)
  waiting for transfers between devices  23.1 us (14%)
  local copies, waits for them, and re-layouts  14.3 us (9%)
    ppermute x35, starting transfers between devices, send(): return lax.ppermute(array, AXES, table)  70.2 us
    all_to_all x4, starting transfers between devices, exchange(): return lax.all_to_all(array, 'seq', 0, 0, tiled=True)  27.1 us
    pallas_call x18, Pallas kernels, call(): pl.pallas_call(body, in_specs=[pl.BlockSpec(a.shape, lambda n=a.ndim: (0,...  23.9 us
    all_to_all x4, waiting for transfers between devices, exchange(): return lax.all_to_all(array, 'seq', 0, 0, tiled=True)  15.7 us
    unnamed x70, local copies, waits for them, and re-layouts  11 us
    ppermute x35, waiting for transfers between devices, send(): return lax.ppermute(array, AXES, table)  7.41 us
  transfers between devices with their start and end apart: 39, of which 8 were waited for; matrix products, arithmetic and copies ran while one was open for 2% of the time, Pallas kernels for 15%

profile of v6, /device:TPU:8, one launch (start us, length us, event | category | flops | bytes accessed | tf_op | source)
XLA Modules:
  0.0 161.3 jit_solution(16328981274440623400)
XLA Ops:
  0.6 2.0 %collective-permute-start = (bf16[192,1024]{1,0:T(8,128)(2,1)}, bf16[192,1024]{1,0:T(8,128)(2,1)}, u32[]{:S(2)}, u32[]{:S(2)}) collective-permute-start(bf16[192,1024]{1,0:T(8,128)(2,1)} %refs_0_.1), channel_id=1, source_target_pairs={{0,16},{1,17},{2,18},{3,19},{4,20},{5,21},{6,22},{7,23},{8,24},{9,... | collective-permute-start | bytes 1179656 | tf_op jit(solution)/shard_map/ppermute | solution.py:50
  2.6 4.0 %collective-permute-start.1 = (bf16[192,1024]{1,0:T(8,128)(2,1)}, bf16[192,1024]{1,0:T(8,128)(2,1)}, u32[]{:S(2)}, u32[]{:S(2)}) collective-permute-start(bf16[192,1024]{1,0:T(8,128)(2,1)} %refs_0_.1), channel_id=1, source_target_pairs={{0,112},{1,113},{2,114},{3,115},{4,116},{5,117},{6,118},{7,119},{8... | collective-permute-start | bytes 1179656 | tf_op jit(solution)/shard_map/ppermute | solution.py:50
  9.2 1.6 key_terms.1
  10.8 7.4 %all-to-all-start = ((bf16[32,48,128]{2,1,0:T(8,128)(2,1)}), bf16[32,48,128]{2,1,0:T(8,128)(2,1)S(1)}, u32[]{:S(2)}, u32[]{:S(2)}) async-start(bf16[32,48,128]{2,1,0:T(8,128)(2,1)} %key_terms.1), calls=%async_computation | async-start | bytes 786432 | tf_op jit(solution)/shard_map/all_to_all | solution.py:334
  21.0 3.3 %collective-permute-start.2 = (bf16[384,128]{1,0:T(8,128)(2,1)S(1)}, bf16[384,128]{1,0:T(8,128)(2,1)S(1)}, u32[]{:S(2)}, u32[]{:S(2)}) collective-permute-start(bf16[384,128]{1,0:T(8,128)(2,1)S(1)} %get-tuple-element.25), channel_id=1, source_target_pairs={{0,0},{1,1},{2,2},{3,3},{4,128},{5,129},{6,130},{7,131},{8,8},{9,9... | collective-permute-start | bytes 294920 | tf_op jit(solution)/shard_map/ppermute | solution.py:50
  26.0 1.6 collective-permute-done.2.a_ref
  27.5 1.6 collective-permute-start.5
  29.1 3.7 %all-to-all-done.decay_ref.terms_ref = bf16[32,48,128]{2,1,0:T(8,128)(2,1)S(1)} async-done(((bf16[32,48,128]{2,1,0:T(8,128)(2,1)}), bf16[32,48,128]{2,1,0:T(8,128)(2,1)S(1)}, u32[]{:S(2)}, u32[]{:S(2)}) %all-to-all-start) | async-done | bytes 393248 | tf_op jit(solution)/shard_map/all_to_all | solution.py:334
  33.6 6.6 %all-to-all-start.1 = ((bf16[32,32,128]{2,1,0:T(8,128)(2,1)}), bf16[32,32,128]{2,1,0:T(8,128)(2,1)S(1)}, u32[]{:S(2)}, u32[]{:S(2)}) async-start(bf16[32,32,128]{2,1,0:T(8,128)(2,1)} %states_before.1), calls=%async_computation.1 | async-start | bytes 524288 | tf_op jit(solution)/shard_map/all_to_all | solution.py:334
  40.4 1.6 collective-permute-start.6
  45.1 6.7 %collective-permute-start.10 = (bf16[192,1024]{1,0:T(8,128)(2,1)S(1)}, bf16[192,1024]{1,0:T(8,128)(2,1)}, u32[]{:S(2)}, u32[]{:S(2)}) collective-permute-start(bf16[192,1024]{1,0:T(8,128)(2,1)S(1)} %collective-permute-done.9.refs_2_.rest_1_), channel_id=1, source_target_pairs={{0,112},{1,113},{2,114},{3,115},{4,116},{5,117},{6,118},{7,119},{8... | collective-permute-start | bytes 1179656 | tf_op jit(solution)/shard_map/ppermute | solution.py:50
  52.0 1.9 %collective-permute-start.19 = (bf16[384,128]{1,0:T(8,128)(2,1)S(1)}, bf16[384,128]{1,0:T(8,128)(2,1)S(1)}, u32[]{:S(2)}, u32[]{:S(2)}) collective-permute-start(bf16[384,128]{1,0:T(8,128)(2,1)S(1)} %get-tuple-element.40), channel_id=1, source_target_pairs={{0,16},{1,48},{2,80},{3,112},{4,20},{5,52},{6,84},{7,116},{8,24},{... | collective-permute-start | bytes 294920 | tf_op jit(solution)/shard_map/ppermute | solution.py:50
  53.9 14.0 %collective-permute-start.8 = (bf16[384,512]{1,0:T(8,128)(2,1)S(1)}, bf16[384,512]{1,0:T(8,128)(2,1)}, u32[]{:S(2)}, u32[]{:S(2)}) collective-permute-start(bf16[384,512]{1,0:T(8,128)(2,1)S(1)} %collective-permute-done.6.left_ref), channel_id=1, source_target_pairs={{0,1},{1,2},{2,3},{3,0},{4,5},{5,6},{6,7},{7,4},{8,9},{9,10},{10,1... | collective-permute-start | bytes 1179656 | tf_op jit(solution)/shard_map/ppermute | solution.py:50
  72.5 4.3 %collective-permute-start.13 = (bf16[96,1024]{1,0:T(8,128)(2,1)S(1)}, bf16[96,1024]{1,0:T(8,128)(2,1)S(1)}, u32[]{:S(2)}, u32[]{:S(2)}) collective-permute-start(bf16[96,1024]{1,0:T(8,128)(2,1)S(1)} %slice.16), channel_id=1, source_target_pairs={{0,16},{1,17},{2,18},{3,19},{4,20},{5,21},{6,22},{7,23},{8,24},{9,... | collective-permute-start | bytes 589832 | tf_op jit(solution)/shard_map/ppermute | solution.py:50
  77.7 7.7 %collective-permute-start.14 = (bf16[96,1024]{1,0:T(8,128)(2,1)S(1)}, bf16[96,1024]{1,0:T(8,128)(2,1)S(1)}, u32[]{:S(2)}, u32[]{:S(2)}) collective-permute-start(bf16[96,1024]{1,0:T(8,128)(2,1)S(1)} %slice.17), channel_id=1, source_target_pairs={{0,112},{1,113},{2,114},{3,115},{4,116},{5,117},{6,118},{7,119},{8... | collective-permute-start | bytes 589832 | tf_op jit(solution)/shard_map/ppermute | solution.py:50
  86.6 1.6 collective-permute-start.28
  91.3 1.6 assemble.1.block_ref
  92.9 3.1 %project.1 = (f32[128,1024]{1,0:T(8,128)S(1)}, f32[128,1024]{1,0:T(8,128)S(1)}, bf16[128,1024]{1,0:T(8,128)(2,1)S(1)}, bf16[128,1024]{1,0:T(8,128)(2,1)S(1)}) custom-call(bf16[512,1536]{1,0:T(8,128)(2,1)S(1)} %assemble.1.block_ref, bf16[192,1024]{1,0:T(8,128)(2,1)S(1)} %copy-done.23, bf16[192,1024]{1,0:T(8,128)(2,1)} %collective-permute-done.1.rest_1_.refs_1_, ...), custom_call_target="tpu_custom_call" | custom-call | flops 1600000000 | bytes 6000000 | tf_op jit(solution)/shard_map/project/pallas_call | solution.py:321
  96.1 2.0 %collective-permute-start.25 = (bf16[128,1024]{1,0:T(8,128)(2,1)S(1)}, bf16[128,1024]{1,0:T(8,128)(2,1)S(1)}, u32[]{:S(2)}, u32[]{:S(2)}) collective-permute-start(bf16[128,1024]{1,0:T(8,128)(2,1)S(1)} %collective-permute-done.24.refs_1_), channel_id=1, source_target_pairs={{0,112},{1,113},{2,114},{3,115},{4,116},{5,117},{6,118},{7,119},{8... | collective-permute-start | bytes 786440 | tf_op jit(solution)/shard_map/ppermute | solution.py:50
  98.3 4.5 %collective-permute-start.22 = (bf16[768,256]{1,0:T(8,128)(2,1)S(1)}, bf16[768,256]{1,0:T(8,128)(2,1)S(1)}, u32[]{:S(2)}, u32[]{:S(2)}) collective-permute-start(bf16[768,256]{1,0:T(8,128)(2,1)S(1)} %join.1.own_ref), channel_id=1, source_target_pairs={{0,3},{1,0},{2,1},{3,2},{4,7},{5,4},{6,5},{7,6},{8,11},{9,8},{10,9... | collective-permute-start | bytes 1179656 | tf_op jit(solution)/shard_map/ppermute | solution.py:50
  102.8 3.2 %collective-permute-start.26 = (bf16[128,1024]{1,0:T(8,128)(2,1)S(1)}, bf16[128,1024]{1,0:T(8,128)(2,1)S(1)}, u32[]{:S(2)}, u32[]{:S(2)}) collective-permute-start(bf16[128,1024]{1,0:T(8,128)(2,1)S(1)} %collective-permute-done.25.refs_2_), channel_id=1, source_target_pairs={{0,112},{1,113},{2,114},{3,115},{4,116},{5,117},{6,118},{7,119},{8... | collective-permute-start | bytes 786440 | tf_op jit(solution)/shard_map/ppermute | solution.py:50
  106.1 1.9 %collective-permute-done.29.refs_6_ = bf16[128,1024]{1,0:T(8,128)(2,1)S(1)} collective-permute-done((bf16[128,1024]{1,0:T(8,128)(2,1)S(1)}, bf16[128,1024]{1,0:T(8,128)(2,1)S(1)}, u32[]{:S(2)}, u32[]{:S(2)}) %collective-permute-start.29) | collective-permute-done | bytes 262176 | tf_op jit(solution)/shard_map/ppermute | solution.py:50
  109.5 2.2 %collective-permute-done.26.refs_3_ = bf16[128,1024]{1,0:T(8,128)(2,1)S(1)} collective-permute-done((bf16[128,1024]{1,0:T(8,128)(2,1)S(1)}, bf16[128,1024]{1,0:T(8,128)(2,1)S(1)}, u32[]{:S(2)}, u32[]{:S(2)}) %collective-permute-start.26) | collective-permute-done | bytes 262176 | tf_op jit(solution)/shard_map/ppermute | solution.py:50
  112.4 3.7 %collective-permute-start.31 = (bf16[64,1024]{1,0:T(8,128)(2,1)}, bf16[64,1024]{1,0:T(8,128)(2,1)}, u32[]{:S(2)}, u32[]{:S(2)}) collective-permute-start(bf16[64,1024]{1,0:T(8,128)(2,1)} %slice.19), channel_id=1, source_target_pairs={{0,112},{1,113},{2,114},{3,115},{4,116},{5,117},{6,118},{7,119},{8... | collective-permute-start | bytes 393224 | tf_op jit(solution)/shard_map/ppermute | solution.py:50
  118.2 7.7 %all-to-all-start.2 = ((bf16[32,32,128]{2,1,0:T(8,128)(2,1)}), bf16[32,32,128]{2,1,0:T(8,128)(2,1)S(1)}, u32[]{:S(2)}, u32[]{:S(2)}) async-start(bf16[32,32,128]{2,1,0:T(8,128)(2,1)} %get-tuple-element.36), calls=%async_computation.2 | async-start | bytes 524288 | tf_op jit(solution)/shard_map/all_to_all | solution.py:334
  127.3 3.5 %weight_terms.1 = (f32[192,1024]{1,0:T(8,128)S(1)}, f32[192,1024]{1,0:T(8,128)S(1)}, bf16[192,1024]{1,0:T(8,128)(2,1)S(1)}, bf16[192,1024]{1,0:T(8,128)(2,1)}) custom-call(bf16[768,1024]{1,0:T(8,128)(2,1)S(1)} %assemble_weight.1.block_ref, bf16[128,1024]{1,0:T(8,128)(2,1)S(1)} %copy-done.26, bf16[128,1024]{1,0:T(8,128)(2,1)S(1)} %copy-done.30, ...), custom_call_target="tpu_custom_call" | custom-call | flops 1600000000 | bytes 6000000 | tf_op jit(solution)/shard_map/weight_terms/pallas_call | solution.py:321
  131.7 6.0 %all-to-all-done.2.terms_ref = bf16[32,32,128]{2,1,0:T(8,128)(2,1)S(1)} async-done(((bf16[32,32,128]{2,1,0:T(8,128)(2,1)}), bf16[32,32,128]{2,1,0:T(8,128)(2,1)S(1)}, u32[]{:S(2)}, u32[]{:S(2)}) %all-to-all-start.2) | async-done | bytes 262176 | tf_op jit(solution)/shard_map/all_to_all | solution.py:334
  138.5 5.3 %all-to-all-start.3 = ((bf16[32,32,128]{2,1,0:T(8,128)(2,1)}), bf16[32,32,128]{2,1,0:T(8,128)(2,1)S(1)}, u32[]{:S(2)}, u32[]{:S(2)}) async-start(bf16[32,32,128]{2,1,0:T(8,128)(2,1)} %states_after.1), calls=%async_computation.3 | async-start | bytes 524288 | tf_op jit(solution)/shard_map/all_to_all | solution.py:334
  144.1 1.8 %sum_weight_theirs.1 = bf16[192,1024]{1,0:T(8,128)(2,1)} custom-call(f32[192,1024]{1,0:T(8,128)S(1)} %get-tuple-element.44.a_ref, bf16[192,1024]{1,0:T(8,128)(2,1)} %collective-permute-done.33.b_ref), custom_call_target="tpu_custom_call" | custom-call | flops 200000 | bytes 1500000 | tf_op jit(solution)/shard_map/sum_weight_theirs/pallas_call | solution.py:321
  146.2 2.7 %inner_grads.1 = (bf16[128,1024]{1,0:T(8,128)(2,1)}, f32[128,1024]{1,0:T(8,128)S(1)}, f32[128,1024]{1,0:T(8,128)S(1)}) custom-call(f32[8,128]{1,0:T(8,128)S(1)} %bitcast.9, bf16[128,1024]{1,0:T(8,128)(2,1)S(1)} %copy-done.4, bf16[128,1024]{1,0:T(8,128)(2,1)S(1)} %copy-done.1, bf16[128,1024]{1,0:T(8,128)(2,1)S(1)} %copy-done.3, ...), custom_call_target="tpu_custom_call" | custom-call | flops 200000000 | bytes 3000000 | tf_op jit(solution)/shard_map/inner_grads/pallas_call | solution.py:321
  149.7 6.0 %all-to-all-done.3 = bf16[32,32,128]{2,1,0:T(8,128)(2,1)S(1)} async-done(((bf16[32,32,128]{2,1,0:T(8,128)(2,1)}), bf16[32,32,128]{2,1,0:T(8,128)(2,1)S(1)}, u32[]{:S(2)}, u32[]{:S(2)}) %all-to-all-start.3) | async-done | bytes 262176 | tf_op jit(solution)/shard_map/all_to_all | solution.py:334
  159.3 2.0 %weight_sum.1 = bf16[192,1024]{1,0:T(8,128)(2,1)} custom-call(f32[192,1024]{1,0:T(8,128)S(1)} %get-tuple-element.42.kept_ref, bf16[192,1024]{1,0:T(8,128)(2,1)} %collective-permute-done.32.core_ref, bf16[192,1024]{1,0:T(8,128)(2,1)} %collective-permute-done.34.other_ref), custom_call_target="tpu_custom_call" | custom-call | flops 400000 | bytes 2000000 | tf_op jit(solution)/shard_map/weight_sum/pallas_call | solution.py:321
  (139 shorter events, 33.4 us)
Async XLA Ops:
  0.6 17.6 %collective-permute-start = (bf16[192,1024]{1,0:T(8,128)(2,1)}, bf16[192,1024]{1,0:T(8,128)(2,1)}, u32[]{:S(2)}, u32[]{:S(2)}) collective-permute-start(bf16[192,1024]{1,0:T(8,128)(2,1)} %refs_0_.1), channel_id=1, source_target_pairs={{0,16},{1,17},{2,18},{3,19},{4,20},{5,21},{6,22},{7,23},{8,24},{9,... | collective-permute-start | bytes 1179656 | tf_op jit(solution)/shard_map/ppermute | solution.py:50
  2.6 17.1 %collective-permute-start.1 = (bf16[192,1024]{1,0:T(8,128)(2,1)}, bf16[192,1024]{1,0:T(8,128)(2,1)}, u32[]{:S(2)}, u32[]{:S(2)}) collective-permute-start(bf16[192,1024]{1,0:T(8,128)(2,1)} %refs_0_.1), channel_id=1, source_target_pairs={{0,112},{1,113},{2,114},{3,115},{4,116},{5,117},{6,118},{7,119},{8... | collective-permute-start | bytes 1179656 | tf_op jit(solution)/shard_map/ppermute | solution.py:50
  10.8 22.0 %all-to-all-start = ((bf16[32,48,128]{2,1,0:T(8,128)(2,1)}), bf16[32,48,128]{2,1,0:T(8,128)(2,1)S(1)}, u32[]{:S(2)}, u32[]{:S(2)}) async-start(bf16[32,48,128]{2,1,0:T(8,128)(2,1)} %key_terms.1), calls=%async_computation | async-start | bytes 786432 | tf_op jit(solution)/shard_map/all_to_all | solution.py:334
  18.2 23.7 %collective-permute-start.11 = (bf16[192,1024]{1,0:T(8,128)(2,1)}, bf16[192,1024]{1,0:T(8,128)(2,1)S(1)}, u32[]{:S(2)}, u32[]{:S(2)}) collective-permute-start(bf16[192,1024]{1,0:T(8,128)(2,1)} %collective-permute-done.rest_0_.refs_8_), channel_id=1, source_target_pairs={{0,16},{1,17},{2,18},{3,19},{4,20},{5,21},{6,22},{7,23},{8,24},{9,... | collective-permute-start | bytes 1179656 | tf_op jit(solution)/shard_map/ppermute | solution.py:50
  24.3 20.8 %collective-permute-start.9 = (bf16[192,1024]{1,0:T(8,128)(2,1)}, bf16[192,1024]{1,0:T(8,128)(2,1)S(1)}, u32[]{:S(2)}, u32[]{:S(2)}) collective-permute-start(bf16[192,1024]{1,0:T(8,128)(2,1)} %collective-permute-done.1.rest_1_.refs_1_), channel_id=1, source_target_pairs={{0,112},{1,113},{2,114},{3,115},{4,116},{5,117},{6,118},{7,119},{8... | collective-permute-start | bytes 1179656 | tf_op jit(solution)/shard_map/ppermute | solution.py:50
  25.8 14.4 %collective-permute-start.3 = (bf16[384,128]{1,0:T(8,128)(2,1)S(1)}, bf16[384,128]{1,0:T(8,128)(2,1)S(1)}, u32[]{:S(2)}, u32[]{:S(2)}) collective-permute-start(bf16[384,128]{1,0:T(8,128)(2,1)S(1)} %get-tuple-element.25), channel_id=1, source_target_pairs={{0,4},{1,5},{2,6},{3,7},{4,132},{5,133},{6,134},{7,135},{8,12},{9,... | collective-permute-start | bytes 294920 | tf_op jit(solution)/shard_map/ppermute | solution.py:50
  25.9 14.4 %collective-permute-start.4 = (bf16[384,128]{1,0:T(8,128)(2,1)S(1)}, bf16[384,128]{1,0:T(8,128)(2,1)S(1)}, u32[]{:S(2)}, u32[]{:S(2)}) collective-permute-start(bf16[384,128]{1,0:T(8,128)(2,1)S(1)} %get-tuple-element.26), channel_id=1, source_target_pairs={{0,8},{1,9},{2,10},{3,11},{4,136},{5,137},{6,138},{7,139},{8,0},{9... | collective-permute-start | bytes 294920 | tf_op jit(solution)/shard_map/ppermute | solution.py:50
  27.5 12.7 %collective-permute-start.5 = (bf16[384,128]{1,0:T(8,128)(2,1)S(1)}, bf16[384,128]{1,0:T(8,128)(2,1)S(1)}, u32[]{:S(2)}, u32[]{:S(2)}) collective-permute-start(bf16[384,128]{1,0:T(8,128)(2,1)S(1)} %get-tuple-element.26), channel_id=1, source_target_pairs={{0,12},{1,13},{2,14},{3,15},{4,140},{5,141},{6,142},{7,143},{8,4},... | collective-permute-start | bytes 294920 | tf_op jit(solution)/shard_map/ppermute | solution.py:50
  33.6 36.6 %all-to-all-start.1 = ((bf16[32,32,128]{2,1,0:T(8,128)(2,1)}), bf16[32,32,128]{2,1,0:T(8,128)(2,1)S(1)}, u32[]{:S(2)}, u32[]{:S(2)}) async-start(bf16[32,32,128]{2,1,0:T(8,128)(2,1)} %states_before.1), calls=%async_computation.1 | async-start | bytes 524288 | tf_op jit(solution)/shard_map/all_to_all | solution.py:334
  40.4 13.5 %collective-permute-start.6 = (bf16[384,512]{1,0:T(8,128)(2,1)S(1)}, bf16[384,512]{1,0:T(8,128)(2,1)S(1)}, u32[]{:S(2)}, u32[]{:S(2)}) collective-permute-start(bf16[384,512]{1,0:T(8,128)(2,1)S(1)} %collect.1.own_ref.rest_0_), channel_id=1, source_target_pairs={{0,1},{1,2},{2,3},{3,0},{4,5},{5,6},{6,7},{7,4},{8,9},{9,10},{10,1... | collective-permute-start | bytes 1179656 | tf_op jit(solution)/shard_map/ppermute | solution.py:50
  41.9 29.4 %collective-permute-start.12 = (bf16[192,1024]{1,0:T(8,128)(2,1)S(1)}, bf16[192,1024]{1,0:T(8,128)(2,1)}, u32[]{:S(2)}, u32[]{:S(2)}) collective-permute-start(bf16[192,1024]{1,0:T(8,128)(2,1)S(1)} %collective-permute-done.11.refs_7_.rest_0_), channel_id=1, source_target_pairs={{0,16},{1,17},{2,18},{3,19},{4,20},{5,21},{6,22},{7,23},{8,24},{9,... | collective-permute-start | bytes 1179656 | tf_op jit(solution)/shard_map/ppermute | solution.py:50
  45.1 27.3 %collective-permute-start.10 = (bf16[192,1024]{1,0:T(8,128)(2,1)S(1)}, bf16[192,1024]{1,0:T(8,128)(2,1)}, u32[]{:S(2)}, u32[]{:S(2)}) collective-permute-start(bf16[192,1024]{1,0:T(8,128)(2,1)S(1)} %collective-permute-done.9.refs_2_.rest_1_), channel_id=1, source_target_pairs={{0,112},{1,113},{2,114},{3,115},{4,116},{5,117},{6,118},{7,119},{8... | collective-permute-start | bytes 1179656 | tf_op jit(solution)/shard_map/ppermute | solution.py:50
  51.8 33.6 %collective-permute-start.7 = (bf16[384,512]{1,0:T(8,128)(2,1)S(1)}, bf16[384,512]{1,0:T(8,128)(2,1)S(1)}, u32[]{:S(2)}, u32[]{:S(2)}) collective-permute-start(bf16[384,512]{1,0:T(8,128)(2,1)S(1)} %collect.1.own_ref.rest_0_), channel_id=1, source_target_pairs={{0,3},{1,0},{2,1},{3,2},{4,7},{5,4},{6,5},{7,6},{8,11},{9,8},{10,9... | collective-permute-start | bytes 1179656 | tf_op jit(solution)/shard_map/ppermute | solution.py:50
  52.0 16.0 %collective-permute-start.19 = (bf16[384,128]{1,0:T(8,128)(2,1)S(1)}, bf16[384,128]{1,0:T(8,128)(2,1)S(1)}, u32[]{:S(2)}, u32[]{:S(2)}) collective-permute-start(bf16[384,128]{1,0:T(8,128)(2,1)S(1)} %get-tuple-element.40), channel_id=1, source_target_pairs={{0,16},{1,48},{2,80},{3,112},{4,20},{5,52},{6,84},{7,116},{8,24},{... | collective-permute-start | bytes 294920 | tf_op jit(solution)/shard_map/ppermute | solution.py:50
  53.9 35.3 %collective-permute-start.8 = (bf16[384,512]{1,0:T(8,128)(2,1)S(1)}, bf16[384,512]{1,0:T(8,128)(2,1)}, u32[]{:S(2)}, u32[]{:S(2)}) collective-permute-start(bf16[384,512]{1,0:T(8,128)(2,1)S(1)} %collective-permute-done.6.left_ref), channel_id=1, source_target_pairs={{0,1},{1,2},{2,3},{3,0},{4,5},{5,6},{6,7},{7,4},{8,9},{9,10},{10,1... | collective-permute-start | bytes 1179656 | tf_op jit(solution)/shard_map/ppermute | solution.py:50
  71.3 15.2 %collective-permute-start.27 = (bf16[128,1024]{1,0:T(8,128)(2,1)S(1)}, bf16[128,1024]{1,0:T(8,128)(2,1)S(1)}, u32[]{:S(2)}, u32[]{:S(2)}) collective-permute-start(bf16[128,1024]{1,0:T(8,128)(2,1)S(1)} %get-tuple-element.41.refs_0_), channel_id=1, source_target_pairs={{0,16},{1,17},{2,18},{3,19},{4,20},{5,21},{6,22},{7,23},{8,24},{9,... | collective-permute-start | bytes 786440 | tf_op jit(solution)/shard_map/ppermute | solution.py:50
  72.5 20.4 %collective-permute-start.13 = (bf16[96,1024]{1,0:T(8,128)(2,1)S(1)}, bf16[96,1024]{1,0:T(8,128)(2,1)S(1)}, u32[]{:S(2)}, u32[]{:S(2)}) collective-permute-start(bf16[96,1024]{1,0:T(8,128)(2,1)S(1)} %slice.16), channel_id=1, source_target_pairs={{0,16},{1,17},{2,18},{3,19},{4,20},{5,21},{6,22},{7,23},{8,24},{9,... | collective-permute-start | bytes 589832 | tf_op jit(solution)/shard_map/ppermute | solution.py:50
  77.7 15.2 %collective-permute-start.14 = (bf16[96,1024]{1,0:T(8,128)(2,1)S(1)}, bf16[96,1024]{1,0:T(8,128)(2,1)S(1)}, u32[]{:S(2)}, u32[]{:S(2)}) collective-permute-start(bf16[96,1024]{1,0:T(8,128)(2,1)S(1)} %slice.17), channel_id=1, source_target_pairs={{0,112},{1,113},{2,114},{3,115},{4,116},{5,117},{6,118},{7,119},{8... | collective-permute-start | bytes 589832 | tf_op jit(solution)/shard_map/ppermute | solution.py:50
  86.1 10.0 %collective-permute-start.24 = (bf16[128,1024]{1,0:T(8,128)(2,1)S(1)}, bf16[128,1024]{1,0:T(8,128)(2,1)S(1)}, u32[]{:S(2)}, u32[]{:S(2)}) collective-permute-start(bf16[128,1024]{1,0:T(8,128)(2,1)S(1)} %get-tuple-element.41.refs_0_), channel_id=1, source_target_pairs={{0,112},{1,113},{2,114},{3,115},{4,116},{5,117},{6,118},{7,119},{8... | collective-permute-start | bytes 786440 | tf_op jit(solution)/shard_map/ppermute | solution.py:50
  86.6 11.5 %collective-permute-start.28 = (bf16[128,1024]{1,0:T(8,128)(2,1)S(1)}, bf16[128,1024]{1,0:T(8,128)(2,1)S(1)}, u32[]{:S(2)}, u32[]{:S(2)}) collective-permute-start(bf16[128,1024]{1,0:T(8,128)(2,1)S(1)} %collective-permute-done.27.refs_8_), channel_id=1, source_target_pairs={{0,16},{1,17},{2,18},{3,19},{4,20},{5,21},{6,22},{7,23},{8,24},{9,... | collective-permute-start | bytes 786440 | tf_op jit(solution)/shard_map/ppermute | solution.py:50
  89.2 13.6 %collective-permute-start.21 = (bf16[768,256]{1,0:T(8,128)(2,1)S(1)}, bf16[768,256]{1,0:T(8,128)(2,1)S(1)}, u32[]{:S(2)}, u32[]{:S(2)}) collective-permute-start(bf16[768,256]{1,0:T(8,128)(2,1)S(1)} %join.1.own_ref), channel_id=1, source_target_pairs={{0,1},{1,2},{2,3},{3,0},{4,5},{5,6},{6,7},{7,4},{8,9},{9,10},{10,1... | collective-permute-start | bytes 1179656 | tf_op jit(solution)/shard_map/ppermute | solution.py:50
  98.1 9.9 %collective-permute-start.29 = (bf16[128,1024]{1,0:T(8,128)(2,1)S(1)}, bf16[128,1024]{1,0:T(8,128)(2,1)S(1)}, u32[]{:S(2)}, u32[]{:S(2)}) collective-permute-start(bf16[128,1024]{1,0:T(8,128)(2,1)S(1)} %collective-permute-done.28.refs_7_), channel_id=1, source_target_pairs={{0,16},{1,17},{2,18},{3,19},{4,20},{5,21},{6,22},{7,23},{8,24},{9,... | collective-permute-start | bytes 786440 | tf_op jit(solution)/shard_map/ppermute | solution.py:50
  98.3 27.7 %collective-permute-start.22 = (bf16[768,256]{1,0:T(8,128)(2,1)S(1)}, bf16[768,256]{1,0:T(8,128)(2,1)S(1)}, u32[]{:S(2)}, u32[]{:S(2)}) collective-permute-start(bf16[768,256]{1,0:T(8,128)(2,1)S(1)} %join.1.own_ref), channel_id=1, source_target_pairs={{0,3},{1,0},{2,1},{3,2},{4,7},{5,4},{6,5},{7,6},{8,11},{9,8},{10,9... | collective-permute-start | bytes 1179656 | tf_op jit(solution)/shard_map/ppermute | solution.py:50
  102.8 23.2 %collective-permute-start.23 = (bf16[768,256]{1,0:T(8,128)(2,1)S(1)}, bf16[768,256]{1,0:T(8,128)(2,1)S(1)}, u32[]{:S(2)}, u32[]{:S(2)}) collective-permute-start(bf16[768,256]{1,0:T(8,128)(2,1)S(1)} %collective-permute-done.21.left_ref), channel_id=1, source_target_pairs={{0,1},{1,2},{2,3},{3,0},{4,5},{5,6},{6,7},{7,4},{8,9},{9,10},{10,1... | collective-permute-start | bytes 1179656 | tf_op jit(solution)/shard_map/ppermute | solution.py:50
  102.8 8.8 %collective-permute-start.26 = (bf16[128,1024]{1,0:T(8,128)(2,1)S(1)}, bf16[128,1024]{1,0:T(8,128)(2,1)S(1)}, u32[]{:S(2)}, u32[]{:S(2)}) collective-permute-start(bf16[128,1024]{1,0:T(8,128)(2,1)S(1)} %collective-permute-done.25.refs_2_), channel_id=1, source_target_pairs={{0,112},{1,113},{2,114},{3,115},{4,116},{5,117},{6,118},{7,119},{8... | collective-permute-start | bytes 786440 | tf_op jit(solution)/shard_map/ppermute | solution.py:50
  111.7 14.9 %collective-permute-start.30 = (bf16[64,1024]{1,0:T(8,128)(2,1)}, bf16[64,1024]{1,0:T(8,128)(2,1)}, u32[]{:S(2)}, u32[]{:S(2)}) collective-permute-start(bf16[64,1024]{1,0:T(8,128)(2,1)} %slice.18), channel_id=1, source_target_pairs={{0,16},{1,17},{2,18},{3,19},{4,20},{5,21},{6,22},{7,23},{8,24},{9,... | collective-permute-start | bytes 393224 | tf_op jit(solution)/shard_map/ppermute | solution.py:50
  112.4 14.2 %collective-permute-start.31 = (bf16[64,1024]{1,0:T(8,128)(2,1)}, bf16[64,1024]{1,0:T(8,128)(2,1)}, u32[]{:S(2)}, u32[]{:S(2)}) collective-permute-start(bf16[64,1024]{1,0:T(8,128)(2,1)} %slice.19), channel_id=1, source_target_pairs={{0,112},{1,113},{2,114},{3,115},{4,116},{5,117},{6,118},{7,119},{8... | collective-permute-start | bytes 393224 | tf_op jit(solution)/shard_map/ppermute | solution.py:50
  118.2 19.5 %all-to-all-start.2 = ((bf16[32,32,128]{2,1,0:T(8,128)(2,1)}), bf16[32,32,128]{2,1,0:T(8,128)(2,1)S(1)}, u32[]{:S(2)}, u32[]{:S(2)}) async-start(bf16[32,32,128]{2,1,0:T(8,128)(2,1)} %get-tuple-element.36), calls=%async_computation.2 | async-start | bytes 524288 | tf_op jit(solution)/shard_map/all_to_all | solution.py:334
  131.5 12.6 %collective-permute-start.33 = (bf16[192,1024]{1,0:T(8,128)(2,1)}, bf16[192,1024]{1,0:T(8,128)(2,1)}, u32[]{:S(2)}, u32[]{:S(2)}) collective-permute-start(bf16[192,1024]{1,0:T(8,128)(2,1)} %get-tuple-element.45), channel_id=1, source_target_pairs={{0,8},{1,9},{2,10},{3,11},{4,12},{5,13},{6,14},{7,15},{8,0},{9,1},... | collective-permute-start | bytes 1179656 | tf_op jit(solution)/shard_map/ppermute | solution.py:50
  138.5 17.2 %all-to-all-start.3 = ((bf16[32,32,128]{2,1,0:T(8,128)(2,1)}), bf16[32,32,128]{2,1,0:T(8,128)(2,1)S(1)}, u32[]{:S(2)}, u32[]{:S(2)}) async-start(bf16[32,32,128]{2,1,0:T(8,128)(2,1)} %states_after.1), calls=%async_computation.3 | async-start | bytes 524288 | tf_op jit(solution)/shard_map/all_to_all | solution.py:334
  143.9 14.2 %collective-permute-start.32 = (bf16[192,1024]{1,0:T(8,128)(2,1)}, bf16[192,1024]{1,0:T(8,128)(2,1)}, u32[]{:S(2)}, u32[]{:S(2)}) collective-permute-start(bf16[192,1024]{1,0:T(8,128)(2,1)} %copy-done.24), channel_id=1, source_target_pairs={{0,8},{1,9},{2,10},{3,11},{4,12},{5,13},{6,14},{7,15},{8,0},{9,1},... | collective-permute-start | bytes 1179656 | tf_op jit(solution)/shard_map/ppermute | solution.py:50
  145.9 13.4 %collective-permute-start.34 = (bf16[192,1024]{1,0:T(8,128)(2,1)}, bf16[192,1024]{1,0:T(8,128)(2,1)}, u32[]{:S(2)}, u32[]{:S(2)}) collective-permute-start(bf16[192,1024]{1,0:T(8,128)(2,1)} %sum_weight_theirs.1), channel_id=1, source_target_pairs={{0,128},{1,129},{2,130},{3,131},{4,132},{5,133},{6,134},{7,135},{8... | collective-permute-start | bytes 1179656 | tf_op jit(solution)/shard_map/ppermute | solution.py:50
  (42 other events, 445.2 us)

commit v7 on v5

--- a/solution.py
+++ b/solution.py
@@ -10,7 +10,8 @@
 HEAD_DIM = 128
 BLOCK = 128
 HEADS_LOCAL = 8
-N_SEQ = 32
+CHIPS = 16
+HALF_ROWS = 512
 ROWS = 32
 NZ = 8
 TILES = 4
@@ -45,6 +46,9 @@
 Y_LO = pairs(lambda yl, z, c, yh, x: (1 - yl, z, c, yh, x))
 
 
+CHIP_GROUPS = [[2 * p + c for p in range(CHIPS)] for c in range(2)]
+
+
 def send(array, table):
     return lax.ppermute(array, AXES, table)
 
@@ -110,7 +114,7 @@
             swap_ref[rows, :] = first
 
 
-def key_terms_kernel(decay_ref, key_hbm, value_hbm, out_ref, key_ref, value_ref, sems):
+def key_terms_kernel(decay_ref, key_hbm, value_hbm, mine_ref, cross_ref, key_ref, value_ref, sems):
     copies = (
         pltpu.make_async_copy(key_hbm, key_ref, sems.at[0]),
         pltpu.make_async_copy(value_hbm, value_ref, sems.at[1]),
@@ -118,36 +122,123 @@
     for copy in copies:
         copy.start()
     within = within_columns(decay_ref[...])
-    row = lax.broadcasted_iota(jnp.int32, (16, HEAD_DIM), 0)
     for copy in copies:
         copy.wait()
-    for h in range(HEADS_LOCAL):
-        col = within[:, h : h + 1]
-        last = col[BLOCK - 1 : BLOCK]
-        scaled = (jnp.exp(last - col) * key_ref[:, head_cols(h)].astype(F32)).astype(BF)
-        terms = mm(scaled, value_ref[:, head_cols(h)], 0, 0).astype(BF)
-        high = last.astype(BF).astype(F32)
-        middle = (last - high).astype(BF).astype(F32)
-        low = last - high - middle
-        parts = jnp.where(row == 0, high, jnp.where(row == 1, middle, jnp.where(row == 2, low, 0.0)))
-        parts = parts.astype(BF)
+    _, _, core, _, _ = coordinates()
+    row = lax.broadcasted_iota(jnp.int32, (16, HEAD_DIM), 0)
+    for half in range(2):
+        decays = jnp.zeros((16, HEAD_DIM), F32)
         for i in range(4):
-            out_ref[4 * h + i, 0:ROWS, :] = terms[i * ROWS : (i + 1) * ROWS]
-            out_ref[4 * h + i, ROWS : ROWS + 16, :] = parts
+            h = 4 * half + i
+            col = within[:, h : h + 1]
+            last = col[BLOCK - 1 : BLOCK]
+            scaled = (jnp.exp(last - col) * key_ref[:, head_cols(h)].astype(F32)).astype(BF)
+            terms = mm(scaled, value_ref[:, head_cols(h)], 0, 0).astype(BF)
+            decays = put_parts(decays, row, 3 * i, last)
+            store_half(core, half, i, terms, mine_ref, cross_ref)
+        decays = decays.astype(BF)
+        rows = pl.ds(HALF_ROWS, 16)
+
+        @pl.when(core == half)
+        def _():
+            mine_ref[rows, :] = decays
+
+        @pl.when(core != half)
+        def _():
+            cross_ref[rows, :] = decays
+
+
+def put_parts(decays, row, at, value):
+    high = value.astype(BF).astype(F32)
+    middle = (value - high).astype(BF).astype(F32)
+    low = value - high - middle
+    decays = jnp.where(row == at, high, decays)
+    decays = jnp.where(row == at + 1, middle, decays)
+    return jnp.where(row == at + 2, low, decays)
+
+
+def add_parts(decays, at):
+    return decays[at : at + 1] + (decays[at + 1 : at + 2] + decays[at + 2 : at + 3])
+
+
+def store_half(core, half, i, value, mine_ref, cross_ref):
+    rows = pl.ds(i * HEAD_DIM, HEAD_DIM)
+
+    @pl.when(core == half)
+    def _():
+        mine_ref[rows, :] = value
+
+    @pl.when(core != half)
+    def _():
+        cross_ref[rows, :] = value
+
+
+def merge_kernel(lead, mine_decay_ref, other_decay_ref, mine_ref, other_ref, *rest):
+    out_ref = rest[-1]
+    _, _, core, _, _ = coordinates()
+    row = lax.broadcasted_iota(jnp.int32, (16, HEAD_DIM), 0)
+    mine_decays = mine_decay_ref[HALF_ROWS : HALF_ROWS + 16, :].astype(F32)
+    other_decays = other_decay_ref[HALF_ROWS : HALF_ROWS + 16, :].astype(F32)
+    for j in range(4):
+        rows = slice(j * HEAD_DIM, (j + 1) * HEAD_DIM)
+        mine_decay, other_decay = add_parts(mine_decays, 3 * j), add_parts(other_decays, 3 * j)
+        mine, other = mine_ref[rows, :].astype(F32), other_ref[rows, :].astype(F32)
+        is_lead = core == lead
+        mine = mine * jnp.where(is_lead, jnp.exp(other_decay), 1.0)
+        other = other * jnp.where(is_lead, 1.0, jnp.exp(mine_decay))
+        terms = (mine + other).astype(BF)
+        for i in range(4):
+            out_ref[4 * j + i, 0:ROWS, :] = terms[i * ROWS : (i + 1) * ROWS]
+        if out_ref.shape[1] > ROWS:
+            parts = put_parts(jnp.zeros((16, HEAD_DIM), F32), row, 0, mine_decay + other_decay)
+            parts = parts.astype(BF)
+            for i in range(4):
+                out_ref[4 * j + i, ROWS : ROWS + 16, :] = parts
+
+
+def spread_kernel(
+    lead, mine_decay_ref, other_decay_ref, mine_ref, other_ref, state_ref, *rest
+):
+    own_out_ref, cross_out_ref = rest[-2:]
+    _, _, core, _, _ = coordinates()
+    mine_decays = mine_decay_ref[HALF_ROWS : HALF_ROWS + 16, :].astype(F32)
+    other_decays = other_decay_ref[HALF_ROWS : HALF_ROWS + 16, :].astype(F32)
+    for j in range(4):
+        rows = slice(j * HEAD_DIM, (j + 1) * HEAD_DIM)
+        state = state_ref[rows, :]
+        wide = state.astype(F32)
+        mine_moved = jnp.exp(add_parts(mine_decays, 3 * j)) * wide + mine_ref[rows, :].astype(F32)
+        other_moved = jnp.exp(add_parts(other_decays, 3 * j)) * wide + other_ref[rows, :].astype(F32)
+
+        @pl.when(core == lead)
+        def _():
+            own_out_ref[rows, :] = state
+            cross_out_ref[rows, :] = mine_moved.astype(BF)
+
+        @pl.when(core != lead)
+        def _():
+            own_out_ref[rows, :] = other_moved.astype(BF)
+            cross_out_ref[rows, :] = state
 
 
 def recurrence_kernel(reverse, decay_ref, terms_ref, *rest):
     out_ref = rest[-1]
     state = jnp.zeros((ROWS, HEAD_DIM), F32)
-    for k in reversed(range(N_SEQ)) if reverse else range(N_SEQ):
+    for k in reversed(range(CHIPS)) if reverse else range(CHIPS):
         out_ref[k] = state.astype(BF)
-        parts = decay_ref[k, ROWS : ROWS + 16, :].astype(F32)
-        factor = jnp.exp(parts[0:1] + (parts[1:2] + parts[2:3]))
+        factor = jnp.exp(add_parts(decay_ref[k, ROWS : ROWS + 16, :].astype(F32), 0))
         state = factor * state + terms_ref[k, 0:ROWS, :].astype(F32)
 
 
-def attended_kernel(decay_ref, query_ref, key_ref, value_ref, state_ref, *rest):
-    att_ref, score_ref = rest[-2:]
+def gather_halves(own_ref, other_ref, out_ref):
+    _, _, core, _, _ = coordinates()
+    out_ref[pl.ds(pl.multiple_of(core * HALF_ROWS, HALF_ROWS), HALF_ROWS), :] = own_ref[...]
+    out_ref[pl.ds(pl.multiple_of((1 - core) * HALF_ROWS, HALF_ROWS), HALF_ROWS), :] = other_ref[...]
+
+
+def attended_kernel(decay_ref, query_ref, key_ref, value_ref, own_ref, other_ref, *rest):
+    att_ref, score_ref, state_ref = rest[-3:]
+    gather_halves(own_ref, other_ref, state_ref)
     within = within_columns(decay_ref[...])
     for h in range(HEADS_LOCAL):
         cols = head_cols(h)
@@ -160,7 +251,8 @@
 
 
 def query_terms_kernel(decay_ref, query_ref, own_ref, core_ref, other_ref, *rest):
-    grad_ref, out_ref = rest[-2:]
+    grad_ref, mine_ref, cross_ref = rest[-3:]
+    _, _, core, _, _ = coordinates()
     within = within_columns(decay_ref[...])
     for h in range(HEADS_LOCAL):
         cols = head_cols(h)
@@ -169,14 +261,13 @@
         grad_ref[:, cols] = grad
         scaled = (jnp.exp(within[:, h : h + 1]) * query_ref[:, cols].astype(F32)).astype(BF)
         terms = mm(scaled, grad, 0, 0).astype(BF)
-        for i in range(4):
-            out_ref[4 * h + i] = terms[i * ROWS : (i + 1) * ROWS]
+        store_half(core, h // 4, h % 4, terms, mine_ref, cross_ref)
 
 
 def inner_grads_kernel(
-    decay_ref, query_ref, key_ref, value_ref, grad_ref, score_ref, state_ref,
-    gq_ref, gk_ref, gv_ref,
+    decay_ref, query_ref, key_ref, value_ref, grad_ref, score_ref, state_ref, *rest
 ):
+    gq_ref, gk_ref, gv_ref = rest[-3:]
     within = within_columns(decay_ref[...])
     for h in range(HEADS_LOCAL):
         cols = head_cols(h)
@@ -191,8 +282,10 @@
 
 
 def outer_grads_kernel(
-    decay_ref, key_ref, value_ref, inner_k_ref, inner_v_ref, after_ref, gk_ref, gv_ref
+    decay_ref, key_ref, value_ref, inner_k_ref, inner_v_ref, own_ref, other_ref,
+    gk_ref, gv_ref, after_ref,
 ):
+    gather_halves(own_ref, other_ref, after_ref)
     within = within_columns(decay_ref[...])
     for h in range(HEADS_LOCAL):
         cols = head_cols(h)
@@ -204,18 +297,19 @@
         gv_ref[:, cols] = gv.astype(BF)
 
 
-def collect_kernel(a_ref, b_ref, c_ref, d_ref, out_ref):
+def collect_kernel(a_ref, b_ref, c_ref, d_ref, *rest):
+    out_ref = rest[-1]
     flip = flip_bit()
     for i, ref in ((flip, a_ref), (1 - flip, b_ref), (2 + flip, c_ref), (3 - flip, d_ref)):
         out_ref[:, pl.ds(pl.multiple_of(i * BLOCK, BLOCK), BLOCK)] = ref[...]
 
 
-def assemble_kernel(share, own_ref, left_ref, right_ref, low_ref, high_ref, out_ref, out_t_ref):
+def assemble_kernel(share, own_ref, left_ref, right_ref, opposite_ref, out_ref, out_t_ref):
     _, z, _, _, x = coordinates()
     for off, ref, start, part in (
         (0, own_ref, 0, 0), (0, own_ref, share, 1),
         (1, right_ref, 0, 0), (1, right_ref, share, 1),
-        (2, low_ref, 0, 0), (2, high_ref, 0, 1),
+        (2, opposite_ref, 0, 0), (2, opposite_ref, share, 1),
         (3, left_ref, 0, 0), (3, left_ref, share, 1),
     ):
         k = (2 * ((x + off) % 4) + part - z + NZ) % NZ
@@ -269,7 +363,8 @@
     down_out_ref[half:] = (down_part_ref[half:].astype(F32) + down_ref[...].astype(F32)).astype(BF)
 
 
-def adds_kernel(up_part_ref, up_ref, down_part_ref, down_ref, up_out_ref, down_out_ref):
+def adds_kernel(up_part_ref, up_ref, down_part_ref, down_ref, *rest):
+    up_out_ref, down_out_ref = rest[-2:]
     up_out_ref[...] = (up_part_ref[...].astype(F32) + up_ref[...].astype(F32)).astype(BF)
     down_out_ref[...] = (down_part_ref[...].astype(F32) + down_ref[...].astype(F32)).astype(BF)
 
@@ -284,12 +379,13 @@
     return jax.ShapeDtypeStruct(dims, dtype)
 
 
-def call(body, outs, name, flops, moved, args, after=()):
+def call(body, outs, name, flops, moved, args, after=(), scratch=()):
     return pl.pallas_call(
         body,
         in_specs=[pl.BlockSpec(a.shape, lambda n=a.ndim: (0,) * n) for a in args]
         + [pl.BlockSpec(memory_space=pltpu.VMEM)] * len(after),
         out_shape=outs,
+        scratch_shapes=list(scratch),
         compiler_params=PARAMS,
         name=name,
         cost_estimate=pl.CostEstimate(flops=flops, bytes_accessed=moved, transcendentals=0),
@@ -297,7 +393,7 @@
 
 
 def exchange(array):
-    return lax.all_to_all(array, "seq", 0, 0, tiled=True)
+    return lax.all_to_all(array, "seq", 0, 0, tiled=True, axis_index_groups=CHIP_GROUPS)
 
 
 def body(cotangent, queries, key_proj, value_proj, log_decay, out_weight):
@@ -308,23 +404,30 @@
     row = shape((tokens, cols))
     row32 = shape((tokens, cols), F32)
     piece = shape((share, cols))
-    state = shape((N_SEQ, ROWS, HEAD_DIM))
+    slices = shape((CHIPS, ROWS, HEAD_DIM))
+    half_state = shape((HALF_ROWS, HEAD_DIM))
+    tagged = shape((HALF_ROWS + 16, HEAD_DIM))
 
     below, above = [send(out_weight, Z_UP)], [send(out_weight, Z_DOWN)]
 
     log_decay = jnp.transpose(log_decay)
-    terms = pl.pallas_call(
+    key_mine, key_cross = pl.pallas_call(
         key_terms_kernel,
         in_specs=[pl.BlockSpec(memory_space=pltpu.VMEM)] + [pl.BlockSpec(memory_space=pltpu.HBM)] * 2,
-        out_shape=shape((N_SEQ, ROWS + 16, HEAD_DIM)),
+        out_shape=(tagged, tagged),
         scratch_shapes=[pltpu.VMEM((tokens, cols), BF)] * 2 + [pltpu.SemaphoreType.DMA((2,))],
         compiler_params=PARAMS,
         name="key_terms",
         cost_estimate=pl.CostEstimate(flops=40_000_000, bytes_accessed=1_000_000, transcendentals=0),
     )(log_decay, key_proj, value_proj)
+    key_other = send(key_cross, CORE)
+    merged = call(
+        functools.partial(merge_kernel, 0), shape((CHIPS, ROWS + 16, HEAD_DIM)), "merge_keys",
+        1_000_000, 500_000, (key_mine, key_other, key_mine, key_other),
+    )
     parts = call(
         cotangent_kernel, (shape((2 * share, tokens)),) * 2, "cotangent_parts", 40_000_000_000, 400_000,
-        (cotangent,), (below[0], above[0]),
+        (cotangent,), (below[0], above[0], merged),
     )
     below.append(send(below[0], Z_UP))
     above.append(send(above[0], Z_DOWN))
@@ -333,29 +436,33 @@
         for b in range(2):
             table = pairs(lambda yl, z, c, yh, x, a=a, b=b: (yh, z, c ^ a, yl ^ b, x))
             pieces.append(send(parts[a], table))
-    gathered = exchange(terms)
-    own = call(collect_kernel, shape((2 * share, 4 * tokens)), "collect", 0, 800_000, pieces)
+    gathered = exchange(merged)
+
+    befores = call(
+        functools.partial(recurrence_kernel, False), slices, "states_before", 1_000_000, 1_000_000,
+        (gathered, gathered),
+    )
+    own = call(collect_kernel, shape((2 * share, 4 * tokens)), "collect", 0, 800_000, pieces, (befores,))
     left, right = send(own, X_UP), send(own, X_DOWN)
-
-    befores = call(
-        functools.partial(recurrence_kernel, False), state, "states_before", 1_000_000, 1_000_000,
-        (gathered, gathered),
-    )
-    states = exchange(befores).reshape(cols, HEAD_DIM)
-    attended, scores = call(
-        attended_kernel, (row, row), "attended", 110_000_000, 2_000_000,
-        (log_decay, queries, key_proj, value_proj, states), (below[1], above[1]),
+    before = exchange(befores).reshape(HALF_ROWS, HEAD_DIM)
+    before_own, before_cross = call(
+        functools.partial(spread_kernel, 0), (half_state, half_state), "spread_before",
+        20_000_000_000, 500_000, (key_mine, key_other, key_mine, key_other, before),
+    )
+    before_other = send(before_cross, CORE)
+    attended, scores, states = call(
+        attended_kernel, (row, row, shape((cols, HEAD_DIM))), "attended", 110_000_000, 2_000_000,
+        (log_decay, queries, key_proj, value_proj, before_own, before_other), (below[1], above[1]),
     )
     below.append(send(below[-1], Z_UP))
     above.append(send(above[-1], Z_DOWN))
     across = send(attended, CORE)
     neighbour = send(attended, Y_LO)
-    opposite_low = send(left[:share], X_UP)
-    opposite_high = send(right[share:], X_DOWN)
+    opposite = send(left, X_UP)
     block, block_t = call(
         functools.partial(assemble_kernel, share),
         (shape((features, 4 * tokens)), shape((4 * tokens, features))), "assemble",
-        1_000_000, 5_000_000, (own, left, right, opposite_low, opposite_high),
+        1_000_000, 5_000_000, (own, left, right, opposite),
     )
     diagonal = send(neighbour, CORE)
     far_low = send(below[2][:half], Z_UP)
@@ -390,36 +497,49 @@
     )(block, attended, neighbour, across, diagonal, passed)
     up, down = send(part[4], Z_UP), send(part[5], Z_DOWN)
 
+    grad_attn, query_mine, query_cross = call(
+        query_terms_kernel, (row, half_state, half_state), "query_terms", 40_000_000, 1_000_000,
+        (log_decay, queries, kept, from_core, arrived),
+    )
     up, down = call(
         first_adds_kernel, (piece, piece), "ring_sum_3", 400_000, 2_000_000,
-        (part[3], up, part[6], down), (arrived,),
+        (part[3], up, part[6], down), (grad_attn,),
     )
     up, down = send(up, Z_UP), send(down, Z_DOWN)
-    grad_attn, query_terms = call(
-        query_terms_kernel, (row, state), "query_terms", 40_000_000, 1_000_000,
-        (log_decay, queries, kept, from_core, arrived),
-    )
-    returned = exchange(query_terms)
+    query_other = send(query_cross, CORE)
+    query_merged = call(
+        functools.partial(merge_kernel, 1), slices, "merge_queries", 1_000_000, 500_000,
+        (key_mine, key_other, query_mine, query_other),
+    )
+    returned = exchange(query_merged)
     up, down = call(
-        adds_kernel, (piece, piece), "ring_sum_2", 400_000, 2_000_000, (part[2], up, part[7], down)
+        adds_kernel, (piece, piece), "ring_sum_2", 400_000, 2_000_000, (part[2], up, part[7], down),
+        (query_merged,),
     )
     afters = call(
-        functools.partial(recurrence_kernel, True), state, "states_after", 1_000_000, 1_000_000,
+        functools.partial(recurrence_kernel, True), slices, "states_after", 1_000_000, 1_000_000,
         (gathered, returned), (up, down),
     )
     up, down = send(up, Z_UP), send(down, Z_DOWN)
-    after = exchange(afters).reshape(cols, HEAD_DIM)
+    after = exchange(afters).reshape(HALF_ROWS, HEAD_DIM)
     grad_queries, inner_k, inner_v = call(
-        inner_grads_kernel, (row, row32, row32), "inner_grads", 200_000_000, 3_000_000,
-        (log_decay, queries, key_proj, value_proj, grad_attn, scores, states),
-    )
+        inner_grads_kernel, (row, row32, row32), "inner_grads", 25_000_000_000, 3_000_000,
+        (log_decay, queries, key_proj, value_proj, grad_attn, scores, states), (afters,),
+    )
+    after_own, after_cross = call(
+        functools.partial(spread_kernel, 1), (half_state, half_state), "spread_after",
+        25_000_000_000, 500_000, (key_mine, key_other, query_mine, query_other, after), (inner_k,),
+    )
+    after_other = send(after_cross, CORE)
     up, down = call(
-        adds_kernel, (piece, piece), "ring_sum_1", 400_000, 2_000_000, (part[1], up, part[8], down)
+        adds_kernel, (piece, piece), "ring_sum_1", 400_000, 2_000_000, (part[1], up, part[8], down),
+        (inner_k,),
     )
     up, down = send(up, Z_UP), send(down, Z_DOWN)
     grad_keys, grad_values = call(
         outer_grads_kernel, (row, row), "outer_grads", 70_000_000, 3_000_000,
-        (log_decay, key_proj, value_proj, inner_k, inner_v, after),
+        (log_decay, key_proj, value_proj, inner_k, inner_v, after_own, after_other),
+        scratch=[pltpu.VMEM((cols, HEAD_DIM), BF)],
     )
     grad_weight = call(last_add_kernel, piece, "ring_sum_0", 400_000, 2_000_000, (part[0], up, down))
     return grad_queries, grad_keys, grad_values, grad_weight

time: 140 us -> 139 us (level)
  waiting for transfers between devices: 34.5 us -> 22.6 us
  Pallas kernels: 25.7 us -> 29.7 us
  local copies, waits for them, and re-layouts: 7.26 us -> 10.8 us
  starting transfers between devices: 70 us -> 73.3 us
    all_to_all x4, waiting for transfers between devices: 11.4 us -> 2.73 us  [exchange(): lax.all_to_all(array, 'seq', 0, 0, tiled=True, axis_index_groups=CHIP_GRO...]
    unnamed x38 -> x54, local copies, waits for them, and re-layouts: 4.41 us -> 8.94 us
    ppermute x30 -> x33, starting transfers between devices: 40.8 us -> 44.3 us  [send(): return lax.ppermute(array, AXES, table)]
    pallas_call x14 -> x18, Pallas kernels: 19.2 us -> 22.4 us  [call(): pl.pallas_call(body, in_specs=[pl.BlockSpec(a.shape, lambda n=a.ndim: (0,...]
    ppermute x30 -> x33, waiting for transfers between devices: 23.1 us -> 19.9 us  [send(): return lax.ppermute(array, AXES, table)]
  transfers between devices with their start and end apart: 34 -> 37, of which waited for: 15 -> 11; matrix products, arithmetic and copies ran while one was open for 2% -> 1% of each run, Pallas kernels for 17% -> 20%
where the time goes in v7:
time: 139 us; the launch traced here: 137 us
  starting transfers between devices  73.3 us (53%)
  Pallas kernels  29.7 us (21%)
  waiting for transfers between devices  22.6 us (16%)
  local copies, waits for them, and re-layouts  10.8 us (8%)
    ppermute x33, starting transfers between devices, send(): return lax.ppermute(array, AXES, table)  44.3 us
    all_to_all x4, starting transfers between devices, exchange(): lax.all_to_all(array, 'seq', 0, 0, tiled=True, axis_index_groups=CHIP_GRO...  28.9 us
    pallas_call x18, Pallas kernels, call(): pl.pallas_call(body, in_specs=[pl.BlockSpec(a.shape, lambda n=a.ndim: (0,...  22.4 us
    ppermute x33, waiting for transfers between devices, send(): return lax.ppermute(array, AXES, table)  19.9 us
    unnamed x54, local copies, waits for them, and re-layouts  8.94 us
    pallas_call x1, Pallas kernels, body(): pl.pallas_call(project_kernel, out_shape=[row32, row32, row, row], scratc...  3.02 us
  transfers between devices with their start and end apart: 37, of which 11 were waited for; matrix products, arithmetic and copies ran while one was open for 1% of the time, Pallas kernels for 20%

profile of v7, /device:TPU:8, one launch (start us, length us, event | category | flops | bytes accessed | tf_op | source)
XLA Modules:
  0.0 137.4 jit_solution(12087657607035968842)
XLA Ops:
  0.6 2.0 %collective-permute-start = (bf16[192,1024]{1,0:T(8,128)(2,1)}, bf16[192,1024]{1,0:T(8,128)(2,1)S(1)}, u32[]{:S(2)}, u32[]{:S(2)}) collective-permute-start(bf16[192,1024]{1,0:T(8,128)(2,1)} %refs_0_.1), channel_id=1, source_target_pairs={{0,16},{1,17},{2,18},{3,19},{4,20},{5,21},{6,22},{7,23},{8,24},{9,... | collective-permute-start | bytes 1179656 | tf_op jit(solution)/shard_map/ppermute | solution.py:53
  2.6 4.0 %collective-permute-start.1 = (bf16[192,1024]{1,0:T(8,128)(2,1)}, bf16[192,1024]{1,0:T(8,128)(2,1)}, u32[]{:S(2)}, u32[]{:S(2)}) collective-permute-start(bf16[192,1024]{1,0:T(8,128)(2,1)} %refs_0_.1), channel_id=1, source_target_pairs={{0,112},{1,113},{2,114},{3,115},{4,116},{5,117},{6,118},{7,119},{8... | collective-permute-start | bytes 1179656 | tf_op jit(solution)/shard_map/ppermute | solution.py:53
  9.2 2.4 %key_terms.1 = (bf16[528,128]{1,0:T(8,128)(2,1)S(1)}, bf16[528,128]{1,0:T(8,128)(2,1)S(1)}) custom-call(f32[8,128]{1,0:T(8,128)S(1)} %bitcast.5, bf16[128,1024]{1,0:T(8,128)(2,1)S(1)} %copy-done, bf16[128,1024]{1,0:T(8,128)(2,1)S(1)} %copy-done.2), custom_call_target="tpu_custom_call" | custom-call | flops 40000000 | bytes 1000000 | tf_op jit(solution)/shard_map/key_terms/pallas_call | solution.py:414
  13.8 7.2 %all-to-all-start = ((bf16[16,48,128]{2,1,0:T(8,128)(2,1)}), bf16[16,48,128]{2,1,0:T(8,128)(2,1)S(1)}, u32[]{:S(2)}, u32[]{:S(2)}) async-start(bf16[16,48,128]{2,1,0:T(8,128)(2,1)} %merge_keys.1.rest_2_), calls=%async_computation | async-start | bytes 393216 | tf_op jit(solution)/shard_map/all_to_all | solution.py:396
  22.4 2.8 %collective-permute-start.3 = (bf16[384,128]{1,0:T(8,128)(2,1)S(1)}, bf16[384,128]{1,0:T(8,128)(2,1)S(1)}, u32[]{:S(2)}, u32[]{:S(2)}) collective-permute-start(bf16[384,128]{1,0:T(8,128)(2,1)S(1)} %get-tuple-element.46), channel_id=1, source_target_pairs={{0,0},{1,1},{2,2},{3,3},{4,128},{5,129},{6,130},{7,131},{8,8},{9,9... | collective-permute-start | bytes 294920 | tf_op jit(solution)/shard_map/ppermute | solution.py:53
  25.4 3.2 %collective-permute-start.6 = (bf16[384,128]{1,0:T(8,128)(2,1)S(1)}, bf16[384,128]{1,0:T(8,128)(2,1)S(1)}, u32[]{:S(2)}, u32[]{:S(2)}) collective-permute-start(bf16[384,128]{1,0:T(8,128)(2,1)S(1)} %get-tuple-element.47), channel_id=1, source_target_pairs={{0,12},{1,13},{2,14},{3,15},{4,140},{5,141},{6,142},{7,143},{8,4},... | collective-permute-start | bytes 294920 | tf_op jit(solution)/shard_map/ppermute | solution.py:53
  28.6 1.5 %collective-permute-start.12 = (bf16[192,1024]{1,0:T(8,128)(2,1)S(1)}, bf16[192,1024]{1,0:T(8,128)(2,1)S(1)}, u32[]{:S(2)}, u32[]{:S(2)}) collective-permute-start(bf16[192,1024]{1,0:T(8,128)(2,1)S(1)} %collective-permute-done.rest_0_.refs_8_), channel_id=1, source_target_pairs={{0,16},{1,17},{2,18},{3,19},{4,20},{5,21},{6,22},{7,23},{8,24},{9,... | collective-permute-start | bytes 1179656 | tf_op jit(solution)/shard_map/ppermute | solution.py:53
  31.0 4.4 %collective-permute-start.10 = (bf16[192,1024]{1,0:T(8,128)(2,1)}, bf16[192,1024]{1,0:T(8,128)(2,1)S(1)}, u32[]{:S(2)}, u32[]{:S(2)}) collective-permute-start(bf16[192,1024]{1,0:T(8,128)(2,1)} %collective-permute-done.1.rest_1_.refs_1_), channel_id=1, source_target_pairs={{0,112},{1,113},{2,114},{3,115},{4,116},{5,117},{6,118},{7,119},{8... | collective-permute-start | bytes 1179656 | tf_op jit(solution)/shard_map/ppermute | solution.py:53
  36.4 1.6 %collective-permute-start.7 = (bf16[384,512]{1,0:T(8,128)(2,1)S(1)}, bf16[384,512]{1,0:T(8,128)(2,1)S(1)}, u32[]{:S(2)}, u32[]{:S(2)}) collective-permute-start(bf16[384,512]{1,0:T(8,128)(2,1)S(1)} %collect.1.own_ref), channel_id=1, source_target_pairs={{0,1},{1,2},{2,3},{3,0},{4,5},{5,6},{6,7},{7,4},{8,9},{9,10},{10,1... | collective-permute-start | bytes 1179656 | tf_op jit(solution)/shard_map/ppermute | solution.py:53
  37.9 7.9 %all-to-all-start.1 = ((bf16[16,32,128]{2,1,0:T(8,128)(2,1)}), bf16[16,32,128]{2,1,0:T(8,128)(2,1)S(1)}, u32[]{:S(2)}, u32[]{:S(2)}) async-start(bf16[16,32,128]{2,1,0:T(8,128)(2,1)} %states_before.1.rest_0_), calls=%async_computation.1 | async-start | bytes 262144 | tf_op jit(solution)/shard_map/all_to_all | solution.py:396
  45.9 1.7 %collective-permute-start.8 = (bf16[384,512]{1,0:T(8,128)(2,1)S(1)}, bf16[384,512]{1,0:T(8,128)(2,1)S(1)}, u32[]{:S(2)}, u32[]{:S(2)}) collective-permute-start(bf16[384,512]{1,0:T(8,128)(2,1)S(1)} %collect.1.own_ref), channel_id=1, source_target_pairs={{0,3},{1,0},{2,1},{3,2},{4,7},{5,4},{6,5},{7,6},{8,11},{9,8},{10,9... | collective-permute-start | bytes 1179656 | tf_op jit(solution)/shard_map/ppermute | solution.py:53
  47.6 1.5 %collective-permute-start.13 = (bf16[192,1024]{1,0:T(8,128)(2,1)S(1)}, bf16[192,1024]{1,0:T(8,128)(2,1)}, u32[]{:S(2)}, u32[]{:S(2)}) collective-permute-start(bf16[192,1024]{1,0:T(8,128)(2,1)S(1)} %collective-permute-done.12.refs_7_.rest_0_), channel_id=1, source_target_pairs={{0,16},{1,17},{2,18},{3,19},{4,20},{5,21},{6,22},{7,23},{8,24},{9,... | collective-permute-start | bytes 1179656 | tf_op jit(solution)/shard_map/ppermute | solution.py:53
  49.1 1.8 %collective-permute-start.11 = (bf16[192,1024]{1,0:T(8,128)(2,1)S(1)}, bf16[192,1024]{1,0:T(8,128)(2,1)}, u32[]{:S(2)}, u32[]{:S(2)}) collective-permute-start(bf16[192,1024]{1,0:T(8,128)(2,1)S(1)} %collective-permute-done.10.refs_2_.rest_1_), channel_id=1, source_target_pairs={{0,112},{1,113},{2,114},{3,115},{4,116},{5,117},{6,118},{7,119},{8... | collective-permute-start | bytes 1179656 | tf_op jit(solution)/shard_map/ppermute | solution.py:53
  51.1 2.7 %all-to-all-done.1 = bf16[16,32,128]{2,1,0:T(8,128)(2,1)S(1)} async-done(((bf16[16,32,128]{2,1,0:T(8,128)(2,1)}), bf16[16,32,128]{2,1,0:T(8,128)(2,1)S(1)}, u32[]{:S(2)}, u32[]{:S(2)}) %all-to-all-start.1) | async-done | bytes 131104 | tf_op jit(solution)/shard_map/all_to_all | solution.py:396
  54.1 6.6 %collective-permute-done.13.refs_6_ = bf16[192,1024]{1,0:T(8,128)(2,1)} collective-permute-done((bf16[192,1024]{1,0:T(8,128)(2,1)S(1)}, bf16[192,1024]{1,0:T(8,128)(2,1)}, u32[]{:S(2)}, u32[]{:S(2)}) %collective-permute-start.13) | collective-permute-done | bytes 393248 | tf_op jit(solution)/shard_map/ppermute | solution.py:53
  62.9 3.3 %collective-permute-start.15 = (bf16[96,1024]{1,0:T(8,128)(2,1)S(1)}, bf16[96,1024]{1,0:T(8,128)(2,1)S(1)}, u32[]{:S(2)}, u32[]{:S(2)}) collective-permute-start(bf16[96,1024]{1,0:T(8,128)(2,1)S(1)} %slice.9), channel_id=1, source_target_pairs={{0,112},{1,113},{2,114},{3,115},{4,116},{5,117},{6,118},{7,119},{8... | collective-permute-start | bytes 589832 | tf_op jit(solution)/shard_map/ppermute | solution.py:53
  68.7 1.6 %assemble.1 = (bf16[1536,512]{1,0:T(8,128)(2,1)S(1)}, bf16[512,1536]{1,0:T(8,128)(2,1)S(1)}) custom-call(bf16[384,512]{1,0:T(8,128)(2,1)S(1)} %collect.1.own_ref, bf16[384,512]{1,0:T(8,128)(2,1)S(1)} %collective-permute-done.7.left_ref, bf16[384,512]{1,0:T(8,128)(2,1)S(1)} %collective-permute-done.8.right_ref, ...), custom_call_target="tpu_custom_call" | custom-call | flops 1000000 | bytes 5000000 | tf_op jit(solution)/shard_map/assemble/pallas_call | solution.py:383
  70.3 3.0 %project.1 = (f32[128,1024]{1,0:T(8,128)S(1)}, f32[128,1024]{1,0:T(8,128)S(1)}, bf16[128,1024]{1,0:T(8,128)(2,1)S(1)}, bf16[128,1024]{1,0:T(8,128)(2,1)S(1)}) custom-call(bf16[512,1536]{1,0:T(8,128)(2,1)S(1)} %get-tuple-element.48.block_ref, bf16[192,1024]{1,0:T(8,128)(2,1)S(1)} %copy-done.19, bf16[192,1024]{1,0:T(8,128)(2,1)} %collective-permute-done.1.rest_1_.refs_1_, ...), custom_call_target="tpu_custom_call" | custom-call | flops 1600000000 | bytes 6000000 | tf_op jit(solution)/shard_map/project/pallas_call | solution.py:472
  76.7 1.9 %weight_partial.1 = (bf16[192,1024]{1,0:T(8,128)(2,1)S(1)}, bf16[192,1024]{1,0:T(8,128)(2,1)S(1)}, bf16[192,1024]{1,0:T(8,128)(2,1)S(1)}, bf16[192,1024]{1,0:T(8...) custom-call(bf16[1536,512]{1,0:T(8,128)(2,1)S(1)} %get-tuple-element, ...), custom_call_target="tpu_custom_call" | custom-call | flops 1600000000 | bytes 6000000 | tf_op jit(solution)/shard_map/weight_partial/pallas_call | solution.py:487
  78.7 3.2 %collective-permute-start.25 = (bf16[96,1024]{1,0:T(8,128)(2,1)S(1)}, bf16[96,1024]{1,0:T(8,128)(2,1)S(1)}, u32[]{:S(2)}, u32[]{:S(2)}) collective-permute-start(bf16[96,1024]{1,0:T(8,128)(2,1)S(1)} %get-tuple-element.66), channel_id=1, source_target_pairs={{0,112},{1,113},{2,114},{3,115},{4,116},{5,117},{6,118},{7,119},{8... | collective-permute-start | bytes 589832 | tf_op jit(solution)/shard_map/ppermute | solution.py:53
  81.9 2.1 %collective-permute-done.18.other_ref = bf16[128,1024]{1,0:T(8,128)(2,1)S(1)} collective-permute-done((bf16[128,1024]{1,0:T(8,128)(2,1)S(1)}, bf16[128,1024]{1,0:T(8,128)(2,1)S(1)}, u32[]{:S(2)}, u32[]{:S(2)}) %collective-permute-start.18) | collective-permute-done | bytes 262176 | tf_op jit(solution)/shard_map/ppermute | solution.py:53
  84.0 2.3 %query_terms.1 = (bf16[128,1024]{1,0:T(8,128)(2,1)S(1)}, bf16[512,128]{1,0:T(8,128)(2,1)S(1)}, bf16[512,128]{1,0:T(8,128)(2,1)S(1)}) custom-call(f32[8,128]{1,0:T(8,128)S(1)} %bitcast.7, bf16[128,1024]{1,0:T(8,128)(2,1)S(1)} %copy-done.4, f32[128,1024]{1,0:T(8,128)S(1)} %get-tuple-element.49.own_ref, bf16[128,1024]{1,0:T(8,128)(2,1)S(1)} %collective-permute-done.16.core_ref, ...), custom_call_target="tpu_custom_call" | custom-call | flops 40000000 | bytes 1000000 | tf_op jit(solution)/shard_map/query_terms/pallas_call | solution.py:383
  88.5 2.6 %collective-permute-start.27 = (bf16[192,1024]{1,0:T(8,128)(2,1)}, bf16[192,1024]{1,0:T(8,128)(2,1)}, u32[]{:S(2)}, u32[]{:S(2)}) collective-permute-start(bf16[192,1024]{1,0:T(8,128)(2,1)} %get-tuple-element.69), channel_id=1, source_target_pairs={{0,112},{1,113},{2,114},{3,115},{4,116},{5,117},{6,118},{7,119},{8... | collective-permute-start | bytes 1179656 | tf_op jit(solution)/shard_map/ppermute | solution.py:53
  93.1 6.0 %all-to-all-start.2 = ((bf16[16,32,128]{2,1,0:T(8,128)(2,1)}), bf16[16,32,128]{2,1,0:T(8,128)(2,1)S(1)}, u32[]{:S(2)}, u32[]{:S(2)}) async-start(bf16[16,32,128]{2,1,0:T(8,128)(2,1)} %merge_queries.1.rest_0_), calls=%async_computation.2 | async-start | bytes 262144 | tf_op jit(solution)/shard_map/all_to_all | solution.py:396
  102.3 2.0 %ring_sum_2.1 = (bf16[192,1024]{1,0:T(8,128)(2,1)}, bf16[192,1024]{1,0:T(8,128)(2,1)}) custom-call(bf16[192,1024]{1,0:T(8,128)(2,1)S(1)} %get-tuple-element.62.up_part_ref, bf16[192,1024]{1,0:T(8,128)(2,1)S(1)} %copy-done.10, bf16[192,1024]{1,0:T(8,128)(2,1)S(1)} %copy-done.8, bf16[192,1024]{1,0:T(8,128)(2,1)} %collective-permute-done.27.down_ref, ...), custom_call_target="tpu_custom_call" | custom-call | flops 400000 | bytes 2000000 | tf_op jit(solution)/shard_map/ring_sum_2/pallas_call | solution.py:383
  105.4 2.2 %collective-permute-start.30 = (bf16[192,1024]{1,0:T(8,128)(2,1)}, bf16[192,1024]{1,0:T(8,128)(2,1)}, u32[]{:S(2)}, u32[]{:S(2)}) collective-permute-start(bf16[192,1024]{1,0:T(8,128)(2,1)} %get-tuple-element.71.rest_1_), channel_id=1, source_target_pairs={{0,112},{1,113},{2,114},{3,115},{4,116},{5,117},{6,118},{7,119},{8... | collective-permute-start | bytes 1179656 | tf_op jit(solution)/shard_map/ppermute | solution.py:53
  107.5 1.8 %states_after.1.rest_0_ = bf16[16,32,128]{2,1,0:T(8,128)(2,1)} custom-call(bf16[16,48,128]{2,1,0:T(8,128)(2,1)S(1)} %all-to-all-done.decay_ref.terms_ref, bf16[16,32,128]{2,1,0:T(8,128)(2,1)S(1)} %all-to-all-done.2.terms_ref, bf16[192,1024]{1,0:T(8,128)(2,1)} %get-tuple-element.70.rest_0_, bf16[192,1024]{1,0:T(8,128)(2,1)} %get-tuple-element.71.rest_1_), custom_call_target="tpu_custom_call" | custom-call | flops 1000000 | bytes 1000000 | tf_op jit(solution)/shard_map/states_after/pallas_call | solution.py:383
  109.3 7.7 %all-to-all-start.3 = ((bf16[16,32,128]{2,1,0:T(8,128)(2,1)}), bf16[16,32,128]{2,1,0:T(8,128)(2,1)S(1)}, u32[]{:S(2)}, u32[]{:S(2)}) async-start(bf16[16,32,128]{2,1,0:T(8,128)(2,1)} %states_after.1.rest_0_), calls=%async_computation.3 | async-start | bytes 262144 | tf_op jit(solution)/shard_map/all_to_all | solution.py:396
  119.9 3.6 %inner_grads.1 = (bf16[128,1024]{1,0:T(8,128)(2,1)}, f32[128,1024]{1,0:T(8,128)S(1)}, f32[128,1024]{1,0:T(8,128)S(1)}) custom-call(f32[8,128]{1,0:T(8,128)S(1)} %bitcast.8, bf16[128,1024]{1,0:T(8,128)(2,1)S(1)} %copy-done.4, bf16[128,1024]{1,0:T(8,128)(2,1)S(1)} %copy-done.1, bf16[128,1024]{1,0:T(8,128)(2,1)S(1)} %copy-done.3, ...), custom_call_target="tpu_custom_call" | custom-call | flops 24999999488 | bytes 3000000 | tf_op jit(solution)/shard_map/inner_grads/pallas_call | solution.py:383
  123.6 2.0 %ring_sum_1.1 = (bf16[192,1024]{1,0:T(8,128)(2,1)}, bf16[192,1024]{1,0:T(8,128)(2,1)}) custom-call(bf16[192,1024]{1,0:T(8,128)(2,1)S(1)} %get-tuple-element.80.up_part_ref, bf16[192,1024]{1,0:T(8,128)(2,1)S(1)} %collective-permute-done.29.up_ref, bf16[192,1024]{1,0:T(8,128)(2,1)S(1)} %get-tuple-element.81.down_part_ref, ...), custom_call_target="tpu_custom_call" | custom-call | flops 400000 | bytes 2000000 | tf_op jit(solution)/shard_map/ring_sum_1/pallas_call | solution.py:383
  127.1 1.8 %collective-permute-start.32 = (bf16[192,1024]{1,0:T(8,128)(2,1)}, bf16[192,1024]{1,0:T(8,128)(2,1)S(1)}, u32[]{:S(2)}, u32[]{:S(2)}) collective-permute-start(bf16[192,1024]{1,0:T(8,128)(2,1)} %get-tuple-element.83), channel_id=1, source_target_pairs={{0,112},{1,113},{2,114},{3,115},{4,116},{5,117},{6,118},{7,119},{8... | collective-permute-start | bytes 1179656 | tf_op jit(solution)/shard_map/ppermute | solution.py:53
  131.7 4.8 %collective-permute-done.31.up_ref = bf16[192,1024]{1,0:T(8,128)(2,1)S(1)} collective-permute-done((bf16[192,1024]{1,0:T(8,128)(2,1)}, bf16[192,1024]{1,0:T(8,128)(2,1)S(1)}, u32[]{:S(2)}, u32[]{:S(2)}) %collective-permute-start.31) | collective-permute-done | bytes 393248 | tf_op jit(solution)/shard_map/ppermute | solution.py:53
  (119 shorter events, 33.2 us)
Async XLA Ops:
  0.6 20.4 %collective-permute-start = (bf16[192,1024]{1,0:T(8,128)(2,1)}, bf16[192,1024]{1,0:T(8,128)(2,1)S(1)}, u32[]{:S(2)}, u32[]{:S(2)}) collective-permute-start(bf16[192,1024]{1,0:T(8,128)(2,1)} %refs_0_.1), channel_id=1, source_target_pairs={{0,16},{1,17},{2,18},{3,19},{4,20},{5,21},{6,22},{7,23},{8,24},{9,... | collective-permute-start | bytes 1179656 | tf_op jit(solution)/shard_map/ppermute | solution.py:53
  2.6 18.4 %collective-permute-start.1 = (bf16[192,1024]{1,0:T(8,128)(2,1)}, bf16[192,1024]{1,0:T(8,128)(2,1)}, u32[]{:S(2)}, u32[]{:S(2)}) collective-permute-start(bf16[192,1024]{1,0:T(8,128)(2,1)} %refs_0_.1), channel_id=1, source_target_pairs={{0,112},{1,113},{2,114},{3,115},{4,116},{5,117},{6,118},{7,119},{8... | collective-permute-start | bytes 1179656 | tf_op jit(solution)/shard_map/ppermute | solution.py:53
  13.8 16.2 %all-to-all-start = ((bf16[16,48,128]{2,1,0:T(8,128)(2,1)}), bf16[16,48,128]{2,1,0:T(8,128)(2,1)S(1)}, u32[]{:S(2)}, u32[]{:S(2)}) async-start(bf16[16,48,128]{2,1,0:T(8,128)(2,1)} %merge_keys.1.rest_2_), calls=%async_computation | async-start | bytes 393216 | tf_op jit(solution)/shard_map/all_to_all | solution.py:396
  22.4 8.6 %collective-permute-start.3 = (bf16[384,128]{1,0:T(8,128)(2,1)S(1)}, bf16[384,128]{1,0:T(8,128)(2,1)S(1)}, u32[]{:S(2)}, u32[]{:S(2)}) collective-permute-start(bf16[384,128]{1,0:T(8,128)(2,1)S(1)} %get-tuple-element.46), channel_id=1, source_target_pairs={{0,0},{1,1},{2,2},{3,3},{4,128},{5,129},{6,130},{7,131},{8,8},{9,9... | collective-permute-start | bytes 294920 | tf_op jit(solution)/shard_map/ppermute | solution.py:53
  25.2 10.1 %collective-permute-start.4 = (bf16[384,128]{1,0:T(8,128)(2,1)S(1)}, bf16[384,128]{1,0:T(8,128)(2,1)S(1)}, u32[]{:S(2)}, u32[]{:S(2)}) collective-permute-start(bf16[384,128]{1,0:T(8,128)(2,1)S(1)} %get-tuple-element.46), channel_id=1, source_target_pairs={{0,4},{1,5},{2,6},{3,7},{4,132},{5,133},{6,134},{7,135},{8,12},{9,... | collective-permute-start | bytes 294920 | tf_op jit(solution)/shard_map/ppermute | solution.py:53
  25.3 10.0 %collective-permute-start.5 = (bf16[384,128]{1,0:T(8,128)(2,1)S(1)}, bf16[384,128]{1,0:T(8,128)(2,1)S(1)}, u32[]{:S(2)}, u32[]{:S(2)}) collective-permute-start(bf16[384,128]{1,0:T(8,128)(2,1)S(1)} %get-tuple-element.47), channel_id=1, source_target_pairs={{0,8},{1,9},{2,10},{3,11},{4,136},{5,137},{6,138},{7,139},{8,0},{9... | collective-permute-start | bytes 294920 | tf_op jit(solution)/shard_map/ppermute | solution.py:53
  25.4 9.9 %collective-permute-start.6 = (bf16[384,128]{1,0:T(8,128)(2,1)S(1)}, bf16[384,128]{1,0:T(8,128)(2,1)S(1)}, u32[]{:S(2)}, u32[]{:S(2)}) collective-permute-start(bf16[384,128]{1,0:T(8,128)(2,1)S(1)} %get-tuple-element.47), channel_id=1, source_target_pairs={{0,12},{1,13},{2,14},{3,15},{4,140},{5,141},{6,142},{7,143},{8,4},... | collective-permute-start | bytes 294920 | tf_op jit(solution)/shard_map/ppermute | solution.py:53
  28.6 19.0 %collective-permute-start.12 = (bf16[192,1024]{1,0:T(8,128)(2,1)S(1)}, bf16[192,1024]{1,0:T(8,128)(2,1)S(1)}, u32[]{:S(2)}, u32[]{:S(2)}) collective-permute-start(bf16[192,1024]{1,0:T(8,128)(2,1)S(1)} %collective-permute-done.rest_0_.refs_8_), channel_id=1, source_target_pairs={{0,16},{1,17},{2,18},{3,19},{4,20},{5,21},{6,22},{7,23},{8,24},{9,... | collective-permute-start | bytes 1179656 | tf_op jit(solution)/shard_map/ppermute | solution.py:53
  31.0 18.1 %collective-permute-start.10 = (bf16[192,1024]{1,0:T(8,128)(2,1)}, bf16[192,1024]{1,0:T(8,128)(2,1)S(1)}, u32[]{:S(2)}, u32[]{:S(2)}) collective-permute-start(bf16[192,1024]{1,0:T(8,128)(2,1)} %collective-permute-done.1.rest_1_.refs_1_), channel_id=1, source_target_pairs={{0,112},{1,113},{2,114},{3,115},{4,116},{5,117},{6,118},{7,119},{8... | collective-permute-start | bytes 1179656 | tf_op jit(solution)/shard_map/ppermute | solution.py:53
  36.4 14.5 %collective-permute-start.7 = (bf16[384,512]{1,0:T(8,128)(2,1)S(1)}, bf16[384,512]{1,0:T(8,128)(2,1)S(1)}, u32[]{:S(2)}, u32[]{:S(2)}) collective-permute-start(bf16[384,512]{1,0:T(8,128)(2,1)S(1)} %collect.1.own_ref), channel_id=1, source_target_pairs={{0,1},{1,2},{2,3},{3,0},{4,5},{5,6},{6,7},{7,4},{8,9},{9,10},{10,1... | collective-permute-start | bytes 1179656 | tf_op jit(solution)/shard_map/ppermute | solution.py:53
  37.9 15.9 %all-to-all-start.1 = ((bf16[16,32,128]{2,1,0:T(8,128)(2,1)}), bf16[16,32,128]{2,1,0:T(8,128)(2,1)S(1)}, u32[]{:S(2)}, u32[]{:S(2)}) async-start(bf16[16,32,128]{2,1,0:T(8,128)(2,1)} %states_before.1.rest_0_), calls=%async_computation.1 | async-start | bytes 262144 | tf_op jit(solution)/shard_map/all_to_all | solution.py:396
  45.9 22.8 %collective-permute-start.8 = (bf16[384,512]{1,0:T(8,128)(2,1)S(1)}, bf16[384,512]{1,0:T(8,128)(2,1)S(1)}, u32[]{:S(2)}, u32[]{:S(2)}) collective-permute-start(bf16[384,512]{1,0:T(8,128)(2,1)S(1)} %collect.1.own_ref), channel_id=1, source_target_pairs={{0,3},{1,0},{2,1},{3,2},{4,7},{5,4},{6,5},{7,6},{8,11},{9,8},{10,9... | collective-permute-start | bytes 1179656 | tf_op jit(solution)/shard_map/ppermute | solution.py:53
  47.6 13.1 %collective-permute-start.13 = (bf16[192,1024]{1,0:T(8,128)(2,1)S(1)}, bf16[192,1024]{1,0:T(8,128)(2,1)}, u32[]{:S(2)}, u32[]{:S(2)}) collective-permute-start(bf16[192,1024]{1,0:T(8,128)(2,1)S(1)} %collective-permute-done.12.refs_7_.rest_0_), channel_id=1, source_target_pairs={{0,16},{1,17},{2,18},{3,19},{4,20},{5,21},{6,22},{7,23},{8,24},{9,... | collective-permute-start | bytes 1179656 | tf_op jit(solution)/shard_map/ppermute | solution.py:53
  49.1 12.9 %collective-permute-start.11 = (bf16[192,1024]{1,0:T(8,128)(2,1)S(1)}, bf16[192,1024]{1,0:T(8,128)(2,1)}, u32[]{:S(2)}, u32[]{:S(2)}) collective-permute-start(bf16[192,1024]{1,0:T(8,128)(2,1)S(1)} %collective-permute-done.10.refs_2_.rest_1_), channel_id=1, source_target_pairs={{0,112},{1,113},{2,114},{3,115},{4,116},{5,117},{6,118},{7,119},{8... | collective-permute-start | bytes 1179656 | tf_op jit(solution)/shard_map/ppermute | solution.py:53
  50.9 17.8 %collective-permute-start.9 = (bf16[384,512]{1,0:T(8,128)(2,1)S(1)}, bf16[384,512]{1,0:T(8,128)(2,1)}, u32[]{:S(2)}, u32[]{:S(2)}) collective-permute-start(bf16[384,512]{1,0:T(8,128)(2,1)S(1)} %collective-permute-done.7.left_ref), channel_id=1, source_target_pairs={{0,1},{1,2},{2,3},{3,0},{4,5},{5,6},{6,7},{7,4},{8,9},{9,10},{10,1... | collective-permute-start | bytes 1179656 | tf_op jit(solution)/shard_map/ppermute | solution.py:53
  54.0 12.2 %collective-permute-start.19 = (bf16[512,128]{1,0:T(8,128)(2,1)S(1)}, bf16[512,128]{1,0:T(8,128)(2,1)S(1)}, u32[]{:S(2)}, u32[]{:S(2)}) collective-permute-start(bf16[512,128]{1,0:T(8,128)(2,1)S(1)} %get-tuple-element.55), channel_id=1, source_target_pairs={{0,8},{1,9},{2,10},{3,11},{4,12},{5,13},{6,14},{7,15},{8,0},{9,1},... | collective-permute-start | bytes 393224 | tf_op jit(solution)/shard_map/ppermute | solution.py:53
  61.7 8.6 %collective-permute-start.14 = (bf16[96,1024]{1,0:T(8,128)(2,1)S(1)}, bf16[96,1024]{1,0:T(8,128)(2,1)S(1)}, u32[]{:S(2)}, u32[]{:S(2)}) collective-permute-start(bf16[96,1024]{1,0:T(8,128)(2,1)S(1)} %slice.8), channel_id=1, source_target_pairs={{0,16},{1,17},{2,18},{3,19},{4,20},{5,21},{6,22},{7,23},{8,24},{9,... | collective-permute-start | bytes 589832 | tf_op jit(solution)/shard_map/ppermute | solution.py:53
  62.9 7.4 %collective-permute-start.15 = (bf16[96,1024]{1,0:T(8,128)(2,1)S(1)}, bf16[96,1024]{1,0:T(8,128)(2,1)S(1)}, u32[]{:S(2)}, u32[]{:S(2)}) collective-permute-start(bf16[96,1024]{1,0:T(8,128)(2,1)S(1)} %slice.9), channel_id=1, source_target_pairs={{0,112},{1,113},{2,114},{3,115},{4,116},{5,117},{6,118},{7,119},{8... | collective-permute-start | bytes 589832 | tf_op jit(solution)/shard_map/ppermute | solution.py:53
  68.1 7.0 %collective-permute-start.21 = (bf16[128,1024]{1,0:T(8,128)(2,1)S(1)}, bf16[128,1024]{1,0:T(8,128)(2,1)S(1)}, u32[]{:S(2)}, u32[]{:S(2)}) collective-permute-start(bf16[128,1024]{1,0:T(8,128)(2,1)S(1)} %get-tuple-element.61.own_ref), channel_id=1, source_target_pairs={{0,128},{1,129},{2,130},{3,131},{4,132},{5,133},{6,134},{7,135},{8... | collective-permute-start | bytes 786440 | tf_op jit(solution)/shard_map/ppermute | solution.py:53
  73.5 3.2 %collective-permute-start.22 = (bf16[128,1024]{1,0:T(8,128)(2,1)S(1)}, bf16[128,1024]{1,0:T(8,128)(2,1)S(1)}, u32[]{:S(2)}, u32[]{:S(2)}) collective-permute-start(bf16[128,1024]{1,0:T(8,128)(2,1)S(1)} %get-tuple-element.61.own_ref), channel_id=1, source_target_pairs={{0,8},{1,9},{2,10},{3,11},{4,12},{5,13},{6,14},{7,15},{8,0},{9,1},... | collective-permute-start | bytes 786440 | tf_op jit(solution)/shard_map/ppermute | solution.py:53
  75.1 6.8 %collective-permute-start.16 = (bf16[128,1024]{1,0:T(8,128)(2,1)S(1)}, bf16[128,1024]{1,0:T(8,128)(2,1)S(1)}, u32[]{:S(2)}, u32[]{:S(2)}) collective-permute-start(bf16[128,1024]{1,0:T(8,128)(2,1)S(1)} %get-tuple-element.50), channel_id=1, source_target_pairs={{0,8},{1,9},{2,10},{3,11},{4,12},{5,13},{6,14},{7,15},{8,0},{9,1},... | collective-permute-start | bytes 786440 | tf_op jit(solution)/shard_map/ppermute | solution.py:53
  75.7 8.3 %collective-permute-start.18 = (bf16[128,1024]{1,0:T(8,128)(2,1)S(1)}, bf16[128,1024]{1,0:T(8,128)(2,1)S(1)}, u32[]{:S(2)}, u32[]{:S(2)}) collective-permute-start(bf16[128,1024]{1,0:T(8,128)(2,1)S(1)} %sum_theirs.1.rest_0_), channel_id=1, source_target_pairs={{0,128},{1,129},{2,130},{3,131},{4,132},{5,133},{6,134},{7,135},{8... | collective-permute-start | bytes 786440 | tf_op jit(solution)/shard_map/ppermute | solution.py:53
  78.6 8.2 %collective-permute-start.24 = (bf16[96,1024]{1,0:T(8,128)(2,1)S(1)}, bf16[96,1024]{1,0:T(8,128)(2,1)S(1)}, u32[]{:S(2)}, u32[]{:S(2)}) collective-permute-start(bf16[96,1024]{1,0:T(8,128)(2,1)S(1)} %get-tuple-element.64), channel_id=1, source_target_pairs={{0,16},{1,17},{2,18},{3,19},{4,20},{5,21},{6,22},{7,23},{8,24},{9,... | collective-permute-start | bytes 589832 | tf_op jit(solution)/shard_map/ppermute | solution.py:53
  78.7 8.1 %collective-permute-start.25 = (bf16[96,1024]{1,0:T(8,128)(2,1)S(1)}, bf16[96,1024]{1,0:T(8,128)(2,1)S(1)}, u32[]{:S(2)}, u32[]{:S(2)}) collective-permute-start(bf16[96,1024]{1,0:T(8,128)(2,1)S(1)} %get-tuple-element.66), channel_id=1, source_target_pairs={{0,112},{1,113},{2,114},{3,115},{4,116},{5,117},{6,118},{7,119},{8... | collective-permute-start | bytes 589832 | tf_op jit(solution)/shard_map/ppermute | solution.py:53
  87.8 11.7 %collective-permute-start.26 = (bf16[192,1024]{1,0:T(8,128)(2,1)}, bf16[192,1024]{1,0:T(8,128)(2,1)S(1)}, u32[]{:S(2)}, u32[]{:S(2)}) collective-permute-start(bf16[192,1024]{1,0:T(8,128)(2,1)} %get-tuple-element.67), channel_id=1, source_target_pairs={{0,16},{1,17},{2,18},{3,19},{4,20},{5,21},{6,22},{7,23},{8,24},{9,... | collective-permute-start | bytes 1179656 | tf_op jit(solution)/shard_map/ppermute | solution.py:53
  88.5 11.8 %collective-permute-start.27 = (bf16[192,1024]{1,0:T(8,128)(2,1)}, bf16[192,1024]{1,0:T(8,128)(2,1)}, u32[]{:S(2)}, u32[]{:S(2)}) collective-permute-start(bf16[192,1024]{1,0:T(8,128)(2,1)} %get-tuple-element.69), channel_id=1, source_target_pairs={{0,112},{1,113},{2,114},{3,115},{4,116},{5,117},{6,118},{7,119},{8... | collective-permute-start | bytes 1179656 | tf_op jit(solution)/shard_map/ppermute | solution.py:53
  93.1 14.4 %all-to-all-start.2 = ((bf16[16,32,128]{2,1,0:T(8,128)(2,1)}), bf16[16,32,128]{2,1,0:T(8,128)(2,1)S(1)}, u32[]{:S(2)}, u32[]{:S(2)}) async-start(bf16[16,32,128]{2,1,0:T(8,128)(2,1)} %merge_queries.1.rest_0_), calls=%async_computation.2 | async-start | bytes 262144 | tf_op jit(solution)/shard_map/all_to_all | solution.py:396
  104.3 19.3 %collective-permute-start.29 = (bf16[192,1024]{1,0:T(8,128)(2,1)}, bf16[192,1024]{1,0:T(8,128)(2,1)S(1)}, u32[]{:S(2)}, u32[]{:S(2)}) collective-permute-start(bf16[192,1024]{1,0:T(8,128)(2,1)} %get-tuple-element.70.rest_0_), channel_id=1, source_target_pairs={{0,16},{1,17},{2,18},{3,19},{4,20},{5,21},{6,22},{7,23},{8,24},{9,... | collective-permute-start | bytes 1179656 | tf_op jit(solution)/shard_map/ppermute | solution.py:53
  105.4 18.2 %collective-permute-start.30 = (bf16[192,1024]{1,0:T(8,128)(2,1)}, bf16[192,1024]{1,0:T(8,128)(2,1)}, u32[]{:S(2)}, u32[]{:S(2)}) collective-permute-start(bf16[192,1024]{1,0:T(8,128)(2,1)} %get-tuple-element.71.rest_1_), channel_id=1, source_target_pairs={{0,112},{1,113},{2,114},{3,115},{4,116},{5,117},{6,118},{7,119},{8... | collective-permute-start | bytes 1179656 | tf_op jit(solution)/shard_map/ppermute | solution.py:53
  109.3 19.5 %all-to-all-start.3 = ((bf16[16,32,128]{2,1,0:T(8,128)(2,1)}), bf16[16,32,128]{2,1,0:T(8,128)(2,1)S(1)}, u32[]{:S(2)}, u32[]{:S(2)}) async-start(bf16[16,32,128]{2,1,0:T(8,128)(2,1)} %states_after.1.rest_0_), calls=%async_computation.3 | async-start | bytes 262144 | tf_op jit(solution)/shard_map/all_to_all | solution.py:396
  125.6 10.9 %collective-permute-start.31 = (bf16[192,1024]{1,0:T(8,128)(2,1)}, bf16[192,1024]{1,0:T(8,128)(2,1)S(1)}, u32[]{:S(2)}, u32[]{:S(2)}) collective-permute-start(bf16[192,1024]{1,0:T(8,128)(2,1)} %get-tuple-element.82), channel_id=1, source_target_pairs={{0,16},{1,17},{2,18},{3,19},{4,20},{5,21},{6,22},{7,23},{8,24},{9,... | collective-permute-start | bytes 1179656 | tf_op jit(solution)/shard_map/ppermute | solution.py:53
  127.1 9.4 %collective-permute-start.32 = (bf16[192,1024]{1,0:T(8,128)(2,1)}, bf16[192,1024]{1,0:T(8,128)(2,1)S(1)}, u32[]{:S(2)}, u32[]{:S(2)}) collective-permute-start(bf16[192,1024]{1,0:T(8,128)(2,1)} %get-tuple-element.83), channel_id=1, source_target_pairs={{0,112},{1,113},{2,114},{3,115},{4,116},{5,117},{6,118},{7,119},{8... | collective-permute-start | bytes 1179656 | tf_op jit(solution)/shard_map/ppermute | solution.py:53
  (32 other events, 161.1 us)

commit v8 on v7

--- a/solution.py
+++ b/solution.py
@@ -442,20 +442,23 @@
         functools.partial(recurrence_kernel, False), slices, "states_before", 1_000_000, 1_000_000,
         (gathered, gathered),
     )
-    own = call(collect_kernel, shape((2 * share, 4 * tokens)), "collect", 0, 800_000, pieces, (befores,))
+    own = call(
+        collect_kernel, shape((2 * share, 4 * tokens)), "collect", 0, 800_000, pieces,
+        (befores, below[1], above[1]),
+    )
     left, right = send(own, X_UP), send(own, X_DOWN)
+    below.append(send(below[1], Z_UP))
+    above.append(send(above[1], Z_DOWN))
     before = exchange(befores).reshape(HALF_ROWS, HEAD_DIM)
     before_own, before_cross = call(
         functools.partial(spread_kernel, 0), (half_state, half_state), "spread_before",
-        20_000_000_000, 500_000, (key_mine, key_other, key_mine, key_other, before),
+        20_000_000_000, 500_000, (key_mine, key_other, key_mine, key_other, before), (below[2], above[2]),
     )
     before_other = send(before_cross, CORE)
     attended, scores, states = call(
         attended_kernel, (row, row, shape((cols, HEAD_DIM))), "attended", 110_000_000, 2_000_000,
-        (log_decay, queries, key_proj, value_proj, before_own, before_other), (below[1], above[1]),
-    )
-    below.append(send(below[-1], Z_UP))
-    above.append(send(above[-1], Z_DOWN))
+        (log_decay, queries, key_proj, value_proj, before_own, before_other),
+    )
     across = send(attended, CORE)
     neighbour = send(attended, Y_LO)
     opposite = send(left, X_UP)

time: 139 us -> 143 us (1.029)
  the two profiles are of different devices: /device:TPU:8 before, /device:TPU:120 now
where the time goes in v8:
time: 143 us; the launch traced here: 142 us
  starting transfers between devices  70.6 us (49%)
  Pallas kernels  29.7 us (21%)
  waiting for transfers between devices  29.2 us (20%)
  local copies, waits for them, and re-layouts  11.5 us (8%)
    all_to_all x4, starting transfers between devices, exchange(): lax.all_to_all(array, 'seq', 0, 0, tiled=True, axis_index_groups=CHIP_GRO...  37.6 us
    ppermute x33, starting transfers between devices, send(): return lax.ppermute(array, AXES, table)  33 us
    ppermute x33, waiting for transfers between devices, send(): return lax.ppermute(array, AXES, table)  25.4 us
    pallas_call x18, Pallas kernels, call(): pl.pallas_call(body, in_specs=[pl.BlockSpec(a.shape, lambda n=a.ndim: (0,...  22.5 us
    unnamed x62, local copies, waits for them, and re-layouts  9.66 us
    all_to_all x4, waiting for transfers between devices, exchange(): lax.all_to_all(array, 'seq', 0, 0, tiled=True, axis_index_groups=CHIP_GRO...  3.8 us
    pallas_call x1, Pallas kernels, body(): pl.pallas_call(project_kernel, out_shape=[row32, row32, row, row], scratc...  2.9 us
  transfers between devices with their start and end apart: 37, of which 15 were waited for; matrix products, arithmetic and copies ran while one was open for 1% of the time, Pallas kernels for 19%

profile of v8, /device:TPU:120, one launch (start us, length us, event | category | flops | bytes accessed | tf_op | source)
XLA Modules:
  0.0 142.1 jit_solution(11914614609125903947)
XLA Ops:
  0.6 3.2 %collective-permute-start = (bf16[192,1024]{1,0:T(8,128)(2,1)}, bf16[192,1024]{1,0:T(8,128)(2,1)S(1)}, u32[]{:S(2)}, u32[]{:S(2)}) collective-permute-start(bf16[192,1024]{1,0:T(8,128)(2,1)} %refs_0_.1), channel_id=1, source_target_pairs={{0,16},{1,17},{2,18},{3,19},{4,20},{5,21},{6,22},{7,23},{8,24},{9,... | collective-permute-start | bytes 1179656 | tf_op jit(solution)/shard_map/ppermute | solution.py:53
  6.4 2.4 %key_terms.1 = (bf16[528,128]{1,0:T(8,128)(2,1)S(1)}, bf16[528,128]{1,0:T(8,128)(2,1)S(1)}) custom-call(f32[8,128]{1,0:T(8,128)S(1)} %bitcast.5, bf16[128,1024]{1,0:T(8,128)(2,1)S(1)} %copy-done, bf16[128,1024]{1,0:T(8,128)(2,1)S(1)} %copy-done.2), custom_call_target="tpu_custom_call" | custom-call | flops 40000000 | bytes 1000000 | tf_op jit(solution)/shard_map/key_terms/pallas_call | solution.py:414
  11.0 8.7 %all-to-all-start = ((bf16[16,48,128]{2,1,0:T(8,128)(2,1)}), bf16[16,48,128]{2,1,0:T(8,128)(2,1)S(1)}, u32[]{:S(2)}, u32[]{:S(2)}) async-start(bf16[16,48,128]{2,1,0:T(8,128)(2,1)} %merge_keys.1.rest_2_), calls=%async_computation | async-start | bytes 393216 | tf_op jit(solution)/shard_map/all_to_all | solution.py:396
  19.7 2.8 %collective-permute-start.7 = (bf16[192,1024]{1,0:T(8,128)(2,1)S(1)}, bf16[192,1024]{1,0:T(8,128)(2,1)S(1)}, u32[]{:S(2)}, u32[]{:S(2)}) collective-permute-start(bf16[192,1024]{1,0:T(8,128)(2,1)S(1)} %collective-permute-done.rest_0_.refs_8_), channel_id=1, source_target_pairs={{0,16},{1,17},{2,18},{3,19},{4,20},{5,21},{6,22},{7,23},{8,24},{9,... | collective-permute-start | bytes 1179656 | tf_op jit(solution)/shard_map/ppermute | solution.py:53
  24.4 3.9 %collective-permute-start.4 = (bf16[384,128]{1,0:T(8,128)(2,1)S(1)}, bf16[384,128]{1,0:T(8,128)(2,1)S(1)}, u32[]{:S(2)}, u32[]{:S(2)}) collective-permute-start(bf16[384,128]{1,0:T(8,128)(2,1)S(1)} %get-tuple-element.46), channel_id=1, source_target_pairs={{0,4},{1,5},{2,6},{3,7},{4,132},{5,133},{6,134},{7,135},{8,12},{9,... | collective-permute-start | bytes 294920 | tf_op jit(solution)/shard_map/ppermute | solution.py:53
  30.5 1.8 %collective-permute-done.6.d_ref = bf16[384,128]{1,0:T(8,128)(2,1)S(1)} collective-permute-done((bf16[384,128]{1,0:T(8,128)(2,1)S(1)}, bf16[384,128]{1,0:T(8,128)(2,1)S(1)}, u32[]{:S(2)}, u32[]{:S(2)}) %collective-permute-start.6) | collective-permute-done | bytes 98336 | tf_op jit(solution)/shard_map/ppermute | solution.py:53
  33.5 2.1 %collective-permute-done.8.rest_2_.refs_2_ = bf16[192,1024]{1,0:T(8,128)(2,1)S(1)} collective-permute-done((bf16[192,1024]{1,0:T(8,128)(2,1)S(1)}, bf16[192,1024]{1,0:T(8,128)(2,1)S(1)}, u32[]{:S(2)}, u32[]{:S(2)}) %collective-permute-start.8) | collective-permute-done | bytes 393248 | tf_op jit(solution)/shard_map/ppermute | solution.py:53
  36.7 1.6 %collective-permute-start.9 = (bf16[384,512]{1,0:T(8,128)(2,1)S(1)}, bf16[384,512]{1,0:T(8,128)(2,1)S(1)}, u32[]{:S(2)}, u32[]{:S(2)}) collective-permute-start(bf16[384,512]{1,0:T(8,128)(2,1)S(1)} %collect.1.own_ref), channel_id=1, source_target_pairs={{0,1},{1,2},{2,3},{3,0},{4,5},{5,6},{6,7},{7,4},{8,9},{9,10},{10,1... | collective-permute-start | bytes 1179656 | tf_op jit(solution)/shard_map/ppermute | solution.py:53
  38.9 1.5 %collective-permute-start.12 = (bf16[192,1024]{1,0:T(8,128)(2,1)S(1)}, bf16[192,1024]{1,0:T(8,128)(2,1)}, u32[]{:S(2)}, u32[]{:S(2)}) collective-permute-start(bf16[192,1024]{1,0:T(8,128)(2,1)S(1)} %collective-permute-done.8.rest_2_.refs_2_), channel_id=1, source_target_pairs={{0,112},{1,113},{2,114},{3,115},{4,116},{5,117},{6,118},{7,119},{8... | collective-permute-start | bytes 1179656 | tf_op jit(solution)/shard_map/ppermute | solution.py:53
  40.3 13.1 %all-to-all-start.1 = ((bf16[16,32,128]{2,1,0:T(8,128)(2,1)}), bf16[16,32,128]{2,1,0:T(8,128)(2,1)S(1)}, u32[]{:S(2)}, u32[]{:S(2)}) async-start(bf16[16,32,128]{2,1,0:T(8,128)(2,1)} %states_before.1.rest_0_), calls=%async_computation.1 | async-start | bytes 262144 | tf_op jit(solution)/shard_map/all_to_all | solution.py:396
  53.4 1.7 %collective-permute-start.10 = (bf16[384,512]{1,0:T(8,128)(2,1)S(1)}, bf16[384,512]{1,0:T(8,128)(2,1)S(1)}, u32[]{:S(2)}, u32[]{:S(2)}) collective-permute-start(bf16[384,512]{1,0:T(8,128)(2,1)S(1)} %collect.1.own_ref), channel_id=1, source_target_pairs={{0,3},{1,0},{2,1},{3,2},{4,7},{5,4},{6,5},{7,6},{8,11},{9,8},{10,9... | collective-permute-start | bytes 1179656 | tf_op jit(solution)/shard_map/ppermute | solution.py:53
  55.4 3.8 %all-to-all-done.1 = bf16[16,32,128]{2,1,0:T(8,128)(2,1)S(1)} async-done(((bf16[16,32,128]{2,1,0:T(8,128)(2,1)}), bf16[16,32,128]{2,1,0:T(8,128)(2,1)S(1)}, u32[]{:S(2)}, u32[]{:S(2)}) %all-to-all-start.1) | async-done | bytes 131104 | tf_op jit(solution)/shard_map/all_to_all | solution.py:396
  63.5 1.5 %collective-permute-start.15 = (bf16[96,1024]{1,0:T(8,128)(2,1)S(1)}, bf16[96,1024]{1,0:T(8,128)(2,1)S(1)}, u32[]{:S(2)}, u32[]{:S(2)}) collective-permute-start(bf16[96,1024]{1,0:T(8,128)(2,1)S(1)} %slice.9), channel_id=1, source_target_pairs={{0,112},{1,113},{2,114},{3,115},{4,116},{5,117},{6,118},{7,119},{8... | collective-permute-start | bytes 589832 | tf_op jit(solution)/shard_map/ppermute | solution.py:53
  69.3 2.5 %collective-permute-done.15.refs_5_ = bf16[96,1024]{1,0:T(8,128)(2,1)S(1)} collective-permute-done((bf16[96,1024]{1,0:T(8,128)(2,1)S(1)}, bf16[96,1024]{1,0:T(8,128)(2,1)S(1)}, u32[]{:S(2)}, u32[]{:S(2)}) %collective-permute-start.15) | collective-permute-done | bytes 196640 | tf_op jit(solution)/shard_map/ppermute | solution.py:53
  71.8 2.9 %project.1 = (f32[128,1024]{1,0:T(8,128)S(1)}, f32[128,1024]{1,0:T(8,128)S(1)}, bf16[128,1024]{1,0:T(8,128)(2,1)S(1)}, bf16[128,1024]{1,0:T(8,128)(2,1)S(1)}) custom-call(bf16[512,1536]{1,0:T(8,128)(2,1)S(1)} %get-tuple-element.48.block_ref, bf16[192,1024]{1,0:T(8,128)(2,1)S(1)} %copy-done.21, bf16[192,1024]{1,0:T(8,128)(2,1)S(1)} %copy-done.25, ...), custom_call_target="tpu_custom_call" | custom-call | flops 1600000000 | bytes 6000000 | tf_op jit(solution)/shard_map/project/pallas_call | solution.py:475
  77.7 1.9 %weight_partial.1 = (bf16[192,1024]{1,0:T(8,128)(2,1)S(1)}, bf16[192,1024]{1,0:T(8,128)(2,1)S(1)}, bf16[192,1024]{1,0:T(8,128)(2,1)S(1)}, bf16[192,1024]{1,0:T(8...) custom-call(bf16[1536,512]{1,0:T(8,128)(2,1)S(1)} %get-tuple-element, ...), custom_call_target="tpu_custom_call" | custom-call | flops 1600000000 | bytes 6000000 | tf_op jit(solution)/shard_map/weight_partial/pallas_call | solution.py:490
  79.6 1.8 %collective-permute-start.24 = (bf16[96,1024]{1,0:T(8,128)(2,1)S(1)}, bf16[96,1024]{1,0:T(8,128)(2,1)S(1)}, u32[]{:S(2)}, u32[]{:S(2)}) collective-permute-start(bf16[96,1024]{1,0:T(8,128)(2,1)S(1)} %get-tuple-element.64), channel_id=1, source_target_pairs={{0,16},{1,17},{2,18},{3,19},{4,20},{5,21},{6,22},{7,23},{8,24},{9,... | collective-permute-start | bytes 589832 | tf_op jit(solution)/shard_map/ppermute | solution.py:53
  81.7 3.1 %collective-permute-done.18.other_ref = bf16[128,1024]{1,0:T(8,128)(2,1)S(1)} collective-permute-done((bf16[128,1024]{1,0:T(8,128)(2,1)S(1)}, bf16[128,1024]{1,0:T(8,128)(2,1)S(1)}, u32[]{:S(2)}, u32[]{:S(2)}) %collective-permute-start.18) | collective-permute-done | bytes 262176 | tf_op jit(solution)/shard_map/ppermute | solution.py:53
  84.8 2.3 %query_terms.1 = (bf16[128,1024]{1,0:T(8,128)(2,1)S(1)}, bf16[512,128]{1,0:T(8,128)(2,1)S(1)}, bf16[512,128]{1,0:T(8,128)(2,1)S(1)}) custom-call(f32[8,128]{1,0:T(8,128)S(1)} %bitcast.7, bf16[128,1024]{1,0:T(8,128)(2,1)S(1)} %copy-done.4, f32[128,1024]{1,0:T(8,128)S(1)} %get-tuple-element.49.own_ref, bf16[128,1024]{1,0:T(8,128)(2,1)S(1)} %collective-permute-done.16.core_ref, ...), custom_call_target="tpu_custom_call" | custom-call | flops 40000000 | bytes 1000000 | tf_op jit(solution)/shard_map/query_terms/pallas_call | solution.py:383
  87.1 1.8 %collective-permute-done.25.down_ref = bf16[96,1024]{1,0:T(8,128)(2,1)S(1)} collective-permute-done((bf16[96,1024]{1,0:T(8,128)(2,1)S(1)}, bf16[96,1024]{1,0:T(8,128)(2,1)S(1)}, u32[]{:S(2)}, u32[]{:S(2)}) %collective-permute-start.25) | collective-permute-done | bytes 196640 | tf_op jit(solution)/shard_map/ppermute | solution.py:53
  90.2 1.7 %collective-permute-start.27 = (bf16[192,1024]{1,0:T(8,128)(2,1)}, bf16[192,1024]{1,0:T(8,128)(2,1)}, u32[]{:S(2)}, u32[]{:S(2)}) collective-permute-start(bf16[192,1024]{1,0:T(8,128)(2,1)} %get-tuple-element.69), channel_id=1, source_target_pairs={{0,112},{1,113},{2,114},{3,115},{4,116},{5,117},{6,118},{7,119},{8... | collective-permute-start | bytes 1179656 | tf_op jit(solution)/shard_map/ppermute | solution.py:53
  91.9 1.3 collective-permute-done.20.other_ref
  94.0 7.2 %all-to-all-start.2 = ((bf16[16,32,128]{2,1,0:T(8,128)(2,1)}), bf16[16,32,128]{2,1,0:T(8,128)(2,1)S(1)}, u32[]{:S(2)}, u32[]{:S(2)}) async-start(bf16[16,32,128]{2,1,0:T(8,128)(2,1)} %merge_queries.1.rest_0_), calls=%async_computation.2 | async-start | bytes 262144 | tf_op jit(solution)/shard_map/all_to_all | solution.py:396
  103.9 2.0 %ring_sum_2.1 = (bf16[192,1024]{1,0:T(8,128)(2,1)}, bf16[192,1024]{1,0:T(8,128)(2,1)}) custom-call(bf16[192,1024]{1,0:T(8,128)(2,1)S(1)} %get-tuple-element.62.up_part_ref, bf16[192,1024]{1,0:T(8,128)(2,1)S(1)} %copy-done.12, bf16[192,1024]{1,0:T(8,128)(2,1)S(1)} %copy-done.10, bf16[192,1024]{1,0:T(8,128)(2,1)} %collective-permute-done.27.down_ref, ...), custom_call_target="tpu_custom_call" | custom-call | flops 400000 | bytes 2000000 | tf_op jit(solution)/shard_map/ring_sum_2/pallas_call | solution.py:383
  105.9 2.7 %collective-permute-start.29 = (bf16[192,1024]{1,0:T(8,128)(2,1)}, bf16[192,1024]{1,0:T(8,128)(2,1)S(1)}, u32[]{:S(2)}, u32[]{:S(2)}) collective-permute-start(bf16[192,1024]{1,0:T(8,128)(2,1)} %get-tuple-element.70.rest_0_), channel_id=1, source_target_pairs={{0,16},{1,17},{2,18},{3,19},{4,20},{5,21},{6,22},{7,23},{8,24},{9,... | collective-permute-start | bytes 1179656 | tf_op jit(solution)/shard_map/ppermute | solution.py:53
  108.6 1.8 %states_after.1.rest_0_ = bf16[16,32,128]{2,1,0:T(8,128)(2,1)} custom-call(bf16[16,48,128]{2,1,0:T(8,128)(2,1)S(1)} %all-to-all-done.decay_ref.terms_ref, bf16[16,32,128]{2,1,0:T(8,128)(2,1)S(1)} %all-to-all-done.2.terms_ref, bf16[192,1024]{1,0:T(8,128)(2,1)} %get-tuple-element.70.rest_0_, bf16[192,1024]{1,0:T(8,128)(2,1)} %get-tuple-element.71.rest_1_), custom_call_target="tpu_custom_call" | custom-call | flops 1000000 | bytes 1000000 | tf_op jit(solution)/shard_map/states_after/pallas_call | solution.py:383
  110.4 8.7 %all-to-all-start.3 = ((bf16[16,32,128]{2,1,0:T(8,128)(2,1)}), bf16[16,32,128]{2,1,0:T(8,128)(2,1)S(1)}, u32[]{:S(2)}, u32[]{:S(2)}) async-start(bf16[16,32,128]{2,1,0:T(8,128)(2,1)} %states_after.1.rest_0_), calls=%async_computation.3 | async-start | bytes 262144 | tf_op jit(solution)/shard_map/all_to_all | solution.py:396
  121.9 3.6 %inner_grads.1 = (bf16[128,1024]{1,0:T(8,128)(2,1)}, f32[128,1024]{1,0:T(8,128)S(1)}, f32[128,1024]{1,0:T(8,128)S(1)}) custom-call(f32[8,128]{1,0:T(8,128)S(1)} %bitcast.8, bf16[128,1024]{1,0:T(8,128)(2,1)S(1)} %copy-done.4, bf16[128,1024]{1,0:T(8,128)(2,1)S(1)} %copy-done.1, bf16[128,1024]{1,0:T(8,128)(2,1)S(1)} %copy-done.3, ...), custom_call_target="tpu_custom_call" | custom-call | flops 24999999488 | bytes 3000000 | tf_op jit(solution)/shard_map/inner_grads/pallas_call | solution.py:383
  125.6 2.0 %ring_sum_1.1 = (bf16[192,1024]{1,0:T(8,128)(2,1)}, bf16[192,1024]{1,0:T(8,128)(2,1)}) custom-call(bf16[192,1024]{1,0:T(8,128)(2,1)S(1)} %get-tuple-element.80.up_part_ref, bf16[192,1024]{1,0:T(8,128)(2,1)S(1)} %collective-permute-done.29.up_ref, bf16[192,1024]{1,0:T(8,128)(2,1)S(1)} %get-tuple-element.81.down_part_ref, ...), custom_call_target="tpu_custom_call" | custom-call | flops 400000 | bytes 2000000 | tf_op jit(solution)/shard_map/ring_sum_1/pallas_call | solution.py:383
  127.6 2.7 %collective-permute-start.31 = (bf16[192,1024]{1,0:T(8,128)(2,1)}, bf16[192,1024]{1,0:T(8,128)(2,1)S(1)}, u32[]{:S(2)}, u32[]{:S(2)}) collective-permute-start(bf16[192,1024]{1,0:T(8,128)(2,1)} %get-tuple-element.82), channel_id=1, source_target_pairs={{0,16},{1,17},{2,18},{3,19},{4,20},{5,21},{6,22},{7,23},{8,24},{9,... | collective-permute-start | bytes 1179656 | tf_op jit(solution)/shard_map/ppermute | solution.py:53
  133.2 4.7 %collective-permute-done.31.up_ref = bf16[192,1024]{1,0:T(8,128)(2,1)S(1)} collective-permute-done((bf16[192,1024]{1,0:T(8,128)(2,1)}, bf16[192,1024]{1,0:T(8,128)(2,1)S(1)}, u32[]{:S(2)}, u32[]{:S(2)}) %collective-permute-start.31) | collective-permute-done | bytes 393248 | tf_op jit(solution)/shard_map/ppermute | solution.py:53
  137.9 3.3 %collective-permute-done.32.down_ref = bf16[192,1024]{1,0:T(8,128)(2,1)S(1)} collective-permute-done((bf16[192,1024]{1,0:T(8,128)(2,1)}, bf16[192,1024]{1,0:T(8,128)(2,1)S(1)}, u32[]{:S(2)}, u32[]{:S(2)}) %collective-permute-start.32) | collective-permute-done | bytes 393248 | tf_op jit(solution)/shard_map/ppermute | solution.py:53
  (127 shorter events, 34.9 us)
Async XLA Ops:
  0.6 19.1 %collective-permute-start = (bf16[192,1024]{1,0:T(8,128)(2,1)}, bf16[192,1024]{1,0:T(8,128)(2,1)S(1)}, u32[]{:S(2)}, u32[]{:S(2)}) collective-permute-start(bf16[192,1024]{1,0:T(8,128)(2,1)} %refs_0_.1), channel_id=1, source_target_pairs={{0,16},{1,17},{2,18},{3,19},{4,20},{5,21},{6,22},{7,23},{8,24},{9,... | collective-permute-start | bytes 1179656 | tf_op jit(solution)/shard_map/ppermute | solution.py:53
  3.8 18.6 %collective-permute-start.1 = (bf16[192,1024]{1,0:T(8,128)(2,1)}, bf16[192,1024]{1,0:T(8,128)(2,1)S(1)}, u32[]{:S(2)}, u32[]{:S(2)}) collective-permute-start(bf16[192,1024]{1,0:T(8,128)(2,1)} %refs_0_.1), channel_id=1, source_target_pairs={{0,112},{1,113},{2,114},{3,115},{4,116},{5,117},{6,118},{7,119},{8... | collective-permute-start | bytes 1179656 | tf_op jit(solution)/shard_map/ppermute | solution.py:53
  11.0 18.5 %all-to-all-start = ((bf16[16,48,128]{2,1,0:T(8,128)(2,1)}), bf16[16,48,128]{2,1,0:T(8,128)(2,1)S(1)}, u32[]{:S(2)}, u32[]{:S(2)}) async-start(bf16[16,48,128]{2,1,0:T(8,128)(2,1)} %merge_keys.1.rest_2_), calls=%async_computation | async-start | bytes 393216 | tf_op jit(solution)/shard_map/all_to_all | solution.py:396
  19.7 13.8 %collective-permute-start.7 = (bf16[192,1024]{1,0:T(8,128)(2,1)S(1)}, bf16[192,1024]{1,0:T(8,128)(2,1)S(1)}, u32[]{:S(2)}, u32[]{:S(2)}) collective-permute-start(bf16[192,1024]{1,0:T(8,128)(2,1)S(1)} %collective-permute-done.rest_0_.refs_8_), channel_id=1, source_target_pairs={{0,16},{1,17},{2,18},{3,19},{4,20},{5,21},{6,22},{7,23},{8,24},{9,... | collective-permute-start | bytes 1179656 | tf_op jit(solution)/shard_map/ppermute | solution.py:53
  22.5 13.2 %collective-permute-start.8 = (bf16[192,1024]{1,0:T(8,128)(2,1)S(1)}, bf16[192,1024]{1,0:T(8,128)(2,1)S(1)}, u32[]{:S(2)}, u32[]{:S(2)}) collective-permute-start(bf16[192,1024]{1,0:T(8,128)(2,1)S(1)} %collective-permute-done.1.rest_1_.refs_1_), channel_id=1, source_target_pairs={{0,112},{1,113},{2,114},{3,115},{4,116},{5,117},{6,118},{7,119},{8... | collective-permute-start | bytes 1179656 | tf_op jit(solution)/shard_map/ppermute | solution.py:53
  23.7 4.6 %collective-permute-start.3 = (bf16[384,128]{1,0:T(8,128)(2,1)S(1)}, bf16[384,128]{1,0:T(8,128)(2,1)S(1)}, u32[]{:S(2)}, u32[]{:S(2)}) collective-permute-start(bf16[384,128]{1,0:T(8,128)(2,1)S(1)} %get-tuple-element.46), channel_id=1, source_target_pairs={{0,0},{1,1},{2,2},{3,3},{4,128},{5,129},{6,130},{7,131},{8,8},{9,9... | collective-permute-start | bytes 294920 | tf_op jit(solution)/shard_map/ppermute | solution.py:53
  24.4 6.2 %collective-permute-start.4 = (bf16[384,128]{1,0:T(8,128)(2,1)S(1)}, bf16[384,128]{1,0:T(8,128)(2,1)S(1)}, u32[]{:S(2)}, u32[]{:S(2)}) collective-permute-start(bf16[384,128]{1,0:T(8,128)(2,1)S(1)} %get-tuple-element.46), channel_id=1, source_target_pairs={{0,4},{1,5},{2,6},{3,7},{4,132},{5,133},{6,134},{7,135},{8,12},{9,... | collective-permute-start | bytes 294920 | tf_op jit(solution)/shard_map/ppermute | solution.py:53
  28.3 2.2 %collective-permute-start.5 = (bf16[384,128]{1,0:T(8,128)(2,1)S(1)}, bf16[384,128]{1,0:T(8,128)(2,1)S(1)}, u32[]{:S(2)}, u32[]{:S(2)}) collective-permute-start(bf16[384,128]{1,0:T(8,128)(2,1)S(1)} %get-tuple-element.47), channel_id=1, source_target_pairs={{0,8},{1,9},{2,10},{3,11},{4,136},{5,137},{6,138},{7,139},{8,0},{9... | collective-permute-start | bytes 294920 | tf_op jit(solution)/shard_map/ppermute | solution.py:53
  28.3 4.0 %collective-permute-start.6 = (bf16[384,128]{1,0:T(8,128)(2,1)S(1)}, bf16[384,128]{1,0:T(8,128)(2,1)S(1)}, u32[]{:S(2)}, u32[]{:S(2)}) collective-permute-start(bf16[384,128]{1,0:T(8,128)(2,1)S(1)} %get-tuple-element.47), channel_id=1, source_target_pairs={{0,12},{1,13},{2,14},{3,15},{4,140},{5,141},{6,142},{7,143},{8,4},... | collective-permute-start | bytes 294920 | tf_op jit(solution)/shard_map/ppermute | solution.py:53
  36.7 18.4 %collective-permute-start.9 = (bf16[384,512]{1,0:T(8,128)(2,1)S(1)}, bf16[384,512]{1,0:T(8,128)(2,1)S(1)}, u32[]{:S(2)}, u32[]{:S(2)}) collective-permute-start(bf16[384,512]{1,0:T(8,128)(2,1)S(1)} %collect.1.own_ref), channel_id=1, source_target_pairs={{0,1},{1,2},{2,3},{3,0},{4,5},{5,6},{6,7},{7,4},{8,9},{9,10},{10,1... | collective-permute-start | bytes 1179656 | tf_op jit(solution)/shard_map/ppermute | solution.py:53
  38.3 20.9 %collective-permute-start.13 = (bf16[192,1024]{1,0:T(8,128)(2,1)S(1)}, bf16[192,1024]{1,0:T(8,128)(2,1)}, u32[]{:S(2)}, u32[]{:S(2)}) collective-permute-start(bf16[192,1024]{1,0:T(8,128)(2,1)S(1)} %collective-permute-done.7.rest_1_.refs_7_), channel_id=1, source_target_pairs={{0,16},{1,17},{2,18},{3,19},{4,20},{5,21},{6,22},{7,23},{8,24},{9,... | collective-permute-start | bytes 1179656 | tf_op jit(solution)/shard_map/ppermute | solution.py:53
  38.9 20.4 %collective-permute-start.12 = (bf16[192,1024]{1,0:T(8,128)(2,1)S(1)}, bf16[192,1024]{1,0:T(8,128)(2,1)}, u32[]{:S(2)}, u32[]{:S(2)}) collective-permute-start(bf16[192,1024]{1,0:T(8,128)(2,1)S(1)} %collective-permute-done.8.rest_2_.refs_2_), channel_id=1, source_target_pairs={{0,112},{1,113},{2,114},{3,115},{4,116},{5,117},{6,118},{7,119},{8... | collective-permute-start | bytes 1179656 | tf_op jit(solution)/shard_map/ppermute | solution.py:53
  40.3 18.9 %all-to-all-start.1 = ((bf16[16,32,128]{2,1,0:T(8,128)(2,1)}), bf16[16,32,128]{2,1,0:T(8,128)(2,1)S(1)}, u32[]{:S(2)}, u32[]{:S(2)}) async-start(bf16[16,32,128]{2,1,0:T(8,128)(2,1)} %states_before.1.rest_0_), calls=%async_computation.1 | async-start | bytes 262144 | tf_op jit(solution)/shard_map/all_to_all | solution.py:396
  53.4 15.2 %collective-permute-start.10 = (bf16[384,512]{1,0:T(8,128)(2,1)S(1)}, bf16[384,512]{1,0:T(8,128)(2,1)S(1)}, u32[]{:S(2)}, u32[]{:S(2)}) collective-permute-start(bf16[384,512]{1,0:T(8,128)(2,1)S(1)} %collect.1.own_ref), channel_id=1, source_target_pairs={{0,3},{1,0},{2,1},{3,2},{4,7},{5,4},{6,5},{7,6},{8,11},{9,8},{10,9... | collective-permute-start | bytes 1179656 | tf_op jit(solution)/shard_map/ppermute | solution.py:53
  55.2 13.5 %collective-permute-start.11 = (bf16[384,512]{1,0:T(8,128)(2,1)S(1)}, bf16[384,512]{1,0:T(8,128)(2,1)S(1)}, u32[]{:S(2)}, u32[]{:S(2)}) collective-permute-start(bf16[384,512]{1,0:T(8,128)(2,1)S(1)} %collective-permute-done.9.left_ref), channel_id=1, source_target_pairs={{0,1},{1,2},{2,3},{3,0},{4,5},{5,6},{6,7},{7,4},{8,9},{9,10},{10,1... | collective-permute-start | bytes 1179656 | tf_op jit(solution)/shard_map/ppermute | solution.py:53
  60.6 4.4 %collective-permute-start.19 = (bf16[512,128]{1,0:T(8,128)(2,1)S(1)}, bf16[512,128]{1,0:T(8,128)(2,1)S(1)}, u32[]{:S(2)}, u32[]{:S(2)}) collective-permute-start(bf16[512,128]{1,0:T(8,128)(2,1)S(1)} %get-tuple-element.55), channel_id=1, source_target_pairs={{0,8},{1,9},{2,10},{3,11},{4,12},{5,13},{6,14},{7,15},{8,0},{9,1},... | collective-permute-start | bytes 393224 | tf_op jit(solution)/shard_map/ppermute | solution.py:53
  61.7 7.6 %collective-permute-start.14 = (bf16[96,1024]{1,0:T(8,128)(2,1)S(1)}, bf16[96,1024]{1,0:T(8,128)(2,1)S(1)}, u32[]{:S(2)}, u32[]{:S(2)}) collective-permute-start(bf16[96,1024]{1,0:T(8,128)(2,1)S(1)} %slice.8), channel_id=1, source_target_pairs={{0,16},{1,17},{2,18},{3,19},{4,20},{5,21},{6,22},{7,23},{8,24},{9,... | collective-permute-start | bytes 589832 | tf_op jit(solution)/shard_map/ppermute | solution.py:53
  63.5 8.3 %collective-permute-start.15 = (bf16[96,1024]{1,0:T(8,128)(2,1)S(1)}, bf16[96,1024]{1,0:T(8,128)(2,1)S(1)}, u32[]{:S(2)}, u32[]{:S(2)}) collective-permute-start(bf16[96,1024]{1,0:T(8,128)(2,1)S(1)} %slice.9), channel_id=1, source_target_pairs={{0,112},{1,113},{2,114},{3,115},{4,116},{5,117},{6,118},{7,119},{8... | collective-permute-start | bytes 589832 | tf_op jit(solution)/shard_map/ppermute | solution.py:53
  67.6 8.1 %collective-permute-start.21 = (bf16[128,1024]{1,0:T(8,128)(2,1)S(1)}, bf16[128,1024]{1,0:T(8,128)(2,1)S(1)}, u32[]{:S(2)}, u32[]{:S(2)}) collective-permute-start(bf16[128,1024]{1,0:T(8,128)(2,1)S(1)} %get-tuple-element.61.own_ref), channel_id=1, source_target_pairs={{0,128},{1,129},{2,130},{3,131},{4,132},{5,133},{6,134},{7,135},{8... | collective-permute-start | bytes 786440 | tf_op jit(solution)/shard_map/ppermute | solution.py:53
  74.8 2.9 %collective-permute-start.22 = (bf16[128,1024]{1,0:T(8,128)(2,1)S(1)}, bf16[128,1024]{1,0:T(8,128)(2,1)S(1)}, u32[]{:S(2)}, u32[]{:S(2)}) collective-permute-start(bf16[128,1024]{1,0:T(8,128)(2,1)S(1)} %get-tuple-element.61.own_ref), channel_id=1, source_target_pairs={{0,8},{1,9},{2,10},{3,11},{4,12},{5,13},{6,14},{7,15},{8,0},{9,1},... | collective-permute-start | bytes 786440 | tf_op jit(solution)/shard_map/ppermute | solution.py:53
  75.7 6.0 %collective-permute-start.16 = (bf16[128,1024]{1,0:T(8,128)(2,1)S(1)}, bf16[128,1024]{1,0:T(8,128)(2,1)S(1)}, u32[]{:S(2)}, u32[]{:S(2)}) collective-permute-start(bf16[128,1024]{1,0:T(8,128)(2,1)S(1)} %get-tuple-element.50), channel_id=1, source_target_pairs={{0,8},{1,9},{2,10},{3,11},{4,12},{5,13},{6,14},{7,15},{8,0},{9,1},... | collective-permute-start | bytes 786440 | tf_op jit(solution)/shard_map/ppermute | solution.py:53
  76.4 8.4 %collective-permute-start.18 = (bf16[128,1024]{1,0:T(8,128)(2,1)S(1)}, bf16[128,1024]{1,0:T(8,128)(2,1)S(1)}, u32[]{:S(2)}, u32[]{:S(2)}) collective-permute-start(bf16[128,1024]{1,0:T(8,128)(2,1)S(1)} %sum_theirs.1.rest_0_), channel_id=1, source_target_pairs={{0,128},{1,129},{2,130},{3,131},{4,132},{5,133},{6,134},{7,135},{8... | collective-permute-start | bytes 786440 | tf_op jit(solution)/shard_map/ppermute | solution.py:53
  79.6 7.5 %collective-permute-start.24 = (bf16[96,1024]{1,0:T(8,128)(2,1)S(1)}, bf16[96,1024]{1,0:T(8,128)(2,1)S(1)}, u32[]{:S(2)}, u32[]{:S(2)}) collective-permute-start(bf16[96,1024]{1,0:T(8,128)(2,1)S(1)} %get-tuple-element.64), channel_id=1, source_target_pairs={{0,16},{1,17},{2,18},{3,19},{4,20},{5,21},{6,22},{7,23},{8,24},{9,... | collective-permute-start | bytes 589832 | tf_op jit(solution)/shard_map/ppermute | solution.py:53
  81.4 7.5 %collective-permute-start.25 = (bf16[96,1024]{1,0:T(8,128)(2,1)S(1)}, bf16[96,1024]{1,0:T(8,128)(2,1)S(1)}, u32[]{:S(2)}, u32[]{:S(2)}) collective-permute-start(bf16[96,1024]{1,0:T(8,128)(2,1)S(1)} %get-tuple-element.66), channel_id=1, source_target_pairs={{0,112},{1,113},{2,114},{3,115},{4,116},{5,117},{6,118},{7,119},{8... | collective-permute-start | bytes 589832 | tf_op jit(solution)/shard_map/ppermute | solution.py:53
  89.9 11.3 %collective-permute-start.26 = (bf16[192,1024]{1,0:T(8,128)(2,1)}, bf16[192,1024]{1,0:T(8,128)(2,1)S(1)}, u32[]{:S(2)}, u32[]{:S(2)}) collective-permute-start(bf16[192,1024]{1,0:T(8,128)(2,1)} %get-tuple-element.67), channel_id=1, source_target_pairs={{0,16},{1,17},{2,18},{3,19},{4,20},{5,21},{6,22},{7,23},{8,24},{9,... | collective-permute-start | bytes 1179656 | tf_op jit(solution)/shard_map/ppermute | solution.py:53
  90.2 11.7 %collective-permute-start.27 = (bf16[192,1024]{1,0:T(8,128)(2,1)}, bf16[192,1024]{1,0:T(8,128)(2,1)}, u32[]{:S(2)}, u32[]{:S(2)}) collective-permute-start(bf16[192,1024]{1,0:T(8,128)(2,1)} %get-tuple-element.69), channel_id=1, source_target_pairs={{0,112},{1,113},{2,114},{3,115},{4,116},{5,117},{6,118},{7,119},{8... | collective-permute-start | bytes 1179656 | tf_op jit(solution)/shard_map/ppermute | solution.py:53
  94.0 14.6 %all-to-all-start.2 = ((bf16[16,32,128]{2,1,0:T(8,128)(2,1)}), bf16[16,32,128]{2,1,0:T(8,128)(2,1)S(1)}, u32[]{:S(2)}, u32[]{:S(2)}) async-start(bf16[16,32,128]{2,1,0:T(8,128)(2,1)} %merge_queries.1.rest_0_), calls=%async_computation.2 | async-start | bytes 262144 | tf_op jit(solution)/shard_map/all_to_all | solution.py:396
  105.9 19.7 %collective-permute-start.29 = (bf16[192,1024]{1,0:T(8,128)(2,1)}, bf16[192,1024]{1,0:T(8,128)(2,1)S(1)}, u32[]{:S(2)}, u32[]{:S(2)}) collective-permute-start(bf16[192,1024]{1,0:T(8,128)(2,1)} %get-tuple-element.70.rest_0_), channel_id=1, source_target_pairs={{0,16},{1,17},{2,18},{3,19},{4,20},{5,21},{6,22},{7,23},{8,24},{9,... | collective-permute-start | bytes 1179656 | tf_op jit(solution)/shard_map/ppermute | solution.py:53
  108.6 17.0 %collective-permute-start.30 = (bf16[192,1024]{1,0:T(8,128)(2,1)}, bf16[192,1024]{1,0:T(8,128)(2,1)}, u32[]{:S(2)}, u32[]{:S(2)}) collective-permute-start(bf16[192,1024]{1,0:T(8,128)(2,1)} %get-tuple-element.71.rest_1_), channel_id=1, source_target_pairs={{0,112},{1,113},{2,114},{3,115},{4,116},{5,117},{6,118},{7,119},{8... | collective-permute-start | bytes 1179656 | tf_op jit(solution)/shard_map/ppermute | solution.py:53
  110.4 19.9 %all-to-all-start.3 = ((bf16[16,32,128]{2,1,0:T(8,128)(2,1)}), bf16[16,32,128]{2,1,0:T(8,128)(2,1)S(1)}, u32[]{:S(2)}, u32[]{:S(2)}) async-start(bf16[16,32,128]{2,1,0:T(8,128)(2,1)} %states_after.1.rest_0_), calls=%async_computation.3 | async-start | bytes 262144 | tf_op jit(solution)/shard_map/all_to_all | solution.py:396
  127.6 10.3 %collective-permute-start.31 = (bf16[192,1024]{1,0:T(8,128)(2,1)}, bf16[192,1024]{1,0:T(8,128)(2,1)S(1)}, u32[]{:S(2)}, u32[]{:S(2)}) collective-permute-start(bf16[192,1024]{1,0:T(8,128)(2,1)} %get-tuple-element.82), channel_id=1, source_target_pairs={{0,16},{1,17},{2,18},{3,19},{4,20},{5,21},{6,22},{7,23},{8,24},{9,... | collective-permute-start | bytes 1179656 | tf_op jit(solution)/shard_map/ppermute | solution.py:53
  130.3 10.9 %collective-permute-start.32 = (bf16[192,1024]{1,0:T(8,128)(2,1)}, bf16[192,1024]{1,0:T(8,128)(2,1)S(1)}, u32[]{:S(2)}, u32[]{:S(2)}) collective-permute-start(bf16[192,1024]{1,0:T(8,128)(2,1)} %get-tuple-element.83), channel_id=1, source_target_pairs={{0,112},{1,113},{2,114},{3,115},{4,116},{5,117},{6,118},{7,119},{8... | collective-permute-start | bytes 1179656 | tf_op jit(solution)/shard_map/ppermute | solution.py:53
  (36 other events, 192.8 us)

commit v9 on v7

--- a/solution.py
+++ b/solution.py
@@ -392,6 +392,10 @@
     )(*args, *after)
 
 
+def add_pieces(a, b):
+    return (a.astype(F32) + b.astype(F32)).astype(BF)
+
+
 def exchange(array):
     return lax.all_to_all(array, "seq", 0, 0, tiled=True, axis_index_groups=CHIP_GROUPS)
 
@@ -512,29 +516,23 @@
         (key_mine, key_other, query_mine, query_other),
     )
     returned = exchange(query_merged)
-    up, down = call(
-        adds_kernel, (piece, piece), "ring_sum_2", 400_000, 2_000_000, (part[2], up, part[7], down),
-        (query_merged,),
-    )
+    up, down = add_pieces(part[2], up), add_pieces(part[7], down)
     afters = call(
         functools.partial(recurrence_kernel, True), slices, "states_after", 1_000_000, 1_000_000,
         (gathered, returned), (up, down),
     )
     up, down = send(up, Z_UP), send(down, Z_DOWN)
     after = exchange(afters).reshape(HALF_ROWS, HEAD_DIM)
+    up, down = add_pieces(part[1], up), add_pieces(part[8], down)
     grad_queries, inner_k, inner_v = call(
-        inner_grads_kernel, (row, row32, row32), "inner_grads", 25_000_000_000, 3_000_000,
-        (log_decay, queries, key_proj, value_proj, grad_attn, scores, states), (afters,),
+        inner_grads_kernel, (row, row32, row32), "inner_grads", 200_000_000, 3_000_000,
+        (log_decay, queries, key_proj, value_proj, grad_attn, scores, states), (up, down),
     )
     after_own, after_cross = call(
         functools.partial(spread_kernel, 1), (half_state, half_state), "spread_after",
         25_000_000_000, 500_000, (key_mine, key_other, query_mine, query_other, after), (inner_k,),
     )
     after_other = send(after_cross, CORE)
-    up, down = call(
-        adds_kernel, (piece, piece), "ring_sum_1", 400_000, 2_000_000, (part[1], up, part[8], down),
-        (inner_k,),
-    )
     up, down = send(up, Z_UP), send(down, Z_DOWN)
     grad_keys, grad_values = call(
         outer_grads_kernel, (row, row), "outer_grads", 70_000_000, 3_000_000,

time: 139 us -> 132 us (0.950)
  Pallas kernels: 29.7 us -> 24.7 us
  local copies, waits for them, and re-layouts: 10.8 us -> 6.14 us
  other arithmetic: 0 us -> 4.62 us
  starting transfers between devices: 73.3 us -> 69.8 us
  waiting for transfers between devices: 22.6 us -> 24.9 us
    pallas_call x18 -> x16, Pallas kernels: 22.4 us -> 17.4 us  [call(): pl.pallas_call(body, in_specs=[pl.BlockSpec(a.shape, lambda n=a.ndim: (0,...]
    unnamed x54 -> x44, local copies, waits for them, and re-layouts: 8.94 us -> 4.26 us
    convert_element_type x0 -> x4, other arithmetic: none -> 4.62 us  [add_pieces(): return (a.astype(F32) + b.astype(F32)).astype(BF)]
    all_to_all x4, waiting for transfers between devices: 2.73 us -> 5.35 us  [exchange(): lax.all_to_all(array, 'seq', 0, 0, tiled=True, axis_index_groups=CHIP_GRO...]
    all_to_all x4, starting transfers between devices: 28.9 us -> 26.6 us  [exchange(): lax.all_to_all(array, 'seq', 0, 0, tiled=True, axis_index_groups=CHIP_GRO...]
  transfers between devices with their start and end apart: 37 -> 37, of which waited for: 11 -> 14; matrix products, arithmetic and copies ran while one was open for 1% -> 5% of each run, Pallas kernels for 20% -> 17%
where the time goes in v9:
time: 132 us; the launch traced here: 131 us
  starting transfers between devices  69.8 us (53%)
  waiting for transfers between devices  24.9 us (19%)
  Pallas kernels  24.7 us (19%)
  local copies, waits for them, and re-layouts  6.14 us (5%)
  other arithmetic  4.62 us (4%)
    ppermute x33, starting transfers between devices, send(): return lax.ppermute(array, AXES, table)  43.2 us
    all_to_all x4, starting transfers between devices, exchange(): lax.all_to_all(array, 'seq', 0, 0, tiled=True, axis_index_groups=CHIP_GRO...  26.6 us
    ppermute x33, waiting for transfers between devices, send(): return lax.ppermute(array, AXES, table)  19.5 us
    pallas_call x16, Pallas kernels, call(): pl.pallas_call(body, in_specs=[pl.BlockSpec(a.shape, lambda n=a.ndim: (0,...  17.4 us
    all_to_all x4, waiting for transfers between devices, exchange(): lax.all_to_all(array, 'seq', 0, 0, tiled=True, axis_index_groups=CHIP_GRO...  5.35 us
    convert_element_type x4, other arithmetic, add_pieces(): return (a.astype(F32) + b.astype(F32)).astype(BF)  4.62 us
    unnamed x44, local copies, waits for them, and re-layouts  4.26 us
    pallas_call x1, Pallas kernels, body(): pl.pallas_call(project_kernel, out_shape=[row32, row32, row, row], scratc...  3.02 us
  transfers between devices with their start and end apart: 37, of which 14 were waited for; matrix products, arithmetic and copies ran while one was open for 5% of the time, Pallas kernels for 17%

profile of v9, /device:TPU:8, one launch (start us, length us, event | category | flops | bytes accessed | tf_op | source)
XLA Modules:
  0.0 131.1 jit_solution(12909427419794892781)
XLA Ops:
  0.6 2.0 %collective-permute-start = (bf16[192,1024]{1,0:T(8,128)(2,1)}, bf16[192,1024]{1,0:T(8,128)(2,1)S(1)}, u32[]{:S(2)}, u32[]{:S(2)}) collective-permute-start(bf16[192,1024]{1,0:T(8,128)(2,1)} %refs_0_.1), channel_id=1, source_target_pairs={{0,16},{1,17},{2,18},{3,19},{4,20},{5,21},{6,22},{7,23},{8,24},{9,... | collective-permute-start | bytes 1179656 | tf_op jit(solution)/shard_map/ppermute | solution.py:53
  2.6 4.0 %collective-permute-start.1 = (bf16[192,1024]{1,0:T(8,128)(2,1)}, bf16[192,1024]{1,0:T(8,128)(2,1)}, u32[]{:S(2)}, u32[]{:S(2)}) collective-permute-start(bf16[192,1024]{1,0:T(8,128)(2,1)} %refs_0_.1), channel_id=1, source_target_pairs={{0,112},{1,113},{2,114},{3,115},{4,116},{5,117},{6,118},{7,119},{8... | collective-permute-start | bytes 1179656 | tf_op jit(solution)/shard_map/ppermute | solution.py:53
  9.2 2.4 %key_terms.1 = (bf16[528,128]{1,0:T(8,128)(2,1)S(1)}, bf16[528,128]{1,0:T(8,128)(2,1)S(1)}) custom-call(f32[8,128]{1,0:T(8,128)S(1)} %bitcast.5, bf16[128,1024]{1,0:T(8,128)(2,1)S(1)} %copy-done, bf16[128,1024]{1,0:T(8,128)(2,1)S(1)} %copy-done.2), custom_call_target="tpu_custom_call" | custom-call | flops 40000000 | bytes 1000000 | tf_op jit(solution)/shard_map/key_terms/pallas_call | solution.py:418
  13.8 7.2 %all-to-all-start = ((bf16[16,48,128]{2,1,0:T(8,128)(2,1)}), bf16[16,48,128]{2,1,0:T(8,128)(2,1)S(1)}, u32[]{:S(2)}, u32[]{:S(2)}) async-start(bf16[16,48,128]{2,1,0:T(8,128)(2,1)} %merge_keys.1.rest_2_), calls=%async_computation | async-start | bytes 393216 | tf_op jit(solution)/shard_map/all_to_all | solution.py:400
  22.4 2.8 %collective-permute-start.3 = (bf16[384,128]{1,0:T(8,128)(2,1)S(1)}, bf16[384,128]{1,0:T(8,128)(2,1)S(1)}, u32[]{:S(2)}, u32[]{:S(2)}) collective-permute-start(bf16[384,128]{1,0:T(8,128)(2,1)S(1)} %get-tuple-element.42), channel_id=1, source_target_pairs={{0,0},{1,1},{2,2},{3,3},{4,128},{5,129},{6,130},{7,131},{8,8},{9,9... | collective-permute-start | bytes 294920 | tf_op jit(solution)/shard_map/ppermute | solution.py:53
  25.4 3.2 %collective-permute-start.6 = (bf16[384,128]{1,0:T(8,128)(2,1)S(1)}, bf16[384,128]{1,0:T(8,128)(2,1)S(1)}, u32[]{:S(2)}, u32[]{:S(2)}) collective-permute-start(bf16[384,128]{1,0:T(8,128)(2,1)S(1)} %get-tuple-element.43), channel_id=1, source_target_pairs={{0,12},{1,13},{2,14},{3,15},{4,140},{5,141},{6,142},{7,143},{8,4},... | collective-permute-start | bytes 294920 | tf_op jit(solution)/shard_map/ppermute | solution.py:53
  28.6 1.5 %collective-permute-start.12 = (bf16[192,1024]{1,0:T(8,128)(2,1)S(1)}, bf16[192,1024]{1,0:T(8,128)(2,1)S(1)}, u32[]{:S(2)}, u32[]{:S(2)}) collective-permute-start(bf16[192,1024]{1,0:T(8,128)(2,1)S(1)} %collective-permute-done.rest_0_.refs_8_), channel_id=1, source_target_pairs={{0,16},{1,17},{2,18},{3,19},{4,20},{5,21},{6,22},{7,23},{8,24},{9,... | collective-permute-start | bytes 1179656 | tf_op jit(solution)/shard_map/ppermute | solution.py:53
  31.0 4.4 %collective-permute-start.10 = (bf16[192,1024]{1,0:T(8,128)(2,1)}, bf16[192,1024]{1,0:T(8,128)(2,1)S(1)}, u32[]{:S(2)}, u32[]{:S(2)}) collective-permute-start(bf16[192,1024]{1,0:T(8,128)(2,1)} %collective-permute-done.1.rest_1_.refs_1_), channel_id=1, source_target_pairs={{0,112},{1,113},{2,114},{3,115},{4,116},{5,117},{6,118},{7,119},{8... | collective-permute-start | bytes 1179656 | tf_op jit(solution)/shard_map/ppermute | solution.py:53
  36.4 1.6 %collective-permute-start.7 = (bf16[384,512]{1,0:T(8,128)(2,1)S(1)}, bf16[384,512]{1,0:T(8,128)(2,1)S(1)}, u32[]{:S(2)}, u32[]{:S(2)}) collective-permute-start(bf16[384,512]{1,0:T(8,128)(2,1)S(1)} %collect.1.own_ref), channel_id=1, source_target_pairs={{0,1},{1,2},{2,3},{3,0},{4,5},{5,6},{6,7},{7,4},{8,9},{9,10},{10,1... | collective-permute-start | bytes 1179656 | tf_op jit(solution)/shard_map/ppermute | solution.py:53
  37.9 7.9 %all-to-all-start.1 = ((bf16[16,32,128]{2,1,0:T(8,128)(2,1)}), bf16[16,32,128]{2,1,0:T(8,128)(2,1)S(1)}, u32[]{:S(2)}, u32[]{:S(2)}) async-start(bf16[16,32,128]{2,1,0:T(8,128)(2,1)} %states_before.1.rest_0_), calls=%async_computation.1 | async-start | bytes 262144 | tf_op jit(solution)/shard_map/all_to_all | solution.py:400
  45.9 1.7 %collective-permute-start.8 = (bf16[384,512]{1,0:T(8,128)(2,1)S(1)}, bf16[384,512]{1,0:T(8,128)(2,1)S(1)}, u32[]{:S(2)}, u32[]{:S(2)}) collective-permute-start(bf16[384,512]{1,0:T(8,128)(2,1)S(1)} %collect.1.own_ref), channel_id=1, source_target_pairs={{0,3},{1,0},{2,1},{3,2},{4,7},{5,4},{6,5},{7,6},{8,11},{9,8},{10,9... | collective-permute-start | bytes 1179656 | tf_op jit(solution)/shard_map/ppermute | solution.py:53
  47.6 1.5 %collective-permute-start.13 = (bf16[192,1024]{1,0:T(8,128)(2,1)S(1)}, bf16[192,1024]{1,0:T(8,128)(2,1)}, u32[]{:S(2)}, u32[]{:S(2)}) collective-permute-start(bf16[192,1024]{1,0:T(8,128)(2,1)S(1)} %collective-permute-done.12.refs_7_.rest_0_), channel_id=1, source_target_pairs={{0,16},{1,17},{2,18},{3,19},{4,20},{5,21},{6,22},{7,23},{8,24},{9,... | collective-permute-start | bytes 1179656 | tf_op jit(solution)/shard_map/ppermute | solution.py:53
  49.1 1.8 %collective-permute-start.11 = (bf16[192,1024]{1,0:T(8,128)(2,1)S(1)}, bf16[192,1024]{1,0:T(8,128)(2,1)}, u32[]{:S(2)}, u32[]{:S(2)}) collective-permute-start(bf16[192,1024]{1,0:T(8,128)(2,1)S(1)} %collective-permute-done.10.refs_2_.rest_1_), channel_id=1, source_target_pairs={{0,112},{1,113},{2,114},{3,115},{4,116},{5,117},{6,118},{7,119},{8... | collective-permute-start | bytes 1179656 | tf_op jit(solution)/shard_map/ppermute | solution.py:53
  51.1 2.7 %all-to-all-done.1 = bf16[16,32,128]{2,1,0:T(8,128)(2,1)S(1)} async-done(((bf16[16,32,128]{2,1,0:T(8,128)(2,1)}), bf16[16,32,128]{2,1,0:T(8,128)(2,1)S(1)}, u32[]{:S(2)}, u32[]{:S(2)}) %all-to-all-start.1) | async-done | bytes 131104 | tf_op jit(solution)/shard_map/all_to_all | solution.py:400
  54.1 6.6 %collective-permute-done.13.refs_6_ = bf16[192,1024]{1,0:T(8,128)(2,1)} collective-permute-done((bf16[192,1024]{1,0:T(8,128)(2,1)S(1)}, bf16[192,1024]{1,0:T(8,128)(2,1)}, u32[]{:S(2)}, u32[]{:S(2)}) %collective-permute-start.13) | collective-permute-done | bytes 393248 | tf_op jit(solution)/shard_map/ppermute | solution.py:53
  62.9 3.3 %collective-permute-start.15 = (bf16[96,1024]{1,0:T(8,128)(2,1)S(1)}, bf16[96,1024]{1,0:T(8,128)(2,1)S(1)}, u32[]{:S(2)}, u32[]{:S(2)}) collective-permute-start(bf16[96,1024]{1,0:T(8,128)(2,1)S(1)} %slice.9), channel_id=1, source_target_pairs={{0,112},{1,113},{2,114},{3,115},{4,116},{5,117},{6,118},{7,119},{8... | collective-permute-start | bytes 589832 | tf_op jit(solution)/shard_map/ppermute | solution.py:53
  68.7 1.6 %assemble.1 = (bf16[1536,512]{1,0:T(8,128)(2,1)S(1)}, bf16[512,1536]{1,0:T(8,128)(2,1)S(1)}) custom-call(bf16[384,512]{1,0:T(8,128)(2,1)S(1)} %collect.1.own_ref, bf16[384,512]{1,0:T(8,128)(2,1)S(1)} %collective-permute-done.7.left_ref, bf16[384,512]{1,0:T(8,128)(2,1)S(1)} %collective-permute-done.8.right_ref, ...), custom_call_target="tpu_custom_call" | custom-call | flops 1000000 | bytes 5000000 | tf_op jit(solution)/shard_map/assemble/pallas_call | solution.py:383
  70.3 3.0 %project.1 = (f32[128,1024]{1,0:T(8,128)S(1)}, f32[128,1024]{1,0:T(8,128)S(1)}, bf16[128,1024]{1,0:T(8,128)(2,1)S(1)}, bf16[128,1024]{1,0:T(8,128)(2,1)S(1)}) custom-call(bf16[512,1536]{1,0:T(8,128)(2,1)S(1)} %get-tuple-element.44.block_ref, bf16[192,1024]{1,0:T(8,128)(2,1)S(1)} %copy-done.18, bf16[192,1024]{1,0:T(8,128)(2,1)} %collective-permute-done.1.rest_1_.refs_1_, ...), custom_call_target="tpu_custom_call" | custom-call | flops 1600000000 | bytes 6000000 | tf_op jit(solution)/shard_map/project/pallas_call | solution.py:476
  76.7 1.9 %weight_partial.1 = (bf16[192,1024]{1,0:T(8,128)(2,1)S(1)}, bf16[192,1024]{1,0:T(8,128)(2,1)S(1)}, bf16[192,1024]{1,0:T(8,128)(2,1)S(1)}, bf16[192,1024]{1,0:T(8...) custom-call(bf16[1536,512]{1,0:T(8,128)(2,1)S(1)} %get-tuple-element, ...), custom_call_target="tpu_custom_call" | custom-call | flops 1600000000 | bytes 6000000 | tf_op jit(solution)/shard_map/weight_partial/pallas_call | solution.py:491
  78.7 3.2 %collective-permute-start.24 = (bf16[96,1024]{1,0:T(8,128)(2,1)S(1)}, bf16[96,1024]{1,0:T(8,128)(2,1)S(1)}, u32[]{:S(2)}, u32[]{:S(2)}) collective-permute-start(bf16[96,1024]{1,0:T(8,128)(2,1)S(1)} %get-tuple-element.61), channel_id=1, source_target_pairs={{0,112},{1,113},{2,114},{3,115},{4,116},{5,117},{6,118},{7,119},{8... | collective-permute-start | bytes 589832 | tf_op jit(solution)/shard_map/ppermute | solution.py:53
  81.9 2.1 %collective-permute-done.18.other_ref = bf16[128,1024]{1,0:T(8,128)(2,1)S(1)} collective-permute-done((bf16[128,1024]{1,0:T(8,128)(2,1)S(1)}, bf16[128,1024]{1,0:T(8,128)(2,1)S(1)}, u32[]{:S(2)}, u32[]{:S(2)}) %collective-permute-start.18) | collective-permute-done | bytes 262176 | tf_op jit(solution)/shard_map/ppermute | solution.py:53
  84.0 2.3 %query_terms.1 = (bf16[128,1024]{1,0:T(8,128)(2,1)S(1)}, bf16[512,128]{1,0:T(8,128)(2,1)S(1)}, bf16[512,128]{1,0:T(8,128)(2,1)S(1)}) custom-call(f32[8,128]{1,0:T(8,128)S(1)} %bitcast.7, bf16[128,1024]{1,0:T(8,128)(2,1)S(1)} %copy-done.4, f32[128,1024]{1,0:T(8,128)S(1)} %get-tuple-element.45.own_ref, bf16[128,1024]{1,0:T(8,128)(2,1)S(1)} %collective-permute-done.16.core_ref, ...), custom_call_target="tpu_custom_call" | custom-call | flops 40000000 | bytes 1000000 | tf_op jit(solution)/shard_map/query_terms/pallas_call | solution.py:383
  87.7 2.9 %collective-permute-start.27 = (bf16[192,1024]{1,0:T(8,128)(2,1)S(1)}, bf16[192,1024]{1,0:T(8,128)(2,1)}, u32[]{:S(2)}, u32[]{:S(2)}) collective-permute-start(bf16[192,1024]{1,0:T(8,128)(2,1)S(1)} %get-tuple-element.65), channel_id=1, source_target_pairs={{0,112},{1,113},{2,114},{3,115},{4,116},{5,117},{6,118},{7,119},{8... | collective-permute-start | bytes 1179656 | tf_op jit(solution)/shard_map/ppermute | solution.py:53
  90.6 1.3 %collective-permute-done.29.other_ref = bf16[512,128]{1,0:T(8,128)(2,1)S(1)} collective-permute-done((bf16[512,128]{1,0:T(8,128)(2,1)S(1)}, bf16[512,128]{1,0:T(8,128)(2,1)S(1)}, u32[]{:S(2)}, u32[]{:S(2)}) %collective-permute-start.29) | collective-permute-done | bytes 131104 | tf_op jit(solution)/shard_map/ppermute | solution.py:53
  92.7 6.6 %all-to-all-start.2 = ((bf16[16,32,128]{2,1,0:T(8,128)(2,1)}), bf16[16,32,128]{2,1,0:T(8,128)(2,1)S(1)}, u32[]{:S(2)}, u32[]{:S(2)}) async-start(bf16[16,32,128]{2,1,0:T(8,128)(2,1)} %merge_queries.1), calls=%async_computation.2 | async-start | bytes 262144 | tf_op jit(solution)/shard_map/all_to_all | solution.py:400
  100.4 2.8 %collective-permute-start.28 = (bf16[192,1024]{1,0:T(8,128)(2,1)S(1)}, bf16[192,1024]{1,0:T(8,128)(2,1)}, u32[]{:S(2)}, u32[]{:S(2)}) collective-permute-start(bf16[192,1024]{1,0:T(8,128)(2,1)S(1)} %add_convert_fusion.1.rest_1_), channel_id=1, source_target_pairs={{0,112},{1,113},{2,114},{3,115},{4,116},{5,117},{6,118},{7,119},{8... | collective-permute-start | bytes 1179656 | tf_op jit(solution)/shard_map/ppermute | solution.py:53
  104.5 2.6 %all-to-all-done.2.terms_ref = bf16[16,32,128]{2,1,0:T(8,128)(2,1)S(1)} async-done(((bf16[16,32,128]{2,1,0:T(8,128)(2,1)}), bf16[16,32,128]{2,1,0:T(8,128)(2,1)S(1)}, u32[]{:S(2)}, u32[]{:S(2)}) %all-to-all-start.2) | async-done | bytes 131104 | tf_op jit(solution)/shard_map/all_to_all | solution.py:400
  107.9 4.8 %all-to-all-start.3 = ((bf16[16,32,128]{2,1,0:T(8,128)(2,1)}), bf16[16,32,128]{2,1,0:T(8,128)(2,1)S(1)}, u32[]{:S(2)}, u32[]{:S(2)}) async-start(bf16[16,32,128]{2,1,0:T(8,128)(2,1)} %states_after.1), calls=%async_computation.3 | async-start | bytes 262144 | tf_op jit(solution)/shard_map/all_to_all | solution.py:400
  114.1 2.7 %collective-permute-start.32 = (bf16[192,1024]{1,0:T(8,128)(2,1)S(1)}, bf16[192,1024]{1,0:T(8,128)(2,1)}, u32[]{:S(2)}, u32[]{:S(2)}) collective-permute-start(bf16[192,1024]{1,0:T(8,128)(2,1)S(1)} %add_convert_fusion.rest_1_), channel_id=1, source_target_pairs={{0,112},{1,113},{2,114},{3,115},{4,116},{5,117},{6,118},{7,119},{8... | collective-permute-start | bytes 1179656 | tf_op jit(solution)/shard_map/ppermute | solution.py:53
  118.6 2.7 %inner_grads.1 = (bf16[128,1024]{1,0:T(8,128)(2,1)}, f32[128,1024]{1,0:T(8,128)S(1)}, f32[128,1024]{1,0:T(8,128)S(1)}) custom-call(f32[8,128]{1,0:T(8,128)S(1)} %bitcast.8, bf16[128,1024]{1,0:T(8,128)(2,1)S(1)} %copy-done.4, bf16[128,1024]{1,0:T(8,128)(2,1)S(1)} %copy-done.1, bf16[128,1024]{1,0:T(8,128)(2,1)S(1)} %copy-done.3, ...), custom_call_target="tpu_custom_call" | custom-call | flops 200000000 | bytes 3000000 | tf_op jit(solution)/shard_map/inner_grads/pallas_call | solution.py:383
  125.9 3.2 %collective-permute-done.31.up_ref = bf16[192,1024]{1,0:T(8,128)(2,1)} collective-permute-done((bf16[192,1024]{1,0:T(8,128)(2,1)S(1)}, bf16[192,1024]{1,0:T(8,128)(2,1)}, u32[]{:S(2)}, u32[]{:S(2)}) %collective-permute-start.31) | collective-permute-done | bytes 393248 | tf_op jit(solution)/shard_map/ppermute | solution.py:53
  129.1 2.0 %ring_sum_0.1 = bf16[192,1024]{1,0:T(8,128)(2,1)} custom-call(bf16[192,1024]{1,0:T(8,128)(2,1)S(1)} %copy-done.6, bf16[192,1024]{1,0:T(8,128)(2,1)} %collective-permute-done.31.up_ref, bf16[192,1024]{1,0:T(8,128)(2,1)} %collective-permute-done.32.down_ref), custom_call_target="tpu_custom_call" | custom-call | flops 400000 | bytes 2000000 | tf_op jit(solution)/shard_map/ring_sum_0/pallas_call | solution.py:383
  (111 shorter events, 29.7 us)
Async XLA Ops:
  0.6 20.4 %collective-permute-start = (bf16[192,1024]{1,0:T(8,128)(2,1)}, bf16[192,1024]{1,0:T(8,128)(2,1)S(1)}, u32[]{:S(2)}, u32[]{:S(2)}) collective-permute-start(bf16[192,1024]{1,0:T(8,128)(2,1)} %refs_0_.1), channel_id=1, source_target_pairs={{0,16},{1,17},{2,18},{3,19},{4,20},{5,21},{6,22},{7,23},{8,24},{9,... | collective-permute-start | bytes 1179656 | tf_op jit(solution)/shard_map/ppermute | solution.py:53
  2.6 18.4 %collective-permute-start.1 = (bf16[192,1024]{1,0:T(8,128)(2,1)}, bf16[192,1024]{1,0:T(8,128)(2,1)}, u32[]{:S(2)}, u32[]{:S(2)}) collective-permute-start(bf16[192,1024]{1,0:T(8,128)(2,1)} %refs_0_.1), channel_id=1, source_target_pairs={{0,112},{1,113},{2,114},{3,115},{4,116},{5,117},{6,118},{7,119},{8... | collective-permute-start | bytes 1179656 | tf_op jit(solution)/shard_map/ppermute | solution.py:53
  13.8 16.2 %all-to-all-start = ((bf16[16,48,128]{2,1,0:T(8,128)(2,1)}), bf16[16,48,128]{2,1,0:T(8,128)(2,1)S(1)}, u32[]{:S(2)}, u32[]{:S(2)}) async-start(bf16[16,48,128]{2,1,0:T(8,128)(2,1)} %merge_keys.1.rest_2_), calls=%async_computation | async-start | bytes 393216 | tf_op jit(solution)/shard_map/all_to_all | solution.py:400
  22.4 8.6 %collective-permute-start.3 = (bf16[384,128]{1,0:T(8,128)(2,1)S(1)}, bf16[384,128]{1,0:T(8,128)(2,1)S(1)}, u32[]{:S(2)}, u32[]{:S(2)}) collective-permute-start(bf16[384,128]{1,0:T(8,128)(2,1)S(1)} %get-tuple-element.42), channel_id=1, source_target_pairs={{0,0},{1,1},{2,2},{3,3},{4,128},{5,129},{6,130},{7,131},{8,8},{9,9... | collective-permute-start | bytes 294920 | tf_op jit(solution)/shard_map/ppermute | solution.py:53
  25.2 10.1 %collective-permute-start.4 = (bf16[384,128]{1,0:T(8,128)(2,1)S(1)}, bf16[384,128]{1,0:T(8,128)(2,1)S(1)}, u32[]{:S(2)}, u32[]{:S(2)}) collective-permute-start(bf16[384,128]{1,0:T(8,128)(2,1)S(1)} %get-tuple-element.42), channel_id=1, source_target_pairs={{0,4},{1,5},{2,6},{3,7},{4,132},{5,133},{6,134},{7,135},{8,12},{9,... | collective-permute-start | bytes 294920 | tf_op jit(solution)/shard_map/ppermute | solution.py:53
  25.3 10.0 %collective-permute-start.5 = (bf16[384,128]{1,0:T(8,128)(2,1)S(1)}, bf16[384,128]{1,0:T(8,128)(2,1)S(1)}, u32[]{:S(2)}, u32[]{:S(2)}) collective-permute-start(bf16[384,128]{1,0:T(8,128)(2,1)S(1)} %get-tuple-element.43), channel_id=1, source_target_pairs={{0,8},{1,9},{2,10},{3,11},{4,136},{5,137},{6,138},{7,139},{8,0},{9... | collective-permute-start | bytes 294920 | tf_op jit(solution)/shard_map/ppermute | solution.py:53
  25.4 9.9 %collective-permute-start.6 = (bf16[384,128]{1,0:T(8,128)(2,1)S(1)}, bf16[384,128]{1,0:T(8,128)(2,1)S(1)}, u32[]{:S(2)}, u32[]{:S(2)}) collective-permute-start(bf16[384,128]{1,0:T(8,128)(2,1)S(1)} %get-tuple-element.43), channel_id=1, source_target_pairs={{0,12},{1,13},{2,14},{3,15},{4,140},{5,141},{6,142},{7,143},{8,4},... | collective-permute-start | bytes 294920 | tf_op jit(solution)/shard_map/ppermute | solution.py:53
  28.6 19.0 %collective-permute-start.12 = (bf16[192,1024]{1,0:T(8,128)(2,1)S(1)}, bf16[192,1024]{1,0:T(8,128)(2,1)S(1)}, u32[]{:S(2)}, u32[]{:S(2)}) collective-permute-start(bf16[192,1024]{1,0:T(8,128)(2,1)S(1)} %collective-permute-done.rest_0_.refs_8_), channel_id=1, source_target_pairs={{0,16},{1,17},{2,18},{3,19},{4,20},{5,21},{6,22},{7,23},{8,24},{9,... | collective-permute-start | bytes 1179656 | tf_op jit(solution)/shard_map/ppermute | solution.py:53
  31.0 18.1 %collective-permute-start.10 = (bf16[192,1024]{1,0:T(8,128)(2,1)}, bf16[192,1024]{1,0:T(8,128)(2,1)S(1)}, u32[]{:S(2)}, u32[]{:S(2)}) collective-permute-start(bf16[192,1024]{1,0:T(8,128)(2,1)} %collective-permute-done.1.rest_1_.refs_1_), channel_id=1, source_target_pairs={{0,112},{1,113},{2,114},{3,115},{4,116},{5,117},{6,118},{7,119},{8... | collective-permute-start | bytes 1179656 | tf_op jit(solution)/shard_map/ppermute | solution.py:53
  36.4 14.5 %collective-permute-start.7 = (bf16[384,512]{1,0:T(8,128)(2,1)S(1)}, bf16[384,512]{1,0:T(8,128)(2,1)S(1)}, u32[]{:S(2)}, u32[]{:S(2)}) collective-permute-start(bf16[384,512]{1,0:T(8,128)(2,1)S(1)} %collect.1.own_ref), channel_id=1, source_target_pairs={{0,1},{1,2},{2,3},{3,0},{4,5},{5,6},{6,7},{7,4},{8,9},{9,10},{10,1... | collective-permute-start | bytes 1179656 | tf_op jit(solution)/shard_map/ppermute | solution.py:53
  37.9 15.9 %all-to-all-start.1 = ((bf16[16,32,128]{2,1,0:T(8,128)(2,1)}), bf16[16,32,128]{2,1,0:T(8,128)(2,1)S(1)}, u32[]{:S(2)}, u32[]{:S(2)}) async-start(bf16[16,32,128]{2,1,0:T(8,128)(2,1)} %states_before.1.rest_0_), calls=%async_computation.1 | async-start | bytes 262144 | tf_op jit(solution)/shard_map/all_to_all | solution.py:400
  45.9 22.8 %collective-permute-start.8 = (bf16[384,512]{1,0:T(8,128)(2,1)S(1)}, bf16[384,512]{1,0:T(8,128)(2,1)S(1)}, u32[]{:S(2)}, u32[]{:S(2)}) collective-permute-start(bf16[384,512]{1,0:T(8,128)(2,1)S(1)} %collect.1.own_ref), channel_id=1, source_target_pairs={{0,3},{1,0},{2,1},{3,2},{4,7},{5,4},{6,5},{7,6},{8,11},{9,8},{10,9... | collective-permute-start | bytes 1179656 | tf_op jit(solution)/shard_map/ppermute | solution.py:53
  47.6 13.1 %collective-permute-start.13 = (bf16[192,1024]{1,0:T(8,128)(2,1)S(1)}, bf16[192,1024]{1,0:T(8,128)(2,1)}, u32[]{:S(2)}, u32[]{:S(2)}) collective-permute-start(bf16[192,1024]{1,0:T(8,128)(2,1)S(1)} %collective-permute-done.12.refs_7_.rest_0_), channel_id=1, source_target_pairs={{0,16},{1,17},{2,18},{3,19},{4,20},{5,21},{6,22},{7,23},{8,24},{9,... | collective-permute-start | bytes 1179656 | tf_op jit(solution)/shard_map/ppermute | solution.py:53
  49.1 12.9 %collective-permute-start.11 = (bf16[192,1024]{1,0:T(8,128)(2,1)S(1)}, bf16[192,1024]{1,0:T(8,128)(2,1)}, u32[]{:S(2)}, u32[]{:S(2)}) collective-permute-start(bf16[192,1024]{1,0:T(8,128)(2,1)S(1)} %collective-permute-done.10.refs_2_.rest_1_), channel_id=1, source_target_pairs={{0,112},{1,113},{2,114},{3,115},{4,116},{5,117},{6,118},{7,119},{8... | collective-permute-start | bytes 1179656 | tf_op jit(solution)/shard_map/ppermute | solution.py:53
  50.9 17.8 %collective-permute-start.9 = (bf16[384,512]{1,0:T(8,128)(2,1)S(1)}, bf16[384,512]{1,0:T(8,128)(2,1)}, u32[]{:S(2)}, u32[]{:S(2)}) collective-permute-start(bf16[384,512]{1,0:T(8,128)(2,1)S(1)} %collective-permute-done.7.left_ref), channel_id=1, source_target_pairs={{0,1},{1,2},{2,3},{3,0},{4,5},{5,6},{6,7},{7,4},{8,9},{9,10},{10,1... | collective-permute-start | bytes 1179656 | tf_op jit(solution)/shard_map/ppermute | solution.py:53
  54.0 12.2 %collective-permute-start.19 = (bf16[512,128]{1,0:T(8,128)(2,1)S(1)}, bf16[512,128]{1,0:T(8,128)(2,1)S(1)}, u32[]{:S(2)}, u32[]{:S(2)}) collective-permute-start(bf16[512,128]{1,0:T(8,128)(2,1)S(1)} %get-tuple-element.51), channel_id=1, source_target_pairs={{0,8},{1,9},{2,10},{3,11},{4,12},{5,13},{6,14},{7,15},{8,0},{9,1},... | collective-permute-start | bytes 393224 | tf_op jit(solution)/shard_map/ppermute | solution.py:53
  61.7 8.6 %collective-permute-start.14 = (bf16[96,1024]{1,0:T(8,128)(2,1)S(1)}, bf16[96,1024]{1,0:T(8,128)(2,1)S(1)}, u32[]{:S(2)}, u32[]{:S(2)}) collective-permute-start(bf16[96,1024]{1,0:T(8,128)(2,1)S(1)} %slice.8), channel_id=1, source_target_pairs={{0,16},{1,17},{2,18},{3,19},{4,20},{5,21},{6,22},{7,23},{8,24},{9,... | collective-permute-start | bytes 589832 | tf_op jit(solution)/shard_map/ppermute | solution.py:53
  62.9 7.4 %collective-permute-start.15 = (bf16[96,1024]{1,0:T(8,128)(2,1)S(1)}, bf16[96,1024]{1,0:T(8,128)(2,1)S(1)}, u32[]{:S(2)}, u32[]{:S(2)}) collective-permute-start(bf16[96,1024]{1,0:T(8,128)(2,1)S(1)} %slice.9), channel_id=1, source_target_pairs={{0,112},{1,113},{2,114},{3,115},{4,116},{5,117},{6,118},{7,119},{8... | collective-permute-start | bytes 589832 | tf_op jit(solution)/shard_map/ppermute | solution.py:53
  68.1 7.0 %collective-permute-start.20 = (bf16[128,1024]{1,0:T(8,128)(2,1)S(1)}, bf16[128,1024]{1,0:T(8,128)(2,1)S(1)}, u32[]{:S(2)}, u32[]{:S(2)}) collective-permute-start(bf16[128,1024]{1,0:T(8,128)(2,1)S(1)} %get-tuple-element.55.own_ref), channel_id=1, source_target_pairs={{0,128},{1,129},{2,130},{3,131},{4,132},{5,133},{6,134},{7,135},{8... | collective-permute-start | bytes 786440 | tf_op jit(solution)/shard_map/ppermute | solution.py:53
  73.5 3.2 %collective-permute-start.21 = (bf16[128,1024]{1,0:T(8,128)(2,1)S(1)}, bf16[128,1024]{1,0:T(8,128)(2,1)S(1)}, u32[]{:S(2)}, u32[]{:S(2)}) collective-permute-start(bf16[128,1024]{1,0:T(8,128)(2,1)S(1)} %get-tuple-element.55.own_ref), channel_id=1, source_target_pairs={{0,8},{1,9},{2,10},{3,11},{4,12},{5,13},{6,14},{7,15},{8,0},{9,1},... | collective-permute-start | bytes 786440 | tf_op jit(solution)/shard_map/ppermute | solution.py:53
  75.1 6.8 %collective-permute-start.16 = (bf16[128,1024]{1,0:T(8,128)(2,1)S(1)}, bf16[128,1024]{1,0:T(8,128)(2,1)S(1)}, u32[]{:S(2)}, u32[]{:S(2)}) collective-permute-start(bf16[128,1024]{1,0:T(8,128)(2,1)S(1)} %get-tuple-element.46), channel_id=1, source_target_pairs={{0,8},{1,9},{2,10},{3,11},{4,12},{5,13},{6,14},{7,15},{8,0},{9,1},... | collective-permute-start | bytes 786440 | tf_op jit(solution)/shard_map/ppermute | solution.py:53
  75.7 8.3 %collective-permute-start.18 = (bf16[128,1024]{1,0:T(8,128)(2,1)S(1)}, bf16[128,1024]{1,0:T(8,128)(2,1)S(1)}, u32[]{:S(2)}, u32[]{:S(2)}) collective-permute-start(bf16[128,1024]{1,0:T(8,128)(2,1)S(1)} %sum_theirs.1.rest_0_), channel_id=1, source_target_pairs={{0,128},{1,129},{2,130},{3,131},{4,132},{5,133},{6,134},{7,135},{8... | collective-permute-start | bytes 786440 | tf_op jit(solution)/shard_map/ppermute | solution.py:53
  78.6 8.2 %collective-permute-start.23 = (bf16[96,1024]{1,0:T(8,128)(2,1)S(1)}, bf16[96,1024]{1,0:T(8,128)(2,1)S(1)}, u32[]{:S(2)}, u32[]{:S(2)}) collective-permute-start(bf16[96,1024]{1,0:T(8,128)(2,1)S(1)} %get-tuple-element.59), channel_id=1, source_target_pairs={{0,16},{1,17},{2,18},{3,19},{4,20},{5,21},{6,22},{7,23},{8,24},{9,... | collective-permute-start | bytes 589832 | tf_op jit(solution)/shard_map/ppermute | solution.py:53
  78.7 8.1 %collective-permute-start.24 = (bf16[96,1024]{1,0:T(8,128)(2,1)S(1)}, bf16[96,1024]{1,0:T(8,128)(2,1)S(1)}, u32[]{:S(2)}, u32[]{:S(2)}) collective-permute-start(bf16[96,1024]{1,0:T(8,128)(2,1)S(1)} %get-tuple-element.61), channel_id=1, source_target_pairs={{0,112},{1,113},{2,114},{3,115},{4,116},{5,117},{6,118},{7,119},{8... | collective-permute-start | bytes 589832 | tf_op jit(solution)/shard_map/ppermute | solution.py:53
  87.7 11.6 %collective-permute-start.27 = (bf16[192,1024]{1,0:T(8,128)(2,1)S(1)}, bf16[192,1024]{1,0:T(8,128)(2,1)}, u32[]{:S(2)}, u32[]{:S(2)}) collective-permute-start(bf16[192,1024]{1,0:T(8,128)(2,1)S(1)} %get-tuple-element.65), channel_id=1, source_target_pairs={{0,112},{1,113},{2,114},{3,115},{4,116},{5,117},{6,118},{7,119},{8... | collective-permute-start | bytes 1179656 | tf_op jit(solution)/shard_map/ppermute | solution.py:53
  90.6 12.6 %collective-permute-start.25 = (bf16[192,1024]{1,0:T(8,128)(2,1)}, bf16[192,1024]{1,0:T(8,128)(2,1)}, u32[]{:S(2)}, u32[]{:S(2)}) collective-permute-start(bf16[192,1024]{1,0:T(8,128)(2,1)} %get-tuple-element.62), channel_id=1, source_target_pairs={{0,16},{1,17},{2,18},{3,19},{4,20},{5,21},{6,22},{7,23},{8,24},{9,... | collective-permute-start | bytes 1179656 | tf_op jit(solution)/shard_map/ppermute | solution.py:53
  92.7 14.5 %all-to-all-start.2 = ((bf16[16,32,128]{2,1,0:T(8,128)(2,1)}), bf16[16,32,128]{2,1,0:T(8,128)(2,1)S(1)}, u32[]{:S(2)}, u32[]{:S(2)}) async-start(bf16[16,32,128]{2,1,0:T(8,128)(2,1)} %merge_queries.1), calls=%async_computation.2 | async-start | bytes 262144 | tf_op jit(solution)/shard_map/all_to_all | solution.py:400
  100.4 12.5 %collective-permute-start.28 = (bf16[192,1024]{1,0:T(8,128)(2,1)S(1)}, bf16[192,1024]{1,0:T(8,128)(2,1)}, u32[]{:S(2)}, u32[]{:S(2)}) collective-permute-start(bf16[192,1024]{1,0:T(8,128)(2,1)S(1)} %add_convert_fusion.1.rest_1_), channel_id=1, source_target_pairs={{0,112},{1,113},{2,114},{3,115},{4,116},{5,117},{6,118},{7,119},{8... | collective-permute-start | bytes 1179656 | tf_op jit(solution)/shard_map/ppermute | solution.py:53
  104.4 12.9 %collective-permute-start.26 = (bf16[192,1024]{1,0:T(8,128)(2,1)S(1)}, bf16[192,1024]{1,0:T(8,128)(2,1)}, u32[]{:S(2)}, u32[]{:S(2)}) collective-permute-start(bf16[192,1024]{1,0:T(8,128)(2,1)S(1)} %add_convert_fusion.3.rest_0_), channel_id=1, source_target_pairs={{0,16},{1,17},{2,18},{3,19},{4,20},{5,21},{6,22},{7,23},{8,24},{9,... | collective-permute-start | bytes 1179656 | tf_op jit(solution)/shard_map/ppermute | solution.py:53
  107.9 13.5 %all-to-all-start.3 = ((bf16[16,32,128]{2,1,0:T(8,128)(2,1)}), bf16[16,32,128]{2,1,0:T(8,128)(2,1)S(1)}, u32[]{:S(2)}, u32[]{:S(2)}) async-start(bf16[16,32,128]{2,1,0:T(8,128)(2,1)} %states_after.1), calls=%async_computation.3 | async-start | bytes 262144 | tf_op jit(solution)/shard_map/all_to_all | solution.py:400
  114.1 11.9 %collective-permute-start.32 = (bf16[192,1024]{1,0:T(8,128)(2,1)S(1)}, bf16[192,1024]{1,0:T(8,128)(2,1)}, u32[]{:S(2)}, u32[]{:S(2)}) collective-permute-start(bf16[192,1024]{1,0:T(8,128)(2,1)S(1)} %add_convert_fusion.rest_1_), channel_id=1, source_target_pairs={{0,112},{1,113},{2,114},{3,115},{4,116},{5,117},{6,118},{7,119},{8... | collective-permute-start | bytes 1179656 | tf_op jit(solution)/shard_map/ppermute | solution.py:53
  118.5 10.6 %collective-permute-start.31 = (bf16[192,1024]{1,0:T(8,128)(2,1)S(1)}, bf16[192,1024]{1,0:T(8,128)(2,1)}, u32[]{:S(2)}, u32[]{:S(2)}) collective-permute-start(bf16[192,1024]{1,0:T(8,128)(2,1)S(1)} %add_convert_fusion.2.rest_0_), channel_id=1, source_target_pairs={{0,16},{1,17},{2,18},{3,19},{4,20},{5,21},{6,22},{7,23},{8,24},{9,... | collective-permute-start | bytes 1179656 | tf_op jit(solution)/shard_map/ppermute | solution.py:53
  (27 other events, 144.4 us)

commit v10 on v9

--- a/solution.py
+++ b/solution.py
@@ -446,20 +446,25 @@
         functools.partial(recurrence_kernel, False), slices, "states_before", 1_000_000, 1_000_000,
         (gathered, gathered),
     )
-    own = call(collect_kernel, shape((2 * share, 4 * tokens)), "collect", 0, 800_000, pieces, (befores,))
+    own = call(
+        collect_kernel, shape((2 * share, 4 * tokens)), "collect", 0, 800_000, pieces,
+        (befores, below[1], above[1]),
+    )
     left, right = send(own, X_UP), send(own, X_DOWN)
+    below.append(send(below[1], Z_UP))
+    above.append(send(above[1], Z_DOWN))
+    far_low = send(below[2][:half], Z_UP)
+    far_high = send(above[2][half:], Z_DOWN)
     before = exchange(befores).reshape(HALF_ROWS, HEAD_DIM)
     before_own, before_cross = call(
         functools.partial(spread_kernel, 0), (half_state, half_state), "spread_before",
-        20_000_000_000, 500_000, (key_mine, key_other, key_mine, key_other, before),
+        1_000_000, 500_000, (key_mine, key_other, key_mine, key_other, before), (far_low, far_high),
     )
     before_other = send(before_cross, CORE)
     attended, scores, states = call(
         attended_kernel, (row, row, shape((cols, HEAD_DIM))), "attended", 110_000_000, 2_000_000,
-        (log_decay, queries, key_proj, value_proj, before_own, before_other), (below[1], above[1]),
-    )
-    below.append(send(below[-1], Z_UP))
-    above.append(send(above[-1], Z_DOWN))
+        (log_decay, queries, key_proj, value_proj, before_own, before_other),
+    )
     across = send(attended, CORE)
     neighbour = send(attended, Y_LO)
     opposite = send(left, X_UP)
@@ -469,8 +474,6 @@
         1_000_000, 5_000_000, (own, left, right, opposite),
     )
     diagonal = send(neighbour, CORE)
-    far_low = send(below[2][:half], Z_UP)
-    far_high = send(above[2][half:], Z_DOWN)
 
     weights = [out_weight] + above + [far_low, far_high] + below[::-1]
     kept, theirs, cross, cross_theirs = pl.pallas_call(

time: 132 us -> 134 us (1.015)
  waiting for transfers between devices: 24.9 us -> 32.3 us
  starting transfers between devices: 69.8 us -> 63.9 us
    ppermute x33, waiting for transfers between devices: 19.5 us -> 29.7 us  [send(): return lax.ppermute(array, AXES, table)]
    ppermute x33, starting transfers between devices: 43.2 us -> 37.3 us  [send(): return lax.ppermute(array, AXES, table)]
    all_to_all x4, waiting for transfers between devices: 5.35 us -> 2.62 us  [exchange(): lax.all_to_all(array, 'seq', 0, 0, tiled=True, axis_index_groups=CHIP_GRO...]
    unnamed x44 -> x56, local copies, waits for them, and re-layouts: 4.26 us -> 4.28 us
  transfers between devices with their start and end apart: 37 -> 37, of which waited for: 14 -> 21; matrix products, arithmetic and copies ran while one was open for 5% -> 5% of each run, Pallas kernels for 17% -> 16%
where the time goes in v10:
time: 134 us; the launch traced here: 133 us
  starting transfers between devices  63.9 us (48%)
  waiting for transfers between devices  32.3 us (24%)
  Pallas kernels  24.2 us (18%)
  local copies, waits for them, and re-layouts  6.64 us (5%)
  other arithmetic  4.62 us (3%)
    ppermute x33, starting transfers between devices, send(): return lax.ppermute(array, AXES, table)  37.3 us
    ppermute x33, waiting for transfers between devices, send(): return lax.ppermute(array, AXES, table)  29.7 us
    all_to_all x4, starting transfers between devices, exchange(): lax.all_to_all(array, 'seq', 0, 0, tiled=True, axis_index_groups=CHIP_GRO...  26.6 us
    pallas_call x16, Pallas kernels, call(): pl.pallas_call(body, in_specs=[pl.BlockSpec(a.shape, lambda n=a.ndim: (0,...  17.1 us
    convert_element_type x4, other arithmetic, add_pieces(): return (a.astype(F32) + b.astype(F32)).astype(BF)  4.62 us
    unnamed x56, local copies, waits for them, and re-layouts  4.28 us
    pallas_call x1, Pallas kernels, body(): pl.pallas_call(project_kernel, out_shape=[row32, row32, row, row], scratc...  2.83 us
  transfers between devices with their start and end apart: 37, of which 21 were waited for; matrix products, arithmetic and copies ran while one was open for 5% of the time, Pallas kernels for 16%

profile of v10, /device:TPU:8, one launch (start us, length us, event | category | flops | bytes accessed | tf_op | source)
XLA Modules:
  0.0 132.8 jit_solution(9029424141658800185)
XLA Ops:
  0.6 2.0 %collective-permute-start = (bf16[192,1024]{1,0:T(8,128)(2,1)}, bf16[192,1024]{1,0:T(8,128)(2,1)S(1)}, u32[]{:S(2)}, u32[]{:S(2)}) collective-permute-start(bf16[192,1024]{1,0:T(8,128)(2,1)} %refs_0_.1), channel_id=1, source_target_pairs={{0,16},{1,17},{2,18},{3,19},{4,20},{5,21},{6,22},{7,23},{8,24},{9,... | collective-permute-start | bytes 1179656 | tf_op jit(solution)/shard_map/ppermute | solution.py:53
  2.6 4.0 %collective-permute-start.1 = (bf16[192,1024]{1,0:T(8,128)(2,1)}, bf16[192,1024]{1,0:T(8,128)(2,1)S(1)}, u32[]{:S(2)}, u32[]{:S(2)}) collective-permute-start(bf16[192,1024]{1,0:T(8,128)(2,1)} %refs_0_.1), channel_id=1, source_target_pairs={{0,112},{1,113},{2,114},{3,115},{4,116},{5,117},{6,118},{7,119},{8... | collective-permute-start | bytes 1179656 | tf_op jit(solution)/shard_map/ppermute | solution.py:53
  9.2 2.4 %key_terms.1 = (bf16[528,128]{1,0:T(8,128)(2,1)S(1)}, bf16[528,128]{1,0:T(8,128)(2,1)S(1)}) custom-call(f32[8,128]{1,0:T(8,128)S(1)} %bitcast.5, bf16[128,1024]{1,0:T(8,128)(2,1)S(1)} %copy-done, bf16[128,1024]{1,0:T(8,128)(2,1)S(1)} %copy-done.2), custom_call_target="tpu_custom_call" | custom-call | flops 40000000 | bytes 1000000 | tf_op jit(solution)/shard_map/key_terms/pallas_call | solution.py:418
  13.8 7.2 %all-to-all-start = ((bf16[16,48,128]{2,1,0:T(8,128)(2,1)}), bf16[16,48,128]{2,1,0:T(8,128)(2,1)S(1)}, u32[]{:S(2)}, u32[]{:S(2)}) async-start(bf16[16,48,128]{2,1,0:T(8,128)(2,1)} %merge_keys.1.rest_2_), calls=%async_computation | async-start | bytes 393216 | tf_op jit(solution)/shard_map/all_to_all | solution.py:400
  21.1 1.5 %collective-permute-start.7 = (bf16[192,1024]{1,0:T(8,128)(2,1)S(1)}, bf16[192,1024]{1,0:T(8,128)(2,1)S(1)}, u32[]{:S(2)}, u32[]{:S(2)}) collective-permute-start(bf16[192,1024]{1,0:T(8,128)(2,1)S(1)} %collective-permute-done.rest_0_.refs_8_), channel_id=1, source_target_pairs={{0,16},{1,17},{2,18},{3,19},{4,20},{5,21},{6,22},{7,23},{8,24},{9,... | collective-permute-start | bytes 1179656 | tf_op jit(solution)/shard_map/ppermute | solution.py:53
  22.6 1.8 %collective-permute-start.8 = (bf16[192,1024]{1,0:T(8,128)(2,1)S(1)}, bf16[192,1024]{1,0:T(8,128)(2,1)S(1)}, u32[]{:S(2)}, u32[]{:S(2)}) collective-permute-start(bf16[192,1024]{1,0:T(8,128)(2,1)S(1)} %collective-permute-done.1.rest_1_.refs_1_), channel_id=1, source_target_pairs={{0,112},{1,113},{2,114},{3,115},{4,116},{5,117},{6,118},{7,119},{8... | collective-permute-start | bytes 1179656 | tf_op jit(solution)/shard_map/ppermute | solution.py:53
  25.5 2.8 %collective-permute-start.3 = (bf16[384,128]{1,0:T(8,128)(2,1)S(1)}, bf16[384,128]{1,0:T(8,128)(2,1)S(1)}, u32[]{:S(2)}, u32[]{:S(2)}) collective-permute-start(bf16[384,128]{1,0:T(8,128)(2,1)S(1)} %get-tuple-element.42), channel_id=1, source_target_pairs={{0,0},{1,1},{2,2},{3,3},{4,128},{5,129},{6,130},{7,131},{8,8},{9,9... | collective-permute-start | bytes 294920 | tf_op jit(solution)/shard_map/ppermute | solution.py:53
  28.5 6.1 %collective-permute-done.3.a_ref = bf16[384,128]{1,0:T(8,128)(2,1)S(1)} collective-permute-done((bf16[384,128]{1,0:T(8,128)(2,1)S(1)}, bf16[384,128]{1,0:T(8,128)(2,1)S(1)}, u32[]{:S(2)}, u32[]{:S(2)}) %collective-permute-start.3) | collective-permute-done | bytes 98336 | tf_op jit(solution)/shard_map/ppermute | solution.py:53
  34.6 2.4 %collective-permute-done.7.rest_1_.refs_7_ = bf16[192,1024]{1,0:T(8,128)(2,1)S(1)} collective-permute-done((bf16[192,1024]{1,0:T(8,128)(2,1)S(1)}, bf16[192,1024]{1,0:T(8,128)(2,1)S(1)}, u32[]{:S(2)}, u32[]{:S(2)}) %collective-permute-start.7) | collective-permute-done | bytes 393248 | tf_op jit(solution)/shard_map/ppermute | solution.py:53
  37.0 3.2 %collective-permute-start.12 = (bf16[192,1024]{1,0:T(8,128)(2,1)S(1)}, bf16[192,1024]{1,0:T(8,128)(2,1)}, u32[]{:S(2)}, u32[]{:S(2)}) collective-permute-start(bf16[192,1024]{1,0:T(8,128)(2,1)S(1)} %collective-permute-done.8.rest_2_.refs_2_), channel_id=1, source_target_pairs={{0,112},{1,113},{2,114},{3,115},{4,116},{5,117},{6,118},{7,119},{8... | collective-permute-start | bytes 1179656 | tf_op jit(solution)/shard_map/ppermute | solution.py:53
  42.1 1.6 %collective-permute-start.9 = (bf16[384,512]{1,0:T(8,128)(2,1)S(1)}, bf16[384,512]{1,0:T(8,128)(2,1)S(1)}, u32[]{:S(2)}, u32[]{:S(2)}) collective-permute-start(bf16[384,512]{1,0:T(8,128)(2,1)S(1)} %collect.1.own_ref), channel_id=1, source_target_pairs={{0,1},{1,2},{2,3},{3,0},{4,5},{5,6},{6,7},{7,4},{8,9},{9,10},{10,1... | collective-permute-start | bytes 1179656 | tf_op jit(solution)/shard_map/ppermute | solution.py:53
  43.6 6.4 %all-to-all-start.1 = ((bf16[16,32,128]{2,1,0:T(8,128)(2,1)}), bf16[16,32,128]{2,1,0:T(8,128)(2,1)S(1)}, u32[]{:S(2)}, u32[]{:S(2)}) async-start(bf16[16,32,128]{2,1,0:T(8,128)(2,1)} %states_before.1.rest_0_), calls=%async_computation.1 | async-start | bytes 262144 | tf_op jit(solution)/shard_map/all_to_all | solution.py:400
  50.8 1.5 %collective-permute-start.14 = (bf16[96,1024]{1,0:T(8,128)(2,1)}, bf16[96,1024]{1,0:T(8,128)(2,1)S(1)}, u32[]{:S(2)}, u32[]{:S(2)}) collective-permute-start(bf16[96,1024]{1,0:T(8,128)(2,1)} %slice.8), channel_id=1, source_target_pairs={{0,16},{1,17},{2,18},{3,19},{4,20},{5,21},{6,22},{7,23},{8,24},{9,... | collective-permute-start | bytes 589832 | tf_op jit(solution)/shard_map/ppermute | solution.py:53
  52.2 1.6 %slice.9 = bf16[96,1024]{1,0:T(8,128)(2,1)} slice(bf16[192,1024]{1,0:T(8,128)(2,1)} %collective-permute-done.12.refs_3_), slice={[96:192], [0:1024]} | slice | bytes 393216 | tf_op jit(solution)/shard_map/slice | solution.py:457
  53.8 1.8 %collective-permute-start.15 = (bf16[96,1024]{1,0:T(8,128)(2,1)}, bf16[96,1024]{1,0:T(8,128)(2,1)}, u32[]{:S(2)}, u32[]{:S(2)}) collective-permute-start(bf16[96,1024]{1,0:T(8,128)(2,1)} %slice.9), channel_id=1, source_target_pairs={{0,112},{1,113},{2,114},{3,115},{4,116},{5,117},{6,118},{7,119},{8... | collective-permute-start | bytes 589832 | tf_op jit(solution)/shard_map/ppermute | solution.py:53
  55.6 1.7 %collective-permute-start.10 = (bf16[384,512]{1,0:T(8,128)(2,1)S(1)}, bf16[384,512]{1,0:T(8,128)(2,1)S(1)}, u32[]{:S(2)}, u32[]{:S(2)}) collective-permute-start(bf16[384,512]{1,0:T(8,128)(2,1)S(1)} %collect.1.own_ref), channel_id=1, source_target_pairs={{0,3},{1,0},{2,1},{3,2},{4,7},{5,4},{6,5},{7,6},{8,11},{9,8},{10,9... | collective-permute-start | bytes 1179656 | tf_op jit(solution)/shard_map/ppermute | solution.py:53
  57.7 3.7 %collective-permute-done.14.refs_4_.rest_0_ = bf16[96,1024]{1,0:T(8,128)(2,1)S(1)} collective-permute-done((bf16[96,1024]{1,0:T(8,128)(2,1)}, bf16[96,1024]{1,0:T(8,128)(2,1)S(1)}, u32[]{:S(2)}, u32[]{:S(2)}) %collective-permute-start.14) | collective-permute-done | bytes 196640 | tf_op jit(solution)/shard_map/ppermute | solution.py:53
  67.6 2.7 %collective-permute-done.11.opposite_ref = bf16[384,512]{1,0:T(8,128)(2,1)S(1)} collective-permute-done((bf16[384,512]{1,0:T(8,128)(2,1)S(1)}, bf16[384,512]{1,0:T(8,128)(2,1)S(1)}, u32[]{:S(2)}, u32[]{:S(2)}) %collective-permute-start.11) | collective-permute-done | bytes 393248 | tf_op jit(solution)/shard_map/ppermute | solution.py:53
  70.9 2.8 %project.1 = (f32[128,1024]{1,0:T(8,128)S(1)}, f32[128,1024]{1,0:T(8,128)S(1)}, bf16[128,1024]{1,0:T(8,128)(2,1)S(1)}, bf16[128,1024]{1,0:T(8,128)(2,1)S(1)}) custom-call(bf16[512,1536]{1,0:T(8,128)(2,1)S(1)} %get-tuple-element.44.block_ref, bf16[192,1024]{1,0:T(8,128)(2,1)S(1)} %copy-done.22, bf16[192,1024]{1,0:T(8,128)(2,1)S(1)} %copy-done.26, ...), custom_call_target="tpu_custom_call" | custom-call | flops 1600000000 | bytes 6000000 | tf_op jit(solution)/shard_map/project/pallas_call | solution.py:479
  76.1 1.9 %weight_partial.1 = (bf16[192,1024]{1,0:T(8,128)(2,1)S(1)}, bf16[192,1024]{1,0:T(8,128)(2,1)S(1)}, bf16[192,1024]{1,0:T(8,128)(2,1)S(1)}, bf16[192,1024]{1,0:T(8...) custom-call(bf16[1536,512]{1,0:T(8,128)(2,1)S(1)} %get-tuple-element, ...), custom_call_target="tpu_custom_call" | custom-call | flops 1600000000 | bytes 6000000 | tf_op jit(solution)/shard_map/weight_partial/pallas_call | solution.py:494
  78.1 1.9 %collective-permute-start.23 = (bf16[96,1024]{1,0:T(8,128)(2,1)S(1)}, bf16[96,1024]{1,0:T(8,128)(2,1)S(1)}, u32[]{:S(2)}, u32[]{:S(2)}) collective-permute-start(bf16[96,1024]{1,0:T(8,128)(2,1)S(1)} %get-tuple-element.59), channel_id=1, source_target_pairs={{0,16},{1,17},{2,18},{3,19},{4,20},{5,21},{6,22},{7,23},{8,24},{9,... | collective-permute-start | bytes 589832 | tf_op jit(solution)/shard_map/ppermute | solution.py:53
  81.4 2.5 %collective-permute-done.18.other_ref = bf16[128,1024]{1,0:T(8,128)(2,1)S(1)} collective-permute-done((bf16[128,1024]{1,0:T(8,128)(2,1)S(1)}, bf16[128,1024]{1,0:T(8,128)(2,1)S(1)}, u32[]{:S(2)}, u32[]{:S(2)}) %collective-permute-start.18) | collective-permute-done | bytes 262176 | tf_op jit(solution)/shard_map/ppermute | solution.py:53
  83.9 2.3 %query_terms.1 = (bf16[128,1024]{1,0:T(8,128)(2,1)S(1)}, bf16[512,128]{1,0:T(8,128)(2,1)S(1)}, bf16[512,128]{1,0:T(8,128)(2,1)S(1)}) custom-call(f32[8,128]{1,0:T(8,128)S(1)} %bitcast.7, bf16[128,1024]{1,0:T(8,128)(2,1)S(1)} %copy-done.4, f32[128,1024]{1,0:T(8,128)S(1)} %get-tuple-element.45.own_ref, bf16[128,1024]{1,0:T(8,128)(2,1)S(1)} %collective-permute-done.16.core_ref, ...), custom_call_target="tpu_custom_call" | custom-call | flops 40000000 | bytes 1000000 | tf_op jit(solution)/shard_map/query_terms/pallas_call | solution.py:383
  87.5 2.7 %collective-permute-start.27 = (bf16[192,1024]{1,0:T(8,128)(2,1)S(1)}, bf16[192,1024]{1,0:T(8,128)(2,1)}, u32[]{:S(2)}, u32[]{:S(2)}) collective-permute-start(bf16[192,1024]{1,0:T(8,128)(2,1)S(1)} %get-tuple-element.65), channel_id=1, source_target_pairs={{0,112},{1,113},{2,114},{3,115},{4,116},{5,117},{6,118},{7,119},{8... | collective-permute-start | bytes 1179656 | tf_op jit(solution)/shard_map/ppermute | solution.py:53
  92.8 8.2 %all-to-all-start.2 = ((bf16[16,32,128]{2,1,0:T(8,128)(2,1)}), bf16[16,32,128]{2,1,0:T(8,128)(2,1)S(1)}, u32[]{:S(2)}, u32[]{:S(2)}) async-start(bf16[16,32,128]{2,1,0:T(8,128)(2,1)} %merge_queries.1), calls=%async_computation.2 | async-start | bytes 262144 | tf_op jit(solution)/shard_map/all_to_all | solution.py:400
  102.1 2.8 %collective-permute-start.28 = (bf16[192,1024]{1,0:T(8,128)(2,1)S(1)}, bf16[192,1024]{1,0:T(8,128)(2,1)}, u32[]{:S(2)}, u32[]{:S(2)}) collective-permute-start(bf16[192,1024]{1,0:T(8,128)(2,1)S(1)} %add_convert_fusion.1.rest_1_), channel_id=1, source_target_pairs={{0,112},{1,113},{2,114},{3,115},{4,116},{5,117},{6,118},{7,119},{8... | collective-permute-start | bytes 1179656 | tf_op jit(solution)/shard_map/ppermute | solution.py:53
  106.2 2.6 %all-to-all-done.2.terms_ref = bf16[16,32,128]{2,1,0:T(8,128)(2,1)S(1)} async-done(((bf16[16,32,128]{2,1,0:T(8,128)(2,1)}), bf16[16,32,128]{2,1,0:T(8,128)(2,1)S(1)}, u32[]{:S(2)}, u32[]{:S(2)}) %all-to-all-start.2) | async-done | bytes 131104 | tf_op jit(solution)/shard_map/all_to_all | solution.py:400
  109.5 4.8 %all-to-all-start.3 = ((bf16[16,32,128]{2,1,0:T(8,128)(2,1)}), bf16[16,32,128]{2,1,0:T(8,128)(2,1)S(1)}, u32[]{:S(2)}, u32[]{:S(2)}) async-start(bf16[16,32,128]{2,1,0:T(8,128)(2,1)} %states_after.1), calls=%async_computation.3 | async-start | bytes 262144 | tf_op jit(solution)/shard_map/all_to_all | solution.py:400
  115.7 2.7 %collective-permute-start.32 = (bf16[192,1024]{1,0:T(8,128)(2,1)S(1)}, bf16[192,1024]{1,0:T(8,128)(2,1)}, u32[]{:S(2)}, u32[]{:S(2)}) collective-permute-start(bf16[192,1024]{1,0:T(8,128)(2,1)S(1)} %add_convert_fusion.rest_1_), channel_id=1, source_target_pairs={{0,112},{1,113},{2,114},{3,115},{4,116},{5,117},{6,118},{7,119},{8... | collective-permute-start | bytes 1179656 | tf_op jit(solution)/shard_map/ppermute | solution.py:53
  120.3 2.7 %inner_grads.1 = (bf16[128,1024]{1,0:T(8,128)(2,1)}, f32[128,1024]{1,0:T(8,128)S(1)}, f32[128,1024]{1,0:T(8,128)S(1)}) custom-call(f32[8,128]{1,0:T(8,128)S(1)} %bitcast.8, bf16[128,1024]{1,0:T(8,128)(2,1)S(1)} %copy-done.4, bf16[128,1024]{1,0:T(8,128)(2,1)S(1)} %copy-done.1, bf16[128,1024]{1,0:T(8,128)(2,1)S(1)} %copy-done.3, ...), custom_call_target="tpu_custom_call" | custom-call | flops 200000000 | bytes 3000000 | tf_op jit(solution)/shard_map/inner_grads/pallas_call | solution.py:383
  127.6 3.2 %collective-permute-done.31.up_ref = bf16[192,1024]{1,0:T(8,128)(2,1)} collective-permute-done((bf16[192,1024]{1,0:T(8,128)(2,1)S(1)}, bf16[192,1024]{1,0:T(8,128)(2,1)}, u32[]{:S(2)}, u32[]{:S(2)}) %collective-permute-start.31) | collective-permute-done | bytes 393248 | tf_op jit(solution)/shard_map/ppermute | solution.py:53
  130.8 2.0 %ring_sum_0.1 = bf16[192,1024]{1,0:T(8,128)(2,1)} custom-call(bf16[192,1024]{1,0:T(8,128)(2,1)S(1)} %copy-done.6, bf16[192,1024]{1,0:T(8,128)(2,1)} %collective-permute-done.31.up_ref, bf16[192,1024]{1,0:T(8,128)(2,1)} %collective-permute-done.32.down_ref), custom_call_target="tpu_custom_call" | custom-call | flops 400000 | bytes 2000000 | tf_op jit(solution)/shard_map/ring_sum_0/pallas_call | solution.py:383
  (123 shorter events, 34.1 us)
Async XLA Ops:
  0.6 20.4 %collective-permute-start = (bf16[192,1024]{1,0:T(8,128)(2,1)}, bf16[192,1024]{1,0:T(8,128)(2,1)S(1)}, u32[]{:S(2)}, u32[]{:S(2)}) collective-permute-start(bf16[192,1024]{1,0:T(8,128)(2,1)} %refs_0_.1), channel_id=1, source_target_pairs={{0,16},{1,17},{2,18},{3,19},{4,20},{5,21},{6,22},{7,23},{8,24},{9,... | collective-permute-start | bytes 1179656 | tf_op jit(solution)/shard_map/ppermute | solution.py:53
  2.6 20.0 %collective-permute-start.1 = (bf16[192,1024]{1,0:T(8,128)(2,1)}, bf16[192,1024]{1,0:T(8,128)(2,1)S(1)}, u32[]{:S(2)}, u32[]{:S(2)}) collective-permute-start(bf16[192,1024]{1,0:T(8,128)(2,1)} %refs_0_.1), channel_id=1, source_target_pairs={{0,112},{1,113},{2,114},{3,115},{4,116},{5,117},{6,118},{7,119},{8... | collective-permute-start | bytes 1179656 | tf_op jit(solution)/shard_map/ppermute | solution.py:53
  13.8 26.4 %all-to-all-start = ((bf16[16,48,128]{2,1,0:T(8,128)(2,1)}), bf16[16,48,128]{2,1,0:T(8,128)(2,1)S(1)}, u32[]{:S(2)}, u32[]{:S(2)}) async-start(bf16[16,48,128]{2,1,0:T(8,128)(2,1)} %merge_keys.1.rest_2_), calls=%async_computation | async-start | bytes 393216 | tf_op jit(solution)/shard_map/all_to_all | solution.py:400
  21.1 15.9 %collective-permute-start.7 = (bf16[192,1024]{1,0:T(8,128)(2,1)S(1)}, bf16[192,1024]{1,0:T(8,128)(2,1)S(1)}, u32[]{:S(2)}, u32[]{:S(2)}) collective-permute-start(bf16[192,1024]{1,0:T(8,128)(2,1)S(1)} %collective-permute-done.rest_0_.refs_8_), channel_id=1, source_target_pairs={{0,16},{1,17},{2,18},{3,19},{4,20},{5,21},{6,22},{7,23},{8,24},{9,... | collective-permute-start | bytes 1179656 | tf_op jit(solution)/shard_map/ppermute | solution.py:53
  22.6 14.4 %collective-permute-start.8 = (bf16[192,1024]{1,0:T(8,128)(2,1)S(1)}, bf16[192,1024]{1,0:T(8,128)(2,1)S(1)}, u32[]{:S(2)}, u32[]{:S(2)}) collective-permute-start(bf16[192,1024]{1,0:T(8,128)(2,1)S(1)} %collective-permute-done.1.rest_1_.refs_1_), channel_id=1, source_target_pairs={{0,112},{1,113},{2,114},{3,115},{4,116},{5,117},{6,118},{7,119},{8... | collective-permute-start | bytes 1179656 | tf_op jit(solution)/shard_map/ppermute | solution.py:53
  25.5 9.2 %collective-permute-start.3 = (bf16[384,128]{1,0:T(8,128)(2,1)S(1)}, bf16[384,128]{1,0:T(8,128)(2,1)S(1)}, u32[]{:S(2)}, u32[]{:S(2)}) collective-permute-start(bf16[384,128]{1,0:T(8,128)(2,1)S(1)} %get-tuple-element.42), channel_id=1, source_target_pairs={{0,0},{1,1},{2,2},{3,3},{4,128},{5,129},{6,130},{7,131},{8,8},{9,9... | collective-permute-start | bytes 294920 | tf_op jit(solution)/shard_map/ppermute | solution.py:53
  28.3 12.7 %collective-permute-start.4 = (bf16[384,128]{1,0:T(8,128)(2,1)S(1)}, bf16[384,128]{1,0:T(8,128)(2,1)S(1)}, u32[]{:S(2)}, u32[]{:S(2)}) collective-permute-start(bf16[384,128]{1,0:T(8,128)(2,1)S(1)} %get-tuple-element.42), channel_id=1, source_target_pairs={{0,4},{1,5},{2,6},{3,7},{4,132},{5,133},{6,134},{7,135},{8,12},{9,... | collective-permute-start | bytes 294920 | tf_op jit(solution)/shard_map/ppermute | solution.py:53
  28.4 12.6 %collective-permute-start.5 = (bf16[384,128]{1,0:T(8,128)(2,1)S(1)}, bf16[384,128]{1,0:T(8,128)(2,1)S(1)}, u32[]{:S(2)}, u32[]{:S(2)}) collective-permute-start(bf16[384,128]{1,0:T(8,128)(2,1)S(1)} %get-tuple-element.43), channel_id=1, source_target_pairs={{0,8},{1,9},{2,10},{3,11},{4,136},{5,137},{6,138},{7,139},{8,0},{9... | collective-permute-start | bytes 294920 | tf_op jit(solution)/shard_map/ppermute | solution.py:53
  34.6 6.4 %collective-permute-start.6 = (bf16[384,128]{1,0:T(8,128)(2,1)S(1)}, bf16[384,128]{1,0:T(8,128)(2,1)S(1)}, u32[]{:S(2)}, u32[]{:S(2)}) collective-permute-start(bf16[384,128]{1,0:T(8,128)(2,1)S(1)} %get-tuple-element.43), channel_id=1, source_target_pairs={{0,12},{1,13},{2,14},{3,15},{4,140},{5,141},{6,142},{7,143},{8,4},... | collective-permute-start | bytes 294920 | tf_op jit(solution)/shard_map/ppermute | solution.py:53
  37.0 13.0 %collective-permute-start.13 = (bf16[192,1024]{1,0:T(8,128)(2,1)S(1)}, bf16[192,1024]{1,0:T(8,128)(2,1)S(1)}, u32[]{:S(2)}, u32[]{:S(2)}) collective-permute-start(bf16[192,1024]{1,0:T(8,128)(2,1)S(1)} %collective-permute-done.7.rest_1_.refs_7_), channel_id=1, source_target_pairs={{0,16},{1,17},{2,18},{3,19},{4,20},{5,21},{6,22},{7,23},{8,24},{9,... | collective-permute-start | bytes 1179656 | tf_op jit(solution)/shard_map/ppermute | solution.py:53
  37.0 15.2 %collective-permute-start.12 = (bf16[192,1024]{1,0:T(8,128)(2,1)S(1)}, bf16[192,1024]{1,0:T(8,128)(2,1)}, u32[]{:S(2)}, u32[]{:S(2)}) collective-permute-start(bf16[192,1024]{1,0:T(8,128)(2,1)S(1)} %collective-permute-done.8.rest_2_.refs_2_), channel_id=1, source_target_pairs={{0,112},{1,113},{2,114},{3,115},{4,116},{5,117},{6,118},{7,119},{8... | collective-permute-start | bytes 1179656 | tf_op jit(solution)/shard_map/ppermute | solution.py:53
  42.1 15.3 %collective-permute-start.9 = (bf16[384,512]{1,0:T(8,128)(2,1)S(1)}, bf16[384,512]{1,0:T(8,128)(2,1)S(1)}, u32[]{:S(2)}, u32[]{:S(2)}) collective-permute-start(bf16[384,512]{1,0:T(8,128)(2,1)S(1)} %collect.1.own_ref), channel_id=1, source_target_pairs={{0,1},{1,2},{2,3},{3,0},{4,5},{5,6},{6,7},{7,4},{8,9},{9,10},{10,1... | collective-permute-start | bytes 1179656 | tf_op jit(solution)/shard_map/ppermute | solution.py:53
  43.6 14.0 %all-to-all-start.1 = ((bf16[16,32,128]{2,1,0:T(8,128)(2,1)}), bf16[16,32,128]{2,1,0:T(8,128)(2,1)S(1)}, u32[]{:S(2)}, u32[]{:S(2)}) async-start(bf16[16,32,128]{2,1,0:T(8,128)(2,1)} %states_before.1.rest_0_), calls=%async_computation.1 | async-start | bytes 262144 | tf_op jit(solution)/shard_map/all_to_all | solution.py:400
  50.8 10.6 %collective-permute-start.14 = (bf16[96,1024]{1,0:T(8,128)(2,1)}, bf16[96,1024]{1,0:T(8,128)(2,1)S(1)}, u32[]{:S(2)}, u32[]{:S(2)}) collective-permute-start(bf16[96,1024]{1,0:T(8,128)(2,1)} %slice.8), channel_id=1, source_target_pairs={{0,16},{1,17},{2,18},{3,19},{4,20},{5,21},{6,22},{7,23},{8,24},{9,... | collective-permute-start | bytes 589832 | tf_op jit(solution)/shard_map/ppermute | solution.py:53
  53.8 7.8 %collective-permute-start.15 = (bf16[96,1024]{1,0:T(8,128)(2,1)}, bf16[96,1024]{1,0:T(8,128)(2,1)}, u32[]{:S(2)}, u32[]{:S(2)}) collective-permute-start(bf16[96,1024]{1,0:T(8,128)(2,1)} %slice.9), channel_id=1, source_target_pairs={{0,112},{1,113},{2,114},{3,115},{4,116},{5,117},{6,118},{7,119},{8... | collective-permute-start | bytes 589832 | tf_op jit(solution)/shard_map/ppermute | solution.py:53
  55.6 12.0 %collective-permute-start.10 = (bf16[384,512]{1,0:T(8,128)(2,1)S(1)}, bf16[384,512]{1,0:T(8,128)(2,1)S(1)}, u32[]{:S(2)}, u32[]{:S(2)}) collective-permute-start(bf16[384,512]{1,0:T(8,128)(2,1)S(1)} %collect.1.own_ref), channel_id=1, source_target_pairs={{0,3},{1,0},{2,1},{3,2},{4,7},{5,4},{6,5},{7,6},{8,11},{9,8},{10,9... | collective-permute-start | bytes 1179656 | tf_op jit(solution)/shard_map/ppermute | solution.py:53
  57.4 12.9 %collective-permute-start.11 = (bf16[384,512]{1,0:T(8,128)(2,1)S(1)}, bf16[384,512]{1,0:T(8,128)(2,1)S(1)}, u32[]{:S(2)}, u32[]{:S(2)}) collective-permute-start(bf16[384,512]{1,0:T(8,128)(2,1)S(1)} %collective-permute-done.9.left_ref), channel_id=1, source_target_pairs={{0,1},{1,2},{2,3},{3,0},{4,5},{5,6},{6,7},{7,4},{8,9},{9,10},{10,1... | collective-permute-start | bytes 1179656 | tf_op jit(solution)/shard_map/ppermute | solution.py:53
  66.1 8.5 %collective-permute-start.20 = (bf16[128,1024]{1,0:T(8,128)(2,1)S(1)}, bf16[128,1024]{1,0:T(8,128)(2,1)S(1)}, u32[]{:S(2)}, u32[]{:S(2)}) collective-permute-start(bf16[128,1024]{1,0:T(8,128)(2,1)S(1)} %get-tuple-element.55.own_ref), channel_id=1, source_target_pairs={{0,128},{1,129},{2,130},{3,131},{4,132},{5,133},{6,134},{7,135},{8... | collective-permute-start | bytes 786440 | tf_op jit(solution)/shard_map/ppermute | solution.py:53
  73.8 1.6 %collective-permute-start.17 = (bf16[128,1024]{1,0:T(8,128)(2,1)S(1)}, bf16[128,1024]{1,0:T(8,128)(2,1)S(1)}, u32[]{:S(2)}, u32[]{:S(2)}) collective-permute-start(bf16[128,1024]{1,0:T(8,128)(2,1)S(1)} %get-tuple-element.48), channel_id=1, source_target_pairs={{0,8},{1,9},{2,10},{3,11},{4,12},{5,13},{6,14},{7,15},{8,0},{9,1},... | collective-permute-start | bytes 786440 | tf_op jit(solution)/shard_map/ppermute | solution.py:53
  73.9 2.1 %collective-permute-start.21 = (bf16[128,1024]{1,0:T(8,128)(2,1)S(1)}, bf16[128,1024]{1,0:T(8,128)(2,1)S(1)}, u32[]{:S(2)}, u32[]{:S(2)}) collective-permute-start(bf16[128,1024]{1,0:T(8,128)(2,1)S(1)} %get-tuple-element.55.own_ref), channel_id=1, source_target_pairs={{0,8},{1,9},{2,10},{3,11},{4,12},{5,13},{6,14},{7,15},{8,0},{9,1},... | collective-permute-start | bytes 786440 | tf_op jit(solution)/shard_map/ppermute | solution.py:53
  74.6 6.8 %collective-permute-start.16 = (bf16[128,1024]{1,0:T(8,128)(2,1)S(1)}, bf16[128,1024]{1,0:T(8,128)(2,1)S(1)}, u32[]{:S(2)}, u32[]{:S(2)}) collective-permute-start(bf16[128,1024]{1,0:T(8,128)(2,1)S(1)} %get-tuple-element.46), channel_id=1, source_target_pairs={{0,8},{1,9},{2,10},{3,11},{4,12},{5,13},{6,14},{7,15},{8,0},{9,1},... | collective-permute-start | bytes 786440 | tf_op jit(solution)/shard_map/ppermute | solution.py:53
  75.5 8.4 %collective-permute-start.18 = (bf16[128,1024]{1,0:T(8,128)(2,1)S(1)}, bf16[128,1024]{1,0:T(8,128)(2,1)S(1)}, u32[]{:S(2)}, u32[]{:S(2)}) collective-permute-start(bf16[128,1024]{1,0:T(8,128)(2,1)S(1)} %sum_theirs.1.rest_0_), channel_id=1, source_target_pairs={{0,128},{1,129},{2,130},{3,131},{4,132},{5,133},{6,134},{7,135},{8... | collective-permute-start | bytes 786440 | tf_op jit(solution)/shard_map/ppermute | solution.py:53
  78.1 8.3 %collective-permute-start.23 = (bf16[96,1024]{1,0:T(8,128)(2,1)S(1)}, bf16[96,1024]{1,0:T(8,128)(2,1)S(1)}, u32[]{:S(2)}, u32[]{:S(2)}) collective-permute-start(bf16[96,1024]{1,0:T(8,128)(2,1)S(1)} %get-tuple-element.59), channel_id=1, source_target_pairs={{0,16},{1,17},{2,18},{3,19},{4,20},{5,21},{6,22},{7,23},{8,24},{9,... | collective-permute-start | bytes 589832 | tf_op jit(solution)/shard_map/ppermute | solution.py:53
  80.0 6.7 %collective-permute-start.24 = (bf16[96,1024]{1,0:T(8,128)(2,1)S(1)}, bf16[96,1024]{1,0:T(8,128)(2,1)S(1)}, u32[]{:S(2)}, u32[]{:S(2)}) collective-permute-start(bf16[96,1024]{1,0:T(8,128)(2,1)S(1)} %get-tuple-element.61), channel_id=1, source_target_pairs={{0,112},{1,113},{2,114},{3,115},{4,116},{5,117},{6,118},{7,119},{8... | collective-permute-start | bytes 589832 | tf_op jit(solution)/shard_map/ppermute | solution.py:53
  87.5 13.5 %collective-permute-start.27 = (bf16[192,1024]{1,0:T(8,128)(2,1)S(1)}, bf16[192,1024]{1,0:T(8,128)(2,1)}, u32[]{:S(2)}, u32[]{:S(2)}) collective-permute-start(bf16[192,1024]{1,0:T(8,128)(2,1)S(1)} %get-tuple-element.65), channel_id=1, source_target_pairs={{0,112},{1,113},{2,114},{3,115},{4,116},{5,117},{6,118},{7,119},{8... | collective-permute-start | bytes 1179656 | tf_op jit(solution)/shard_map/ppermute | solution.py:53
  90.2 14.7 %collective-permute-start.25 = (bf16[192,1024]{1,0:T(8,128)(2,1)}, bf16[192,1024]{1,0:T(8,128)(2,1)}, u32[]{:S(2)}, u32[]{:S(2)}) collective-permute-start(bf16[192,1024]{1,0:T(8,128)(2,1)} %get-tuple-element.62), channel_id=1, source_target_pairs={{0,16},{1,17},{2,18},{3,19},{4,20},{5,21},{6,22},{7,23},{8,24},{9,... | collective-permute-start | bytes 1179656 | tf_op jit(solution)/shard_map/ppermute | solution.py:53
  92.8 16.1 %all-to-all-start.2 = ((bf16[16,32,128]{2,1,0:T(8,128)(2,1)}), bf16[16,32,128]{2,1,0:T(8,128)(2,1)S(1)}, u32[]{:S(2)}, u32[]{:S(2)}) async-start(bf16[16,32,128]{2,1,0:T(8,128)(2,1)} %merge_queries.1), calls=%async_computation.2 | async-start | bytes 262144 | tf_op jit(solution)/shard_map/all_to_all | solution.py:400
  102.1 12.5 %collective-permute-start.28 = (bf16[192,1024]{1,0:T(8,128)(2,1)S(1)}, bf16[192,1024]{1,0:T(8,128)(2,1)}, u32[]{:S(2)}, u32[]{:S(2)}) collective-permute-start(bf16[192,1024]{1,0:T(8,128)(2,1)S(1)} %add_convert_fusion.1.rest_1_), channel_id=1, source_target_pairs={{0,112},{1,113},{2,114},{3,115},{4,116},{5,117},{6,118},{7,119},{8... | collective-permute-start | bytes 1179656 | tf_op jit(solution)/shard_map/ppermute | solution.py:53
  106.1 12.9 %collective-permute-start.26 = (bf16[192,1024]{1,0:T(8,128)(2,1)S(1)}, bf16[192,1024]{1,0:T(8,128)(2,1)}, u32[]{:S(2)}, u32[]{:S(2)}) collective-permute-start(bf16[192,1024]{1,0:T(8,128)(2,1)S(1)} %add_convert_fusion.3.rest_0_), channel_id=1, source_target_pairs={{0,16},{1,17},{2,18},{3,19},{4,20},{5,21},{6,22},{7,23},{8,24},{9,... | collective-permute-start | bytes 1179656 | tf_op jit(solution)/shard_map/ppermute | solution.py:53
  109.5 13.5 %all-to-all-start.3 = ((bf16[16,32,128]{2,1,0:T(8,128)(2,1)}), bf16[16,32,128]{2,1,0:T(8,128)(2,1)S(1)}, u32[]{:S(2)}, u32[]{:S(2)}) async-start(bf16[16,32,128]{2,1,0:T(8,128)(2,1)} %states_after.1), calls=%async_computation.3 | async-start | bytes 262144 | tf_op jit(solution)/shard_map/all_to_all | solution.py:400
  115.7 11.9 %collective-permute-start.32 = (bf16[192,1024]{1,0:T(8,128)(2,1)S(1)}, bf16[192,1024]{1,0:T(8,128)(2,1)}, u32[]{:S(2)}, u32[]{:S(2)}) collective-permute-start(bf16[192,1024]{1,0:T(8,128)(2,1)S(1)} %add_convert_fusion.rest_1_), channel_id=1, source_target_pairs={{0,112},{1,113},{2,114},{3,115},{4,116},{5,117},{6,118},{7,119},{8... | collective-permute-start | bytes 1179656 | tf_op jit(solution)/shard_map/ppermute | solution.py:53
  120.2 10.6 %collective-permute-start.31 = (bf16[192,1024]{1,0:T(8,128)(2,1)S(1)}, bf16[192,1024]{1,0:T(8,128)(2,1)}, u32[]{:S(2)}, u32[]{:S(2)}) collective-permute-start(bf16[192,1024]{1,0:T(8,128)(2,1)S(1)} %add_convert_fusion.2.rest_0_), channel_id=1, source_target_pairs={{0,16},{1,17},{2,18},{3,19},{4,20},{5,21},{6,22},{7,23},{8,24},{9,... | collective-permute-start | bytes 1179656 | tf_op jit(solution)/shard_map/ppermute | solution.py:53
  (33 other events, 252.4 us)

commit v11 on v9

--- a/solution.py
+++ b/solution.py
@@ -420,7 +420,7 @@
         in_specs=[pl.BlockSpec(memory_space=pltpu.VMEM)] + [pl.BlockSpec(memory_space=pltpu.HBM)] * 2,
         out_shape=(tagged, tagged),
         scratch_shapes=[pltpu.VMEM((tokens, cols), BF)] * 2 + [pltpu.SemaphoreType.DMA((2,))],
-        compiler_params=PARAMS,
+        compiler_params=pltpu.CompilerParams(vmem_limit_bytes=60 * 1024 * 1024),
         name="key_terms",
         cost_estimate=pl.CostEstimate(flops=40_000_000, bytes_accessed=1_000_000, transcendentals=0),
     )(log_decay, key_proj, value_proj)

time: 132 us -> 133 us (level)
  Pallas kernels: 24.7 us -> 26.8 us
  local copies, waits for them, and re-layouts: 6.14 us -> 4.47 us
    pallas_call x1, Pallas kernels: 2.36 us -> 4.52 us  [body(): pl.pallas_call(key_terms_kernel, in_specs=[pl.BlockSpec(memory_space=pltp...]
    unnamed x44 -> x42, local copies, waits for them, and re-layouts: 4.26 us -> 2.59 us
  transfers between devices with their start and end apart: 37 -> 37, of which waited for: 14 -> 13; matrix products, arithmetic and copies ran while one was open for 5% -> 5% of each run, Pallas kernels for 17% -> 18%
where the time goes in v11:
time: 133 us; the launch traced here: 132 us
  starting transfers between devices  70.1 us (53%)
  Pallas kernels  26.8 us (20%)
  waiting for transfers between devices  24.9 us (19%)
  other arithmetic  4.62 us (3%)
  local copies, waits for them, and re-layouts  4.47 us (3%)
    ppermute x33, starting transfers between devices, send(): return lax.ppermute(array, AXES, table)  43.5 us
    all_to_all x4, starting transfers between devices, exchange(): lax.all_to_all(array, 'seq', 0, 0, tiled=True, axis_index_groups=CHIP_GRO...  26.6 us
    ppermute x33, waiting for transfers between devices, send(): return lax.ppermute(array, AXES, table)  19.6 us
    pallas_call x16, Pallas kernels, call(): pl.pallas_call(body, in_specs=[pl.BlockSpec(a.shape, lambda n=a.ndim: (0,...  17.4 us
    all_to_all x4, waiting for transfers between devices, exchange(): lax.all_to_all(array, 'seq', 0, 0, tiled=True, axis_index_groups=CHIP_GRO...  5.35 us
    convert_element_type x4, other arithmetic, add_pieces(): return (a.astype(F32) + b.astype(F32)).astype(BF)  4.62 us
    pallas_call x1, Pallas kernels, body(): pl.pallas_call(key_terms_kernel, in_specs=[pl.BlockSpec(memory_space=pltp...  4.52 us
    pallas_call x1, Pallas kernels, body(): pl.pallas_call(project_kernel, out_shape=[row32, row32, row, row], scratc...  3.02 us
  transfers between devices with their start and end apart: 37, of which 13 were waited for; matrix products, arithmetic and copies ran while one was open for 5% of the time, Pallas kernels for 18%

profile of v11, /device:TPU:8, one launch (start us, length us, event | category | flops | bytes accessed | tf_op | source)
XLA Modules:
  0.0 132.0 jit_solution(14583501170737960651)
XLA Ops:
  0.6 2.0 %collective-permute-start = (bf16[192,1024]{1,0:T(8,128)(2,1)}, bf16[192,1024]{1,0:T(8,128)(2,1)S(1)}, u32[]{:S(2)}, u32[]{:S(2)}) collective-permute-start(bf16[192,1024]{1,0:T(8,128)(2,1)} %refs_0_.1), channel_id=1, source_target_pairs={{0,16},{1,17},{2,18},{3,19},{4,20},{5,21},{6,22},{7,23},{8,24},{9,... | collective-permute-start | bytes 1179656 | tf_op jit(solution)/shard_map/ppermute | solution.py:53
  2.6 4.0 %collective-permute-start.1 = (bf16[192,1024]{1,0:T(8,128)(2,1)}, bf16[192,1024]{1,0:T(8,128)(2,1)}, u32[]{:S(2)}, u32[]{:S(2)}) collective-permute-start(bf16[192,1024]{1,0:T(8,128)(2,1)} %refs_0_.1), channel_id=1, source_target_pairs={{0,112},{1,113},{2,114},{3,115},{4,116},{5,117},{6,118},{7,119},{8... | collective-permute-start | bytes 1179656 | tf_op jit(solution)/shard_map/ppermute | solution.py:53
  6.7 4.5 %key_terms.1 = (bf16[528,128]{1,0:T(8,128)(2,1)}, bf16[528,128]{1,0:T(8,128)(2,1)}) custom-call(f32[8,128]{1,0:T(8,128)} %bitcast.5, bf16[128,1024]{1,0:T(8,128)(2,1)} %key_ref.5, bf16[128,1024]{1,0:T(8,128)(2,1)} %value_ref.5), custom_call_target="tpu_custom_call" | custom-call | flops 40000000 | bytes 1000000 | tf_op jit(solution)/shard_map/key_terms/pallas_call | solution.py:418
  11.3 1.6 %collective-permute-done.2.other_decay_ref.other_ref = bf16[528,128]{1,0:T(8,128)(2,1)S(1)} collective-permute-done((bf16[528,128]{1,0:T(8,128)(2,1)}, bf16[528,128]{1,0:T(8,128)(2,1)S(1)}, u32[]{:S(2)}, u32[]{:S(2)}) %collective-permute-start.2) | collective-permute-done | bytes 135200 | tf_op jit(solution)/shard_map/ppermute | solution.py:53
  14.5 7.2 %all-to-all-start = ((bf16[16,48,128]{2,1,0:T(8,128)(2,1)}), bf16[16,48,128]{2,1,0:T(8,128)(2,1)S(1)}, u32[]{:S(2)}, u32[]{:S(2)}) async-start(bf16[16,48,128]{2,1,0:T(8,128)(2,1)} %merge_keys.1.rest_2_), calls=%async_computation | async-start | bytes 393216 | tf_op jit(solution)/shard_map/all_to_all | solution.py:400
  23.1 3.0 %collective-permute-start.3 = (bf16[384,128]{1,0:T(8,128)(2,1)S(1)}, bf16[384,128]{1,0:T(8,128)(2,1)S(1)}, u32[]{:S(2)}, u32[]{:S(2)}) collective-permute-start(bf16[384,128]{1,0:T(8,128)(2,1)S(1)} %get-tuple-element.42), channel_id=1, source_target_pairs={{0,0},{1,1},{2,2},{3,3},{4,128},{5,129},{6,130},{7,131},{8,8},{9,9... | collective-permute-start | bytes 294920 | tf_op jit(solution)/shard_map/ppermute | solution.py:53
  26.3 3.2 %collective-permute-start.6 = (bf16[384,128]{1,0:T(8,128)(2,1)S(1)}, bf16[384,128]{1,0:T(8,128)(2,1)S(1)}, u32[]{:S(2)}, u32[]{:S(2)}) collective-permute-start(bf16[384,128]{1,0:T(8,128)(2,1)S(1)} %get-tuple-element.43), channel_id=1, source_target_pairs={{0,12},{1,13},{2,14},{3,15},{4,140},{5,141},{6,142},{7,143},{8,4},... | collective-permute-start | bytes 294920 | tf_op jit(solution)/shard_map/ppermute | solution.py:53
  29.4 1.5 %collective-permute-start.12 = (bf16[192,1024]{1,0:T(8,128)(2,1)S(1)}, bf16[192,1024]{1,0:T(8,128)(2,1)S(1)}, u32[]{:S(2)}, u32[]{:S(2)}) collective-permute-start(bf16[192,1024]{1,0:T(8,128)(2,1)S(1)} %collective-permute-done.rest_0_.refs_8_), channel_id=1, source_target_pairs={{0,16},{1,17},{2,18},{3,19},{4,20},{5,21},{6,22},{7,23},{8,24},{9,... | collective-permute-start | bytes 1179656 | tf_op jit(solution)/shard_map/ppermute | solution.py:53
  31.7 4.5 %collective-permute-start.10 = (bf16[192,1024]{1,0:T(8,128)(2,1)}, bf16[192,1024]{1,0:T(8,128)(2,1)S(1)}, u32[]{:S(2)}, u32[]{:S(2)}) collective-permute-start(bf16[192,1024]{1,0:T(8,128)(2,1)} %collective-permute-done.1.rest_1_.refs_1_), channel_id=1, source_target_pairs={{0,112},{1,113},{2,114},{3,115},{4,116},{5,117},{6,118},{7,119},{8... | collective-permute-start | bytes 1179656 | tf_op jit(solution)/shard_map/ppermute | solution.py:53
  37.2 1.6 %collective-permute-start.7 = (bf16[384,512]{1,0:T(8,128)(2,1)S(1)}, bf16[384,512]{1,0:T(8,128)(2,1)S(1)}, u32[]{:S(2)}, u32[]{:S(2)}) collective-permute-start(bf16[384,512]{1,0:T(8,128)(2,1)S(1)} %collect.1.own_ref), channel_id=1, source_target_pairs={{0,1},{1,2},{2,3},{3,0},{4,5},{5,6},{6,7},{7,4},{8,9},{9,10},{10,1... | collective-permute-start | bytes 1179656 | tf_op jit(solution)/shard_map/ppermute | solution.py:53
  38.8 7.9 %all-to-all-start.1 = ((bf16[16,32,128]{2,1,0:T(8,128)(2,1)}), bf16[16,32,128]{2,1,0:T(8,128)(2,1)S(1)}, u32[]{:S(2)}, u32[]{:S(2)}) async-start(bf16[16,32,128]{2,1,0:T(8,128)(2,1)} %states_before.1.rest_0_), calls=%async_computation.1 | async-start | bytes 262144 | tf_op jit(solution)/shard_map/all_to_all | solution.py:400
  46.7 1.7 %collective-permute-start.8 = (bf16[384,512]{1,0:T(8,128)(2,1)S(1)}, bf16[384,512]{1,0:T(8,128)(2,1)S(1)}, u32[]{:S(2)}, u32[]{:S(2)}) collective-permute-start(bf16[384,512]{1,0:T(8,128)(2,1)S(1)} %collect.1.own_ref), channel_id=1, source_target_pairs={{0,3},{1,0},{2,1},{3,2},{4,7},{5,4},{6,5},{7,6},{8,11},{9,8},{10,9... | collective-permute-start | bytes 1179656 | tf_op jit(solution)/shard_map/ppermute | solution.py:53
  48.5 1.5 %collective-permute-start.13 = (bf16[192,1024]{1,0:T(8,128)(2,1)S(1)}, bf16[192,1024]{1,0:T(8,128)(2,1)}, u32[]{:S(2)}, u32[]{:S(2)}) collective-permute-start(bf16[192,1024]{1,0:T(8,128)(2,1)S(1)} %collective-permute-done.12.refs_7_.rest_0_), channel_id=1, source_target_pairs={{0,16},{1,17},{2,18},{3,19},{4,20},{5,21},{6,22},{7,23},{8,24},{9,... | collective-permute-start | bytes 1179656 | tf_op jit(solution)/shard_map/ppermute | solution.py:53
  49.9 1.8 %collective-permute-start.11 = (bf16[192,1024]{1,0:T(8,128)(2,1)S(1)}, bf16[192,1024]{1,0:T(8,128)(2,1)}, u32[]{:S(2)}, u32[]{:S(2)}) collective-permute-start(bf16[192,1024]{1,0:T(8,128)(2,1)S(1)} %collective-permute-done.10.refs_2_.rest_1_), channel_id=1, source_target_pairs={{0,112},{1,113},{2,114},{3,115},{4,116},{5,117},{6,118},{7,119},{8... | collective-permute-start | bytes 1179656 | tf_op jit(solution)/shard_map/ppermute | solution.py:53
  52.0 2.7 %all-to-all-done.1 = bf16[16,32,128]{2,1,0:T(8,128)(2,1)S(1)} async-done(((bf16[16,32,128]{2,1,0:T(8,128)(2,1)}), bf16[16,32,128]{2,1,0:T(8,128)(2,1)S(1)}, u32[]{:S(2)}, u32[]{:S(2)}) %all-to-all-start.1) | async-done | bytes 131104 | tf_op jit(solution)/shard_map/all_to_all | solution.py:400
  55.0 6.6 %collective-permute-done.13.refs_6_ = bf16[192,1024]{1,0:T(8,128)(2,1)} collective-permute-done((bf16[192,1024]{1,0:T(8,128)(2,1)S(1)}, bf16[192,1024]{1,0:T(8,128)(2,1)}, u32[]{:S(2)}, u32[]{:S(2)}) %collective-permute-start.13) | collective-permute-done | bytes 393248 | tf_op jit(solution)/shard_map/ppermute | solution.py:53
  63.8 3.3 %collective-permute-start.15 = (bf16[96,1024]{1,0:T(8,128)(2,1)S(1)}, bf16[96,1024]{1,0:T(8,128)(2,1)S(1)}, u32[]{:S(2)}, u32[]{:S(2)}) collective-permute-start(bf16[96,1024]{1,0:T(8,128)(2,1)S(1)} %slice.9), channel_id=1, source_target_pairs={{0,112},{1,113},{2,114},{3,115},{4,116},{5,117},{6,118},{7,119},{8... | collective-permute-start | bytes 589832 | tf_op jit(solution)/shard_map/ppermute | solution.py:53
  69.5 1.6 %assemble.1 = (bf16[1536,512]{1,0:T(8,128)(2,1)S(1)}, bf16[512,1536]{1,0:T(8,128)(2,1)S(1)}) custom-call(bf16[384,512]{1,0:T(8,128)(2,1)S(1)} %collect.1.own_ref, bf16[384,512]{1,0:T(8,128)(2,1)S(1)} %collective-permute-done.7.left_ref, bf16[384,512]{1,0:T(8,128)(2,1)S(1)} %collective-permute-done.8.right_ref, ...), custom_call_target="tpu_custom_call" | custom-call | flops 1000000 | bytes 5000000 | tf_op jit(solution)/shard_map/assemble/pallas_call | solution.py:383
  71.2 3.0 %project.1 = (f32[128,1024]{1,0:T(8,128)S(1)}, f32[128,1024]{1,0:T(8,128)S(1)}, bf16[128,1024]{1,0:T(8,128)(2,1)S(1)}, bf16[128,1024]{1,0:T(8,128)(2,1)S(1)}) custom-call(bf16[512,1536]{1,0:T(8,128)(2,1)S(1)} %get-tuple-element.44.block_ref, bf16[192,1024]{1,0:T(8,128)(2,1)S(1)} %copy-done.17, bf16[192,1024]{1,0:T(8,128)(2,1)} %collective-permute-done.1.rest_1_.refs_1_, ...), custom_call_target="tpu_custom_call" | custom-call | flops 1600000000 | bytes 6000000 | tf_op jit(solution)/shard_map/project/pallas_call | solution.py:476
  77.5 1.9 %weight_partial.1 = (bf16[192,1024]{1,0:T(8,128)(2,1)S(1)}, bf16[192,1024]{1,0:T(8,128)(2,1)S(1)}, bf16[192,1024]{1,0:T(8,128)(2,1)S(1)}, bf16[192,1024]{1,0:T(8...) custom-call(bf16[1536,512]{1,0:T(8,128)(2,1)S(1)} %get-tuple-element, ...), custom_call_target="tpu_custom_call" | custom-call | flops 1600000000 | bytes 6000000 | tf_op jit(solution)/shard_map/weight_partial/pallas_call | solution.py:491
  79.5 3.2 %collective-permute-start.24 = (bf16[96,1024]{1,0:T(8,128)(2,1)S(1)}, bf16[96,1024]{1,0:T(8,128)(2,1)S(1)}, u32[]{:S(2)}, u32[]{:S(2)}) collective-permute-start(bf16[96,1024]{1,0:T(8,128)(2,1)S(1)} %get-tuple-element.61), channel_id=1, source_target_pairs={{0,112},{1,113},{2,114},{3,115},{4,116},{5,117},{6,118},{7,119},{8... | collective-permute-start | bytes 589832 | tf_op jit(solution)/shard_map/ppermute | solution.py:53
  82.8 2.1 %collective-permute-done.18.other_ref = bf16[128,1024]{1,0:T(8,128)(2,1)S(1)} collective-permute-done((bf16[128,1024]{1,0:T(8,128)(2,1)S(1)}, bf16[128,1024]{1,0:T(8,128)(2,1)S(1)}, u32[]{:S(2)}, u32[]{:S(2)}) %collective-permute-start.18) | collective-permute-done | bytes 262176 | tf_op jit(solution)/shard_map/ppermute | solution.py:53
  84.8 2.3 %query_terms.1 = (bf16[128,1024]{1,0:T(8,128)(2,1)S(1)}, bf16[512,128]{1,0:T(8,128)(2,1)S(1)}, bf16[512,128]{1,0:T(8,128)(2,1)S(1)}) custom-call(f32[8,128]{1,0:T(8,128)S(1)} %bitcast.7, bf16[128,1024]{1,0:T(8,128)(2,1)S(1)} %copy-done.2, f32[128,1024]{1,0:T(8,128)S(1)} %get-tuple-element.45.own_ref, bf16[128,1024]{1,0:T(8,128)(2,1)S(1)} %collective-permute-done.16.core_ref, ...), custom_call_target="tpu_custom_call" | custom-call | flops 40000000 | bytes 1000000 | tf_op jit(solution)/shard_map/query_terms/pallas_call | solution.py:383
  88.5 2.9 %collective-permute-start.27 = (bf16[192,1024]{1,0:T(8,128)(2,1)S(1)}, bf16[192,1024]{1,0:T(8,128)(2,1)}, u32[]{:S(2)}, u32[]{:S(2)}) collective-permute-start(bf16[192,1024]{1,0:T(8,128)(2,1)S(1)} %get-tuple-element.65), channel_id=1, source_target_pairs={{0,112},{1,113},{2,114},{3,115},{4,116},{5,117},{6,118},{7,119},{8... | collective-permute-start | bytes 1179656 | tf_op jit(solution)/shard_map/ppermute | solution.py:53
  93.5 6.6 %all-to-all-start.2 = ((bf16[16,32,128]{2,1,0:T(8,128)(2,1)}), bf16[16,32,128]{2,1,0:T(8,128)(2,1)S(1)}, u32[]{:S(2)}, u32[]{:S(2)}) async-start(bf16[16,32,128]{2,1,0:T(8,128)(2,1)} %merge_queries.1), calls=%async_computation.2 | async-start | bytes 262144 | tf_op jit(solution)/shard_map/all_to_all | solution.py:400
  101.3 2.8 %collective-permute-start.28 = (bf16[192,1024]{1,0:T(8,128)(2,1)S(1)}, bf16[192,1024]{1,0:T(8,128)(2,1)}, u32[]{:S(2)}, u32[]{:S(2)}) collective-permute-start(bf16[192,1024]{1,0:T(8,128)(2,1)S(1)} %add_convert_fusion.1.rest_1_), channel_id=1, source_target_pairs={{0,112},{1,113},{2,114},{3,115},{4,116},{5,117},{6,118},{7,119},{8... | collective-permute-start | bytes 1179656 | tf_op jit(solution)/shard_map/ppermute | solution.py:53
  105.4 2.6 %all-to-all-done.2.terms_ref = bf16[16,32,128]{2,1,0:T(8,128)(2,1)S(1)} async-done(((bf16[16,32,128]{2,1,0:T(8,128)(2,1)}), bf16[16,32,128]{2,1,0:T(8,128)(2,1)S(1)}, u32[]{:S(2)}, u32[]{:S(2)}) %all-to-all-start.2) | async-done | bytes 131104 | tf_op jit(solution)/shard_map/all_to_all | solution.py:400
  108.7 4.8 %all-to-all-start.3 = ((bf16[16,32,128]{2,1,0:T(8,128)(2,1)}), bf16[16,32,128]{2,1,0:T(8,128)(2,1)S(1)}, u32[]{:S(2)}, u32[]{:S(2)}) async-start(bf16[16,32,128]{2,1,0:T(8,128)(2,1)} %states_after.1), calls=%async_computation.3 | async-start | bytes 262144 | tf_op jit(solution)/shard_map/all_to_all | solution.py:400
  114.9 2.7 %collective-permute-start.32 = (bf16[192,1024]{1,0:T(8,128)(2,1)S(1)}, bf16[192,1024]{1,0:T(8,128)(2,1)}, u32[]{:S(2)}, u32[]{:S(2)}) collective-permute-start(bf16[192,1024]{1,0:T(8,128)(2,1)S(1)} %add_convert_fusion.rest_1_), channel_id=1, source_target_pairs={{0,112},{1,113},{2,114},{3,115},{4,116},{5,117},{6,118},{7,119},{8... | collective-permute-start | bytes 1179656 | tf_op jit(solution)/shard_map/ppermute | solution.py:53
  119.5 2.7 %inner_grads.1 = (bf16[128,1024]{1,0:T(8,128)(2,1)}, f32[128,1024]{1,0:T(8,128)S(1)}, f32[128,1024]{1,0:T(8,128)S(1)}) custom-call(f32[8,128]{1,0:T(8,128)S(1)} %bitcast.8, bf16[128,1024]{1,0:T(8,128)(2,1)S(1)} %copy-done.2, bf16[128,1024]{1,0:T(8,128)(2,1)S(1)} %copy-done, bf16[128,1024]{1,0:T(8,128)(2,1)S(1)} %copy-done.1, ...), custom_call_target="tpu_custom_call" | custom-call | flops 200000000 | bytes 3000000 | tf_op jit(solution)/shard_map/inner_grads/pallas_call | solution.py:383
  126.8 3.2 %collective-permute-done.31.up_ref = bf16[192,1024]{1,0:T(8,128)(2,1)} collective-permute-done((bf16[192,1024]{1,0:T(8,128)(2,1)S(1)}, bf16[192,1024]{1,0:T(8,128)(2,1)}, u32[]{:S(2)}, u32[]{:S(2)}) %collective-permute-start.31) | collective-permute-done | bytes 393248 | tf_op jit(solution)/shard_map/ppermute | solution.py:53
  130.0 2.0 %ring_sum_0.1 = bf16[192,1024]{1,0:T(8,128)(2,1)} custom-call(bf16[192,1024]{1,0:T(8,128)(2,1)S(1)} %copy-done.6, bf16[192,1024]{1,0:T(8,128)(2,1)} %collective-permute-done.31.up_ref, bf16[192,1024]{1,0:T(8,128)(2,1)} %collective-permute-done.32.down_ref), custom_call_target="tpu_custom_call" | custom-call | flops 400000 | bytes 2000000 | tf_op jit(solution)/shard_map/ring_sum_0/pallas_call | solution.py:383
  (109 shorter events, 27.8 us)
Async XLA Ops:
  0.6 21.1 %collective-permute-start = (bf16[192,1024]{1,0:T(8,128)(2,1)}, bf16[192,1024]{1,0:T(8,128)(2,1)S(1)}, u32[]{:S(2)}, u32[]{:S(2)}) collective-permute-start(bf16[192,1024]{1,0:T(8,128)(2,1)} %refs_0_.1), channel_id=1, source_target_pairs={{0,16},{1,17},{2,18},{3,19},{4,20},{5,21},{6,22},{7,23},{8,24},{9,... | collective-permute-start | bytes 1179656 | tf_op jit(solution)/shard_map/ppermute | solution.py:53
  2.6 19.1 %collective-permute-start.1 = (bf16[192,1024]{1,0:T(8,128)(2,1)}, bf16[192,1024]{1,0:T(8,128)(2,1)}, u32[]{:S(2)}, u32[]{:S(2)}) collective-permute-start(bf16[192,1024]{1,0:T(8,128)(2,1)} %refs_0_.1), channel_id=1, source_target_pairs={{0,112},{1,113},{2,114},{3,115},{4,116},{5,117},{6,118},{7,119},{8... | collective-permute-start | bytes 1179656 | tf_op jit(solution)/shard_map/ppermute | solution.py:53
  14.5 16.4 %all-to-all-start = ((bf16[16,48,128]{2,1,0:T(8,128)(2,1)}), bf16[16,48,128]{2,1,0:T(8,128)(2,1)S(1)}, u32[]{:S(2)}, u32[]{:S(2)}) async-start(bf16[16,48,128]{2,1,0:T(8,128)(2,1)} %merge_keys.1.rest_2_), calls=%async_computation | async-start | bytes 393216 | tf_op jit(solution)/shard_map/all_to_all | solution.py:400
  23.1 8.6 %collective-permute-start.3 = (bf16[384,128]{1,0:T(8,128)(2,1)S(1)}, bf16[384,128]{1,0:T(8,128)(2,1)S(1)}, u32[]{:S(2)}, u32[]{:S(2)}) collective-permute-start(bf16[384,128]{1,0:T(8,128)(2,1)S(1)} %get-tuple-element.42), channel_id=1, source_target_pairs={{0,0},{1,1},{2,2},{3,3},{4,128},{5,129},{6,130},{7,131},{8,8},{9,9... | collective-permute-start | bytes 294920 | tf_op jit(solution)/shard_map/ppermute | solution.py:53
  26.1 10.1 %collective-permute-start.4 = (bf16[384,128]{1,0:T(8,128)(2,1)S(1)}, bf16[384,128]{1,0:T(8,128)(2,1)S(1)}, u32[]{:S(2)}, u32[]{:S(2)}) collective-permute-start(bf16[384,128]{1,0:T(8,128)(2,1)S(1)} %get-tuple-element.42), channel_id=1, source_target_pairs={{0,4},{1,5},{2,6},{3,7},{4,132},{5,133},{6,134},{7,135},{8,12},{9,... | collective-permute-start | bytes 294920 | tf_op jit(solution)/shard_map/ppermute | solution.py:53
  26.2 10.0 %collective-permute-start.5 = (bf16[384,128]{1,0:T(8,128)(2,1)S(1)}, bf16[384,128]{1,0:T(8,128)(2,1)S(1)}, u32[]{:S(2)}, u32[]{:S(2)}) collective-permute-start(bf16[384,128]{1,0:T(8,128)(2,1)S(1)} %get-tuple-element.43), channel_id=1, source_target_pairs={{0,8},{1,9},{2,10},{3,11},{4,136},{5,137},{6,138},{7,139},{8,0},{9... | collective-permute-start | bytes 294920 | tf_op jit(solution)/shard_map/ppermute | solution.py:53
  26.3 9.9 %collective-permute-start.6 = (bf16[384,128]{1,0:T(8,128)(2,1)S(1)}, bf16[384,128]{1,0:T(8,128)(2,1)S(1)}, u32[]{:S(2)}, u32[]{:S(2)}) collective-permute-start(bf16[384,128]{1,0:T(8,128)(2,1)S(1)} %get-tuple-element.43), channel_id=1, source_target_pairs={{0,12},{1,13},{2,14},{3,15},{4,140},{5,141},{6,142},{7,143},{8,4},... | collective-permute-start | bytes 294920 | tf_op jit(solution)/shard_map/ppermute | solution.py:53
  29.4 19.0 %collective-permute-start.12 = (bf16[192,1024]{1,0:T(8,128)(2,1)S(1)}, bf16[192,1024]{1,0:T(8,128)(2,1)S(1)}, u32[]{:S(2)}, u32[]{:S(2)}) collective-permute-start(bf16[192,1024]{1,0:T(8,128)(2,1)S(1)} %collective-permute-done.rest_0_.refs_8_), channel_id=1, source_target_pairs={{0,16},{1,17},{2,18},{3,19},{4,20},{5,21},{6,22},{7,23},{8,24},{9,... | collective-permute-start | bytes 1179656 | tf_op jit(solution)/shard_map/ppermute | solution.py:53
  31.7 18.3 %collective-permute-start.10 = (bf16[192,1024]{1,0:T(8,128)(2,1)}, bf16[192,1024]{1,0:T(8,128)(2,1)S(1)}, u32[]{:S(2)}, u32[]{:S(2)}) collective-permute-start(bf16[192,1024]{1,0:T(8,128)(2,1)} %collective-permute-done.1.rest_1_.refs_1_), channel_id=1, source_target_pairs={{0,112},{1,113},{2,114},{3,115},{4,116},{5,117},{6,118},{7,119},{8... | collective-permute-start | bytes 1179656 | tf_op jit(solution)/shard_map/ppermute | solution.py:53
  37.2 14.5 %collective-permute-start.7 = (bf16[384,512]{1,0:T(8,128)(2,1)S(1)}, bf16[384,512]{1,0:T(8,128)(2,1)S(1)}, u32[]{:S(2)}, u32[]{:S(2)}) collective-permute-start(bf16[384,512]{1,0:T(8,128)(2,1)S(1)} %collect.1.own_ref), channel_id=1, source_target_pairs={{0,1},{1,2},{2,3},{3,0},{4,5},{5,6},{6,7},{7,4},{8,9},{9,10},{10,1... | collective-permute-start | bytes 1179656 | tf_op jit(solution)/shard_map/ppermute | solution.py:53
  38.8 15.9 %all-to-all-start.1 = ((bf16[16,32,128]{2,1,0:T(8,128)(2,1)}), bf16[16,32,128]{2,1,0:T(8,128)(2,1)S(1)}, u32[]{:S(2)}, u32[]{:S(2)}) async-start(bf16[16,32,128]{2,1,0:T(8,128)(2,1)} %states_before.1.rest_0_), calls=%async_computation.1 | async-start | bytes 262144 | tf_op jit(solution)/shard_map/all_to_all | solution.py:400
  46.7 22.8 %collective-permute-start.8 = (bf16[384,512]{1,0:T(8,128)(2,1)S(1)}, bf16[384,512]{1,0:T(8,128)(2,1)S(1)}, u32[]{:S(2)}, u32[]{:S(2)}) collective-permute-start(bf16[384,512]{1,0:T(8,128)(2,1)S(1)} %collect.1.own_ref), channel_id=1, source_target_pairs={{0,3},{1,0},{2,1},{3,2},{4,7},{5,4},{6,5},{7,6},{8,11},{9,8},{10,9... | collective-permute-start | bytes 1179656 | tf_op jit(solution)/shard_map/ppermute | solution.py:53
  48.5 13.1 %collective-permute-start.13 = (bf16[192,1024]{1,0:T(8,128)(2,1)S(1)}, bf16[192,1024]{1,0:T(8,128)(2,1)}, u32[]{:S(2)}, u32[]{:S(2)}) collective-permute-start(bf16[192,1024]{1,0:T(8,128)(2,1)S(1)} %collective-permute-done.12.refs_7_.rest_0_), channel_id=1, source_target_pairs={{0,16},{1,17},{2,18},{3,19},{4,20},{5,21},{6,22},{7,23},{8,24},{9,... | collective-permute-start | bytes 1179656 | tf_op jit(solution)/shard_map/ppermute | solution.py:53
  49.9 12.9 %collective-permute-start.11 = (bf16[192,1024]{1,0:T(8,128)(2,1)S(1)}, bf16[192,1024]{1,0:T(8,128)(2,1)}, u32[]{:S(2)}, u32[]{:S(2)}) collective-permute-start(bf16[192,1024]{1,0:T(8,128)(2,1)S(1)} %collective-permute-done.10.refs_2_.rest_1_), channel_id=1, source_target_pairs={{0,112},{1,113},{2,114},{3,115},{4,116},{5,117},{6,118},{7,119},{8... | collective-permute-start | bytes 1179656 | tf_op jit(solution)/shard_map/ppermute | solution.py:53
  51.7 17.8 %collective-permute-start.9 = (bf16[384,512]{1,0:T(8,128)(2,1)S(1)}, bf16[384,512]{1,0:T(8,128)(2,1)}, u32[]{:S(2)}, u32[]{:S(2)}) collective-permute-start(bf16[384,512]{1,0:T(8,128)(2,1)S(1)} %collective-permute-done.7.left_ref), channel_id=1, source_target_pairs={{0,1},{1,2},{2,3},{3,0},{4,5},{5,6},{6,7},{7,4},{8,9},{9,10},{10,1... | collective-permute-start | bytes 1179656 | tf_op jit(solution)/shard_map/ppermute | solution.py:53
  54.9 12.2 %collective-permute-start.19 = (bf16[512,128]{1,0:T(8,128)(2,1)S(1)}, bf16[512,128]{1,0:T(8,128)(2,1)S(1)}, u32[]{:S(2)}, u32[]{:S(2)}) collective-permute-start(bf16[512,128]{1,0:T(8,128)(2,1)S(1)} %get-tuple-element.51), channel_id=1, source_target_pairs={{0,8},{1,9},{2,10},{3,11},{4,12},{5,13},{6,14},{7,15},{8,0},{9,1},... | collective-permute-start | bytes 393224 | tf_op jit(solution)/shard_map/ppermute | solution.py:53
  62.5 8.6 %collective-permute-start.14 = (bf16[96,1024]{1,0:T(8,128)(2,1)S(1)}, bf16[96,1024]{1,0:T(8,128)(2,1)S(1)}, u32[]{:S(2)}, u32[]{:S(2)}) collective-permute-start(bf16[96,1024]{1,0:T(8,128)(2,1)S(1)} %slice.8), channel_id=1, source_target_pairs={{0,16},{1,17},{2,18},{3,19},{4,20},{5,21},{6,22},{7,23},{8,24},{9,... | collective-permute-start | bytes 589832 | tf_op jit(solution)/shard_map/ppermute | solution.py:53
  63.8 7.4 %collective-permute-start.15 = (bf16[96,1024]{1,0:T(8,128)(2,1)S(1)}, bf16[96,1024]{1,0:T(8,128)(2,1)S(1)}, u32[]{:S(2)}, u32[]{:S(2)}) collective-permute-start(bf16[96,1024]{1,0:T(8,128)(2,1)S(1)} %slice.9), channel_id=1, source_target_pairs={{0,112},{1,113},{2,114},{3,115},{4,116},{5,117},{6,118},{7,119},{8... | collective-permute-start | bytes 589832 | tf_op jit(solution)/shard_map/ppermute | solution.py:53
  69.0 7.0 %collective-permute-start.20 = (bf16[128,1024]{1,0:T(8,128)(2,1)S(1)}, bf16[128,1024]{1,0:T(8,128)(2,1)S(1)}, u32[]{:S(2)}, u32[]{:S(2)}) collective-permute-start(bf16[128,1024]{1,0:T(8,128)(2,1)S(1)} %get-tuple-element.55.own_ref), channel_id=1, source_target_pairs={{0,128},{1,129},{2,130},{3,131},{4,132},{5,133},{6,134},{7,135},{8... | collective-permute-start | bytes 786440 | tf_op jit(solution)/shard_map/ppermute | solution.py:53
  74.3 3.2 %collective-permute-start.21 = (bf16[128,1024]{1,0:T(8,128)(2,1)S(1)}, bf16[128,1024]{1,0:T(8,128)(2,1)S(1)}, u32[]{:S(2)}, u32[]{:S(2)}) collective-permute-start(bf16[128,1024]{1,0:T(8,128)(2,1)S(1)} %get-tuple-element.55.own_ref), channel_id=1, source_target_pairs={{0,8},{1,9},{2,10},{3,11},{4,12},{5,13},{6,14},{7,15},{8,0},{9,1},... | collective-permute-start | bytes 786440 | tf_op jit(solution)/shard_map/ppermute | solution.py:53
  76.0 6.8 %collective-permute-start.16 = (bf16[128,1024]{1,0:T(8,128)(2,1)S(1)}, bf16[128,1024]{1,0:T(8,128)(2,1)S(1)}, u32[]{:S(2)}, u32[]{:S(2)}) collective-permute-start(bf16[128,1024]{1,0:T(8,128)(2,1)S(1)} %get-tuple-element.46), channel_id=1, source_target_pairs={{0,8},{1,9},{2,10},{3,11},{4,12},{5,13},{6,14},{7,15},{8,0},{9,1},... | collective-permute-start | bytes 786440 | tf_op jit(solution)/shard_map/ppermute | solution.py:53
  76.5 8.3 %collective-permute-start.18 = (bf16[128,1024]{1,0:T(8,128)(2,1)S(1)}, bf16[128,1024]{1,0:T(8,128)(2,1)S(1)}, u32[]{:S(2)}, u32[]{:S(2)}) collective-permute-start(bf16[128,1024]{1,0:T(8,128)(2,1)S(1)} %sum_theirs.1.rest_0_), channel_id=1, source_target_pairs={{0,128},{1,129},{2,130},{3,131},{4,132},{5,133},{6,134},{7,135},{8... | collective-permute-start | bytes 786440 | tf_op jit(solution)/shard_map/ppermute | solution.py:53
  79.5 8.2 %collective-permute-start.23 = (bf16[96,1024]{1,0:T(8,128)(2,1)S(1)}, bf16[96,1024]{1,0:T(8,128)(2,1)S(1)}, u32[]{:S(2)}, u32[]{:S(2)}) collective-permute-start(bf16[96,1024]{1,0:T(8,128)(2,1)S(1)} %get-tuple-element.59), channel_id=1, source_target_pairs={{0,16},{1,17},{2,18},{3,19},{4,20},{5,21},{6,22},{7,23},{8,24},{9,... | collective-permute-start | bytes 589832 | tf_op jit(solution)/shard_map/ppermute | solution.py:53
  79.5 8.1 %collective-permute-start.24 = (bf16[96,1024]{1,0:T(8,128)(2,1)S(1)}, bf16[96,1024]{1,0:T(8,128)(2,1)S(1)}, u32[]{:S(2)}, u32[]{:S(2)}) collective-permute-start(bf16[96,1024]{1,0:T(8,128)(2,1)S(1)} %get-tuple-element.61), channel_id=1, source_target_pairs={{0,112},{1,113},{2,114},{3,115},{4,116},{5,117},{6,118},{7,119},{8... | collective-permute-start | bytes 589832 | tf_op jit(solution)/shard_map/ppermute | solution.py:53
  88.5 11.6 %collective-permute-start.27 = (bf16[192,1024]{1,0:T(8,128)(2,1)S(1)}, bf16[192,1024]{1,0:T(8,128)(2,1)}, u32[]{:S(2)}, u32[]{:S(2)}) collective-permute-start(bf16[192,1024]{1,0:T(8,128)(2,1)S(1)} %get-tuple-element.65), channel_id=1, source_target_pairs={{0,112},{1,113},{2,114},{3,115},{4,116},{5,117},{6,118},{7,119},{8... | collective-permute-start | bytes 1179656 | tf_op jit(solution)/shard_map/ppermute | solution.py:53
  91.5 12.6 %collective-permute-start.25 = (bf16[192,1024]{1,0:T(8,128)(2,1)}, bf16[192,1024]{1,0:T(8,128)(2,1)}, u32[]{:S(2)}, u32[]{:S(2)}) collective-permute-start(bf16[192,1024]{1,0:T(8,128)(2,1)} %get-tuple-element.62), channel_id=1, source_target_pairs={{0,16},{1,17},{2,18},{3,19},{4,20},{5,21},{6,22},{7,23},{8,24},{9,... | collective-permute-start | bytes 1179656 | tf_op jit(solution)/shard_map/ppermute | solution.py:53
  93.5 14.4 %all-to-all-start.2 = ((bf16[16,32,128]{2,1,0:T(8,128)(2,1)}), bf16[16,32,128]{2,1,0:T(8,128)(2,1)S(1)}, u32[]{:S(2)}, u32[]{:S(2)}) async-start(bf16[16,32,128]{2,1,0:T(8,128)(2,1)} %merge_queries.1), calls=%async_computation.2 | async-start | bytes 262144 | tf_op jit(solution)/shard_map/all_to_all | solution.py:400
  101.3 12.5 %collective-permute-start.28 = (bf16[192,1024]{1,0:T(8,128)(2,1)S(1)}, bf16[192,1024]{1,0:T(8,128)(2,1)}, u32[]{:S(2)}, u32[]{:S(2)}) collective-permute-start(bf16[192,1024]{1,0:T(8,128)(2,1)S(1)} %add_convert_fusion.1.rest_1_), channel_id=1, source_target_pairs={{0,112},{1,113},{2,114},{3,115},{4,116},{5,117},{6,118},{7,119},{8... | collective-permute-start | bytes 1179656 | tf_op jit(solution)/shard_map/ppermute | solution.py:53
  105.3 12.9 %collective-permute-start.26 = (bf16[192,1024]{1,0:T(8,128)(2,1)S(1)}, bf16[192,1024]{1,0:T(8,128)(2,1)}, u32[]{:S(2)}, u32[]{:S(2)}) collective-permute-start(bf16[192,1024]{1,0:T(8,128)(2,1)S(1)} %add_convert_fusion.3.rest_0_), channel_id=1, source_target_pairs={{0,16},{1,17},{2,18},{3,19},{4,20},{5,21},{6,22},{7,23},{8,24},{9,... | collective-permute-start | bytes 1179656 | tf_op jit(solution)/shard_map/ppermute | solution.py:53
  108.7 13.5 %all-to-all-start.3 = ((bf16[16,32,128]{2,1,0:T(8,128)(2,1)}), bf16[16,32,128]{2,1,0:T(8,128)(2,1)S(1)}, u32[]{:S(2)}, u32[]{:S(2)}) async-start(bf16[16,32,128]{2,1,0:T(8,128)(2,1)} %states_after.1), calls=%async_computation.3 | async-start | bytes 262144 | tf_op jit(solution)/shard_map/all_to_all | solution.py:400
  114.9 11.9 %collective-permute-start.32 = (bf16[192,1024]{1,0:T(8,128)(2,1)S(1)}, bf16[192,1024]{1,0:T(8,128)(2,1)}, u32[]{:S(2)}, u32[]{:S(2)}) collective-permute-start(bf16[192,1024]{1,0:T(8,128)(2,1)S(1)} %add_convert_fusion.rest_1_), channel_id=1, source_target_pairs={{0,112},{1,113},{2,114},{3,115},{4,116},{5,117},{6,118},{7,119},{8... | collective-permute-start | bytes 1179656 | tf_op jit(solution)/shard_map/ppermute | solution.py:53
  119.4 10.6 %collective-permute-start.31 = (bf16[192,1024]{1,0:T(8,128)(2,1)S(1)}, bf16[192,1024]{1,0:T(8,128)(2,1)}, u32[]{:S(2)}, u32[]{:S(2)}) collective-permute-start(bf16[192,1024]{1,0:T(8,128)(2,1)S(1)} %add_convert_fusion.2.rest_0_), channel_id=1, source_target_pairs={{0,16},{1,17},{2,18},{3,19},{4,20},{5,21},{6,22},{7,23},{8,24},{9,... | collective-permute-start | bytes 1179656 | tf_op jit(solution)/shard_map/ppermute | solution.py:53
  (26 other events, 184.0 us)

commit v12 on v10

--- a/solution.py
+++ b/solution.py
@@ -458,7 +458,7 @@
     before = exchange(befores).reshape(HALF_ROWS, HEAD_DIM)
     before_own, before_cross = call(
         functools.partial(spread_kernel, 0), (half_state, half_state), "spread_before",
-        1_000_000, 500_000, (key_mine, key_other, key_mine, key_other, before), (far_low, far_high),
+        1_000_000, 500_000, (key_mine, key_other, key_mine, key_other, before), (far_low, far_high, right),
     )
     before_other = send(before_cross, CORE)
     attended, scores, states = call(

time: 134 us -> 136 us (1.015)
  starting transfers between devices: 63.9 us -> 65.7 us
    ppermute x33, waiting for transfers between devices: 29.7 us -> 28.2 us  [send(): return lax.ppermute(array, AXES, table)]
    unnamed x56 -> x52, local copies, waits for them, and re-layouts: 4.28 us -> 4.29 us
  transfers between devices with their start and end apart: 37 -> 37, of which waited for: 21 -> 18; matrix products, arithmetic and copies ran while one was open for 5% -> 6% of each run, Pallas kernels for 16% -> 16%
where the time goes in v12:
time: 136 us; the launch traced here: 135 us
  starting transfers between devices  65.7 us (48%)
  waiting for transfers between devices  31.3 us (23%)
  Pallas kernels  24.3 us (18%)
  local copies, waits for them, and re-layouts  7.52 us (6%)
  other arithmetic  4.62 us (3%)
    ppermute x33, starting transfers between devices, send(): return lax.ppermute(array, AXES, table)  38.4 us
    ppermute x33, waiting for transfers between devices, send(): return lax.ppermute(array, AXES, table)  28.2 us
    all_to_all x4, starting transfers between devices, exchange(): lax.all_to_all(array, 'seq', 0, 0, tiled=True, axis_index_groups=CHIP_GRO...  27.3 us
    pallas_call x16, Pallas kernels, call(): pl.pallas_call(body, in_specs=[pl.BlockSpec(a.shape, lambda n=a.ndim: (0,...  17 us
    convert_element_type x4, other arithmetic, add_pieces(): return (a.astype(F32) + b.astype(F32)).astype(BF)  4.62 us
    unnamed x52, local copies, waits for them, and re-layouts  4.29 us
    all_to_all x4, waiting for transfers between devices, exchange(): lax.all_to_all(array, 'seq', 0, 0, tiled=True, axis_index_groups=CHIP_GRO...  3.16 us
    pallas_call x1, Pallas kernels, body(): pl.pallas_call(project_kernel, out_shape=[row32, row32, row, row], scratc...  3.01 us
  transfers between devices with their start and end apart: 37, of which 18 were waited for; matrix products, arithmetic and copies ran while one was open for 6% of the time, Pallas kernels for 16%

profile of v12, /device:TPU:8, one launch (start us, length us, event | category | flops | bytes accessed | tf_op | source)
XLA Modules:
  0.0 134.5 jit_solution(12830515684803118384)
XLA Ops:
  0.6 2.0 %collective-permute-start = (bf16[192,1024]{1,0:T(8,128)(2,1)}, bf16[192,1024]{1,0:T(8,128)(2,1)S(1)}, u32[]{:S(2)}, u32[]{:S(2)}) collective-permute-start(bf16[192,1024]{1,0:T(8,128)(2,1)} %refs_0_.1), channel_id=1, source_target_pairs={{0,16},{1,17},{2,18},{3,19},{4,20},{5,21},{6,22},{7,23},{8,24},{9,... | collective-permute-start | bytes 1179656 | tf_op jit(solution)/shard_map/ppermute | solution.py:53
  2.6 4.0 %collective-permute-start.1 = (bf16[192,1024]{1,0:T(8,128)(2,1)}, bf16[192,1024]{1,0:T(8,128)(2,1)S(1)}, u32[]{:S(2)}, u32[]{:S(2)}) collective-permute-start(bf16[192,1024]{1,0:T(8,128)(2,1)} %refs_0_.1), channel_id=1, source_target_pairs={{0,112},{1,113},{2,114},{3,115},{4,116},{5,117},{6,118},{7,119},{8... | collective-permute-start | bytes 1179656 | tf_op jit(solution)/shard_map/ppermute | solution.py:53
  9.2 2.4 %key_terms.1 = (bf16[528,128]{1,0:T(8,128)(2,1)S(1)}, bf16[528,128]{1,0:T(8,128)(2,1)S(1)}) custom-call(f32[8,128]{1,0:T(8,128)S(1)} %bitcast.5, bf16[128,1024]{1,0:T(8,128)(2,1)S(1)} %copy-done, bf16[128,1024]{1,0:T(8,128)(2,1)S(1)} %copy-done.2), custom_call_target="tpu_custom_call" | custom-call | flops 40000000 | bytes 1000000 | tf_op jit(solution)/shard_map/key_terms/pallas_call | solution.py:418
  13.8 7.2 %all-to-all-start = ((bf16[16,48,128]{2,1,0:T(8,128)(2,1)}), bf16[16,48,128]{2,1,0:T(8,128)(2,1)S(1)}, u32[]{:S(2)}, u32[]{:S(2)}) async-start(bf16[16,48,128]{2,1,0:T(8,128)(2,1)} %merge_keys.1.rest_2_), calls=%async_computation | async-start | bytes 393216 | tf_op jit(solution)/shard_map/all_to_all | solution.py:400
  22.6 1.8 %collective-permute-start.8 = (bf16[192,1024]{1,0:T(8,128)(2,1)S(1)}, bf16[192,1024]{1,0:T(8,128)(2,1)S(1)}, u32[]{:S(2)}, u32[]{:S(2)}) collective-permute-start(bf16[192,1024]{1,0:T(8,128)(2,1)S(1)} %collective-permute-done.1.rest_1_.refs_1_), channel_id=1, source_target_pairs={{0,112},{1,113},{2,114},{3,115},{4,116},{5,117},{6,118},{7,119},{8... | collective-permute-start | bytes 1179656 | tf_op jit(solution)/shard_map/ppermute | solution.py:53
  25.5 2.8 %collective-permute-start.3 = (bf16[384,128]{1,0:T(8,128)(2,1)S(1)}, bf16[384,128]{1,0:T(8,128)(2,1)S(1)}, u32[]{:S(2)}, u32[]{:S(2)}) collective-permute-start(bf16[384,128]{1,0:T(8,128)(2,1)S(1)} %get-tuple-element.42), channel_id=1, source_target_pairs={{0,0},{1,1},{2,2},{3,3},{4,128},{5,129},{6,130},{7,131},{8,8},{9,9... | collective-permute-start | bytes 294920 | tf_op jit(solution)/shard_map/ppermute | solution.py:53
  28.5 6.1 %collective-permute-done.3.a_ref = bf16[384,128]{1,0:T(8,128)(2,1)S(1)} collective-permute-done((bf16[384,128]{1,0:T(8,128)(2,1)S(1)}, bf16[384,128]{1,0:T(8,128)(2,1)S(1)}, u32[]{:S(2)}, u32[]{:S(2)}) %collective-permute-start.3) | collective-permute-done | bytes 98336 | tf_op jit(solution)/shard_map/ppermute | solution.py:53
  34.6 2.4 %collective-permute-done.7.rest_1_.refs_7_ = bf16[192,1024]{1,0:T(8,128)(2,1)S(1)} collective-permute-done((bf16[192,1024]{1,0:T(8,128)(2,1)S(1)}, bf16[192,1024]{1,0:T(8,128)(2,1)S(1)}, u32[]{:S(2)}, u32[]{:S(2)}) %collective-permute-start.7) | collective-permute-done | bytes 393248 | tf_op jit(solution)/shard_map/ppermute | solution.py:53
  37.0 3.2 %collective-permute-start.12 = (bf16[192,1024]{1,0:T(8,128)(2,1)S(1)}, bf16[192,1024]{1,0:T(8,128)(2,1)}, u32[]{:S(2)}, u32[]{:S(2)}) collective-permute-start(bf16[192,1024]{1,0:T(8,128)(2,1)S(1)} %collective-permute-done.8.rest_2_.refs_2_), channel_id=1, source_target_pairs={{0,112},{1,113},{2,114},{3,115},{4,116},{5,117},{6,118},{7,119},{8... | collective-permute-start | bytes 1179656 | tf_op jit(solution)/shard_map/ppermute | solution.py:53
  43.6 1.7 %collective-permute-start.10 = (bf16[384,512]{1,0:T(8,128)(2,1)S(1)}, bf16[384,512]{1,0:T(8,128)(2,1)S(1)}, u32[]{:S(2)}, u32[]{:S(2)}) collective-permute-start(bf16[384,512]{1,0:T(8,128)(2,1)S(1)} %collect.1.own_ref), channel_id=1, source_target_pairs={{0,3},{1,0},{2,1},{3,2},{4,7},{5,4},{6,5},{7,6},{8,11},{9,8},{10,9... | collective-permute-start | bytes 1179656 | tf_op jit(solution)/shard_map/ppermute | solution.py:53
  45.3 6.5 %all-to-all-start.1 = ((bf16[16,32,128]{2,1,0:T(8,128)(2,1)}), bf16[16,32,128]{2,1,0:T(8,128)(2,1)S(1)}, u32[]{:S(2)}, u32[]{:S(2)}) async-start(bf16[16,32,128]{2,1,0:T(8,128)(2,1)} %states_before.1.rest_0_), calls=%async_computation.1 | async-start | bytes 262144 | tf_op jit(solution)/shard_map/all_to_all | solution.py:400
  51.8 1.6 %slice.8 = bf16[96,1024]{1,0:T(8,128)(2,1)} slice(bf16[192,1024]{1,0:T(8,128)(2,1)} %collective-permute-done.13.refs_6_), slice={[0:96], [0:1024]} | slice | bytes 393216 | tf_op jit(solution)/shard_map/slice | solution.py:456
  54.9 1.6 %slice.9 = bf16[96,1024]{1,0:T(8,128)(2,1)} slice(bf16[192,1024]{1,0:T(8,128)(2,1)} %collective-permute-done.12.refs_3_), slice={[96:192], [0:1024]} | slice | bytes 393216 | tf_op jit(solution)/shard_map/slice | solution.py:457
  56.5 1.8 %collective-permute-start.15 = (bf16[96,1024]{1,0:T(8,128)(2,1)}, bf16[96,1024]{1,0:T(8,128)(2,1)}, u32[]{:S(2)}, u32[]{:S(2)}) collective-permute-start(bf16[96,1024]{1,0:T(8,128)(2,1)} %slice.9), channel_id=1, source_target_pairs={{0,112},{1,113},{2,114},{3,115},{4,116},{5,117},{6,118},{7,119},{8... | collective-permute-start | bytes 589832 | tf_op jit(solution)/shard_map/ppermute | solution.py:53
  59.4 3.9 %collective-permute-done.14.refs_4_.rest_0_ = bf16[96,1024]{1,0:T(8,128)(2,1)S(1)} collective-permute-done((bf16[96,1024]{1,0:T(8,128)(2,1)}, bf16[96,1024]{1,0:T(8,128)(2,1)S(1)}, u32[]{:S(2)}, u32[]{:S(2)}) %collective-permute-start.14) | collective-permute-done | bytes 196640 | tf_op jit(solution)/shard_map/ppermute | solution.py:53
  69.5 1.6 %collective-permute-done.11.opposite_ref = bf16[384,512]{1,0:T(8,128)(2,1)S(1)} collective-permute-done((bf16[384,512]{1,0:T(8,128)(2,1)S(1)}, bf16[384,512]{1,0:T(8,128)(2,1)S(1)}, u32[]{:S(2)}, u32[]{:S(2)}) %collective-permute-start.11) | collective-permute-done | bytes 393248 | tf_op jit(solution)/shard_map/ppermute | solution.py:53
  71.7 3.0 %project.1 = (f32[128,1024]{1,0:T(8,128)S(1)}, f32[128,1024]{1,0:T(8,128)S(1)}, bf16[128,1024]{1,0:T(8,128)(2,1)S(1)}, bf16[128,1024]{1,0:T(8,128)(2,1)S(1)}) custom-call(bf16[512,1536]{1,0:T(8,128)(2,1)S(1)} %get-tuple-element.44.block_ref, bf16[192,1024]{1,0:T(8,128)(2,1)S(1)} %copy-done.20, bf16[192,1024]{1,0:T(8,128)(2,1)S(1)} %copy-done.24, ...), custom_call_target="tpu_custom_call" | custom-call | flops 1600000000 | bytes 6000000 | tf_op jit(solution)/shard_map/project/pallas_call | solution.py:479
  75.4 1.9 %collective-permute-done.20.neighbour_ref = bf16[128,1024]{1,0:T(8,128)(2,1)S(1)} collective-permute-done((bf16[128,1024]{1,0:T(8,128)(2,1)S(1)}, bf16[128,1024]{1,0:T(8,128)(2,1)S(1)}, u32[]{:S(2)}, u32[]{:S(2)}) %collective-permute-start.20) | collective-permute-done | bytes 262176 | tf_op jit(solution)/shard_map/ppermute | solution.py:53
  78.8 1.9 %weight_partial.1 = (bf16[192,1024]{1,0:T(8,128)(2,1)S(1)}, bf16[192,1024]{1,0:T(8,128)(2,1)S(1)}, bf16[192,1024]{1,0:T(8,128)(2,1)S(1)}, bf16[192,1024]{1,0:T(8...) custom-call(bf16[1536,512]{1,0:T(8,128)(2,1)S(1)} %get-tuple-element, ...), custom_call_target="tpu_custom_call" | custom-call | flops 1600000000 | bytes 6000000 | tf_op jit(solution)/shard_map/weight_partial/pallas_call | solution.py:494
  80.8 1.7 %collective-permute-start.23 = (bf16[96,1024]{1,0:T(8,128)(2,1)S(1)}, bf16[96,1024]{1,0:T(8,128)(2,1)S(1)}, u32[]{:S(2)}, u32[]{:S(2)}) collective-permute-start(bf16[96,1024]{1,0:T(8,128)(2,1)S(1)} %get-tuple-element.59), channel_id=1, source_target_pairs={{0,16},{1,17},{2,18},{3,19},{4,20},{5,21},{6,22},{7,23},{8,24},{9,... | collective-permute-start | bytes 589832 | tf_op jit(solution)/shard_map/ppermute | solution.py:53
  82.4 1.7 %collective-permute-start.24 = (bf16[96,1024]{1,0:T(8,128)(2,1)S(1)}, bf16[96,1024]{1,0:T(8,128)(2,1)S(1)}, u32[]{:S(2)}, u32[]{:S(2)}) collective-permute-start(bf16[96,1024]{1,0:T(8,128)(2,1)S(1)} %get-tuple-element.61), channel_id=1, source_target_pairs={{0,112},{1,113},{2,114},{3,115},{4,116},{5,117},{6,118},{7,119},{8... | collective-permute-start | bytes 589832 | tf_op jit(solution)/shard_map/ppermute | solution.py:53
  84.1 2.1 %collective-permute-done.18.other_ref = bf16[128,1024]{1,0:T(8,128)(2,1)S(1)} collective-permute-done((bf16[128,1024]{1,0:T(8,128)(2,1)S(1)}, bf16[128,1024]{1,0:T(8,128)(2,1)S(1)}, u32[]{:S(2)}, u32[]{:S(2)}) %collective-permute-start.18) | collective-permute-done | bytes 262176 | tf_op jit(solution)/shard_map/ppermute | solution.py:53
  86.1 2.3 %query_terms.1 = (bf16[128,1024]{1,0:T(8,128)(2,1)S(1)}, bf16[512,128]{1,0:T(8,128)(2,1)S(1)}, bf16[512,128]{1,0:T(8,128)(2,1)S(1)}) custom-call(f32[8,128]{1,0:T(8,128)S(1)} %bitcast.7, bf16[128,1024]{1,0:T(8,128)(2,1)S(1)} %copy-done.4, f32[128,1024]{1,0:T(8,128)S(1)} %get-tuple-element.45.own_ref, bf16[128,1024]{1,0:T(8,128)(2,1)S(1)} %collective-permute-done.16.core_ref, ...), custom_call_target="tpu_custom_call" | custom-call | flops 40000000 | bytes 1000000 | tf_op jit(solution)/shard_map/query_terms/pallas_call | solution.py:383
  90.1 3.3 %collective-permute-start.25 = (bf16[192,1024]{1,0:T(8,128)(2,1)S(1)}, bf16[192,1024]{1,0:T(8,128)(2,1)}, u32[]{:S(2)}, u32[]{:S(2)}) collective-permute-start(bf16[192,1024]{1,0:T(8,128)(2,1)S(1)} %get-tuple-element.62), channel_id=1, source_target_pairs={{0,16},{1,17},{2,18},{3,19},{4,20},{5,21},{6,22},{7,23},{8,24},{9,... | collective-permute-start | bytes 1179656 | tf_op jit(solution)/shard_map/ppermute | solution.py:53
  95.5 7.8 %all-to-all-start.2 = ((bf16[16,32,128]{2,1,0:T(8,128)(2,1)}), bf16[16,32,128]{2,1,0:T(8,128)(2,1)S(1)}, u32[]{:S(2)}, u32[]{:S(2)}) async-start(bf16[16,32,128]{2,1,0:T(8,128)(2,1)} %merge_queries.1), calls=%async_computation.2 | async-start | bytes 262144 | tf_op jit(solution)/shard_map/all_to_all | solution.py:400
  107.2 1.9 %collective-permute-start.28 = (bf16[192,1024]{1,0:T(8,128)(2,1)S(1)}, bf16[192,1024]{1,0:T(8,128)(2,1)}, u32[]{:S(2)}, u32[]{:S(2)}) collective-permute-start(bf16[192,1024]{1,0:T(8,128)(2,1)S(1)} %add_convert_fusion.1.rest_1_), channel_id=1, source_target_pairs={{0,112},{1,113},{2,114},{3,115},{4,116},{5,117},{6,118},{7,119},{8... | collective-permute-start | bytes 1179656 | tf_op jit(solution)/shard_map/ppermute | solution.py:53
  109.1 2.3 %all-to-all-done.2.terms_ref = bf16[16,32,128]{2,1,0:T(8,128)(2,1)S(1)} async-done(((bf16[16,32,128]{2,1,0:T(8,128)(2,1)}), bf16[16,32,128]{2,1,0:T(8,128)(2,1)S(1)}, u32[]{:S(2)}, u32[]{:S(2)}) %all-to-all-start.2) | async-done | bytes 131104 | tf_op jit(solution)/shard_map/all_to_all | solution.py:400
  112.2 5.8 %all-to-all-start.3 = ((bf16[16,32,128]{2,1,0:T(8,128)(2,1)}), bf16[16,32,128]{2,1,0:T(8,128)(2,1)S(1)}, u32[]{:S(2)}, u32[]{:S(2)}) async-start(bf16[16,32,128]{2,1,0:T(8,128)(2,1)} %states_after.1), calls=%async_computation.3 | async-start | bytes 262144 | tf_op jit(solution)/shard_map/all_to_all | solution.py:400
  121.8 2.2 %collective-permute-start.32 = (bf16[192,1024]{1,0:T(8,128)(2,1)S(1)}, bf16[192,1024]{1,0:T(8,128)(2,1)}, u32[]{:S(2)}, u32[]{:S(2)}) collective-permute-start(bf16[192,1024]{1,0:T(8,128)(2,1)S(1)} %add_convert_fusion.rest_1_), channel_id=1, source_target_pairs={{0,112},{1,113},{2,114},{3,115},{4,116},{5,117},{6,118},{7,119},{8... | collective-permute-start | bytes 1179656 | tf_op jit(solution)/shard_map/ppermute | solution.py:53
  124.0 2.7 %inner_grads.1 = (bf16[128,1024]{1,0:T(8,128)(2,1)}, f32[128,1024]{1,0:T(8,128)S(1)}, f32[128,1024]{1,0:T(8,128)S(1)}) custom-call(f32[8,128]{1,0:T(8,128)S(1)} %bitcast.8, bf16[128,1024]{1,0:T(8,128)(2,1)S(1)} %copy-done.4, bf16[128,1024]{1,0:T(8,128)(2,1)S(1)} %copy-done.1, bf16[128,1024]{1,0:T(8,128)(2,1)S(1)} %copy-done.3, ...), custom_call_target="tpu_custom_call" | custom-call | flops 200000000 | bytes 3000000 | tf_op jit(solution)/shard_map/inner_grads/pallas_call | solution.py:383
  130.5 2.0 %collective-permute-done.31.up_ref = bf16[192,1024]{1,0:T(8,128)(2,1)} collective-permute-done((bf16[192,1024]{1,0:T(8,128)(2,1)S(1)}, bf16[192,1024]{1,0:T(8,128)(2,1)}, u32[]{:S(2)}, u32[]{:S(2)}) %collective-permute-start.31) | collective-permute-done | bytes 393248 | tf_op jit(solution)/shard_map/ppermute | solution.py:53
  132.5 2.0 %ring_sum_0.1 = bf16[192,1024]{1,0:T(8,128)(2,1)} custom-call(bf16[192,1024]{1,0:T(8,128)(2,1)S(1)} %copy-done.6, bf16[192,1024]{1,0:T(8,128)(2,1)} %collective-permute-done.31.up_ref, bf16[192,1024]{1,0:T(8,128)(2,1)} %collective-permute-done.32.down_ref), custom_call_target="tpu_custom_call" | custom-call | flops 400000 | bytes 2000000 | tf_op jit(solution)/shard_map/ring_sum_0/pallas_call | solution.py:383
  (119 shorter events, 38.3 us)
Async XLA Ops:
  0.6 20.4 %collective-permute-start = (bf16[192,1024]{1,0:T(8,128)(2,1)}, bf16[192,1024]{1,0:T(8,128)(2,1)S(1)}, u32[]{:S(2)}, u32[]{:S(2)}) collective-permute-start(bf16[192,1024]{1,0:T(8,128)(2,1)} %refs_0_.1), channel_id=1, source_target_pairs={{0,16},{1,17},{2,18},{3,19},{4,20},{5,21},{6,22},{7,23},{8,24},{9,... | collective-permute-start | bytes 1179656 | tf_op jit(solution)/shard_map/ppermute | solution.py:53
  2.6 20.0 %collective-permute-start.1 = (bf16[192,1024]{1,0:T(8,128)(2,1)}, bf16[192,1024]{1,0:T(8,128)(2,1)S(1)}, u32[]{:S(2)}, u32[]{:S(2)}) collective-permute-start(bf16[192,1024]{1,0:T(8,128)(2,1)} %refs_0_.1), channel_id=1, source_target_pairs={{0,112},{1,113},{2,114},{3,115},{4,116},{5,117},{6,118},{7,119},{8... | collective-permute-start | bytes 1179656 | tf_op jit(solution)/shard_map/ppermute | solution.py:53
  13.8 26.4 %all-to-all-start = ((bf16[16,48,128]{2,1,0:T(8,128)(2,1)}), bf16[16,48,128]{2,1,0:T(8,128)(2,1)S(1)}, u32[]{:S(2)}, u32[]{:S(2)}) async-start(bf16[16,48,128]{2,1,0:T(8,128)(2,1)} %merge_keys.1.rest_2_), calls=%async_computation | async-start | bytes 393216 | tf_op jit(solution)/shard_map/all_to_all | solution.py:400
  21.1 15.9 %collective-permute-start.7 = (bf16[192,1024]{1,0:T(8,128)(2,1)S(1)}, bf16[192,1024]{1,0:T(8,128)(2,1)S(1)}, u32[]{:S(2)}, u32[]{:S(2)}) collective-permute-start(bf16[192,1024]{1,0:T(8,128)(2,1)S(1)} %collective-permute-done.rest_0_.refs_8_), channel_id=1, source_target_pairs={{0,16},{1,17},{2,18},{3,19},{4,20},{5,21},{6,22},{7,23},{8,24},{9,... | collective-permute-start | bytes 1179656 | tf_op jit(solution)/shard_map/ppermute | solution.py:53
  22.6 14.4 %collective-permute-start.8 = (bf16[192,1024]{1,0:T(8,128)(2,1)S(1)}, bf16[192,1024]{1,0:T(8,128)(2,1)S(1)}, u32[]{:S(2)}, u32[]{:S(2)}) collective-permute-start(bf16[192,1024]{1,0:T(8,128)(2,1)S(1)} %collective-permute-done.1.rest_1_.refs_1_), channel_id=1, source_target_pairs={{0,112},{1,113},{2,114},{3,115},{4,116},{5,117},{6,118},{7,119},{8... | collective-permute-start | bytes 1179656 | tf_op jit(solution)/shard_map/ppermute | solution.py:53
  25.5 9.2 %collective-permute-start.3 = (bf16[384,128]{1,0:T(8,128)(2,1)S(1)}, bf16[384,128]{1,0:T(8,128)(2,1)S(1)}, u32[]{:S(2)}, u32[]{:S(2)}) collective-permute-start(bf16[384,128]{1,0:T(8,128)(2,1)S(1)} %get-tuple-element.42), channel_id=1, source_target_pairs={{0,0},{1,1},{2,2},{3,3},{4,128},{5,129},{6,130},{7,131},{8,8},{9,9... | collective-permute-start | bytes 294920 | tf_op jit(solution)/shard_map/ppermute | solution.py:53
  28.3 12.7 %collective-permute-start.4 = (bf16[384,128]{1,0:T(8,128)(2,1)S(1)}, bf16[384,128]{1,0:T(8,128)(2,1)S(1)}, u32[]{:S(2)}, u32[]{:S(2)}) collective-permute-start(bf16[384,128]{1,0:T(8,128)(2,1)S(1)} %get-tuple-element.42), channel_id=1, source_target_pairs={{0,4},{1,5},{2,6},{3,7},{4,132},{5,133},{6,134},{7,135},{8,12},{9,... | collective-permute-start | bytes 294920 | tf_op jit(solution)/shard_map/ppermute | solution.py:53
  28.4 12.6 %collective-permute-start.5 = (bf16[384,128]{1,0:T(8,128)(2,1)S(1)}, bf16[384,128]{1,0:T(8,128)(2,1)S(1)}, u32[]{:S(2)}, u32[]{:S(2)}) collective-permute-start(bf16[384,128]{1,0:T(8,128)(2,1)S(1)} %get-tuple-element.43), channel_id=1, source_target_pairs={{0,8},{1,9},{2,10},{3,11},{4,136},{5,137},{6,138},{7,139},{8,0},{9... | collective-permute-start | bytes 294920 | tf_op jit(solution)/shard_map/ppermute | solution.py:53
  34.6 6.3 %collective-permute-start.6 = (bf16[384,128]{1,0:T(8,128)(2,1)S(1)}, bf16[384,128]{1,0:T(8,128)(2,1)S(1)}, u32[]{:S(2)}, u32[]{:S(2)}) collective-permute-start(bf16[384,128]{1,0:T(8,128)(2,1)S(1)} %get-tuple-element.43), channel_id=1, source_target_pairs={{0,12},{1,13},{2,14},{3,15},{4,140},{5,141},{6,142},{7,143},{8,4},... | collective-permute-start | bytes 294920 | tf_op jit(solution)/shard_map/ppermute | solution.py:53
  37.0 14.8 %collective-permute-start.13 = (bf16[192,1024]{1,0:T(8,128)(2,1)S(1)}, bf16[192,1024]{1,0:T(8,128)(2,1)}, u32[]{:S(2)}, u32[]{:S(2)}) collective-permute-start(bf16[192,1024]{1,0:T(8,128)(2,1)S(1)} %collective-permute-done.7.rest_1_.refs_7_), channel_id=1, source_target_pairs={{0,16},{1,17},{2,18},{3,19},{4,20},{5,21},{6,22},{7,23},{8,24},{9,... | collective-permute-start | bytes 1179656 | tf_op jit(solution)/shard_map/ppermute | solution.py:53
  37.0 17.9 %collective-permute-start.12 = (bf16[192,1024]{1,0:T(8,128)(2,1)S(1)}, bf16[192,1024]{1,0:T(8,128)(2,1)}, u32[]{:S(2)}, u32[]{:S(2)}) collective-permute-start(bf16[192,1024]{1,0:T(8,128)(2,1)S(1)} %collective-permute-done.8.rest_2_.refs_2_), channel_id=1, source_target_pairs={{0,112},{1,113},{2,114},{3,115},{4,116},{5,117},{6,118},{7,119},{8... | collective-permute-start | bytes 1179656 | tf_op jit(solution)/shard_map/ppermute | solution.py:53
  42.0 16.3 %collective-permute-start.9 = (bf16[384,512]{1,0:T(8,128)(2,1)S(1)}, bf16[384,512]{1,0:T(8,128)(2,1)S(1)}, u32[]{:S(2)}, u32[]{:S(2)}) collective-permute-start(bf16[384,512]{1,0:T(8,128)(2,1)S(1)} %collect.1.own_ref), channel_id=1, source_target_pairs={{0,1},{1,2},{2,3},{3,0},{4,5},{5,6},{6,7},{7,4},{8,9},{9,10},{10,1... | collective-permute-start | bytes 1179656 | tf_op jit(solution)/shard_map/ppermute | solution.py:53
  43.6 15.8 %collective-permute-start.10 = (bf16[384,512]{1,0:T(8,128)(2,1)S(1)}, bf16[384,512]{1,0:T(8,128)(2,1)S(1)}, u32[]{:S(2)}, u32[]{:S(2)}) collective-permute-start(bf16[384,512]{1,0:T(8,128)(2,1)S(1)} %collect.1.own_ref), channel_id=1, source_target_pairs={{0,3},{1,0},{2,1},{3,2},{4,7},{5,4},{6,5},{7,6},{8,11},{9,8},{10,9... | collective-permute-start | bytes 1179656 | tf_op jit(solution)/shard_map/ppermute | solution.py:53
  45.3 14.0 %all-to-all-start.1 = ((bf16[16,32,128]{2,1,0:T(8,128)(2,1)}), bf16[16,32,128]{2,1,0:T(8,128)(2,1)S(1)}, u32[]{:S(2)}, u32[]{:S(2)}) async-start(bf16[16,32,128]{2,1,0:T(8,128)(2,1)} %states_before.1.rest_0_), calls=%async_computation.1 | async-start | bytes 262144 | tf_op jit(solution)/shard_map/all_to_all | solution.py:400
  53.4 9.9 %collective-permute-start.14 = (bf16[96,1024]{1,0:T(8,128)(2,1)}, bf16[96,1024]{1,0:T(8,128)(2,1)S(1)}, u32[]{:S(2)}, u32[]{:S(2)}) collective-permute-start(bf16[96,1024]{1,0:T(8,128)(2,1)} %slice.8), channel_id=1, source_target_pairs={{0,16},{1,17},{2,18},{3,19},{4,20},{5,21},{6,22},{7,23},{8,24},{9,... | collective-permute-start | bytes 589832 | tf_op jit(solution)/shard_map/ppermute | solution.py:53
  56.5 8.0 %collective-permute-start.15 = (bf16[96,1024]{1,0:T(8,128)(2,1)}, bf16[96,1024]{1,0:T(8,128)(2,1)}, u32[]{:S(2)}, u32[]{:S(2)}) collective-permute-start(bf16[96,1024]{1,0:T(8,128)(2,1)} %slice.9), channel_id=1, source_target_pairs={{0,112},{1,113},{2,114},{3,115},{4,116},{5,117},{6,118},{7,119},{8... | collective-permute-start | bytes 589832 | tf_op jit(solution)/shard_map/ppermute | solution.py:53
  58.3 12.8 %collective-permute-start.11 = (bf16[384,512]{1,0:T(8,128)(2,1)S(1)}, bf16[384,512]{1,0:T(8,128)(2,1)S(1)}, u32[]{:S(2)}, u32[]{:S(2)}) collective-permute-start(bf16[384,512]{1,0:T(8,128)(2,1)S(1)} %collective-permute-done.9.left_ref), channel_id=1, source_target_pairs={{0,1},{1,2},{2,3},{3,0},{4,5},{5,6},{6,7},{7,4},{8,9},{9,10},{10,1... | collective-permute-start | bytes 1179656 | tf_op jit(solution)/shard_map/ppermute | solution.py:53
  68.9 8.4 %collective-permute-start.20 = (bf16[128,1024]{1,0:T(8,128)(2,1)S(1)}, bf16[128,1024]{1,0:T(8,128)(2,1)S(1)}, u32[]{:S(2)}, u32[]{:S(2)}) collective-permute-start(bf16[128,1024]{1,0:T(8,128)(2,1)S(1)} %get-tuple-element.55.own_ref), channel_id=1, source_target_pairs={{0,128},{1,129},{2,130},{3,131},{4,132},{5,133},{6,134},{7,135},{8... | collective-permute-start | bytes 786440 | tf_op jit(solution)/shard_map/ppermute | solution.py:53
  74.8 3.0 %collective-permute-start.17 = (bf16[128,1024]{1,0:T(8,128)(2,1)S(1)}, bf16[128,1024]{1,0:T(8,128)(2,1)S(1)}, u32[]{:S(2)}, u32[]{:S(2)}) collective-permute-start(bf16[128,1024]{1,0:T(8,128)(2,1)S(1)} %get-tuple-element.48), channel_id=1, source_target_pairs={{0,8},{1,9},{2,10},{3,11},{4,12},{5,13},{6,14},{7,15},{8,0},{9,1},... | collective-permute-start | bytes 786440 | tf_op jit(solution)/shard_map/ppermute | solution.py:53
  74.9 3.6 %collective-permute-start.21 = (bf16[128,1024]{1,0:T(8,128)(2,1)S(1)}, bf16[128,1024]{1,0:T(8,128)(2,1)S(1)}, u32[]{:S(2)}, u32[]{:S(2)}) collective-permute-start(bf16[128,1024]{1,0:T(8,128)(2,1)S(1)} %get-tuple-element.55.own_ref), channel_id=1, source_target_pairs={{0,8},{1,9},{2,10},{3,11},{4,12},{5,13},{6,14},{7,15},{8,0},{9,1},... | collective-permute-start | bytes 786440 | tf_op jit(solution)/shard_map/ppermute | solution.py:53
  77.3 6.8 %collective-permute-start.16 = (bf16[128,1024]{1,0:T(8,128)(2,1)S(1)}, bf16[128,1024]{1,0:T(8,128)(2,1)S(1)}, u32[]{:S(2)}, u32[]{:S(2)}) collective-permute-start(bf16[128,1024]{1,0:T(8,128)(2,1)S(1)} %get-tuple-element.46), channel_id=1, source_target_pairs={{0,8},{1,9},{2,10},{3,11},{4,12},{5,13},{6,14},{7,15},{8,0},{9,1},... | collective-permute-start | bytes 786440 | tf_op jit(solution)/shard_map/ppermute | solution.py:53
  77.8 8.3 %collective-permute-start.18 = (bf16[128,1024]{1,0:T(8,128)(2,1)S(1)}, bf16[128,1024]{1,0:T(8,128)(2,1)S(1)}, u32[]{:S(2)}, u32[]{:S(2)}) collective-permute-start(bf16[128,1024]{1,0:T(8,128)(2,1)S(1)} %sum_theirs.1.rest_0_), channel_id=1, source_target_pairs={{0,128},{1,129},{2,130},{3,131},{4,132},{5,133},{6,134},{7,135},{8... | collective-permute-start | bytes 786440 | tf_op jit(solution)/shard_map/ppermute | solution.py:53
  80.8 8.3 %collective-permute-start.23 = (bf16[96,1024]{1,0:T(8,128)(2,1)S(1)}, bf16[96,1024]{1,0:T(8,128)(2,1)S(1)}, u32[]{:S(2)}, u32[]{:S(2)}) collective-permute-start(bf16[96,1024]{1,0:T(8,128)(2,1)S(1)} %get-tuple-element.59), channel_id=1, source_target_pairs={{0,16},{1,17},{2,18},{3,19},{4,20},{5,21},{6,22},{7,23},{8,24},{9,... | collective-permute-start | bytes 589832 | tf_op jit(solution)/shard_map/ppermute | solution.py:53
  82.4 6.9 %collective-permute-start.24 = (bf16[96,1024]{1,0:T(8,128)(2,1)S(1)}, bf16[96,1024]{1,0:T(8,128)(2,1)S(1)}, u32[]{:S(2)}, u32[]{:S(2)}) collective-permute-start(bf16[96,1024]{1,0:T(8,128)(2,1)S(1)} %get-tuple-element.61), channel_id=1, source_target_pairs={{0,112},{1,113},{2,114},{3,115},{4,116},{5,117},{6,118},{7,119},{8... | collective-permute-start | bytes 589832 | tf_op jit(solution)/shard_map/ppermute | solution.py:53
  90.1 13.2 %collective-permute-start.25 = (bf16[192,1024]{1,0:T(8,128)(2,1)S(1)}, bf16[192,1024]{1,0:T(8,128)(2,1)}, u32[]{:S(2)}, u32[]{:S(2)}) collective-permute-start(bf16[192,1024]{1,0:T(8,128)(2,1)S(1)} %get-tuple-element.62), channel_id=1, source_target_pairs={{0,16},{1,17},{2,18},{3,19},{4,20},{5,21},{6,22},{7,23},{8,24},{9,... | collective-permute-start | bytes 1179656 | tf_op jit(solution)/shard_map/ppermute | solution.py:53
  93.4 12.6 %collective-permute-start.27 = (bf16[192,1024]{1,0:T(8,128)(2,1)}, bf16[192,1024]{1,0:T(8,128)(2,1)}, u32[]{:S(2)}, u32[]{:S(2)}) collective-permute-start(bf16[192,1024]{1,0:T(8,128)(2,1)} %get-tuple-element.65), channel_id=1, source_target_pairs={{0,112},{1,113},{2,114},{3,115},{4,116},{5,117},{6,118},{7,119},{8... | collective-permute-start | bytes 1179656 | tf_op jit(solution)/shard_map/ppermute | solution.py:53
  95.5 16.0 %all-to-all-start.2 = ((bf16[16,32,128]{2,1,0:T(8,128)(2,1)}), bf16[16,32,128]{2,1,0:T(8,128)(2,1)S(1)}, u32[]{:S(2)}, u32[]{:S(2)}) async-start(bf16[16,32,128]{2,1,0:T(8,128)(2,1)} %merge_queries.1), calls=%async_computation.2 | async-start | bytes 262144 | tf_op jit(solution)/shard_map/all_to_all | solution.py:400
  104.5 13.9 %collective-permute-start.26 = (bf16[192,1024]{1,0:T(8,128)(2,1)S(1)}, bf16[192,1024]{1,0:T(8,128)(2,1)}, u32[]{:S(2)}, u32[]{:S(2)}) collective-permute-start(bf16[192,1024]{1,0:T(8,128)(2,1)S(1)} %add_convert_fusion.3.rest_0_), channel_id=1, source_target_pairs={{0,16},{1,17},{2,18},{3,19},{4,20},{5,21},{6,22},{7,23},{8,24},{9,... | collective-permute-start | bytes 1179656 | tf_op jit(solution)/shard_map/ppermute | solution.py:53
  107.2 13.4 %collective-permute-start.28 = (bf16[192,1024]{1,0:T(8,128)(2,1)S(1)}, bf16[192,1024]{1,0:T(8,128)(2,1)}, u32[]{:S(2)}, u32[]{:S(2)}) collective-permute-start(bf16[192,1024]{1,0:T(8,128)(2,1)S(1)} %add_convert_fusion.1.rest_1_), channel_id=1, source_target_pairs={{0,112},{1,113},{2,114},{3,115},{4,116},{5,117},{6,118},{7,119},{8... | collective-permute-start | bytes 1179656 | tf_op jit(solution)/shard_map/ppermute | solution.py:53
  112.2 14.6 %all-to-all-start.3 = ((bf16[16,32,128]{2,1,0:T(8,128)(2,1)}), bf16[16,32,128]{2,1,0:T(8,128)(2,1)S(1)}, u32[]{:S(2)}, u32[]{:S(2)}) async-start(bf16[16,32,128]{2,1,0:T(8,128)(2,1)} %states_after.1), calls=%async_computation.3 | async-start | bytes 262144 | tf_op jit(solution)/shard_map/all_to_all | solution.py:400
  119.5 13.1 %collective-permute-start.31 = (bf16[192,1024]{1,0:T(8,128)(2,1)S(1)}, bf16[192,1024]{1,0:T(8,128)(2,1)}, u32[]{:S(2)}, u32[]{:S(2)}) collective-permute-start(bf16[192,1024]{1,0:T(8,128)(2,1)S(1)} %add_convert_fusion.2.rest_0_), channel_id=1, source_target_pairs={{0,16},{1,17},{2,18},{3,19},{4,20},{5,21},{6,22},{7,23},{8,24},{9,... | collective-permute-start | bytes 1179656 | tf_op jit(solution)/shard_map/ppermute | solution.py:53
  121.8 10.7 %collective-permute-start.32 = (bf16[192,1024]{1,0:T(8,128)(2,1)S(1)}, bf16[192,1024]{1,0:T(8,128)(2,1)}, u32[]{:S(2)}, u32[]{:S(2)}) collective-permute-start(bf16[192,1024]{1,0:T(8,128)(2,1)S(1)} %add_convert_fusion.rest_1_), channel_id=1, source_target_pairs={{0,112},{1,113},{2,114},{3,115},{4,116},{5,117},{6,118},{7,119},{8... | collective-permute-start | bytes 1179656 | tf_op jit(solution)/shard_map/ppermute | solution.py:53
  (31 other events, 237.0 us)

commit v13 on v9

--- a/solution.py
+++ b/solution.py
@@ -539,7 +539,7 @@
         (log_decay, key_proj, value_proj, inner_k, inner_v, after_own, after_other),
         scratch=[pltpu.VMEM((cols, HEAD_DIM), BF)],
     )
-    grad_weight = call(last_add_kernel, piece, "ring_sum_0", 400_000, 2_000_000, (part[0], up, down))
+    grad_weight = (part[0].astype(F32) + (up.astype(F32) + down.astype(F32))).astype(BF)
     return grad_queries, grad_keys, grad_values, grad_weight
 
 

time: 132 us -> 132 us (level)
  Pallas kernels: 24.7 us -> 22.6 us
  other arithmetic: 4.62 us -> 6.68 us
    convert_element_type x0 -> x1, other arithmetic: none -> 2.06 us  [body(): (part[0].astype(F32) + (up.astype(F32) + down.astype(F32))).astype(BF)]
    pallas_call x16 -> x15, Pallas kernels: 17.4 us -> 15.4 us  [call(): pl.pallas_call(body, in_specs=[pl.BlockSpec(a.shape, lambda n=a.ndim: (0,...]
where the time goes in v13:
time: 132 us; the launch traced here: 131 us
  starting transfers between devices  69.8 us (53%)
  waiting for transfers between devices  24.9 us (19%)
  Pallas kernels  22.6 us (17%)
  other arithmetic  6.68 us (5%)
  local copies, waits for them, and re-layouts  6.14 us (5%)
    ppermute x33, starting transfers between devices, send(): return lax.ppermute(array, AXES, table)  43.2 us
    all_to_all x4, starting transfers between devices, exchange(): lax.all_to_all(array, 'seq', 0, 0, tiled=True, axis_index_groups=CHIP_GRO...  26.6 us
    ppermute x33, waiting for transfers between devices, send(): return lax.ppermute(array, AXES, table)  19.5 us
    pallas_call x15, Pallas kernels, call(): pl.pallas_call(body, in_specs=[pl.BlockSpec(a.shape, lambda n=a.ndim: (0,...  15.4 us
    all_to_all x4, waiting for transfers between devices, exchange(): lax.all_to_all(array, 'seq', 0, 0, tiled=True, axis_index_groups=CHIP_GRO...  5.35 us
    convert_element_type x4, other arithmetic, add_pieces(): return (a.astype(F32) + b.astype(F32)).astype(BF)  4.62 us
    unnamed x44, local copies, waits for them, and re-layouts  4.26 us
    pallas_call x1, Pallas kernels, body(): pl.pallas_call(project_kernel, out_shape=[row32, row32, row, row], scratc...  3.02 us
  transfers between devices with their start and end apart: 37, of which 14 were waited for; matrix products, arithmetic and copies ran while one was open for 5% of the time, Pallas kernels for 17%

profile of v13, /device:TPU:8, one launch (start us, length us, event | category | flops | bytes accessed | tf_op | source)
XLA Modules:
  0.0 131.2 jit_solution(13118014683278901424)
XLA Ops:
  0.6 2.0 %collective-permute-start = (bf16[192,1024]{1,0:T(8,128)(2,1)}, bf16[192,1024]{1,0:T(8,128)(2,1)S(1)}, u32[]{:S(2)}, u32[]{:S(2)}) collective-permute-start(bf16[192,1024]{1,0:T(8,128)(2,1)} %refs_0_.1), channel_id=1, source_target_pairs={{0,16},{1,17},{2,18},{3,19},{4,20},{5,21},{6,22},{7,23},{8,24},{9,... | collective-permute-start | bytes 1179656 | tf_op jit(solution)/shard_map/ppermute | solution.py:53
  2.6 4.0 %collective-permute-start.1 = (bf16[192,1024]{1,0:T(8,128)(2,1)}, bf16[192,1024]{1,0:T(8,128)(2,1)}, u32[]{:S(2)}, u32[]{:S(2)}) collective-permute-start(bf16[192,1024]{1,0:T(8,128)(2,1)} %refs_0_.1), channel_id=1, source_target_pairs={{0,112},{1,113},{2,114},{3,115},{4,116},{5,117},{6,118},{7,119},{8... | collective-permute-start | bytes 1179656 | tf_op jit(solution)/shard_map/ppermute | solution.py:53
  9.2 2.4 %key_terms.1 = (bf16[528,128]{1,0:T(8,128)(2,1)S(1)}, bf16[528,128]{1,0:T(8,128)(2,1)S(1)}) custom-call(f32[8,128]{1,0:T(8,128)S(1)} %bitcast.5, bf16[128,1024]{1,0:T(8,128)(2,1)S(1)} %copy-done, bf16[128,1024]{1,0:T(8,128)(2,1)S(1)} %copy-done.2), custom_call_target="tpu_custom_call" | custom-call | flops 40000000 | bytes 1000000 | tf_op jit(solution)/shard_map/key_terms/pallas_call | solution.py:418
  13.8 7.2 %all-to-all-start = ((bf16[16,48,128]{2,1,0:T(8,128)(2,1)}), bf16[16,48,128]{2,1,0:T(8,128)(2,1)S(1)}, u32[]{:S(2)}, u32[]{:S(2)}) async-start(bf16[16,48,128]{2,1,0:T(8,128)(2,1)} %merge_keys.1.rest_2_), calls=%async_computation | async-start | bytes 393216 | tf_op jit(solution)/shard_map/all_to_all | solution.py:400
  22.4 2.8 %collective-permute-start.3 = (bf16[384,128]{1,0:T(8,128)(2,1)S(1)}, bf16[384,128]{1,0:T(8,128)(2,1)S(1)}, u32[]{:S(2)}, u32[]{:S(2)}) collective-permute-start(bf16[384,128]{1,0:T(8,128)(2,1)S(1)} %get-tuple-element.42), channel_id=1, source_target_pairs={{0,0},{1,1},{2,2},{3,3},{4,128},{5,129},{6,130},{7,131},{8,8},{9,9... | collective-permute-start | bytes 294920 | tf_op jit(solution)/shard_map/ppermute | solution.py:53
  25.4 3.2 %collective-permute-start.6 = (bf16[384,128]{1,0:T(8,128)(2,1)S(1)}, bf16[384,128]{1,0:T(8,128)(2,1)S(1)}, u32[]{:S(2)}, u32[]{:S(2)}) collective-permute-start(bf16[384,128]{1,0:T(8,128)(2,1)S(1)} %get-tuple-element.43), channel_id=1, source_target_pairs={{0,12},{1,13},{2,14},{3,15},{4,140},{5,141},{6,142},{7,143},{8,4},... | collective-permute-start | bytes 294920 | tf_op jit(solution)/shard_map/ppermute | solution.py:53
  28.6 1.5 %collective-permute-start.12 = (bf16[192,1024]{1,0:T(8,128)(2,1)S(1)}, bf16[192,1024]{1,0:T(8,128)(2,1)S(1)}, u32[]{:S(2)}, u32[]{:S(2)}) collective-permute-start(bf16[192,1024]{1,0:T(8,128)(2,1)S(1)} %collective-permute-done.rest_0_.refs_8_), channel_id=1, source_target_pairs={{0,16},{1,17},{2,18},{3,19},{4,20},{5,21},{6,22},{7,23},{8,24},{9,... | collective-permute-start | bytes 1179656 | tf_op jit(solution)/shard_map/ppermute | solution.py:53
  31.0 4.4 %collective-permute-start.10 = (bf16[192,1024]{1,0:T(8,128)(2,1)}, bf16[192,1024]{1,0:T(8,128)(2,1)S(1)}, u32[]{:S(2)}, u32[]{:S(2)}) collective-permute-start(bf16[192,1024]{1,0:T(8,128)(2,1)} %collective-permute-done.1.rest_1_.refs_1_), channel_id=1, source_target_pairs={{0,112},{1,113},{2,114},{3,115},{4,116},{5,117},{6,118},{7,119},{8... | collective-permute-start | bytes 1179656 | tf_op jit(solution)/shard_map/ppermute | solution.py:53
  36.4 1.6 %collective-permute-start.7 = (bf16[384,512]{1,0:T(8,128)(2,1)S(1)}, bf16[384,512]{1,0:T(8,128)(2,1)S(1)}, u32[]{:S(2)}, u32[]{:S(2)}) collective-permute-start(bf16[384,512]{1,0:T(8,128)(2,1)S(1)} %collect.1.own_ref), channel_id=1, source_target_pairs={{0,1},{1,2},{2,3},{3,0},{4,5},{5,6},{6,7},{7,4},{8,9},{9,10},{10,1... | collective-permute-start | bytes 1179656 | tf_op jit(solution)/shard_map/ppermute | solution.py:53
  37.9 7.9 %all-to-all-start.1 = ((bf16[16,32,128]{2,1,0:T(8,128)(2,1)}), bf16[16,32,128]{2,1,0:T(8,128)(2,1)S(1)}, u32[]{:S(2)}, u32[]{:S(2)}) async-start(bf16[16,32,128]{2,1,0:T(8,128)(2,1)} %states_before.1.rest_0_), calls=%async_computation.1 | async-start | bytes 262144 | tf_op jit(solution)/shard_map/all_to_all | solution.py:400
  45.9 1.7 %collective-permute-start.8 = (bf16[384,512]{1,0:T(8,128)(2,1)S(1)}, bf16[384,512]{1,0:T(8,128)(2,1)S(1)}, u32[]{:S(2)}, u32[]{:S(2)}) collective-permute-start(bf16[384,512]{1,0:T(8,128)(2,1)S(1)} %collect.1.own_ref), channel_id=1, source_target_pairs={{0,3},{1,0},{2,1},{3,2},{4,7},{5,4},{6,5},{7,6},{8,11},{9,8},{10,9... | collective-permute-start | bytes 1179656 | tf_op jit(solution)/shard_map/ppermute | solution.py:53
  47.6 1.5 %collective-permute-start.13 = (bf16[192,1024]{1,0:T(8,128)(2,1)S(1)}, bf16[192,1024]{1,0:T(8,128)(2,1)}, u32[]{:S(2)}, u32[]{:S(2)}) collective-permute-start(bf16[192,1024]{1,0:T(8,128)(2,1)S(1)} %collective-permute-done.12.refs_7_.rest_0_), channel_id=1, source_target_pairs={{0,16},{1,17},{2,18},{3,19},{4,20},{5,21},{6,22},{7,23},{8,24},{9,... | collective-permute-start | bytes 1179656 | tf_op jit(solution)/shard_map/ppermute | solution.py:53
  49.1 1.8 %collective-permute-start.11 = (bf16[192,1024]{1,0:T(8,128)(2,1)S(1)}, bf16[192,1024]{1,0:T(8,128)(2,1)}, u32[]{:S(2)}, u32[]{:S(2)}) collective-permute-start(bf16[192,1024]{1,0:T(8,128)(2,1)S(1)} %collective-permute-done.10.refs_2_.rest_1_), channel_id=1, source_target_pairs={{0,112},{1,113},{2,114},{3,115},{4,116},{5,117},{6,118},{7,119},{8... | collective-permute-start | bytes 1179656 | tf_op jit(solution)/shard_map/ppermute | solution.py:53
  51.1 2.7 %all-to-all-done.1 = bf16[16,32,128]{2,1,0:T(8,128)(2,1)S(1)} async-done(((bf16[16,32,128]{2,1,0:T(8,128)(2,1)}), bf16[16,32,128]{2,1,0:T(8,128)(2,1)S(1)}, u32[]{:S(2)}, u32[]{:S(2)}) %all-to-all-start.1) | async-done | bytes 131104 | tf_op jit(solution)/shard_map/all_to_all | solution.py:400
  54.1 6.6 %collective-permute-done.13.refs_6_ = bf16[192,1024]{1,0:T(8,128)(2,1)} collective-permute-done((bf16[192,1024]{1,0:T(8,128)(2,1)S(1)}, bf16[192,1024]{1,0:T(8,128)(2,1)}, u32[]{:S(2)}, u32[]{:S(2)}) %collective-permute-start.13) | collective-permute-done | bytes 393248 | tf_op jit(solution)/shard_map/ppermute | solution.py:53
  62.9 3.3 %collective-permute-start.15 = (bf16[96,1024]{1,0:T(8,128)(2,1)S(1)}, bf16[96,1024]{1,0:T(8,128)(2,1)S(1)}, u32[]{:S(2)}, u32[]{:S(2)}) collective-permute-start(bf16[96,1024]{1,0:T(8,128)(2,1)S(1)} %slice.9), channel_id=1, source_target_pairs={{0,112},{1,113},{2,114},{3,115},{4,116},{5,117},{6,118},{7,119},{8... | collective-permute-start | bytes 589832 | tf_op jit(solution)/shard_map/ppermute | solution.py:53
  68.7 1.6 %assemble.1 = (bf16[1536,512]{1,0:T(8,128)(2,1)S(1)}, bf16[512,1536]{1,0:T(8,128)(2,1)S(1)}) custom-call(bf16[384,512]{1,0:T(8,128)(2,1)S(1)} %collect.1.own_ref, bf16[384,512]{1,0:T(8,128)(2,1)S(1)} %collective-permute-done.7.left_ref, bf16[384,512]{1,0:T(8,128)(2,1)S(1)} %collective-permute-done.8.right_ref, ...), custom_call_target="tpu_custom_call" | custom-call | flops 1000000 | bytes 5000000 | tf_op jit(solution)/shard_map/assemble/pallas_call | solution.py:383
  70.3 3.0 %project.1 = (f32[128,1024]{1,0:T(8,128)S(1)}, f32[128,1024]{1,0:T(8,128)S(1)}, bf16[128,1024]{1,0:T(8,128)(2,1)S(1)}, bf16[128,1024]{1,0:T(8,128)(2,1)S(1)}) custom-call(bf16[512,1536]{1,0:T(8,128)(2,1)S(1)} %get-tuple-element.44.block_ref, bf16[192,1024]{1,0:T(8,128)(2,1)S(1)} %copy-done.18, bf16[192,1024]{1,0:T(8,128)(2,1)} %collective-permute-done.1.rest_1_.refs_1_, ...), custom_call_target="tpu_custom_call" | custom-call | flops 1600000000 | bytes 6000000 | tf_op jit(solution)/shard_map/project/pallas_call | solution.py:476
  76.7 1.9 %weight_partial.1 = (bf16[192,1024]{1,0:T(8,128)(2,1)S(1)}, bf16[192,1024]{1,0:T(8,128)(2,1)S(1)}, bf16[192,1024]{1,0:T(8,128)(2,1)S(1)}, bf16[192,1024]{1,0:T(8...) custom-call(bf16[1536,512]{1,0:T(8,128)(2,1)S(1)} %get-tuple-element, ...), custom_call_target="tpu_custom_call" | custom-call | flops 1600000000 | bytes 6000000 | tf_op jit(solution)/shard_map/weight_partial/pallas_call | solution.py:491
  78.7 3.2 %collective-permute-start.24 = (bf16[96,1024]{1,0:T(8,128)(2,1)S(1)}, bf16[96,1024]{1,0:T(8,128)(2,1)S(1)}, u32[]{:S(2)}, u32[]{:S(2)}) collective-permute-start(bf16[96,1024]{1,0:T(8,128)(2,1)S(1)} %get-tuple-element.61), channel_id=1, source_target_pairs={{0,112},{1,113},{2,114},{3,115},{4,116},{5,117},{6,118},{7,119},{8... | collective-permute-start | bytes 589832 | tf_op jit(solution)/shard_map/ppermute | solution.py:53
  81.9 2.1 %collective-permute-done.18.other_ref = bf16[128,1024]{1,0:T(8,128)(2,1)S(1)} collective-permute-done((bf16[128,1024]{1,0:T(8,128)(2,1)S(1)}, bf16[128,1024]{1,0:T(8,128)(2,1)S(1)}, u32[]{:S(2)}, u32[]{:S(2)}) %collective-permute-start.18) | collective-permute-done | bytes 262176 | tf_op jit(solution)/shard_map/ppermute | solution.py:53
  84.0 2.3 %query_terms.1 = (bf16[128,1024]{1,0:T(8,128)(2,1)S(1)}, bf16[512,128]{1,0:T(8,128)(2,1)S(1)}, bf16[512,128]{1,0:T(8,128)(2,1)S(1)}) custom-call(f32[8,128]{1,0:T(8,128)S(1)} %bitcast.7, bf16[128,1024]{1,0:T(8,128)(2,1)S(1)} %copy-done.4, f32[128,1024]{1,0:T(8,128)S(1)} %get-tuple-element.45.own_ref, bf16[128,1024]{1,0:T(8,128)(2,1)S(1)} %collective-permute-done.16.core_ref, ...), custom_call_target="tpu_custom_call" | custom-call | flops 40000000 | bytes 1000000 | tf_op jit(solution)/shard_map/query_terms/pallas_call | solution.py:383
  87.7 2.9 %collective-permute-start.27 = (bf16[192,1024]{1,0:T(8,128)(2,1)S(1)}, bf16[192,1024]{1,0:T(8,128)(2,1)}, u32[]{:S(2)}, u32[]{:S(2)}) collective-permute-start(bf16[192,1024]{1,0:T(8,128)(2,1)S(1)} %get-tuple-element.65), channel_id=1, source_target_pairs={{0,112},{1,113},{2,114},{3,115},{4,116},{5,117},{6,118},{7,119},{8... | collective-permute-start | bytes 1179656 | tf_op jit(solution)/shard_map/ppermute | solution.py:53
  90.6 1.3 %collective-permute-done.29.other_ref = bf16[512,128]{1,0:T(8,128)(2,1)S(1)} collective-permute-done((bf16[512,128]{1,0:T(8,128)(2,1)S(1)}, bf16[512,128]{1,0:T(8,128)(2,1)S(1)}, u32[]{:S(2)}, u32[]{:S(2)}) %collective-permute-start.29) | collective-permute-done | bytes 131104 | tf_op jit(solution)/shard_map/ppermute | solution.py:53
  92.7 6.6 %all-to-all-start.2 = ((bf16[16,32,128]{2,1,0:T(8,128)(2,1)}), bf16[16,32,128]{2,1,0:T(8,128)(2,1)S(1)}, u32[]{:S(2)}, u32[]{:S(2)}) async-start(bf16[16,32,128]{2,1,0:T(8,128)(2,1)} %merge_queries.1), calls=%async_computation.2 | async-start | bytes 262144 | tf_op jit(solution)/shard_map/all_to_all | solution.py:400
  100.4 2.8 %collective-permute-start.28 = (bf16[192,1024]{1,0:T(8,128)(2,1)S(1)}, bf16[192,1024]{1,0:T(8,128)(2,1)}, u32[]{:S(2)}, u32[]{:S(2)}) collective-permute-start(bf16[192,1024]{1,0:T(8,128)(2,1)S(1)} %add_convert_fusion.2.rest_1_), channel_id=1, source_target_pairs={{0,112},{1,113},{2,114},{3,115},{4,116},{5,117},{6,118},{7,119},{8... | collective-permute-start | bytes 1179656 | tf_op jit(solution)/shard_map/ppermute | solution.py:53
  104.5 2.6 %all-to-all-done.2.terms_ref = bf16[16,32,128]{2,1,0:T(8,128)(2,1)S(1)} async-done(((bf16[16,32,128]{2,1,0:T(8,128)(2,1)}), bf16[16,32,128]{2,1,0:T(8,128)(2,1)S(1)}, u32[]{:S(2)}, u32[]{:S(2)}) %all-to-all-start.2) | async-done | bytes 131104 | tf_op jit(solution)/shard_map/all_to_all | solution.py:400
  107.9 4.8 %all-to-all-start.3 = ((bf16[16,32,128]{2,1,0:T(8,128)(2,1)}), bf16[16,32,128]{2,1,0:T(8,128)(2,1)S(1)}, u32[]{:S(2)}, u32[]{:S(2)}) async-start(bf16[16,32,128]{2,1,0:T(8,128)(2,1)} %states_after.1), calls=%async_computation.3 | async-start | bytes 262144 | tf_op jit(solution)/shard_map/all_to_all | solution.py:400
  114.1 2.7 %collective-permute-start.32 = (bf16[192,1024]{1,0:T(8,128)(2,1)S(1)}, bf16[192,1024]{1,0:T(8,128)(2,1)}, u32[]{:S(2)}, u32[]{:S(2)}) collective-permute-start(bf16[192,1024]{1,0:T(8,128)(2,1)S(1)} %add_convert_fusion.1.rest_1_), channel_id=1, source_target_pairs={{0,112},{1,113},{2,114},{3,115},{4,116},{5,117},{6,118},{7,119},{8... | collective-permute-start | bytes 1179656 | tf_op jit(solution)/shard_map/ppermute | solution.py:53
  118.6 2.7 %inner_grads.1 = (bf16[128,1024]{1,0:T(8,128)(2,1)}, f32[128,1024]{1,0:T(8,128)S(1)}, f32[128,1024]{1,0:T(8,128)S(1)}) custom-call(f32[8,128]{1,0:T(8,128)S(1)} %bitcast.8, bf16[128,1024]{1,0:T(8,128)(2,1)S(1)} %copy-done.4, bf16[128,1024]{1,0:T(8,128)(2,1)S(1)} %copy-done.1, bf16[128,1024]{1,0:T(8,128)(2,1)S(1)} %copy-done.3, ...), custom_call_target="tpu_custom_call" | custom-call | flops 200000000 | bytes 3000000 | tf_op jit(solution)/shard_map/inner_grads/pallas_call | solution.py:383
  125.9 3.2 %collective-permute-done.31 = bf16[192,1024]{1,0:T(8,128)(2,1)} collective-permute-done((bf16[192,1024]{1,0:T(8,128)(2,1)S(1)}, bf16[192,1024]{1,0:T(8,128)(2,1)}, u32[]{:S(2)}, u32[]{:S(2)}) %collective-permute-start.31) | collective-permute-done | bytes 393248 | tf_op jit(solution)/shard_map/ppermute | solution.py:53
  129.1 2.1 %add_convert_fusion = bf16[192,1024]{1,0:T(8,128)(2,1)} fusion(bf16[192,1024]{1,0:T(8,128)(2,1)} %collective-permute-done.32, bf16[192,1024]{1,0:T(8,128)(2,1)} %collective-permute-done.31, bf16[192,1024]{1,0:T(8,128)(2,1)S(1)} %copy-done.6), kind=kLoop, calls=%fused_computation | loop fusion | flops 1179648 | bytes 1572864 | tf_op jit(solution)/shard_map/convert_element_type | solution.py:542
  (111 shorter events, 29.7 us)
Async XLA Ops:
  0.6 20.4 %collective-permute-start = (bf16[192,1024]{1,0:T(8,128)(2,1)}, bf16[192,1024]{1,0:T(8,128)(2,1)S(1)}, u32[]{:S(2)}, u32[]{:S(2)}) collective-permute-start(bf16[192,1024]{1,0:T(8,128)(2,1)} %refs_0_.1), channel_id=1, source_target_pairs={{0,16},{1,17},{2,18},{3,19},{4,20},{5,21},{6,22},{7,23},{8,24},{9,... | collective-permute-start | bytes 1179656 | tf_op jit(solution)/shard_map/ppermute | solution.py:53
  2.6 18.4 %collective-permute-start.1 = (bf16[192,1024]{1,0:T(8,128)(2,1)}, bf16[192,1024]{1,0:T(8,128)(2,1)}, u32[]{:S(2)}, u32[]{:S(2)}) collective-permute-start(bf16[192,1024]{1,0:T(8,128)(2,1)} %refs_0_.1), channel_id=1, source_target_pairs={{0,112},{1,113},{2,114},{3,115},{4,116},{5,117},{6,118},{7,119},{8... | collective-permute-start | bytes 1179656 | tf_op jit(solution)/shard_map/ppermute | solution.py:53
  13.8 16.2 %all-to-all-start = ((bf16[16,48,128]{2,1,0:T(8,128)(2,1)}), bf16[16,48,128]{2,1,0:T(8,128)(2,1)S(1)}, u32[]{:S(2)}, u32[]{:S(2)}) async-start(bf16[16,48,128]{2,1,0:T(8,128)(2,1)} %merge_keys.1.rest_2_), calls=%async_computation | async-start | bytes 393216 | tf_op jit(solution)/shard_map/all_to_all | solution.py:400
  22.4 8.6 %collective-permute-start.3 = (bf16[384,128]{1,0:T(8,128)(2,1)S(1)}, bf16[384,128]{1,0:T(8,128)(2,1)S(1)}, u32[]{:S(2)}, u32[]{:S(2)}) collective-permute-start(bf16[384,128]{1,0:T(8,128)(2,1)S(1)} %get-tuple-element.42), channel_id=1, source_target_pairs={{0,0},{1,1},{2,2},{3,3},{4,128},{5,129},{6,130},{7,131},{8,8},{9,9... | collective-permute-start | bytes 294920 | tf_op jit(solution)/shard_map/ppermute | solution.py:53
  25.2 10.1 %collective-permute-start.4 = (bf16[384,128]{1,0:T(8,128)(2,1)S(1)}, bf16[384,128]{1,0:T(8,128)(2,1)S(1)}, u32[]{:S(2)}, u32[]{:S(2)}) collective-permute-start(bf16[384,128]{1,0:T(8,128)(2,1)S(1)} %get-tuple-element.42), channel_id=1, source_target_pairs={{0,4},{1,5},{2,6},{3,7},{4,132},{5,133},{6,134},{7,135},{8,12},{9,... | collective-permute-start | bytes 294920 | tf_op jit(solution)/shard_map/ppermute | solution.py:53
  25.3 10.0 %collective-permute-start.5 = (bf16[384,128]{1,0:T(8,128)(2,1)S(1)}, bf16[384,128]{1,0:T(8,128)(2,1)S(1)}, u32[]{:S(2)}, u32[]{:S(2)}) collective-permute-start(bf16[384,128]{1,0:T(8,128)(2,1)S(1)} %get-tuple-element.43), channel_id=1, source_target_pairs={{0,8},{1,9},{2,10},{3,11},{4,136},{5,137},{6,138},{7,139},{8,0},{9... | collective-permute-start | bytes 294920 | tf_op jit(solution)/shard_map/ppermute | solution.py:53
  25.4 9.9 %collective-permute-start.6 = (bf16[384,128]{1,0:T(8,128)(2,1)S(1)}, bf16[384,128]{1,0:T(8,128)(2,1)S(1)}, u32[]{:S(2)}, u32[]{:S(2)}) collective-permute-start(bf16[384,128]{1,0:T(8,128)(2,1)S(1)} %get-tuple-element.43), channel_id=1, source_target_pairs={{0,12},{1,13},{2,14},{3,15},{4,140},{5,141},{6,142},{7,143},{8,4},... | collective-permute-start | bytes 294920 | tf_op jit(solution)/shard_map/ppermute | solution.py:53
  28.6 19.0 %collective-permute-start.12 = (bf16[192,1024]{1,0:T(8,128)(2,1)S(1)}, bf16[192,1024]{1,0:T(8,128)(2,1)S(1)}, u32[]{:S(2)}, u32[]{:S(2)}) collective-permute-start(bf16[192,1024]{1,0:T(8,128)(2,1)S(1)} %collective-permute-done.rest_0_.refs_8_), channel_id=1, source_target_pairs={{0,16},{1,17},{2,18},{3,19},{4,20},{5,21},{6,22},{7,23},{8,24},{9,... | collective-permute-start | bytes 1179656 | tf_op jit(solution)/shard_map/ppermute | solution.py:53
  31.0 18.1 %collective-permute-start.10 = (bf16[192,1024]{1,0:T(8,128)(2,1)}, bf16[192,1024]{1,0:T(8,128)(2,1)S(1)}, u32[]{:S(2)}, u32[]{:S(2)}) collective-permute-start(bf16[192,1024]{1,0:T(8,128)(2,1)} %collective-permute-done.1.rest_1_.refs_1_), channel_id=1, source_target_pairs={{0,112},{1,113},{2,114},{3,115},{4,116},{5,117},{6,118},{7,119},{8... | collective-permute-start | bytes 1179656 | tf_op jit(solution)/shard_map/ppermute | solution.py:53
  36.4 14.5 %collective-permute-start.7 = (bf16[384,512]{1,0:T(8,128)(2,1)S(1)}, bf16[384,512]{1,0:T(8,128)(2,1)S(1)}, u32[]{:S(2)}, u32[]{:S(2)}) collective-permute-start(bf16[384,512]{1,0:T(8,128)(2,1)S(1)} %collect.1.own_ref), channel_id=1, source_target_pairs={{0,1},{1,2},{2,3},{3,0},{4,5},{5,6},{6,7},{7,4},{8,9},{9,10},{10,1... | collective-permute-start | bytes 1179656 | tf_op jit(solution)/shard_map/ppermute | solution.py:53
  37.9 15.9 %all-to-all-start.1 = ((bf16[16,32,128]{2,1,0:T(8,128)(2,1)}), bf16[16,32,128]{2,1,0:T(8,128)(2,1)S(1)}, u32[]{:S(2)}, u32[]{:S(2)}) async-start(bf16[16,32,128]{2,1,0:T(8,128)(2,1)} %states_before.1.rest_0_), calls=%async_computation.1 | async-start | bytes 262144 | tf_op jit(solution)/shard_map/all_to_all | solution.py:400
  45.9 22.8 %collective-permute-start.8 = (bf16[384,512]{1,0:T(8,128)(2,1)S(1)}, bf16[384,512]{1,0:T(8,128)(2,1)S(1)}, u32[]{:S(2)}, u32[]{:S(2)}) collective-permute-start(bf16[384,512]{1,0:T(8,128)(2,1)S(1)} %collect.1.own_ref), channel_id=1, source_target_pairs={{0,3},{1,0},{2,1},{3,2},{4,7},{5,4},{6,5},{7,6},{8,11},{9,8},{10,9... | collective-permute-start | bytes 1179656 | tf_op jit(solution)/shard_map/ppermute | solution.py:53
  47.6 13.1 %collective-permute-start.13 = (bf16[192,1024]{1,0:T(8,128)(2,1)S(1)}, bf16[192,1024]{1,0:T(8,128)(2,1)}, u32[]{:S(2)}, u32[]{:S(2)}) collective-permute-start(bf16[192,1024]{1,0:T(8,128)(2,1)S(1)} %collective-permute-done.12.refs_7_.rest_0_), channel_id=1, source_target_pairs={{0,16},{1,17},{2,18},{3,19},{4,20},{5,21},{6,22},{7,23},{8,24},{9,... | collective-permute-start | bytes 1179656 | tf_op jit(solution)/shard_map/ppermute | solution.py:53
  49.1 12.9 %collective-permute-start.11 = (bf16[192,1024]{1,0:T(8,128)(2,1)S(1)}, bf16[192,1024]{1,0:T(8,128)(2,1)}, u32[]{:S(2)}, u32[]{:S(2)}) collective-permute-start(bf16[192,1024]{1,0:T(8,128)(2,1)S(1)} %collective-permute-done.10.refs_2_.rest_1_), channel_id=1, source_target_pairs={{0,112},{1,113},{2,114},{3,115},{4,116},{5,117},{6,118},{7,119},{8... | collective-permute-start | bytes 1179656 | tf_op jit(solution)/shard_map/ppermute | solution.py:53
  50.9 17.8 %collective-permute-start.9 = (bf16[384,512]{1,0:T(8,128)(2,1)S(1)}, bf16[384,512]{1,0:T(8,128)(2,1)}, u32[]{:S(2)}, u32[]{:S(2)}) collective-permute-start(bf16[384,512]{1,0:T(8,128)(2,1)S(1)} %collective-permute-done.7.left_ref), channel_id=1, source_target_pairs={{0,1},{1,2},{2,3},{3,0},{4,5},{5,6},{6,7},{7,4},{8,9},{9,10},{10,1... | collective-permute-start | bytes 1179656 | tf_op jit(solution)/shard_map/ppermute | solution.py:53
  54.0 12.2 %collective-permute-start.19 = (bf16[512,128]{1,0:T(8,128)(2,1)S(1)}, bf16[512,128]{1,0:T(8,128)(2,1)S(1)}, u32[]{:S(2)}, u32[]{:S(2)}) collective-permute-start(bf16[512,128]{1,0:T(8,128)(2,1)S(1)} %get-tuple-element.51), channel_id=1, source_target_pairs={{0,8},{1,9},{2,10},{3,11},{4,12},{5,13},{6,14},{7,15},{8,0},{9,1},... | collective-permute-start | bytes 393224 | tf_op jit(solution)/shard_map/ppermute | solution.py:53
  61.7 8.6 %collective-permute-start.14 = (bf16[96,1024]{1,0:T(8,128)(2,1)S(1)}, bf16[96,1024]{1,0:T(8,128)(2,1)S(1)}, u32[]{:S(2)}, u32[]{:S(2)}) collective-permute-start(bf16[96,1024]{1,0:T(8,128)(2,1)S(1)} %slice.8), channel_id=1, source_target_pairs={{0,16},{1,17},{2,18},{3,19},{4,20},{5,21},{6,22},{7,23},{8,24},{9,... | collective-permute-start | bytes 589832 | tf_op jit(solution)/shard_map/ppermute | solution.py:53
  62.9 7.4 %collective-permute-start.15 = (bf16[96,1024]{1,0:T(8,128)(2,1)S(1)}, bf16[96,1024]{1,0:T(8,128)(2,1)S(1)}, u32[]{:S(2)}, u32[]{:S(2)}) collective-permute-start(bf16[96,1024]{1,0:T(8,128)(2,1)S(1)} %slice.9), channel_id=1, source_target_pairs={{0,112},{1,113},{2,114},{3,115},{4,116},{5,117},{6,118},{7,119},{8... | collective-permute-start | bytes 589832 | tf_op jit(solution)/shard_map/ppermute | solution.py:53
  68.1 7.0 %collective-permute-start.20 = (bf16[128,1024]{1,0:T(8,128)(2,1)S(1)}, bf16[128,1024]{1,0:T(8,128)(2,1)S(1)}, u32[]{:S(2)}, u32[]{:S(2)}) collective-permute-start(bf16[128,1024]{1,0:T(8,128)(2,1)S(1)} %get-tuple-element.55.own_ref), channel_id=1, source_target_pairs={{0,128},{1,129},{2,130},{3,131},{4,132},{5,133},{6,134},{7,135},{8... | collective-permute-start | bytes 786440 | tf_op jit(solution)/shard_map/ppermute | solution.py:53
  73.5 3.2 %collective-permute-start.21 = (bf16[128,1024]{1,0:T(8,128)(2,1)S(1)}, bf16[128,1024]{1,0:T(8,128)(2,1)S(1)}, u32[]{:S(2)}, u32[]{:S(2)}) collective-permute-start(bf16[128,1024]{1,0:T(8,128)(2,1)S(1)} %get-tuple-element.55.own_ref), channel_id=1, source_target_pairs={{0,8},{1,9},{2,10},{3,11},{4,12},{5,13},{6,14},{7,15},{8,0},{9,1},... | collective-permute-start | bytes 786440 | tf_op jit(solution)/shard_map/ppermute | solution.py:53
  75.1 6.8 %collective-permute-start.16 = (bf16[128,1024]{1,0:T(8,128)(2,1)S(1)}, bf16[128,1024]{1,0:T(8,128)(2,1)S(1)}, u32[]{:S(2)}, u32[]{:S(2)}) collective-permute-start(bf16[128,1024]{1,0:T(8,128)(2,1)S(1)} %get-tuple-element.46), channel_id=1, source_target_pairs={{0,8},{1,9},{2,10},{3,11},{4,12},{5,13},{6,14},{7,15},{8,0},{9,1},... | collective-permute-start | bytes 786440 | tf_op jit(solution)/shard_map/ppermute | solution.py:53
  75.7 8.3 %collective-permute-start.18 = (bf16[128,1024]{1,0:T(8,128)(2,1)S(1)}, bf16[128,1024]{1,0:T(8,128)(2,1)S(1)}, u32[]{:S(2)}, u32[]{:S(2)}) collective-permute-start(bf16[128,1024]{1,0:T(8,128)(2,1)S(1)} %sum_theirs.1.rest_0_), channel_id=1, source_target_pairs={{0,128},{1,129},{2,130},{3,131},{4,132},{5,133},{6,134},{7,135},{8... | collective-permute-start | bytes 786440 | tf_op jit(solution)/shard_map/ppermute | solution.py:53
  78.6 8.2 %collective-permute-start.23 = (bf16[96,1024]{1,0:T(8,128)(2,1)S(1)}, bf16[96,1024]{1,0:T(8,128)(2,1)S(1)}, u32[]{:S(2)}, u32[]{:S(2)}) collective-permute-start(bf16[96,1024]{1,0:T(8,128)(2,1)S(1)} %get-tuple-element.59), channel_id=1, source_target_pairs={{0,16},{1,17},{2,18},{3,19},{4,20},{5,21},{6,22},{7,23},{8,24},{9,... | collective-permute-start | bytes 589832 | tf_op jit(solution)/shard_map/ppermute | solution.py:53
  78.7 8.1 %collective-permute-start.24 = (bf16[96,1024]{1,0:T(8,128)(2,1)S(1)}, bf16[96,1024]{1,0:T(8,128)(2,1)S(1)}, u32[]{:S(2)}, u32[]{:S(2)}) collective-permute-start(bf16[96,1024]{1,0:T(8,128)(2,1)S(1)} %get-tuple-element.61), channel_id=1, source_target_pairs={{0,112},{1,113},{2,114},{3,115},{4,116},{5,117},{6,118},{7,119},{8... | collective-permute-start | bytes 589832 | tf_op jit(solution)/shard_map/ppermute | solution.py:53
  87.7 11.6 %collective-permute-start.27 = (bf16[192,1024]{1,0:T(8,128)(2,1)S(1)}, bf16[192,1024]{1,0:T(8,128)(2,1)}, u32[]{:S(2)}, u32[]{:S(2)}) collective-permute-start(bf16[192,1024]{1,0:T(8,128)(2,1)S(1)} %get-tuple-element.65), channel_id=1, source_target_pairs={{0,112},{1,113},{2,114},{3,115},{4,116},{5,117},{6,118},{7,119},{8... | collective-permute-start | bytes 1179656 | tf_op jit(solution)/shard_map/ppermute | solution.py:53
  90.6 12.6 %collective-permute-start.25 = (bf16[192,1024]{1,0:T(8,128)(2,1)}, bf16[192,1024]{1,0:T(8,128)(2,1)}, u32[]{:S(2)}, u32[]{:S(2)}) collective-permute-start(bf16[192,1024]{1,0:T(8,128)(2,1)} %get-tuple-element.62), channel_id=1, source_target_pairs={{0,16},{1,17},{2,18},{3,19},{4,20},{5,21},{6,22},{7,23},{8,24},{9,... | collective-permute-start | bytes 1179656 | tf_op jit(solution)/shard_map/ppermute | solution.py:53
  92.7 14.5 %all-to-all-start.2 = ((bf16[16,32,128]{2,1,0:T(8,128)(2,1)}), bf16[16,32,128]{2,1,0:T(8,128)(2,1)S(1)}, u32[]{:S(2)}, u32[]{:S(2)}) async-start(bf16[16,32,128]{2,1,0:T(8,128)(2,1)} %merge_queries.1), calls=%async_computation.2 | async-start | bytes 262144 | tf_op jit(solution)/shard_map/all_to_all | solution.py:400
  100.4 12.5 %collective-permute-start.28 = (bf16[192,1024]{1,0:T(8,128)(2,1)S(1)}, bf16[192,1024]{1,0:T(8,128)(2,1)}, u32[]{:S(2)}, u32[]{:S(2)}) collective-permute-start(bf16[192,1024]{1,0:T(8,128)(2,1)S(1)} %add_convert_fusion.2.rest_1_), channel_id=1, source_target_pairs={{0,112},{1,113},{2,114},{3,115},{4,116},{5,117},{6,118},{7,119},{8... | collective-permute-start | bytes 1179656 | tf_op jit(solution)/shard_map/ppermute | solution.py:53
  104.4 12.9 %collective-permute-start.26 = (bf16[192,1024]{1,0:T(8,128)(2,1)S(1)}, bf16[192,1024]{1,0:T(8,128)(2,1)}, u32[]{:S(2)}, u32[]{:S(2)}) collective-permute-start(bf16[192,1024]{1,0:T(8,128)(2,1)S(1)} %add_convert_fusion.4.rest_0_), channel_id=1, source_target_pairs={{0,16},{1,17},{2,18},{3,19},{4,20},{5,21},{6,22},{7,23},{8,24},{9,... | collective-permute-start | bytes 1179656 | tf_op jit(solution)/shard_map/ppermute | solution.py:53
  107.9 13.5 %all-to-all-start.3 = ((bf16[16,32,128]{2,1,0:T(8,128)(2,1)}), bf16[16,32,128]{2,1,0:T(8,128)(2,1)S(1)}, u32[]{:S(2)}, u32[]{:S(2)}) async-start(bf16[16,32,128]{2,1,0:T(8,128)(2,1)} %states_after.1), calls=%async_computation.3 | async-start | bytes 262144 | tf_op jit(solution)/shard_map/all_to_all | solution.py:400
  114.1 11.9 %collective-permute-start.32 = (bf16[192,1024]{1,0:T(8,128)(2,1)S(1)}, bf16[192,1024]{1,0:T(8,128)(2,1)}, u32[]{:S(2)}, u32[]{:S(2)}) collective-permute-start(bf16[192,1024]{1,0:T(8,128)(2,1)S(1)} %add_convert_fusion.1.rest_1_), channel_id=1, source_target_pairs={{0,112},{1,113},{2,114},{3,115},{4,116},{5,117},{6,118},{7,119},{8... | collective-permute-start | bytes 1179656 | tf_op jit(solution)/shard_map/ppermute | solution.py:53
  118.5 10.6 %collective-permute-start.31 = (bf16[192,1024]{1,0:T(8,128)(2,1)S(1)}, bf16[192,1024]{1,0:T(8,128)(2,1)}, u32[]{:S(2)}, u32[]{:S(2)}) collective-permute-start(bf16[192,1024]{1,0:T(8,128)(2,1)S(1)} %add_convert_fusion.3.rest_0_), channel_id=1, source_target_pairs={{0,16},{1,17},{2,18},{3,19},{4,20},{5,21},{6,22},{7,23},{8,24},{9,... | collective-permute-start | bytes 1179656 | tf_op jit(solution)/shard_map/ppermute | solution.py:53
  (27 other events, 144.4 us)
